TPU v7x, 512 devices: a whole 4x8x8 slice. The times are simulated.
512 devices in a mesh: leaf: 128 (over z, y, core), rhs: 4 (over x).
Axes of the slice: x: 4, y: 8, z: 8, core: 2. Of those that a mesh axis runs over, the one named last changes fastest.
Arguments:
- right_sides: float32 [64, 131072], P('rhs', 'leaf'), may hold values from -8 to 8
- leaf_inverse: float32 [131072, 1024], P('leaf', 'rhs'), may hold values from -1 to 5, as said below
- bases: bfloat16 [7, 128, 131072], P(None, None, 'leaf'), may hold values from -1 to 1
- ordering: int32 [128, 1024], P('leaf'), may hold values from 0 to 1023, as said below
Outputs:
- solution: float32 [64, 131072], P('rhs', 'leaf')
Inputs may be any that keep to these rules, and one draw needn't show every extreme that they name: `leaf_inverse`: each leaf's block of 1024 rows is symmetric positive definite. `ordering`: each row is a permutation of 0 to 1023.
All inputs are finite; a program needn't handle non-finite values.
Results may differ from a plain program's by a relative error of at most 0.0003.
Values sent between devices are 32-bit elements; how exact they have to be, the bound alone decides.
No kernel may reach another device: no remote copies, remote signals or barrier semaphores. Data moves between devices by JAX's collectives and lax.ppermute only.
A program may use at most 64 MiB of HBM per device.

v0:
```python
import jax
import jax.numpy as jnp
from jax import lax
from jax.sharding import PartitionSpec as P


def swapped(block, axis, apart):
    count = lax.axis_size(axis)
    route = []
    for low in range(count):
        high = low | 1 << apart
        if high != low and high < count:
            route += [(low, high), (high, low)]
    return lax.ppermute(block, axis, route)


def solve_factor(factor, values):
    middle = lax.linalg.triangular_solve(factor, values, left_side=True, lower=True)
    return lax.linalg.triangular_solve(factor, middle, left_side=True, lower=True, transpose_a=True)


def pair_sums(sums, bit_count):
    for step_bit in range(bit_count):
        partner = swapped((sums[0], sums[1]), "leaf", step_bit)
        sums = (sums[0] + partner[0], sums[1] + partner[1])
    return sums


def merge_level(height, level_basis, level_solved, carried):
    highest = lax.Precision.HIGHEST
    inner = (((1,), (1,)), ((), ()))
    capacity = lax.dot_general(level_basis, level_solved, inner, precision=highest)
    projected = lax.dot_general(level_basis, carried, inner, precision=highest)
    capacity, projected = pair_sums((capacity, projected), height + 1)
    capacity = capacity + jnp.eye(capacity.shape[0], dtype=jnp.float32)
    factor = jnp.linalg.cholesky(capacity)
    weights = solve_factor(factor, projected)
    update = lax.dot_general(weights, level_solved, (((0,), (0,)), ((), ())), precision=highest)
    return carried - update


def local(right_sides, leaf_inverse, bases, ordering):
    highest = lax.Precision.HIGHEST
    own_rows = right_sides.shape[0]
    piece_cols = leaf_inverse.shape[1]
    levels = bases.shape[0]
    basis_rank = bases.shape[1]
    groups = lax.axis_size("rhs")
    position = lax.axis_index("rhs")
    tree_order = jnp.take(right_sides, ordering[0], axis=1)
    tree_cols = lax.all_to_all(tree_order, "rhs", split_axis=1, concat_axis=0, tiled=True)
    basis_cols = lax.dynamic_slice_in_dim(bases, position * piece_cols, piece_cols, 2).astype(
        jnp.float32
    )
    stacked = jnp.concatenate([tree_cols, basis_cols.reshape(levels * basis_rank, piece_cols)], 0)
    summed = lax.psum(
        lax.dot_general(stacked, leaf_inverse, (((1,), (1,)), ((), ())), precision=highest), "rhs"
    )
    all_sides = own_rows * groups
    solved = lax.dynamic_slice_in_dim(summed, position * own_rows, own_rows, 0)
    pending = [
        summed[all_sides + offset * basis_rank : all_sides + (offset + 1) * basis_rank]
        for offset in range(levels)
    ]
    for height in range(levels):
        carried = jnp.concatenate([solved] + pending[height + 1 :], 0)
        carried = merge_level(height, bases[height].astype(jnp.float32), pending[height], carried)
        solved = carried[:own_rows]
        later = [
            carried[own_rows + offset * basis_rank : own_rows + (offset + 1) * basis_rank]
            for offset in range(levels - height - 1)
        ]
        pending = pending[: height + 1] + later
    result = jnp.zeros_like(solved).at[:, ordering[0]].set(solved)
    return result


def solution(mesh):
    placed = (P("rhs", "leaf"), P("leaf", "rhs"), P(None, None, "leaf"), P("leaf", None))
    return jax.shard_map(
        local, mesh=mesh, in_specs=placed, out_specs=P("rhs", "leaf"), check_vma=False
    )
```

profile of v0, /device:TPU:2, one launch (start us, length us, event | category | flops | bytes accessed | tf_op | source)
XLA Modules:
  0.0 633.5 jit_solution(782333866733219382)
XLA Ops:
  16.2 9.2 %all-to-all-start = ((f32[16,4,256]{2,0,1:T(8,128)}), f32[16,4,256]{2,0,1:T(8,128)S(1)}, u32[]{:S(2)}, u32[]{:S(2)}) async-start(f32[16,4,256]{2,0,1:T(8,128)} %broadcast_select_fusion), calls=%async_computation | async-start | bytes 131072 | tf_op jit(solution)/shard_map/all_to_all | solution.py:51
  29.5 6.4 %fusion.12 = f32[960,1024]{1,0:T(8,128)} fusion(f32[1024,256]{1,0:T(8,128)S(1)} %copy-done, f32[896,256]{1,0:T(8,128)} %bitcast_convert_fusion, f32[64,256]{1,0:T(8,128)S(1)} %bitcast.171), kind=kOutput, calls=%fused_computation.33 | convolution fusion | flops 3020144640 | bytes 5963776 | tf_op jit(solution)/shard_map/dot_general | solution.py:57
  35.9 97.7 %all-reduce.2.cloned.1.call-done = f32[960,1024]{1,0:T(8,128)} async-done(((f32[960,1024]{1,0:T(8,128)}), f32[960,1024]{1,0:T(8,128)}) %all-reduce.2.cloned.1.call-update) | async-done | bytes 3932176 | tf_op jit(solution)/shard_map/psum | solution.py:56
  145.0 11.7 %cholesky.119 = f32[128,128]{1,0:T(8,128)S(1)} custom-call(f32[128,128]{1,0:T(8,128)S(1)} %fusion.107), custom_call_target="Cholesky" | custom-call | tf_op jit(solution)/shard_map/jit(cholesky)/cholesky | solution.py:36
  158.1 9.8 %custom-call.37 = f32[1,128,128]{1,2,0:T(8,128)S(1)} custom-call(f32[1,128,128]{2,1,0:T(8,128)S(1)} %fusion.72), custom_call_target="InvertDiagBlocksLowerTriangular" | custom-call | tf_op jit(solution)/shard_map/triangular_solve | solution.py:19
  170.1 4.9 fusion
  185.6 11.7 %cholesky.130 = f32[128,128]{1,0:T(8,128)S(1)} custom-call(f32[128,128]{1,0:T(8,128)S(1)} %fusion.103), custom_call_target="Cholesky" | custom-call | tf_op jit(solution)/shard_map/jit(cholesky)/cholesky | solution.py:36
  204.0 9.8 %custom-call.38 = f32[1,128,128]{1,2,0:T(8,128)S(1)} custom-call(f32[1,128,128]{2,1,0:T(8,128)S(1)} %fusion.73), custom_call_target="InvertDiagBlocksLowerTriangular" | custom-call | tf_op jit(solution)/shard_map/triangular_solve | solution.py:19
  246.1 12.5 %cholesky.141 = f32[128,128]{1,0:T(8,128)S(1)} custom-call(f32[128,128]{1,0:T(8,128)} %fusion.99), custom_call_target="Cholesky" | custom-call | tf_op jit(solution)/shard_map/jit(cholesky)/cholesky | solution.py:36
  264.4 10.6 %custom-call.39 = f32[1,128,128]{1,2,0:T(8,128)S(1)} custom-call(f32[1,128,128]{2,1,0:T(8,128)} %fusion.74), custom_call_target="InvertDiagBlocksLowerTriangular" | custom-call | tf_op jit(solution)/shard_map/triangular_solve | solution.py:19
  297.9 4.9 collective-permute-done.14
  302.9 5.4 collective-permute-start.15
  313.7 11.7 %cholesky.152 = f32[128,128]{1,0:T(8,128)S(1)} custom-call(f32[128,128]{1,0:T(8,128)S(1)} %fusion.95), custom_call_target="Cholesky" | custom-call | tf_op jit(solution)/shard_map/jit(cholesky)/cholesky | solution.py:36
  328.5 7.6 %collective-permute-done.18 = f32[128,400]{0,1:T(8,128)S(1)} collective-permute-done((f32[128,400]{0,1:T(8,128)S(1)}, f32[128,400]{0,1:T(8,128)S(1)}, u32[]{:S(2)}, u32[]{:S(2)}) %collective-permute-start.18) | collective-permute-done | bytes 204832 | tf_op jit(solution)/shard_map/ppermute | solution.py:14
  336.2 5.6 collective-permute-start.19
  342.4 9.8 %custom-call.40 = f32[1,128,128]{1,2,0:T(8,128)S(1)} custom-call(f32[1,128,128]{2,1,0:T(8,128)S(1)} %fusion.75), custom_call_target="InvertDiagBlocksLowerTriangular" | custom-call | tf_op jit(solution)/shard_map/triangular_solve | solution.py:19
  381.0 5.9 collective-permute-done.23
  393.1 11.7 %cholesky.163 = f32[128,128]{1,0:T(8,128)S(1)} custom-call(f32[128,128]{1,0:T(8,128)S(1)} %fusion.91), custom_call_target="Cholesky" | custom-call | tf_op jit(solution)/shard_map/jit(cholesky)/cholesky | solution.py:36
  409.8 6.1 collective-permute-done.28
  415.9 4.8 collective-permute-start.29
  421.3 9.8 %custom-call.41 = f32[1,128,128]{1,2,0:T(8,128)S(1)} custom-call(f32[1,128,128]{2,1,0:T(8,128)S(1)} %fusion.76), custom_call_target="InvertDiagBlocksLowerTriangular" | custom-call | tf_op jit(solution)/shard_map/triangular_solve | solution.py:19
  457.6 7.8 %collective-permute-start.39 = (f32[128,144]{0,1:T(8,128)S(1)}, f32[128,144]{0,1:T(8,128)S(1)}, u32[]{:S(2)}, u32[]{:S(2)}) collective-permute-start(f32[128,144]{0,1:T(8,128)S(1)} %add.306), channel_id=1, source_target_pairs={{0,32},{32,0},{4,36},{36,4},{8,40},{40,8},{12,44},{44,12},{16,48},... | collective-permute-start | bytes 221192 | tf_op jit(solution)/shard_map/ppermute | solution.py:14
  483.1 11.7 %cholesky.174 = f32[128,128]{1,0:T(8,128)S(1)} custom-call(f32[128,128]{1,0:T(8,128)S(1)} %fusion.87), custom_call_target="Cholesky" | custom-call | tf_op jit(solution)/shard_map/jit(cholesky)/cholesky | solution.py:36
  496.2 9.8 %custom-call.42 = f32[1,128,128]{1,2,0:T(8,128)S(1)} custom-call(f32[1,128,128]{2,1,0:T(8,128)S(1)} %fusion.77), custom_call_target="InvertDiagBlocksLowerTriangular" | custom-call | tf_op jit(solution)/shard_map/triangular_solve | solution.py:19
  521.1 5.3 collective-permute-done.44
  530.2 7.0 %collective-permute-done.45 = f32[128,128]{0,1:T(8,128)S(1)} collective-permute-done((f32[128,128]{0,1:T(8,128)S(1)}, f32[128,128]{0,1:T(8,128)S(1)}, u32[]{:S(2)}, u32[]{:S(2)}) %collective-permute-start.45) | collective-permute-done | bytes 65568 | tf_op jit(solution)/shard_map/ppermute | solution.py:14
  545.7 4.9 collective-permute-done.47
  550.6 4.9 collective-permute-start.48
  571.8 5.6 collective-permute-start.52
  593.2 5.0 collective-permute-start.55
  598.4 11.7 %cholesky.185 = f32[128,128]{1,0:T(8,128)S(1)} custom-call(f32[128,128]{1,0:T(8,128)S(1)} %fusion.83), custom_call_target="Cholesky" | custom-call | tf_op jit(solution)/shard_map/jit(cholesky)/cholesky | solution.py:36
  611.5 9.8 %custom-call.43 = f32[1,128,128]{1,2,0:T(8,128)S(1)} custom-call(f32[1,128,128]{2,1,0:T(8,128)S(1)} %fusion.78), custom_call_target="InvertDiagBlocksLowerTriangular" | custom-call | tf_op jit(solution)/shard_map/triangular_solve | solution.py:19
  (276 shorter events, 267.3 us)
Async XLA Ops:
  16.2 13.3 %all-to-all-start = ((f32[16,4,256]{2,0,1:T(8,128)}), f32[16,4,256]{2,0,1:T(8,128)S(1)}, u32[]{:S(2)}, u32[]{:S(2)}) async-start(f32[16,4,256]{2,0,1:T(8,128)} %broadcast_select_fusion), calls=%async_computation | async-start | bytes 131072 | tf_op jit(solution)/shard_map/all_to_all | solution.py:51
  25.4 108.2 %all-reduce.2.cloned.1.call-start = ((), (), s32[]{:S(2)}) async-start(), calls=%async_computation.1 | async-start | bytes 7864320 | tf_op jit(solution)/shard_map/psum | solution.py:56
  135.0 9.9 %collective-permute-start = (f32[128,128]{0,1:T(8,128)S(1)}, f32[128,128]{0,1:T(8,128)S(1)}, u32[]{:S(2)}, u32[]{:S(2)}) collective-permute-start(f32[128,128]{0,1:T(8,128)S(1)} %convolution_bitcast_fusion.8), channel_id=1, source_target_pairs={{0,4},{4,0},{8,12},{12,8},{16,20},{20,16},{24,28},{28,24},{32,36},... | collective-permute-start | bytes 196616 | tf_op jit(solution)/shard_map/ppermute | solution.py:14
  142.3 25.6 %collective-permute-start.1 = (f32[128,784]{0,1:T(8,128)S(1)}, f32[128,784]{0,1:T(8,128)}, u32[]{:S(2)}, u32[]{:S(2)}) collective-permute-start(f32[128,784]{0,1:T(8,128)S(1)} %fusion.7), channel_id=1, source_target_pairs={{0,4},{4,0},{8,12},{12,8},{16,20},{20,16},{24,28},{28,24},{32,36},... | collective-permute-start | bytes 1204232 | tf_op jit(solution)/shard_map/ppermute | solution.py:14
  183.3 14.6 %collective-permute-start.4 = (f32[128,656]{0,1:T(8,128)S(1)}, f32[128,656]{0,1:T(8,128)}, u32[]{:S(2)}, u32[]{:S(2)}) collective-permute-start(f32[128,656]{0,1:T(8,128)S(1)} %fusion.8), channel_id=1, source_target_pairs={{0,4},{4,0},{8,12},{12,8},{16,20},{20,16},{24,28},{28,24},{32,36},... | collective-permute-start | bytes 1007624 | tf_op jit(solution)/shard_map/ppermute | solution.py:14
  199.0 14.8 %collective-permute-start.5 = (f32[128,656]{0,1:T(8,128)S(1)}, f32[128,656]{0,1:T(8,128)}, u32[]{:S(2)}, u32[]{:S(2)}) collective-permute-start(f32[128,656]{0,1:T(8,128)S(1)} %add.268), channel_id=1, source_target_pairs={{0,8},{8,0},{4,12},{12,4},{16,24},{24,16},{20,28},{28,20},{32,40},... | collective-permute-start | bytes 1007624 | tf_op jit(solution)/shard_map/ppermute | solution.py:14
  229.9 8.3 %collective-permute-start.8 = (f32[128,128]{0,1:T(8,128)S(1)}, f32[128,128]{0,1:T(8,128)S(1)}, u32[]{:S(2)}, u32[]{:S(2)}) collective-permute-start(f32[128,128]{0,1:T(8,128)S(1)} %add.271), channel_id=1, source_target_pairs={{0,16},{16,0},{4,20},{20,4},{8,24},{24,8},{12,28},{28,12},{32,48},... | collective-permute-start | bytes 196616 | tf_op jit(solution)/shard_map/ppermute | solution.py:14
  241.0 17.7 %collective-permute-start.10 = (f32[128,528]{0,1:T(8,128)S(1)}, f32[128,528]{0,1:T(8,128)}, u32[]{:S(2)}, u32[]{:S(2)}) collective-permute-start(f32[128,528]{0,1:T(8,128)S(1)} %add.274), channel_id=1, source_target_pairs={{0,8},{8,0},{4,12},{12,4},{16,24},{24,16},{20,28},{28,20},{32,40},... | collective-permute-start | bytes 811016 | tf_op jit(solution)/shard_map/ppermute | solution.py:14
  259.7 16.9 %collective-permute-start.11 = (f32[128,528]{0,1:T(8,128)S(1)}, f32[128,528]{0,1:T(8,128)}, u32[]{:S(2)}, u32[]{:S(2)}) collective-permute-start(f32[128,528]{0,1:T(8,128)S(1)} %add.275), channel_id=1, source_target_pairs={{0,16},{16,0},{4,20},{20,4},{8,24},{24,8},{12,28},{28,12},{32,48},... | collective-permute-start | bytes 811016 | tf_op jit(solution)/shard_map/ppermute | solution.py:14
  287.0 21.2 %collective-permute-start.16 = (f32[128,400]{0,1:T(8,128)S(1)}, f32[128,400]{0,1:T(8,128)S(1)}, u32[]{:S(2)}, u32[]{:S(2)}) collective-permute-start(f32[128,400]{0,1:T(8,128)S(1)} %fusion.10), channel_id=1, source_target_pairs={{0,4},{4,0},{8,12},{12,8},{16,20},{20,16},{24,28},{28,24},{32,36},... | collective-permute-start | bytes 614408 | tf_op jit(solution)/shard_map/ppermute | solution.py:14
  302.9 10.7 %collective-permute-start.15 = (f32[128,128]{0,1:T(8,128)S(1)}, f32[128,128]{0,1:T(8,128)S(1)}, u32[]{:S(2)}, u32[]{:S(2)}) collective-permute-start(f32[128,128]{0,1:T(8,128)S(1)} %add.279), channel_id=1, source_target_pairs={{0,32},{32,0},{4,36},{36,4},{8,40},{40,8},{12,44},{44,12},{16,48},... | collective-permute-start | bytes 196616 | tf_op jit(solution)/shard_map/ppermute | solution.py:14
  308.3 17.2 %collective-permute-start.17 = (f32[128,400]{0,1:T(8,128)S(1)}, f32[128,400]{0,1:T(8,128)S(1)}, u32[]{:S(2)}, u32[]{:S(2)}) collective-permute-start(f32[128,400]{0,1:T(8,128)S(1)} %add.282), channel_id=1, source_target_pairs={{0,8},{8,0},{4,12},{12,4},{16,24},{24,16},{20,28},{28,20},{32,40},... | collective-permute-start | bytes 614408 | tf_op jit(solution)/shard_map/ppermute | solution.py:14
  325.5 10.6 %collective-permute-start.18 = (f32[128,400]{0,1:T(8,128)S(1)}, f32[128,400]{0,1:T(8,128)S(1)}, u32[]{:S(2)}, u32[]{:S(2)}) collective-permute-start(f32[128,400]{0,1:T(8,128)S(1)} %add.283), channel_id=1, source_target_pairs={{0,16},{16,0},{4,20},{20,4},{8,24},{24,8},{12,28},{28,12},{32,48},... | collective-permute-start | bytes 614408 | tf_op jit(solution)/shard_map/ppermute | solution.py:14
  336.2 16.1 %collective-permute-start.19 = (f32[128,400]{0,1:T(8,128)S(1)}, f32[128,400]{0,1:T(8,128)S(1)}, u32[]{:S(2)}, u32[]{:S(2)}) collective-permute-start(f32[128,400]{0,1:T(8,128)S(1)} %add.284), channel_id=1, source_target_pairs={{0,32},{32,0},{4,36},{36,4},{8,40},{40,8},{12,44},{44,12},{16,48},... | collective-permute-start | bytes 614408 | tf_op jit(solution)/shard_map/ppermute | solution.py:14
  360.8 10.9 %collective-permute-start.25 = (f32[128,272]{0,1:T(8,128)S(1)}, f32[128,272]{0,1:T(8,128)S(1)}, u32[]{:S(2)}, u32[]{:S(2)}) collective-permute-start(f32[128,272]{0,1:T(8,128)S(1)} %convolution_bitcast_fusion), channel_id=1, source_target_pairs={{0,4},{4,0},{8,12},{12,8},{16,20},{20,16},{24,28},{28,24},{32,36},... | collective-permute-start | bytes 417800 | tf_op jit(solution)/shard_map/ppermute | solution.py:14
  371.7 18.7 %collective-permute-start.26 = (f32[128,272]{0,1:T(8,128)S(1)}, f32[128,272]{0,1:T(8,128)S(1)}, u32[]{:S(2)}, u32[]{:S(2)}) collective-permute-start(f32[128,272]{0,1:T(8,128)S(1)} %add.292), channel_id=1, source_target_pairs={{0,8},{8,0},{4,12},{12,4},{16,24},{24,16},{20,28},{28,20},{32,40},... | collective-permute-start | bytes 417800 | tf_op jit(solution)/shard_map/ppermute | solution.py:14
  376.7 10.1 %collective-permute-start.23 = (f32[128,128]{0,1:T(8,128)S(1)}, f32[128,128]{0,1:T(8,128)S(1)}, u32[]{:S(2)}, u32[]{:S(2)}) collective-permute-start(f32[128,128]{0,1:T(8,128)S(1)} %add.288), channel_id=1, source_target_pairs={{0,32},{32,0},{4,36},{36,4},{8,40},{40,8},{12,44},{44,12},{16,48},... | collective-permute-start | bytes 196616 | tf_op jit(solution)/shard_map/ppermute | solution.py:14
  390.4 14.4 %collective-permute-start.27 = (f32[128,272]{0,1:T(8,128)S(1)}, f32[128,272]{0,1:T(8,128)S(1)}, u32[]{:S(2)}, u32[]{:S(2)}) collective-permute-start(f32[128,272]{0,1:T(8,128)S(1)} %add.293), channel_id=1, source_target_pairs={{0,16},{16,0},{4,20},{20,4},{8,24},{24,8},{12,28},{28,12},{32,48},... | collective-permute-start | bytes 417800 | tf_op jit(solution)/shard_map/ppermute | solution.py:14
  404.9 11.0 %collective-permute-start.28 = (f32[128,272]{0,1:T(8,128)S(1)}, f32[128,272]{0,1:T(8,128)S(1)}, u32[]{:S(2)}, u32[]{:S(2)}) collective-permute-start(f32[128,272]{0,1:T(8,128)S(1)} %add.294), channel_id=1, source_target_pairs={{0,32},{32,0},{4,36},{36,4},{8,40},{40,8},{12,44},{44,12},{16,48},... | collective-permute-start | bytes 417800 | tf_op jit(solution)/shard_map/ppermute | solution.py:14
  415.9 15.3 %collective-permute-start.29 = (f32[128,272]{0,1:T(8,128)S(1)}, f32[128,272]{0,1:T(8,128)S(1)}, u32[]{:S(2)}, u32[]{:S(2)}) collective-permute-start(f32[128,272]{0,1:T(8,128)S(1)} %add.295), channel_id=1, source_target_pairs={{0,64},{64,0},{4,68},{68,4},{8,72},{72,8},{12,76},{76,12},{16,80},... | collective-permute-start | bytes 417800 | tf_op jit(solution)/shard_map/ppermute | solution.py:14
  447.4 8.2 %collective-permute-start.32 = (f32[128,128]{0,1:T(8,128)S(1)}, f32[128,128]{0,1:T(8,128)S(1)}, u32[]{:S(2)}, u32[]{:S(2)}) collective-permute-start(f32[128,128]{0,1:T(8,128)S(1)} %add.298), channel_id=1, source_target_pairs={{0,16},{16,0},{4,20},{20,4},{8,24},{24,8},{12,28},{28,12},{32,48},... | collective-permute-start | bytes 196616 | tf_op jit(solution)/shard_map/ppermute | solution.py:14
  450.2 7.3 %collective-permute-start.38 = (f32[128,144]{0,1:T(8,128)S(1)}, f32[128,144]{0,1:T(8,128)S(1)}, u32[]{:S(2)}, u32[]{:S(2)}) collective-permute-start(f32[128,144]{0,1:T(8,128)S(1)} %add.305), channel_id=1, source_target_pairs={{0,16},{16,0},{4,20},{20,4},{8,24},{24,8},{12,28},{28,12},{32,48},... | collective-permute-start | bytes 221192 | tf_op jit(solution)/shard_map/ppermute | solution.py:14
  455.6 12.2 %collective-permute-start.33 = (f32[128,128]{0,1:T(8,128)S(1)}, f32[128,128]{0,1:T(8,128)S(1)}, u32[]{:S(2)}, u32[]{:S(2)}) collective-permute-start(f32[128,128]{0,1:T(8,128)S(1)} %add.299), channel_id=1, source_target_pairs={{0,32},{32,0},{4,36},{36,4},{8,40},{40,8},{12,44},{44,12},{16,48},... | collective-permute-start | bytes 196616 | tf_op jit(solution)/shard_map/ppermute | solution.py:14
  457.6 12.2 %collective-permute-start.39 = (f32[128,144]{0,1:T(8,128)S(1)}, f32[128,144]{0,1:T(8,128)S(1)}, u32[]{:S(2)}, u32[]{:S(2)}) collective-permute-start(f32[128,144]{0,1:T(8,128)S(1)} %add.306), channel_id=1, source_target_pairs={{0,32},{32,0},{4,36},{36,4},{8,40},{40,8},{12,44},{44,12},{16,48},... | collective-permute-start | bytes 221192 | tf_op jit(solution)/shard_map/ppermute | solution.py:14
  469.8 8.3 %collective-permute-start.40 = (f32[128,144]{0,1:T(8,128)S(1)}, f32[128,144]{0,1:T(8,128)S(1)}, u32[]{:S(2)}, u32[]{:S(2)}) collective-permute-start(f32[128,144]{0,1:T(8,128)S(1)} %add.307), channel_id=1, source_target_pairs={{0,64},{64,0},{4,68},{68,4},{8,72},{72,8},{12,76},{76,12},{16,80},... | collective-permute-start | bytes 221192 | tf_op jit(solution)/shard_map/ppermute | solution.py:14
  474.3 8.7 %collective-permute-start.35 = (f32[128,128]{0,1:T(8,128)S(1)}, f32[128,128]{0,1:T(8,128)S(1)}, u32[]{:S(2)}, u32[]{:S(2)}) collective-permute-start(f32[128,128]{0,1:T(8,128)S(1)} %add.301), channel_id=1, source_target_pairs={{0,128},{128,0},{4,132},{132,4},{8,136},{136,8},{12,140},{140,12},... | collective-permute-start | bytes 196616 | tf_op jit(solution)/shard_map/ppermute | solution.py:14
  478.1 27.9 %collective-permute-start.41 = (f32[128,144]{0,1:T(8,128)S(1)}, f32[128,144]{0,1:T(8,128)S(1)}, u32[]{:S(2)}, u32[]{:S(2)}) collective-permute-start(f32[128,144]{0,1:T(8,128)S(1)} %add.308), channel_id=1, source_target_pairs={{0,128},{128,0},{4,132},{132,4},{8,136},{136,8},{12,140},{140,12},... | collective-permute-start | bytes 221192 | tf_op jit(solution)/shard_map/ppermute | solution.py:14
  519.0 7.4 %collective-permute-start.44 = (f32[128,128]{0,1:T(8,128)S(1)}, f32[128,128]{0,1:T(8,128)S(1)}, u32[]{:S(2)}, u32[]{:S(2)}) collective-permute-start(f32[128,128]{0,1:T(8,128)S(1)} %add.311), channel_id=1, source_target_pairs={{0,16},{16,0},{4,20},{20,4},{8,24},{24,8},{12,28},{28,12},{32,48},... | collective-permute-start | bytes 196616 | tf_op jit(solution)/shard_map/ppermute | solution.py:14
  526.4 10.8 %collective-permute-start.45 = (f32[128,128]{0,1:T(8,128)S(1)}, f32[128,128]{0,1:T(8,128)S(1)}, u32[]{:S(2)}, u32[]{:S(2)}) collective-permute-start(f32[128,128]{0,1:T(8,128)S(1)} %add.312), channel_id=1, source_target_pairs={{0,32},{32,0},{4,36},{36,4},{8,40},{40,8},{12,44},{44,12},{16,48},... | collective-permute-start | bytes 196616 | tf_op jit(solution)/shard_map/ppermute | solution.py:14
  550.6 47.7 %collective-permute-start.48 = (f32[128,128]{0,1:T(8,128)S(1)}, f32[128,128]{0,1:T(8,128)S(1)}, u32[]{:S(2)}, u32[]{:S(2)}) collective-permute-start(f32[128,128]{0,1:T(8,128)S(1)} %add.315), channel_id=1, source_target_pairs={{0,256},{256,0},{4,260},{260,4},{8,264},{264,8},{12,268},{268,12},... | collective-permute-start | bytes 196616 | tf_op jit(solution)/shard_map/ppermute | solution.py:14
  571.8 9.4 %collective-permute-start.52 = (f32[128,16]{0,1:T(8,128)S(1)}, f32[128,16]{0,1:T(8,128)S(1)}, u32[]{:S(2)}, u32[]{:S(2)}) collective-permute-start(f32[128,16]{0,1:T(8,128)S(1)} %add.320), channel_id=1, source_target_pairs={{0,32},{32,0},{4,36},{36,4},{8,40},{40,8},{12,44},{44,12},{16,48},... | collective-permute-start | bytes 24584 | tf_op jit(solution)/shard_map/ppermute | solution.py:14
  593.2 28.1 %collective-permute-start.55 = (f32[128,16]{0,1:T(8,128)S(1)}, f32[128,16]{0,1:T(8,128)S(1)}, u32[]{:S(2)}, u32[]{:S(2)}) collective-permute-start(f32[128,16]{0,1:T(8,128)S(1)} %add.323), channel_id=1, source_target_pairs={{0,256},{256,0},{4,260},{260,4},{8,264},{264,8},{12,268},{268,12},... | collective-permute-start | bytes 24584 | tf_op jit(solution)/shard_map/ppermute | solution.py:14
  (41 other events, 262.1 us)
Sparse Core Ops, SparseCore 0:
  36.0 97.4 all-reduce.1
where the time goes:
time: 642 us; the launch traced here: 634 us
  waiting for transfers between devices  194 us (30%)
  starting transfers between devices  182 us (28%)
  other arithmetic  172 us (27%)
  matrix products  52.8 us (8%)
  local copies, waits for them, and re-layouts  17.7 us (3%)
  between operations  15.2 us (2%)
    ppermute x56, starting transfers between devices, swapped(): return lax.ppermute(block, axis, route)  173 us
    psum x1, waiting for transfers between devices, local(): lax.psum(lax.dot_general(stacked, leaf_inverse, (((1,), (1,)), ((), ())),...  97.7 us
    ppermute x56, waiting for transfers between devices, swapped(): return lax.ppermute(block, axis, route)  93.2 us
    another operation x21, other arithmetic, merge_level(): factor = jnp.linalg.cholesky(capacity)  87.6 us
    another operation x14, other arithmetic, solve_factor(): lax.linalg.triangular_solve(factor, middle, left_side=True, lower=True, t...  75.5 us
    dot_general x7, matrix products, merge_level(): lax.dot_general(weights, level_solved, (((0,), (0,)), ((), ())), precisio...  18.9 us
  transfers between devices with their start and end apart: 58, of which 33 were waited for; matrix products, arithmetic and copies ran while one was open for 29% of the time, Pallas kernels for 0%

commit v1 on v0

v1 whole, which is shorter than its diff:
```python
import functools

import jax
import jax.numpy as jnp
from jax import lax
from jax.experimental import pallas as pl
from jax.experimental.pallas import tpu as pltpu
from jax.sharding import PartitionSpec as P

HIGHEST = lax.Precision.HIGHEST
NN = (((1,), (0,)), ((), ()))
NT = (((1,), (1,)), ((), ()))


def exact_dot(left, right, dims):
    return lax.dot_general(left, right, dims, precision=HIGHEST, preferred_element_type=jnp.float32)


def short_dot(left, right, dims):
    return lax.dot_general(left, right, dims, preferred_element_type=jnp.float32)


def three_parts(values):
    high = values.astype(jnp.bfloat16)
    rest = values - high.astype(jnp.float32)
    middle = rest.astype(jnp.bfloat16)
    low = (rest - middle.astype(jnp.float32)).astype(jnp.bfloat16)
    return high, middle, low


def dot_left_parts(left, right16, dims):
    high, middle, low = three_parts(left)
    return short_dot(low, right16, dims) + short_dot(middle, right16, dims) + short_dot(high, right16, dims)


def dot_right_parts(left16, right, dims):
    high, middle, low = three_parts(right)
    return short_dot(left16, low, dims) + short_dot(left16, middle, dims) + short_dot(left16, high, dims)


def inverse_of(capacity):
    size = capacity.shape[0]
    shape = (size, size)
    eye = jnp.where(
        lax.broadcasted_iota(jnp.int32, shape, 0) == lax.broadcasted_iota(jnp.int32, shape, 1), 1.0, 0.0
    )
    bound = jnp.max(jnp.sum(jnp.abs(capacity), axis=1, keepdims=True), axis=0, keepdims=True)
    scale = 2.0 / (1.0 + bound)
    begin = 2.0 * scale * eye - scale * scale * capacity
    guess = begin
    short = capacity.astype(jnp.bfloat16)
    for _ in range(4):
        guess16 = guess.astype(jnp.bfloat16)
        factor = 2.0 * eye - short_dot(short, guess16, NN)
        guess = short_dot(guess16, factor.astype(jnp.bfloat16), NN)

    def unfinished(state):
        return (state[1] == 0) | ((state[1] < 80) & jnp.logical_not(state[2] < 1e-6))

    def improve(state):
        inverse, count, _ = state
        residual = eye - exact_dot(capacity, inverse, NN)
        size2 = jnp.sum(residual * residual)
        better = inverse + exact_dot(inverse, residual, NN)
        restart = (count == 0) & jnp.logical_not(size2 < 0.25)
        return jnp.where(restart, begin, better), count + 1, size2

    return lax.while_loop(unfinished, improve, (guess, 0, jnp.float32(1.0)))[0]


def run(body, outs, *args):
    vmem = pl.BlockSpec(memory_space=pltpu.VMEM)
    return pl.pallas_call(
        body,
        out_shape=[jax.ShapeDtypeStruct(shape, jnp.float32) for shape in outs],
        in_specs=[vmem] * len(args),
        out_specs=[vmem] * len(outs),
        compiler_params=pltpu.CompilerParams(vmem_limit_bytes=48 * 1024 * 1024),
    )(*args)


def one_hot(order):
    size = order.shape[1]
    rows = lax.broadcasted_iota(jnp.int32, (size, size), 0)
    return jnp.where(rows == order, 1.0, 0.0).astype(jnp.bfloat16)


def start_body(sides, order, inverse_cols, bases, send):
    levels, rank, leaf = bases.shape
    groups, _, piece = send.shape
    share = rank // groups
    own = sides.shape[0]
    tree = dot_left_parts(sides[...], one_hot(order[...]), NN)
    applied = dot_right_parts(bases[...].reshape(levels * rank, leaf), inverse_cols[...], NN)
    for group in range(groups):
        for level in range(levels):
            low = level * rank + group * share
            send[group, level * share : (level + 1) * share, :] = applied[low : low + share]
        for part in range(groups):
            low = levels * share + part * own
            send[group, low : low + own, :] = tree[:, part * piece : (part + 1) * piece]


def gram_body(got, bases, gram, tree):
    levels, rank, leaf = bases.shape
    groups = got.shape[0]
    share = rank // groups
    sides = tree.shape[0]
    own = sides // groups
    rows = levels * share
    applied = jnp.concatenate([got[group, :rows, :] for group in range(groups)], 1)
    for group in range(groups):
        low = rows
        tree[group * own : (group + 1) * own, :] = jnp.concatenate(
            [got[group, low + part * own : low + (part + 1) * own, :] for part in range(groups)], 1
        )
    product = dot_left_parts(applied, bases[...].reshape(levels * rank, leaf), NT)
    with_sides = exact_dot(applied, tree[...], NT)
    block = lambda level, column: product[
        level * share : (level + 1) * share, column * rank : (column + 1) * rank
    ]
    at = 0

    def put(value):
        nonlocal at
        gram[at : at + value.shape[0], :] = value
        at += value.shape[0]

    for level in range(levels):
        put(block(level, 0))
    for column in (1, 2, 3):
        for level in range(column, 4):
            put(block(level, column))
    put(
        jnp.concatenate(
            [
                with_sides[: 4 * share],
                jnp.concatenate([with_sides[4 * share :], jnp.zeros((share, sides), jnp.float32)], 0),
            ],
            1,
        )
    )
    for column in (1, 2, 3):
        for level in (4, 5, 6):
            put(block(level, column))
    for column in (4, 5, 6):
        for level in range(column, 7):
            put(block(level, column))


def first_body(everyone, mine, arrived, second, third, fourth, border, weights):
    groups = everyone.shape[0]
    rank = everyone.shape[2]
    share = rank // groups
    sides = rank // 2
    joined = lambda low: jnp.concatenate(
        [everyone[group, low : low + share, :] for group in range(groups)], 0
    )
    eye = jnp.where(
        lax.broadcasted_iota(jnp.int32, (rank, rank), 0) == lax.broadcasted_iota(jnp.int32, (rank, rank), 1),
        1.0,
        0.0,
    )
    inverse = inverse_of(joined(0) + eye)
    turned = [joined((13 + pair) * share).T for pair in range(4)]
    side_rows = lambda level: (turned[level] if level < 4 else turned[level - 4])[
        (0 if level < 4 else sides) : (sides if level < 4 else 2 * sides)
    ]
    upper = jnp.concatenate([joined(level * share) for level in range(1, 7)] + [side_rows(0)], 0)
    scaled = exact_dot(upper, inverse, NN)
    weights[...] = scaled
    own_sum = lambda low, count: (
        mine[low * share : (low + count) * share, :] + arrived[low * share : (low + count) * share, :]
    )
    own_scaled = exact_dot(own_sum(4, 3), inverse, NN)
    side_scaled = scaled[6 * rank :]
    block = lambda level: upper[(level - 1) * rank : level * rank]
    place = 7
    low_own = 17
    for column, panel in ((1, second), (2, third), (3, fourth)):
        at = 0
        factors = jnp.concatenate([scaled[(column - 1) * rank : 3 * rank], own_scaled, side_scaled], 0)
        update = exact_dot(factors, block(column), NT)
        for level in range(column, 4):
            panel[at : at + rank, :] = joined(place * share) - update[at : at + rank]
            place += 1
            at += rank
        panel[at : at + 3 * share, :] = own_sum(low_own, 3) - update[at : at + 3 * share]
        at += 3 * share
        low_own += 3
        panel[at : at + sides, :] = side_rows(column) - update[at : at + sides]
    at = 0
    for column in (4, 5, 6):
        count = 7 - column
        rows = count * share
        factors = jnp.concatenate([own_scaled[(column - 4) * share :], side_scaled], 0)
        update = exact_dot(factors, block(column), NT)
        border[at : at + rows, :] = own_sum(low_own, count) - update[:rows]
        low_own += count
        at += rows
        border[at : at + sides, :] = side_rows(column) - update[rows:]
        at += sides


def factor_body(mine, arrived, upper, weights, inverse):
    rank = mine.shape[1]
    total = mine[...] + arrived[...]
    eye = jnp.where(
        lax.broadcasted_iota(jnp.int32, (rank, rank), 0) == lax.broadcasted_iota(jnp.int32, (rank, rank), 1),
        1.0,
        0.0,
    )
    inverse[...] = inverse_of(total[:rank] + eye)
    upper[...] = total[rank:]
    weights[...] = exact_dot(total[rank:], inverse[...], NN)


def update_body(count, *refs):
    mine, arrived, upper, weights = refs[:4]
    panels = refs[4:]
    rank = upper.shape[1]
    height = upper.shape[0]
    at = 0
    for step in range(count):
        rows = height - step * rank
        update = exact_dot(weights[step * rank :, :], upper[step * rank : (step + 1) * rank, :], NT)
        panels[step][...] = mine[at : at + rows, :] + arrived[at : at + rows, :] - update
        at += rows


def border_body(rows_before, mine, arrived, weights, inverse, everyone, border, far_weights):
    groups, rows, rank = everyone.shape
    share = rank // groups
    sides = rank // 2
    far = jnp.concatenate(
        [everyone[group, level * share : (level + 1) * share, :] for level in range(3) for group in range(groups)], 0
    )
    far_weights[...] = exact_dot(far, inverse[...], NN)
    at = 0
    for column in range(3):
        count = (3 - column) * share + sides
        factors = weights[rows_before + column * share :, :]
        update = exact_dot(factors, far[column * rank : (column + 1) * rank], NT)
        border[at : at + count, :] = mine[at : at + count, :] + arrived[at : at + count, :] - update
        at += count


def spread_body(everyone, mine, arrived, upper, weights, inverse, fifth, rest, far_weights):
    groups, _, rank = everyone.shape
    share = rank // groups
    sides = rank // 2
    joined = lambda low: jnp.concatenate(
        [everyone[group, low * share : (low + 1) * share, :] for group in range(groups)], 0
    )
    far = jnp.concatenate([joined(0), joined(1), joined(2)], 0)
    scaled = exact_dot(far, inverse[...], NN)
    far_weights[...] = scaled
    factors = jnp.concatenate([scaled, weights[3 * share :, :]], 0)
    place = 3
    side_at = 0
    at = 0
    for column in range(3):
        update = exact_dot(factors[column * rank :], far[column * rank : (column + 1) * rank], NT)
        panel = fifth if column == 0 else rest
        side_at += (3 - column) * share
        for level in range(column, 3):
            low = (level - column) * rank
            panel[at : at + rank, :] = joined(place) - update[low : low + rank]
            place += 1
            at += rank
        low = (3 - column) * rank
        panel[at : at + sides, :] = (
            mine[side_at : side_at + sides, :] + arrived[side_at : side_at + sides, :] - update[low:]
        )
        side_at += sides
        at = 0 if column == 0 else at + sides


def finish_body(
    mine, arrived, w1, w2, f2, w3, f3, w4, f4, w5, w6, tree, bases, inverse_cols, solved
):
    levels, rank, leaf = bases.shape
    sides = tree.shape[0]
    total = mine[...] + arrived[...]
    eye = jnp.where(
        lax.broadcasted_iota(jnp.int32, (rank, rank), 0) == lax.broadcasted_iota(jnp.int32, (rank, rank), 1),
        1.0,
        0.0,
    )
    top = exact_dot(total[rank:], inverse_of(total[:rank] + eye), NN)
    last = lambda ref: ref[ref.shape[0] - sides :, :]
    found = top

    def lower(side_part, blocks):
        return side_part - exact_dot(found, blocks, NN)

    found = jnp.concatenate([lower(last(w6), w6[:rank, :]), found], 1)
    found = jnp.concatenate([lower(last(w5), w5[: 2 * rank, :]), found], 1)
    found = jnp.concatenate([lower(last(w4), f4[...]), found], 1)
    found = jnp.concatenate([lower(last(w3), jnp.concatenate([w3[:rank, :], f3[...]], 0)), found], 1)
    found = jnp.concatenate([lower(last(w2), jnp.concatenate([w2[: 2 * rank, :], f2[...]], 0)), found], 1)
    found = jnp.concatenate([lower(last(w1), w1[: 6 * rank, :]), found], 1)
    rest = tree[...] - dot_left_parts(found, bases[...].reshape(levels * rank, leaf), NN)
    solved[...] = exact_dot(rest, inverse_cols[...], NN)


def untangle_body(solved, order, out):
    groups = solved.shape[0]
    whole = jnp.concatenate([solved[group] for group in range(groups)], 1)
    out[...] = dot_left_parts(whole, one_hot(order[...]), NT)


def to_all(block, axis):
    count = lax.axis_size(axis)
    return lax.all_to_all(jnp.broadcast_to(block[None], (count,) + block.shape), axis, 0, 0)


def route(height):
    pairs = []
    for leaf in range(128):
        if height in (4, 7):
            low = 1 if height == 4 else 4
            ring = (leaf >> low) & 7
            pairs.append((leaf, leaf & ~(7 << low) | ((ring ^ 6) << low)))
        else:
            pairs.append((leaf, leaf ^ (1 << (height - 1))))
    return pairs


def local(right_sides, leaf_inverse, bases, ordering):
    own, leaf = right_sides.shape
    piece = leaf_inverse.shape[1]
    levels, rank, _ = bases.shape
    groups = lax.axis_size("rhs")
    share = rank // groups
    sides = own * groups
    swap = lambda block, height: lax.ppermute(block, "leaf", route(height))

    (send,) = run(
        start_body, [(groups, levels * share + sides, piece)], right_sides, ordering, leaf_inverse, bases
    )
    got = lax.all_to_all(send, "rhs", 0, 0)
    shared_rows = 17 * share
    gram, tree = run(gram_body, [(shared_rows + 15 * share, rank), (sides, leaf)], got, bases)
    other = swap(gram, 1)
    everyone = to_all(gram[:shared_rows] + other[:shared_rows], "rhs")

    mine_rows = 3 * share + sides
    panels = [(step * rank + mine_rows, rank) for step in (3, 2, 1)]
    border_shape = (6 * share + 3 * sides, rank)
    p2, p3, p4, border, w1 = run(
        first_body, panels + [border_shape, (6 * rank + sides, rank)], everyone, gram, other
    )

    square = (rank, rank)
    kept = []
    panel, later = p2, jnp.concatenate([p3, p4], 0)
    for height in (2, 3, 4):
        near = (4 - height) * rank
        arrived = swap(panel, height)
        if height < 4:
            later_arrived = swap(later, height)
        border_arrived = swap(border, height)
        upper_shape = (near + mine_rows, rank)
        upper, weights, inverse = run(factor_body, [upper_shape, upper_shape, square], panel, arrived)
        if height < 4:
            shapes = [(step * rank + mine_rows, rank) for step in range(4 - height, 0, -1)]
            updated = run(
                functools.partial(update_body, len(shapes)), shapes, later, later_arrived, upper, weights
            )
            panel = updated[0]
            later = updated[-1]
            spread = to_all(upper[near : near + 3 * share], "rhs")
            border, far = run(
                functools.partial(border_body, near),
                [border_shape, (3 * rank, rank)],
                border,
                border_arrived,
                weights,
                inverse,
                spread,
            )
            kept += [weights, far]
        else:
            total = border + border_arrived
            pieces = [upper[: 3 * share], total[: 3 * share]]
            at = 3 * share + sides
            pieces.append(total[at : at + 2 * share])
            at += 2 * share + sides
            pieces.append(total[at : at + share])
            spread = to_all(jnp.concatenate(pieces, 0), "rhs")
            panel, later, far = run(
                spread_body,
                [(3 * rank + sides, rank), (3 * rank + 2 * sides, rank), (3 * rank, rank)],
                spread,
                border,
                border_arrived,
                upper,
                weights,
                inverse,
            )
            kept += [weights, far]

    for height in (5, 6):
        arrived = swap(panel, height)
        later_arrived = swap(later, height)
        upper_shape = ((7 - height) * rank + sides, rank)
        upper, weights, inverse = run(factor_body, [upper_shape, upper_shape, square], panel, arrived)
        shapes = [(step * rank + sides, rank) for step in range(7 - height, 0, -1)]
        updated = run(
            functools.partial(update_body, len(shapes)), shapes, later, later_arrived, upper, weights
        )
        panel = updated[0]
        later = updated[-1]
        kept.append(weights)

    arrived = swap(panel, 7)
    (solved,) = run(
        finish_body, [(sides, piece)], panel, arrived, w1, *kept, tree, bases, leaf_inverse
    )
    back = lax.all_to_all(solved.reshape(groups, own, piece), "rhs", 0, 0)
    (result,) = run(untangle_body, [(own, leaf)], back, ordering)
    return result


def solution(mesh):
    placed = (P("rhs", "leaf"), P("leaf", "rhs"), P(None, None, "leaf"), P("leaf", None))
    return jax.shard_map(
        local, mesh=mesh, in_specs=placed, out_specs=P("rhs", "leaf"), check_vma=False
    )
```

time: 642 us -> 228 us (0.36)
  the two profiles are of different devices: /device:TPU:2 before, /device:TPU:80 now
where the time goes in v1:
time: 228 us; the launch traced here: 227 us
  Pallas kernels  60.7 us (27%)
  blocking collectives  58.3 us (26%)
  starting transfers between devices  58 us (25%)
  waiting for transfers between devices  42 us (18%)
  local copies, waits for them, and re-layouts  7.35 us (3%)
    pallas_call x17, Pallas kernels, run(): pl.pallas_call(body, out_shape=[jax.ShapeDtypeStruct(shape, jnp.float32)...  60.7 us
    ppermute x14, starting transfers between devices, local(): swap = lambda block, height: lax.ppermute(block, 'leaf', route(height))  51.3 us
    ppermute x14, waiting for transfers between devices, local(): swap = lambda block, height: lax.ppermute(block, 'leaf', route(height))  31.7 us
    all_to_all x2, blocking collectives, to_all(): lax.all_to_all(jnp.broadcast_to(block[None], (count,) + block.shape), axi...  29.6 us
    all_to_all x1, blocking collectives, local(): got = lax.all_to_all(send, 'rhs', 0, 0)  20.7 us
    all_to_all x2, waiting for transfers between devices, to_all(): lax.all_to_all(jnp.broadcast_to(block[None], (count,) + block.shape), axi...  10.3 us
    all_to_all x1, blocking collectives, local(): back = lax.all_to_all(solved.reshape(groups, own, piece), 'rhs', 0, 0)  7.99 us
    all_to_all x2, starting transfers between devices, to_all(): lax.all_to_all(jnp.broadcast_to(block[None], (count,) + block.shape), axi...  6.73 us
  transfers between devices with their start and end apart: 16, of which 8 were waited for; matrix products, arithmetic and copies ran while one was open for 1% of the time, Pallas kernels for 15%

profile of v1, /device:TPU:80, one launch (start us, length us, event | category | flops | bytes accessed | tf_op | source)
XLA Modules:
  0.0 226.9 jit_solution(11502581569247460658)
XLA Ops:
  4.3 2.6 %shard_map.46 = f32[4,288,256]{2,1,0:T(8,128)S(1)} custom-call(f32[16,1024]{1,0:T(8,128)S(1)} %copy-done.8, s32[1,1024]{1,0:T(1,128)S(1)} %copy-done.11, f32[1024,256]{1,0:T(8,128)S(1)} %copy-done.2, bf16[7,128,1024]{2,1,0:T(8,128)(2,1)S(1)} %copy-done), custom_call_target="tpu_custom_call" | custom-call | tf_op jit(solution)/shard_map/pallas_call | solution.py:73
  6.8 20.7 %all_to_all.30.got = f32[4,288,256]{2,1,0:T(8,128)S(1)} all-to-all(f32[4,288,256]{2,1,0:T(8,128)S(1)} %shard_map.46), channel_id=1, replica_groups=mesh['leaf'=128,'rhs'=4] {'rhs'}, dimensions={0} | all-to-all | bytes 2359296 | tf_op jit(solution)/shard_map/all_to_all | solution.py:342
  27.6 2.5 %shard_map.47 = (f32[1024,128]{1,0:T(8,128)S(1)}, f32[64,1024]{1,0:T(8,128)S(1)}) custom-call(f32[4,288,256]{2,1,0:T(8,128)S(1)} %all_to_all.30.got, bf16[7,128,1024]{2,1,0:T(8,128)(2,1)S(1)} %copy-done.1), custom_call_target="tpu_custom_call" | custom-call | tf_op jit(solution)/shard_map/pallas_call | solution.py:73
  34.0 18.8 %all_to_all.31.everyone = f32[4,544,128]{2,1,0:T(8,128)S(1)} all-to-all(f32[4,544,128]{2,1,0:T(8,128)S(1)} %broadcast_in_dim.8), channel_id=1, replica_groups=mesh['leaf'=128,'rhs'=4] {'rhs'}, dimensions={0} | all-to-all | bytes 2228224 | tf_op jit(solution)/shard_map/all_to_all | solution.py:315
  52.8 8.3 %shard_map.48 = (f32[544,128]{1,0:T(8,128)S(1)}, f32[416,128]{1,0:T(8,128)S(1)}, f32[288,128]{1,0:T(8,128)S(1)}, f32[384,128]{1,0:T(8,128)}, f32[832,128]{1,0:T(8,128)S(1)}) custom-call(f32[4,544,128]{2,1,0:T(8,128)S(1)} %all_to_all.31.everyone, f32[1024,128]{1,0:T(8,128)S(1)} %get-tuple-element.36.mine, f32[1024,128]{1,0:T(8,128)S(1)} %collective-permute-done.arrived), custom_call_target="tpu_custom_call" | custom-call | tf_op jit(solution)/shard_map/pallas_call | solution.py:73
  61.2 3.5 %collective-permute-start.1 = (f32[704,128]{1,0:T(8,128)S(1)}, f32[704,128]{1,0:T(8,128)S(1)}, u32[]{:S(2)}, u32[]{:S(2)}) collective-permute-start(f32[704,128]{1,0:T(8,128)S(1)} %constant_dynamic-update-slice_fusion.refs_0_), channel_id=1, source_target_pairs={{0,8},{4,12},{8,0},{12,4},{16,24},{20,28},{24,16},{28,20},{32,40},... | collective-permute-start | bytes 1081352 | tf_op jit(solution)/shard_map/ppermute | solution.py:337
  64.7 2.4 %collective-permute-start.2 = (f32[544,128]{1,0:T(8,128)S(1)}, f32[544,128]{1,0:T(8,128)S(1)}, u32[]{:S(2)}, u32[]{:S(2)}) collective-permute-start(f32[544,128]{1,0:T(8,128)S(1)} %get-tuple-element.39.mine), channel_id=1, source_target_pairs={{0,8},{4,12},{8,0},{12,4},{16,24},{20,28},{24,16},{28,20},{32,40},... | collective-permute-start | bytes 835592 | tf_op jit(solution)/shard_map/ppermute | solution.py:337
  67.1 3.5 %collective-permute-start.6 = (f32[384,128]{1,0:T(8,128)}, f32[384,128]{1,0:T(8,128)}, u32[]{:S(2)}, u32[]{:S(2)}) collective-permute-start(f32[384,128]{1,0:T(8,128)} %get-tuple-element.47.mine), channel_id=1, source_target_pairs={{0,8},{4,12},{8,0},{12,4},{16,24},{20,28},{24,16},{28,20},{32,40},... | collective-permute-start | bytes 589832 | tf_op jit(solution)/shard_map/ppermute | solution.py:337
  70.5 9.9 %collective-permute-done.2.arrived = f32[544,128]{1,0:T(8,128)S(1)} collective-permute-done((f32[544,128]{1,0:T(8,128)S(1)}, f32[544,128]{1,0:T(8,128)S(1)}, u32[]{:S(2)}, u32[]{:S(2)}) %collective-permute-start.2) | collective-permute-done | bytes 278560 | tf_op jit(solution)/shard_map/ppermute | solution.py:337
  80.4 5.6 %shard_map.49 = (f32[416,128]{1,0:T(8,128)S(1)}, f32[416,128]{1,0:T(8,128)S(1)}, f32[128,128]{1,0:T(8,128)S(1)}) custom-call(f32[544,128]{1,0:T(8,128)S(1)} %get-tuple-element.39.mine, f32[544,128]{1,0:T(8,128)S(1)} %collective-permute-done.2.arrived), custom_call_target="tpu_custom_call" | custom-call | tf_op jit(solution)/shard_map/pallas_call | solution.py:73
  89.5 3.4 %all-to-all-start.2 = ((f32[4,96,128]{2,1,0:T(8,128)}), f32[4,96,128]{2,1,0:T(8,128)S(1)}, u32[]{:S(2)}, u32[]{:S(2)}) async-start(f32[4,96,128]{2,1,0:T(8,128)} %broadcast_in_dim.9), calls=%async_computation.2 | async-start | bytes 393216 | tf_op jit(solution)/shard_map/all_to_all | solution.py:315
  92.9 6.3 %all-to-all-done.2.everyone = f32[4,96,128]{2,1,0:T(8,128)S(1)} async-done(((f32[4,96,128]{2,1,0:T(8,128)}), f32[4,96,128]{2,1,0:T(8,128)S(1)}, u32[]{:S(2)}, u32[]{:S(2)}) %all-to-all-start.2) | async-done | bytes 196640 | tf_op jit(solution)/shard_map/all_to_all | solution.py:315
  99.1 2.3 %shard_map.54 = (f32[384,128]{1,0:T(8,128)}, f32[384,128]{1,0:T(8,128)S(1)}) custom-call(f32[384,128]{1,0:T(8,128)} %get-tuple-element.47.mine, f32[384,128]{1,0:T(8,128)} %collective-permute-done.6.arrived, f32[416,128]{1,0:T(8,128)S(1)} %get-tuple-element.41.refs_3_.weights.w2, f32[128,128]{1,0:T(8,128)S(1)} %get-tuple-element.48.inverse, ...), custom_call_target="tpu_custom_call" | custom-call | tf_op jit(solution)/shard_map/pallas_call | solution.py:73
  102.2 4.5 %collective-permute-start.7 = (f32[384,128]{1,0:T(8,128)}, f32[384,128]{1,0:T(8,128)}, u32[]{:S(2)}, u32[]{:S(2)}) collective-permute-start(f32[384,128]{1,0:T(8,128)} %get-tuple-element.49.mine), channel_id=1, source_target_pairs={{0,16},{4,20},{8,24},{12,28},{16,0},{20,4},{24,8},{28,12},{32,48},... | collective-permute-start | bytes 589832 | tf_op jit(solution)/shard_map/ppermute | solution.py:337
  106.7 6.5 %shard_map.51 = (f32[288,128]{1,0:T(8,128)S(1)}, f32[288,128]{1,0:T(8,128)S(1)}, f32[128,128]{1,0:T(8,128)S(1)}) custom-call(f32[416,128]{1,0:T(8,128)S(1)} %get-tuple-element.43.mine, f32[416,128]{1,0:T(8,128)} %collective-permute-done.4.arrived), custom_call_target="tpu_custom_call" | custom-call | tf_op jit(solution)/shard_map/pallas_call | solution.py:73
  113.9 3.4 %all-to-all-start.3 = ((f32[4,96,128]{2,1,0:T(8,128)}), f32[4,96,128]{2,1,0:T(8,128)S(1)}, u32[]{:S(2)}, u32[]{:S(2)}) async-start(f32[4,96,128]{2,1,0:T(8,128)} %broadcast_in_dim.10), calls=%async_computation.3 | async-start | bytes 393216 | tf_op jit(solution)/shard_map/all_to_all | solution.py:315
  119.5 4.0 %all-to-all-done.3.everyone = f32[4,96,128]{2,1,0:T(8,128)S(1)} async-done(((f32[4,96,128]{2,1,0:T(8,128)}), f32[4,96,128]{2,1,0:T(8,128)S(1)}, u32[]{:S(2)}, u32[]{:S(2)}) %all-to-all-start.3) | async-done | bytes 196640 | tf_op jit(solution)/shard_map/all_to_all | solution.py:315
  126.1 6.2 %collective-permute-start.8 = (f32[384,128]{1,0:T(8,128)S(1)}, f32[384,128]{1,0:T(8,128)S(1)}, u32[]{:S(2)}, u32[]{:S(2)}) collective-permute-start(f32[384,128]{1,0:T(8,128)S(1)} %get-tuple-element.51.mine), channel_id=1, source_target_pairs={{0,48},{4,52},{8,56},{12,60},{16,32},{20,36},{24,40},{28,44},{32,1... | collective-permute-start | bytes 589832 | tf_op jit(solution)/shard_map/ppermute | solution.py:337
  134.5 8.8 %collective-permute-done.5.arrived = f32[288,128]{1,0:T(8,128)S(1)} collective-permute-done((f32[288,128]{1,0:T(8,128)S(1)}, f32[288,128]{1,0:T(8,128)S(1)}, u32[]{:S(2)}, u32[]{:S(2)}) %collective-permute-start.5) | collective-permute-done | bytes 147488 | tf_op jit(solution)/shard_map/ppermute | solution.py:337
  143.3 5.5 %shard_map.53 = (f32[160,128]{1,0:T(8,128)S(1)}, f32[160,128]{1,0:T(8,128)S(1)}, f32[128,128]{1,0:T(8,128)S(1)}) custom-call(f32[288,128]{1,0:T(8,128)S(1)} %shard_map.52.mine, f32[288,128]{1,0:T(8,128)S(1)} %collective-permute-done.5.arrived), custom_call_target="tpu_custom_call" | custom-call | tf_op jit(solution)/shard_map/pallas_call | solution.py:73
  148.9 10.8 %all_to_all.32.everyone = f32[4,288,128]{2,1,0:T(8,128)S(1)} all-to-all(f32[4,288,128]{2,1,0:T(8,128)S(1)} %broadcast_in_dim.11), channel_id=1, replica_groups=mesh['leaf'=128,'rhs'=4] {'rhs'}, dimensions={0} | all-to-all | bytes 1179648 | tf_op jit(solution)/shard_map/all_to_all | solution.py:315
  163.1 3.9 %collective-permute-start.10 = (f32[448,128]{1,0:T(8,128)S(1)}, f32[448,128]{1,0:T(8,128)S(1)}, u32[]{:S(2)}, u32[]{:S(2)}) collective-permute-start(f32[448,128]{1,0:T(8,128)S(1)} %get-tuple-element.55.mine), channel_id=1, source_target_pairs={{0,64},{4,68},{8,72},{12,76},{16,80},{20,84},{24,88},{28,92},{32,9... | collective-permute-start | bytes 688136 | tf_op jit(solution)/shard_map/ppermute | solution.py:337
  167.0 4.9 %collective-permute-done.10.arrived = f32[448,128]{1,0:T(8,128)S(1)} collective-permute-done((f32[448,128]{1,0:T(8,128)S(1)}, f32[448,128]{1,0:T(8,128)S(1)}, u32[]{:S(2)}, u32[]{:S(2)}) %collective-permute-start.10) | collective-permute-done | bytes 229408 | tf_op jit(solution)/shard_map/ppermute | solution.py:337
  171.9 5.9 %shard_map.57 = (f32[320,128]{1,0:T(8,128)S(1)}, f32[320,128]{1,0:T(8,128)S(1)}, f32[128,128]{1,0:T(8,128)}) custom-call(f32[448,128]{1,0:T(8,128)S(1)} %get-tuple-element.55.mine, f32[448,128]{1,0:T(8,128)S(1)} %collective-permute-done.10.arrived), custom_call_target="tpu_custom_call" | custom-call | tf_op jit(solution)/shard_map/pallas_call | solution.py:73
  178.2 5.6 %collective-permute-start.12 = (f32[320,128]{1,0:T(8,128)S(1)}, f32[320,128]{1,0:T(8,128)S(1)}, u32[]{:S(2)}, u32[]{:S(2)}) collective-permute-start(f32[320,128]{1,0:T(8,128)S(1)} %get-tuple-element.59.mine), channel_id=1, source_target_pairs={{0,128},{4,132},{8,136},{12,140},{16,144},{20,148},{24,152},{28,15... | collective-permute-start | bytes 491528 | tf_op jit(solution)/shard_map/ppermute | solution.py:337
  185.8 3.7 %collective-permute-done.12.arrived = f32[320,128]{1,0:T(8,128)S(1)} collective-permute-done((f32[320,128]{1,0:T(8,128)S(1)}, f32[320,128]{1,0:T(8,128)S(1)}, u32[]{:S(2)}, u32[]{:S(2)}) %collective-permute-start.12) | collective-permute-done | bytes 163872 | tf_op jit(solution)/shard_map/ppermute | solution.py:337
  189.5 5.9 %shard_map.59 = (f32[192,128]{1,0:T(8,128)S(1)}, f32[192,128]{1,0:T(8,128)S(1)}, f32[128,128]{1,0:T(8,128)}) custom-call(f32[320,128]{1,0:T(8,128)S(1)} %get-tuple-element.59.mine, f32[320,128]{1,0:T(8,128)S(1)} %collective-permute-done.12.arrived), custom_call_target="tpu_custom_call" | custom-call | tf_op jit(solution)/shard_map/pallas_call | solution.py:73
  195.7 9.3 %collective-permute-start.13 = (f32[192,128]{1,0:T(8,128)S(1)}, f32[192,128]{1,0:T(8,128)S(1)}, u32[]{:S(2)}, u32[]{:S(2)}) collective-permute-start(f32[192,128]{1,0:T(8,128)S(1)} %shard_map.60.mine), channel_id=1, source_target_pairs={{0,384},{4,388},{8,392},{12,396},{16,400},{20,404},{24,408},{28,41... | collective-permute-start | bytes 294920 | tf_op jit(solution)/shard_map/ppermute | solution.py:337
  204.9 2.6 %collective-permute-done.13.arrived = f32[192,128]{1,0:T(8,128)S(1)} collective-permute-done((f32[192,128]{1,0:T(8,128)S(1)}, f32[192,128]{1,0:T(8,128)S(1)}, u32[]{:S(2)}, u32[]{:S(2)}) %collective-permute-start.13) | collective-permute-done | bytes 98336 | tf_op jit(solution)/shard_map/ppermute | solution.py:337
  207.5 9.0 %shard_map.61 = f32[64,256]{1,0:T(8,128)S(1)} custom-call(f32[192,128]{1,0:T(8,128)S(1)} %shard_map.60.mine, f32[192,128]{1,0:T(8,128)S(1)} %collective-permute-done.13.arrived, f32[832,128]{1,0:T(8,128)S(1)} %get-tuple-element.62.w1, f32[416,128]{1,0:T(8,128)S(1)} %get-tuple-element.41.refs_3_.weights.w2, f32[384,128]{1,0:T(8,128)S(1)} %copy-done.5, ...), custom_call_target="tpu_custom_call" | custom-call | tf_op jit(solution)/shard_map/pallas_call | solution.py:73
  216.6 8.0 %all_to_all.33.solved = f32[4,16,256]{2,1,0:T(8,128)S(1)} all-to-all(f32[4,16,256]{2,1,0:T(8,128)S(1)} %bitcast.1), channel_id=1, replica_groups=mesh['leaf'=128,'rhs'=4] {'rhs'}, dimensions={0} | all-to-all | bytes 131072 | tf_op jit(solution)/shard_map/all_to_all | solution.py:421
  224.6 2.4 %shard_map.62 = f32[16,1024]{1,0:T(8,128)} custom-call(f32[4,16,256]{2,1,0:T(8,128)S(1)} %all_to_all.33.solved, s32[1,1024]{1,0:T(1,128)S(1)} %copy-done.12), custom_call_target="tpu_custom_call" | custom-call | tf_op jit(solution)/shard_map/pallas_call | solution.py:73
  (62 shorter events, 25.9 us)
Async XLA Ops:
  0.0 1.5 copy-start
  1.5 1.2 copy-start.2
  2.7 0.8 copy-start.8
  3.6 0.7 copy-start.11
  6.8 20.7 %copy-start.1 = (bf16[7,128,1024]{2,1,0:T(8,128)(2,1)S(1)}, bf16[7,128,1024]{2,1,0:T(8,128)(2,1)}, u32[]{:S(2)}) copy-start(bf16[7,128,1024]{2,1,0:T(8,128)(2,1)} %bases.5) | copy-start | bytes 5505028
  30.1 3.8 %collective-permute-start = (f32[1024,128]{1,0:T(8,128)S(1)}, f32[1024,128]{1,0:T(8,128)S(1)}, u32[]{:S(2)}, u32[]{:S(2)}) collective-permute-start(f32[1024,128]{1,0:T(8,128)S(1)} %get-tuple-element.36.mine), channel_id=1, source_target_pairs={{0,4},{4,0},{8,12},{12,8},{16,20},{20,16},{24,28},{28,24},{32,36},... | collective-permute-start | bytes 1572872 | tf_op jit(solution)/shard_map/ppermute | solution.py:337
  61.2 24.8 %collective-permute-start.1 = (f32[704,128]{1,0:T(8,128)S(1)}, f32[704,128]{1,0:T(8,128)S(1)}, u32[]{:S(2)}, u32[]{:S(2)}) collective-permute-start(f32[704,128]{1,0:T(8,128)S(1)} %constant_dynamic-update-slice_fusion.refs_0_), channel_id=1, source_target_pairs={{0,8},{4,12},{8,0},{12,4},{16,24},{20,28},{24,16},{28,20},{32,40},... | collective-permute-start | bytes 1081352 | tf_op jit(solution)/shard_map/ppermute | solution.py:337
  64.7 15.7 %collective-permute-start.2 = (f32[544,128]{1,0:T(8,128)S(1)}, f32[544,128]{1,0:T(8,128)S(1)}, u32[]{:S(2)}, u32[]{:S(2)}) collective-permute-start(f32[544,128]{1,0:T(8,128)S(1)} %get-tuple-element.39.mine), channel_id=1, source_target_pairs={{0,8},{4,12},{8,0},{12,4},{16,24},{20,28},{24,16},{28,20},{32,40},... | collective-permute-start | bytes 835592 | tf_op jit(solution)/shard_map/ppermute | solution.py:337
  67.1 25.8 %collective-permute-start.6 = (f32[384,128]{1,0:T(8,128)}, f32[384,128]{1,0:T(8,128)}, u32[]{:S(2)}, u32[]{:S(2)}) collective-permute-start(f32[384,128]{1,0:T(8,128)} %get-tuple-element.47.mine), channel_id=1, source_target_pairs={{0,8},{4,12},{8,0},{12,4},{16,24},{20,28},{24,16},{28,20},{32,40},... | collective-permute-start | bytes 589832 | tf_op jit(solution)/shard_map/ppermute | solution.py:337
  86.5 20.1 %copy-start.6 = (f32[288,128]{1,0:T(8,128)}, f32[288,128]{1,0:T(8,128)S(1)}, u32[]{:S(2)}) copy-start(f32[288,128]{1,0:T(8,128)S(1)} %get-tuple-element.42.refs_0_) | copy-start | bytes 442372
  86.5 20.1 %collective-permute-start.4 = (f32[416,128]{1,0:T(8,128)S(1)}, f32[416,128]{1,0:T(8,128)}, u32[]{:S(2)}, u32[]{:S(2)}) collective-permute-start(f32[416,128]{1,0:T(8,128)S(1)} %get-tuple-element.43.mine), channel_id=1, source_target_pairs={{0,16},{4,20},{8,24},{12,28},{16,0},{20,4},{24,8},{28,12},{32,48},... | collective-permute-start | bytes 638984 | tf_op jit(solution)/shard_map/ppermute | solution.py:337
  89.5 9.7 %all-to-all-start.2 = ((f32[4,96,128]{2,1,0:T(8,128)}), f32[4,96,128]{2,1,0:T(8,128)S(1)}, u32[]{:S(2)}, u32[]{:S(2)}) async-start(f32[4,96,128]{2,1,0:T(8,128)} %broadcast_in_dim.9), calls=%async_computation.2 | async-start | bytes 393216 | tf_op jit(solution)/shard_map/all_to_all | solution.py:315
  101.5 0.7 copy-start.4
  102.2 17.4 %collective-permute-start.7 = (f32[384,128]{1,0:T(8,128)}, f32[384,128]{1,0:T(8,128)}, u32[]{:S(2)}, u32[]{:S(2)}) collective-permute-start(f32[384,128]{1,0:T(8,128)} %get-tuple-element.49.mine), channel_id=1, source_target_pairs={{0,16},{4,20},{8,24},{12,28},{16,0},{20,4},{24,8},{28,12},{32,48},... | collective-permute-start | bytes 589832 | tf_op jit(solution)/shard_map/ppermute | solution.py:337
  113.2 0.7 copy-start.9
  113.2 19.1 %copy-start.7 = (f32[288,128]{1,0:T(8,128)S(1)}, f32[288,128]{1,0:T(8,128)}, u32[]{:S(2)}) copy-start(f32[288,128]{1,0:T(8,128)} %copy-done.6) | copy-start | bytes 442372
  113.9 9.7 %all-to-all-start.3 = ((f32[4,96,128]{2,1,0:T(8,128)}), f32[4,96,128]{2,1,0:T(8,128)S(1)}, u32[]{:S(2)}, u32[]{:S(2)}) async-start(f32[4,96,128]{2,1,0:T(8,128)} %broadcast_in_dim.10), calls=%async_computation.3 | async-start | bytes 393216 | tf_op jit(solution)/shard_map/all_to_all | solution.py:315
  117.3 15.0 %collective-permute-start.3 = (f32[288,128]{1,0:T(8,128)}, f32[288,128]{1,0:T(8,128)S(1)}, u32[]{:S(2)}, u32[]{:S(2)}) collective-permute-start(f32[288,128]{1,0:T(8,128)} %copy-done.6), channel_id=1, source_target_pairs={{0,16},{4,20},{8,24},{12,28},{16,0},{20,4},{24,8},{28,12},{32,48},... | collective-permute-start | bytes 442376 | tf_op jit(solution)/shard_map/ppermute | solution.py:337
  123.6 0.8 copy-start.10
  126.1 22.7 %collective-permute-start.8 = (f32[384,128]{1,0:T(8,128)S(1)}, f32[384,128]{1,0:T(8,128)S(1)}, u32[]{:S(2)}, u32[]{:S(2)}) collective-permute-start(f32[384,128]{1,0:T(8,128)S(1)} %get-tuple-element.51.mine), channel_id=1, source_target_pairs={{0,48},{4,52},{8,56},{12,60},{16,32},{20,36},{24,40},{28,44},{32,1... | collective-permute-start | bytes 589832 | tf_op jit(solution)/shard_map/ppermute | solution.py:337
  132.5 10.7 %collective-permute-start.5 = (f32[288,128]{1,0:T(8,128)S(1)}, f32[288,128]{1,0:T(8,128)S(1)}, u32[]{:S(2)}, u32[]{:S(2)}) collective-permute-start(f32[288,128]{1,0:T(8,128)S(1)} %shard_map.52.mine), channel_id=1, source_target_pairs={{0,48},{4,52},{8,56},{12,60},{16,32},{20,36},{24,40},{28,44},{32,1... | collective-permute-start | bytes 442376 | tf_op jit(solution)/shard_map/ppermute | solution.py:337
  160.8 46.7 %copy-start.3 = (f32[1024,256]{1,0:T(8,128)S(1)}, f32[1024,256]{1,0:T(8,128)}, u32[]{:S(2)}) copy-start(f32[1024,256]{1,0:T(8,128)} %inverse_cols.3) | copy-start | bytes 3145732
  160.8 46.7 %copy-start.5 = (f32[384,128]{1,0:T(8,128)S(1)}, f32[384,128]{1,0:T(8,128)}, u32[]{:S(2)}) copy-start(f32[384,128]{1,0:T(8,128)} %copy-done.4) | copy-start | bytes 589828
  160.8 17.0 %collective-permute-start.9 = (f32[512,128]{1,0:T(8,128)S(1)}, f32[512,128]{1,0:T(8,128)S(1)}, u32[]{:S(2)}, u32[]{:S(2)}) collective-permute-start(f32[512,128]{1,0:T(8,128)S(1)} %get-tuple-element.54.refs_0_), channel_id=1, source_target_pairs={{0,64},{4,68},{8,72},{12,76},{16,80},{20,84},{24,88},{28,92},{32,9... | collective-permute-start | bytes 786440 | tf_op jit(solution)/shard_map/ppermute | solution.py:337
  163.1 8.8 %collective-permute-start.10 = (f32[448,128]{1,0:T(8,128)S(1)}, f32[448,128]{1,0:T(8,128)S(1)}, u32[]{:S(2)}, u32[]{:S(2)}) collective-permute-start(f32[448,128]{1,0:T(8,128)S(1)} %get-tuple-element.55.mine), channel_id=1, source_target_pairs={{0,64},{4,68},{8,72},{12,76},{16,80},{20,84},{24,88},{28,92},{32,9... | collective-permute-start | bytes 688136 | tf_op jit(solution)/shard_map/ppermute | solution.py:337
  178.2 11.3 %collective-permute-start.12 = (f32[320,128]{1,0:T(8,128)S(1)}, f32[320,128]{1,0:T(8,128)S(1)}, u32[]{:S(2)}, u32[]{:S(2)}) collective-permute-start(f32[320,128]{1,0:T(8,128)S(1)} %get-tuple-element.59.mine), channel_id=1, source_target_pairs={{0,128},{4,132},{8,136},{12,140},{16,144},{20,148},{24,152},{28,15... | collective-permute-start | bytes 491528 | tf_op jit(solution)/shard_map/ppermute | solution.py:337
  183.9 11.5 %collective-permute-start.11 = (f32[192,128]{1,0:T(8,128)S(1)}, f32[192,128]{1,0:T(8,128)S(1)}, u32[]{:S(2)}, u32[]{:S(2)}) collective-permute-start(f32[192,128]{1,0:T(8,128)S(1)} %get-tuple-element.58.refs_0_), channel_id=1, source_target_pairs={{0,128},{4,132},{8,136},{12,140},{16,144},{20,148},{24,152},{28,15... | collective-permute-start | bytes 294920 | tf_op jit(solution)/shard_map/ppermute | solution.py:337
  195.7 11.9 %collective-permute-start.13 = (f32[192,128]{1,0:T(8,128)S(1)}, f32[192,128]{1,0:T(8,128)S(1)}, u32[]{:S(2)}, u32[]{:S(2)}) collective-permute-start(f32[192,128]{1,0:T(8,128)S(1)} %shard_map.60.mine), channel_id=1, source_target_pairs={{0,384},{4,388},{8,392},{12,396},{16,400},{20,404},{24,408},{28,41... | collective-permute-start | bytes 294920 | tf_op jit(solution)/shard_map/ppermute | solution.py:337
  207.5 17.0 %copy-start.12 = (s32[1,1024]{1,0:T(1,128)S(1)}, s32[1,1024]{1,0:T(1,128)}, u32[]{:S(2)}) copy-start(s32[1,1024]{1,0:T(1,128)} %order.3) | copy-start | bytes 12292

commit v2 on v0

v2 whole, which is shorter than its diff:
```python
import functools

import jax
import jax.numpy as jnp
from jax import lax
from jax.experimental import pallas as pl
from jax.experimental.pallas import tpu as pltpu
from jax.sharding import PartitionSpec as P

HIGHEST = lax.Precision.HIGHEST
NN = (((1,), (0,)), ((), ()))
NT = (((1,), (1,)), ((), ()))


def exact_dot(left, right, dims):
    return lax.dot_general(left, right, dims, precision=HIGHEST, preferred_element_type=jnp.float32)


def short_dot(left, right, dims):
    return lax.dot_general(left, right, dims, preferred_element_type=jnp.float32)


def three_parts(values):
    high = values.astype(jnp.bfloat16)
    rest = values - high.astype(jnp.float32)
    middle = rest.astype(jnp.bfloat16)
    low = (rest - middle.astype(jnp.float32)).astype(jnp.bfloat16)
    return high, middle, low


def dot_left_parts(left, right16, dims):
    high, middle, low = three_parts(left)
    return short_dot(low, right16, dims) + short_dot(middle, right16, dims) + short_dot(high, right16, dims)


def dot_right_parts(left16, right, dims):
    high, middle, low = three_parts(right)
    return short_dot(left16, low, dims) + short_dot(left16, middle, dims) + short_dot(left16, high, dims)


def inverse_of(capacity):
    size = capacity.shape[0]
    shape = (size, size)
    eye = jnp.where(
        lax.broadcasted_iota(jnp.int32, shape, 0) == lax.broadcasted_iota(jnp.int32, shape, 1), 1.0, 0.0
    )
    bound = jnp.max(jnp.sum(jnp.abs(capacity), axis=1, keepdims=True), axis=0, keepdims=True)
    scale = 2.0 / (1.0 + bound)
    begin = 2.0 * scale * eye - scale * scale * capacity
    guess = begin
    short = capacity.astype(jnp.bfloat16)
    for _ in range(4):
        guess16 = guess.astype(jnp.bfloat16)
        factor = 2.0 * eye - short_dot(short, guess16, NN)
        guess = short_dot(guess16, factor.astype(jnp.bfloat16), NN)

    def unfinished(state):
        return (state[1] == 0) | ((state[1] < 80) & jnp.logical_not(state[2] < 1e-6))

    def improve(state):
        inverse, count, _ = state
        residual = eye - exact_dot(capacity, inverse, NN)
        size2 = jnp.sum(residual * residual)
        better = inverse + exact_dot(inverse, residual, NN)
        restart = (count == 0) & jnp.logical_not(size2 < 0.25)
        return jnp.where(restart, begin, better), count + 1, size2

    return lax.while_loop(unfinished, improve, (guess, 0, jnp.float32(1.0)))[0]


def run(body, outs, *args, cost=3):
    vmem = pl.BlockSpec(memory_space=pltpu.VMEM)
    return pl.pallas_call(
        body,
        out_shape=[jax.ShapeDtypeStruct(shape, jnp.float32) for shape in outs],
        in_specs=[vmem] * len(args),
        out_specs=[vmem] * len(outs),
        cost_estimate=pl.CostEstimate(flops=cost * 1_000_000_000, bytes_accessed=0, transcendentals=0),
        compiler_params=pltpu.CompilerParams(vmem_limit_bytes=48 * 1024 * 1024),
    )(*args)


def one_hot(order):
    size = order.shape[1]
    rows = lax.broadcasted_iota(jnp.int32, (size, size), 0)
    return jnp.where(rows == order, 1.0, 0.0).astype(jnp.bfloat16)


def identity(size):
    shape = (size, size)
    return jnp.where(
        lax.broadcasted_iota(jnp.int32, shape, 0) == lax.broadcasted_iota(jnp.int32, shape, 1), 1.0, 0.0
    )


def stacked(everyone, low, count):
    return jnp.concatenate([everyone[group, low : low + count, :] for group in range(everyone.shape[0])], 0)


def start_body(sides, order, inverse_cols, bases, send, tree):
    levels, rank, leaf = bases.shape
    groups, _, piece = send.shape
    share = rank // groups
    tree[...] = dot_left_parts(sides[...], one_hot(order[...]), NN)
    applied = dot_right_parts(bases[...].reshape(levels * rank, leaf), inverse_cols[...], NN)
    for group in range(groups):
        for level in range(levels):
            low = level * rank + group * share
            send[group, level * share : (level + 1) * share, :] = applied[low : low + share]
        send[group, levels * share :, :] = tree[:, group * piece : (group + 1) * piece]


def gram_body(got, send, bases, gram):
    levels, rank, leaf = bases.shape
    groups, rows, piece = got.shape
    share = rank // groups
    own = rows - levels * share
    applied = jnp.concatenate([got[group, : levels * share, :] for group in range(groups)], 1)
    product = dot_left_parts(applied, bases[...].reshape(levels * rank, leaf), NT)
    at = 0
    for column in range(levels):
        count = (levels - column) * share
        gram[at : at + count, :] = product[column * share :, column * rank : (column + 1) * rank]
        at += count
    sides = stacked(got, levels * share, own)
    for level in range(levels):
        block = exact_dot(sides, stacked(send, level * share, share), NT)
        for group in range(groups):
            low = at + (group * levels + level) * own
            gram[low : low + own, :] = block[group * own : (group + 1) * own]


def first_body(everyone, mine, arrived, panel, weights, own_weights, inverse, side_upper):
    groups, _, rank = everyone.shape
    share = rank // groups
    own = side_upper.shape[0]
    far = jnp.concatenate([stacked(everyone, level * share, share) for level in range(1, 7)], 0)
    inverse[...] = inverse_of(stacked(everyone, 0, share) + identity(rank))
    side_row = lambda level: sum(
        everyone[group, 7 * share + level * own : 7 * share + (level + 1) * own, :] for group in range(groups)
    )
    side_upper[...] = side_row(0)
    upper = jnp.concatenate([mine[share : 7 * share, :] + arrived[share : 7 * share, :], side_upper[...]], 0)
    own_weights[...] = exact_dot(upper, inverse[...], NN)
    update = exact_dot(own_weights[...], far[:rank], NT)
    panel[: 6 * share, :] = mine[7 * share : 13 * share, :] + arrived[7 * share : 13 * share, :] - update[: 6 * share]
    panel[6 * share :, :] = side_row(1) - update[6 * share :]
    weights[...] = far


def first_rest_body(everyone, mine, arrived, far, own_weights, rest):
    groups, _, rank = everyone.shape
    share = rank // groups
    own = own_weights.shape[0] - 6 * share
    side_row = lambda level: sum(
        everyone[group, 7 * share + level * own : 7 * share + (level + 1) * own, :] for group in range(groups)
    )
    at = 0
    source = 13 * share
    for column in range(2, 7):
        count = (7 - column) * share
        update = exact_dot(own_weights[(column - 1) * share :, :], far[(column - 1) * rank : column * rank, :], NT)
        rest[at : at + count, :] = (
            mine[source : source + count, :] + arrived[source : source + count, :] - update[:count]
        )
        rest[at + count : at + count + own, :] = side_row(column) - update[count:]
        source += count
        at += count + own


def level_body(everyone, mine, arrived, later, later_arrived, panel, far, own_weights, inverse):
    groups, rows, rank = everyone.shape
    share = rank // groups
    above = rows // share - 1
    far[...] = jnp.concatenate([stacked(everyone, level * share, share) for level in range(1, above + 1)], 0)
    inverse[...] = inverse_of(stacked(everyone, 0, share) + identity(rank))
    own_weights[...] = exact_dot(mine[share:, :] + arrived[share:, :], inverse[...], NN)
    count = panel.shape[0]
    panel[...] = later[:count, :] + later_arrived[:count, :] - exact_dot(own_weights[...], far[:rank, :], NT)


def level_rest_body(later, later_arrived, far, own_weights, rest):
    rank = far.shape[1]
    share = rank // 4
    at = 0
    source = own_weights.shape[0]
    for column in range(1, far.shape[0] // rank):
        count = own_weights.shape[0] - column * share
        update = exact_dot(own_weights[column * share :, :], far[column * rank : (column + 1) * rank, :], NT)
        rest[at : at + count, :] = (
            later[source : source + count, :] + later_arrived[source : source + count, :] - update
        )
        source += count
        at += count


def spread_body(everyone, fifth, far, weights, side_weights, inverse):
    groups, _, rank = everyone.shape
    share = rank // groups
    own = fifth.shape[0] - 3 * rank
    own = own // groups
    blocks = [stacked(everyone, level * share, share) for level in range(4)]
    inverse[...] = inverse_of(blocks[0] + identity(rank))
    far[: 3 * rank, :] = jnp.concatenate(blocks[1:], 0)
    far[3 * rank :, :] = stacked(everyone, 4 * share, own)
    weights[...] = exact_dot(far[...], inverse[...], NN)
    update = exact_dot(weights[...], far[:rank, :], NT)
    at = 4 * share + own
    for level in range(3):
        fifth[level * rank : (level + 1) * rank, :] = (
            stacked(everyone, at + level * share, share) - update[level * rank : (level + 1) * rank]
        )
    fifth[3 * rank :, :] = stacked(everyone, at + 3 * share, own) - update[3 * rank :]
    side_weights[...] = weights[3 * rank :, :]


def spread_rest_body(everyone, far, weights, rest):
    groups, _, rank = everyone.shape
    share = rank // groups
    own = (far.shape[0] - 3 * rank) // groups
    source = 7 * share + 2 * own
    at = 0
    for column in (1, 2):
        update = exact_dot(weights[column * rank :, :], far[column * rank : (column + 1) * rank, :], NT)
        for level in range(column, 3):
            low = (level - column) * rank
            rest[at : at + rank, :] = stacked(everyone, source, share) - update[low : low + rank]
            at += rank
            source += share
        rest[at : at + groups * own, :] = stacked(everyone, source, own) - update[(3 - column) * rank :]
        at += groups * own
        source += own


def factor_body(mine, arrived, later, later_arrived, panel, upper, weights):
    rank = mine.shape[1]
    upper[...] = mine[rank:, :] + arrived[rank:, :]
    inverse = inverse_of(mine[:rank, :] + arrived[:rank, :] + identity(rank))
    weights[...] = exact_dot(upper[...], inverse, NN)
    count = panel.shape[0]
    panel[...] = later[:count, :] + later_arrived[:count, :] - exact_dot(weights[...], upper[:rank, :], NT)


def factor_rest_body(later, later_arrived, upper, weights, rest):
    rank = upper.shape[1]
    source = weights.shape[0]
    rest[...] = (
        later[source:, :] + later_arrived[source:, :]
        - exact_dot(weights[rank:, :], upper[rank : 2 * rank, :], NT)
    )


def prepare_body(
    tree, everyone, send, inverse_cols, f1, i1, f2, i2, f3, i3, w4, w5, w6, base, slope
):
    groups, _, rank = everyone.shape
    share = rank // groups
    sides = base.shape[0]
    own = sides // groups
    none = jnp.zeros((rank, rank), jnp.float32)
    found = jnp.concatenate([jnp.zeros((sides, rank), jnp.float32), identity(rank)], 0)

    def lower(side_weights, blocks):
        return jnp.concatenate([side_weights, none], 0) - exact_dot(found, blocks, NN)

    for weights in (w6, w5, w4):
        count = weights.shape[0] - sides
        found = jnp.concatenate([lower(weights[count:, :], weights[:count, :]), found], 1)
    source = everyone.shape[1] - 3 * own
    for level, far, inverse in ((2, f3, i3), (1, f2, i2), (0, f1, i1)):
        low = source + level * own
        side_weights = exact_dot(stacked(everyone, low, own), inverse[...], NN)
        blocks = exact_dot(far[...], inverse[...], NN)
        found = jnp.concatenate([lower(side_weights, blocks), found], 1)
    applied = jnp.concatenate([stacked(send, level * share, share) for level in range(7)], 0)
    total = exact_dot(found, applied, NN)
    base[...] = exact_dot(tree[...], inverse_cols[...], NN) - total[:sides]
    slope[...] = total[sides:]


def finish_body(mine, arrived, base, slope, solved):
    rank = mine.shape[1]
    inverse = inverse_of(mine[:rank, :] + arrived[:rank, :] + identity(rank))
    top = exact_dot(mine[rank:, :] + arrived[rank:, :], inverse, NN)
    solved[...] = base[...] - exact_dot(top, slope[...], NN)


def untangle_body(solved, order, out):
    groups = solved.shape[0]
    whole = jnp.concatenate([solved[group] for group in range(groups)], 1)
    out[...] = dot_left_parts(whole, one_hot(order[...]), NT)


def to_all(block, axis):
    count = lax.axis_size(axis)
    return lax.all_to_all(jnp.broadcast_to(block[None], (count,) + block.shape), axis, 0, 0)


def route(height):
    pairs = []
    for leaf in range(128):
        if height in (4, 7):
            low = 1 if height == 4 else 4
            ring = (leaf >> low) & 7
            pairs.append((leaf, leaf & ~(7 << low) | ((ring ^ 6) << low)))
        else:
            pairs.append((leaf, leaf ^ (1 << (height - 1))))
    return pairs


def local(right_sides, leaf_inverse, bases, ordering):
    own, leaf = right_sides.shape
    piece = leaf_inverse.shape[1]
    levels, rank, _ = bases.shape
    groups = lax.axis_size("rhs")
    share = rank // groups
    sides = own * groups
    square = (rank, rank)
    swap = lambda block, height: lax.ppermute(block, "leaf", route(height))

    send, tree = run(
        start_body,
        [(groups, levels * share + own, piece), (own, leaf)],
        right_sides,
        ordering,
        leaf_inverse,
        bases,
    )
    got = lax.all_to_all(send, "rhs", 0, 0)
    rows = 28 * share
    (gram,) = run(gram_body, [(rows + groups * levels * own, rank)], got, send, bases)
    other = swap(gram, 1)
    total = gram + other
    shared = jnp.broadcast_to(total[: 7 * share][None], (groups, 7 * share, rank))
    parts = total[rows:].reshape(groups, levels * own, rank)
    everyone = lax.all_to_all(jnp.concatenate([shared, parts], 1), "rhs", 0, 0)

    panel, far1, own_weights, inverse1, side1 = run(
        first_body,
        [(6 * share + own, rank), (6 * rank, rank), (6 * share + own, rank), square, (own, rank)],
        everyone,
        gram,
        other,
    )
    arrived = swap(panel, 2)
    (later,) = run(
        first_rest_body, [(15 * share + 5 * own, rank)], everyone, gram, other, far1, own_weights
    )
    far, inverses, side_uppers = [far1], [inverse1], [side1]
    for height in (2, 3):
        above = 7 - height
        later_arrived = swap(later, height)
        near = panel[: (above + 1) * share] + arrived[: (above + 1) * share]
        near, later = lax.optimization_barrier((near, later))
        everyone = to_all(near, "rhs")
        side_uppers.append(panel[(above + 1) * share :] + arrived[(above + 1) * share :])
        next_panel, level_far, own_weights, inverse = run(
            level_body,
            [(above * share + own, rank), (above * rank, rank), (above * share + own, rank), square],
            everyone,
            panel,
            arrived,
            later,
            later_arrived,
        )
        arrived = swap(next_panel, height + 1)
        rest_rows = above * (above - 1) // 2 * share + (above - 1) * own
        (later,) = run(
            level_rest_body, [(rest_rows, rank)], later, later_arrived, level_far, own_weights
        )
        panel = next_panel
        far.append(level_far)
        inverses.append(inverse)

    later_arrived = swap(later, 4)
    everyone = to_all(
        jnp.concatenate([panel + arrived, later + later_arrived] + side_uppers, 0), "rhs"
    )
    upper_shape = (3 * rank + sides, rank)
    panel, upper, weights, _, _ = run(
        spread_body, [upper_shape, upper_shape, upper_shape, (sides, rank), square], everyone
    )
    arrived = swap(panel, 5)
    (later,) = run(spread_rest_body, [(3 * rank + 2 * sides, rank)], everyone, upper, weights)
    later_arrived = swap(later, 5)
    kept = [weights]
    tree, later = lax.optimization_barrier((tree, later))
    whole_tree = to_all(tree, "rhs").reshape(sides, leaf)
    next_panel, upper, weights = run(
        factor_body,
        [(2 * rank + sides, rank)] * 3,
        panel,
        arrived,
        later,
        later_arrived,
    )
    kept.append(weights)
    arrived = swap(next_panel, 6)
    (later,) = run(factor_rest_body, [(rank + sides, rank)], later, later_arrived, upper, weights)
    later_arrived = swap(later, 6)
    panel, upper, weights = run(
        factor_body,
        [(rank + sides, rank)] * 3,
        next_panel,
        arrived,
        later,
        later_arrived,
    )
    kept.append(weights)
    arrived = swap(panel, 7)
    pairs = [item for pair in zip(far, inverses) for item in pair]
    base, slope = run(
        prepare_body, [(sides, piece), (rank, piece)], whole_tree, everyone, send, leaf_inverse, *pairs, *kept
    )
    (solved,) = run(finish_body, [(sides, piece)], panel, arrived, base, slope)
    back = lax.all_to_all(solved.reshape(groups, own, piece), "rhs", 0, 0)
    (result,) = run(untangle_body, [(own, leaf)], back, ordering)
    return result


def solution(mesh):
    placed = (P("rhs", "leaf"), P("leaf", "rhs"), P(None, None, "leaf"), P("leaf", None))
    return jax.shard_map(
        local, mesh=mesh, in_specs=placed, out_specs=P("rhs", "leaf"), check_vma=False
    )
```

time: 642 us -> 228 us (0.36)
  the two profiles are of different devices: /device:TPU:2 before, /device:TPU:8 now
where the time goes in v2:
time: 228 us; the launch traced here: 227 us
  Pallas kernels  60.7 us (27%)
  blocking collectives  57.6 us (25%)
  starting transfers between devices  57.2 us (25%)
  waiting for transfers between devices  34.4 us (15%)
  local copies, waits for them, and re-layouts  16.4 us (7%)
    pallas_call x16, Pallas kernels, run(): pl.pallas_call(body, out_shape=[jax.ShapeDtypeStruct(shape, jnp.float32)...  60.7 us
    ppermute x12, starting transfers between devices, local(): swap = lambda block, height: lax.ppermute(block, 'leaf', route(height))  45.7 us
    ppermute x12, waiting for transfers between devices, local(): swap = lambda block, height: lax.ppermute(block, 'leaf', route(height))  34.4 us
    all_to_all x1, blocking collectives, local(): got = lax.all_to_all(send, 'rhs', 0, 0)  18.6 us
    all_to_all x1, blocking collectives, to_all(): lax.all_to_all(jnp.broadcast_to(block[None], (count,) + block.shape), axi...  14.6 us
    all_to_all x1, blocking collectives, local(): everyone = lax.all_to_all(jnp.concatenate([shared, parts], 1), 'rhs', 0, 0)  14.2 us
    unnamed x51, local copies, waits for them, and re-layouts  14 us
    all_to_all x3, starting transfers between devices, to_all(): lax.all_to_all(jnp.broadcast_to(block[None], (count,) + block.shape), axi...  11.5 us
  transfers between devices with their start and end apart: 15, of which 9 were waited for; matrix products, arithmetic and copies ran while one was open for 0% of the time, Pallas kernels for 7%

profile of v2, /device:TPU:8, one launch (start us, length us, event | category | flops | bytes accessed | tf_op | source)
XLA Modules:
  0.0 226.9 jit_solution(17137376276230908222)
XLA Ops:
  4.3 2.6 %shard_map.46 = (f32[4,240,256]{2,1,0:T(8,128)S(1)}, f32[16,1024]{1,0:T(8,128)S(1)}) custom-call(f32[16,1024]{1,0:T(8,128)S(1)} %copy-done.4, s32[1,1024]{1,0:T(1,128)S(1)} %copy-done.5, f32[1024,256]{1,0:T(8,128)S(1)} %copy-done.2, bf16[7,128,1024]{2,1,0:T(8,128)(2,1)S(1)} %copy-done), custom_call_target="tpu_custom_call" | custom-call | flops 3000000000 | tf_op jit(solution)/shard_map/pallas_call | solution.py:73
  6.8 18.6 %all_to_all.35.got = f32[4,240,256]{2,1,0:T(8,128)S(1)} all-to-all(f32[4,240,256]{2,1,0:T(8,128)S(1)} %get-tuple-element.36.send), channel_id=1, replica_groups=mesh['leaf'=128,'rhs'=4] {'rhs'}, dimensions={0} | all-to-all | bytes 1966080 | tf_op jit(solution)/shard_map/all_to_all | solution.py:329
  25.4 2.6 %shard_map.47.mine = f32[1344,128]{1,0:T(8,128)S(1)} custom-call(f32[4,240,256]{2,1,0:T(8,128)S(1)} %all_to_all.35.got, f32[4,240,256]{2,1,0:T(8,128)S(1)} %get-tuple-element.36.send, bf16[7,128,1024]{2,1,0:T(8,128)(2,1)S(1)} %copy-done.1), custom_call_target="tpu_custom_call" | custom-call | flops 3000000000 | tf_op jit(solution)/shard_map/pallas_call | solution.py:73
  32.3 14.2 %all_to_all.36.everyone = f32[4,336,128]{2,1,0:T(8,128)S(1)} all-to-all(f32[4,336,128]{2,1,0:T(8,128)S(1)} %pad_maximum_fusion), channel_id=1, replica_groups=mesh['leaf'=128,'rhs'=4] {'rhs'}, dimensions={0} | all-to-all | bytes 1376256 | tf_op jit(solution)/shard_map/all_to_all | solution.py:336
  46.5 6.3 %shard_map.48 = (f32[208,128]{1,0:T(8,128)S(1)}, f32[768,128]{1,0:T(8,128)S(1)}, f32[208,128]{1,0:T(8,128)S(1)}, f32[128,128]{1,0:T(8,128)S(1)}, f32[16,128]{1,0:T(8,128)S(1)}) custom-call(f32[4,336,128]{2,1,0:T(8,128)S(1)} %all_to_all.36.everyone, f32[1344,128]{1,0:T(8,128)S(1)} %shard_map.47.mine, f32[1344,128]{1,0:T(8,128)S(1)} %collective-permute-done.arrived), custom_call_target="tpu_custom_call" | custom-call | flops 3000000000 | tf_op jit(solution)/shard_map/pallas_call | solution.py:73
  52.8 2.4 %collective-permute-start.1 = (f32[208,128]{1,0:T(8,128)S(1)}, f32[208,128]{1,0:T(8,128)S(1)}, u32[]{:S(2)}, u32[]{:S(2)}) collective-permute-start(f32[208,128]{1,0:T(8,128)S(1)} %get-tuple-element.37.mine), channel_id=1, source_target_pairs={{0,8},{4,12},{8,0},{12,4},{16,24},{20,28},{24,16},{28,20},{32,40},... | collective-permute-start | bytes 319496 | tf_op jit(solution)/shard_map/ppermute | solution.py:319
  56.0 3.5 %collective-permute-done.1.arrived = f32[208,128]{1,0:T(8,128)S(1)} collective-permute-done((f32[208,128]{1,0:T(8,128)S(1)}, f32[208,128]{1,0:T(8,128)S(1)}, u32[]{:S(2)}, u32[]{:S(2)}) %collective-permute-start.1) | collective-permute-done | bytes 106528 | tf_op jit(solution)/shard_map/ppermute | solution.py:319
  60.2 3.5 %all-to-all-start.2 = ((f32[4,192,128]{2,1,0:T(8,128)}), f32[4,192,128]{2,1,0:T(8,128)S(1)}, u32[]{:S(2)}, u32[]{:S(2)}) async-start(f32[4,192,128]{2,1,0:T(8,128)} %broadcast_in_dim.11), calls=%async_computation.2 | async-start | bytes 786432 | tf_op jit(solution)/shard_map/all_to_all | solution.py:296
  66.1 6.3 %collective-permute-done.2.later_arrived = f32[560,128]{1,0:T(8,128)S(1)} collective-permute-done((f32[560,128]{1,0:T(8,128)S(1)}, f32[560,128]{1,0:T(8,128)S(1)}, u32[]{:S(2)}, u32[]{:S(2)}) %collective-permute-start.2) | collective-permute-done | bytes 286752 | tf_op jit(solution)/shard_map/ppermute | solution.py:319
  72.3 6.3 %shard_map.50 = (f32[176,128]{1,0:T(8,128)S(1)}, f32[640,128]{1,0:T(8,128)S(1)}, f32[176,128]{1,0:T(8,128)S(1)}, f32[128,128]{1,0:T(8,128)S(1)}) custom-call(f32[4,192,128]{2,1,0:T(8,128)S(1)} %all-to-all-done.2.everyone, f32[208,128]{1,0:T(8,128)S(1)} %get-tuple-element.37.mine, f32[208,128]{1,0:T(8,128)S(1)} %collective-permute-done.1.arrived, ...), custom_call_target="tpu_custom_call" | custom-call | flops 3000000000 | tf_op jit(solution)/shard_map/pallas_call | solution.py:73
  79.2 4.0 %collective-permute-start.3 = (f32[176,128]{1,0:T(8,128)S(1)}, f32[176,128]{1,0:T(8,128)S(1)}, u32[]{:S(2)}, u32[]{:S(2)}) collective-permute-start(f32[176,128]{1,0:T(8,128)S(1)} %get-tuple-element.42.mine), channel_id=1, source_target_pairs={{0,16},{4,20},{8,24},{12,28},{16,0},{20,4},{24,8},{28,12},{32,48},... | collective-permute-start | bytes 270344 | tf_op jit(solution)/shard_map/ppermute | solution.py:319
  83.9 2.6 %collective-permute-done.3.arrived = f32[176,128]{1,0:T(8,128)S(1)} collective-permute-done((f32[176,128]{1,0:T(8,128)S(1)}, f32[176,128]{1,0:T(8,128)S(1)}, u32[]{:S(2)}, u32[]{:S(2)}) %collective-permute-start.3) | collective-permute-done | bytes 90144 | tf_op jit(solution)/shard_map/ppermute | solution.py:319
  87.3 4.6 %all-to-all-start.3 = ((f32[4,160,128]{2,1,0:T(8,128)}), f32[4,160,128]{2,1,0:T(8,128)S(1)}, u32[]{:S(2)}, u32[]{:S(2)}) async-start(f32[4,160,128]{2,1,0:T(8,128)} %broadcast_in_dim.12), calls=%async_computation.3 | async-start | bytes 655360 | tf_op jit(solution)/shard_map/all_to_all | solution.py:296
  91.9 4.9 %collective-permute-start.4 = (f32[384,128]{1,0:T(8,128)S(1)}, f32[384,128]{1,0:T(8,128)S(1)}, u32[]{:S(2)}, u32[]{:S(2)}) collective-permute-start(f32[384,128]{1,0:T(8,128)S(1)} %shard_map.51.later), channel_id=1, source_target_pairs={{0,16},{4,20},{8,24},{12,28},{16,0},{20,4},{24,8},{28,12},{32,48},... | collective-permute-start | bytes 589832 | tf_op jit(solution)/shard_map/ppermute | solution.py:319
  96.8 4.4 %collective-permute-done.4.later_arrived = f32[384,128]{1,0:T(8,128)S(1)} collective-permute-done((f32[384,128]{1,0:T(8,128)S(1)}, f32[384,128]{1,0:T(8,128)S(1)}, u32[]{:S(2)}, u32[]{:S(2)}) %collective-permute-start.4) | collective-permute-done | bytes 196640 | tf_op jit(solution)/shard_map/ppermute | solution.py:319
  101.2 5.8 %shard_map.52 = (f32[144,128]{1,0:T(8,128)S(1)}, f32[512,128]{1,0:T(8,128)S(1)}, f32[144,128]{1,0:T(8,128)S(1)}, f32[128,128]{1,0:T(8,128)S(1)}) custom-call(f32[4,160,128]{2,1,0:T(8,128)S(1)} %all-to-all-done.3.everyone, f32[176,128]{1,0:T(8,128)S(1)} %get-tuple-element.42.mine, f32[176,128]{1,0:T(8,128)S(1)} %collective-permute-done.3.arrived, ...), custom_call_target="tpu_custom_call" | custom-call | flops 3000000000 | tf_op jit(solution)/shard_map/pallas_call | solution.py:73
  107.1 7.0 %collective-permute-start.5 = (f32[144,128]{1,0:T(8,128)S(1)}, f32[144,128]{1,0:T(8,128)S(1)}, u32[]{:S(2)}, u32[]{:S(2)}) collective-permute-start(f32[144,128]{1,0:T(8,128)S(1)} %get-tuple-element.47), channel_id=1, source_target_pairs={{0,48},{4,52},{8,56},{12,60},{16,32},{20,36},{24,40},{28,44},{32,1... | collective-permute-start | bytes 221192 | tf_op jit(solution)/shard_map/ppermute | solution.py:319
  118.0 5.6 %collective-permute-done.6 = f32[240,128]{1,0:T(8,128)S(1)} collective-permute-done((f32[240,128]{1,0:T(8,128)S(1)}, f32[240,128]{1,0:T(8,128)S(1)}, u32[]{:S(2)}, u32[]{:S(2)}) %collective-permute-start.6) | collective-permute-done | bytes 122912 | tf_op jit(solution)/shard_map/ppermute | solution.py:319
  123.7 14.6 %all_to_all.37.everyone = f32[4,432,128]{2,1,0:T(8,128)S(1)} all-to-all(f32[4,432,128]{2,1,0:T(8,128)S(1)} %broadcast_in_dim.13), channel_id=1, replica_groups=mesh['leaf'=128,'rhs'=4] {'rhs'}, dimensions={0} | all-to-all | bytes 1769472 | tf_op jit(solution)/shard_map/all_to_all | solution.py:296
  138.3 6.4 %shard_map.54 = (f32[448,128]{1,0:T(8,128)S(1)}, f32[448,128]{1,0:T(8,128)S(1)}, f32[448,128]{1,0:T(8,128)S(1)}, f32[64,128]{1,0:T(8,128)}, f32[128,128]{1,0:T(8,128)}) custom-call(f32[4,432,128]{2,1,0:T(8,128)S(1)} %all_to_all.37.everyone), custom_call_target="tpu_custom_call" | custom-call | flops 3000000000 | tf_op jit(solution)/shard_map/pallas_call | solution.py:73
  145.5 4.3 %collective-permute-start.8 = (f32[512,128]{1,0:T(8,128)S(1)}, f32[512,128]{1,0:T(8,128)S(1)}, u32[]{:S(2)}, u32[]{:S(2)}) collective-permute-start(f32[512,128]{1,0:T(8,128)S(1)} %shard_map.55.later), channel_id=1, source_target_pairs={{0,64},{4,68},{8,72},{12,76},{16,80},{20,84},{24,88},{28,92},{32,9... | collective-permute-start | bytes 786440 | tf_op jit(solution)/shard_map/ppermute | solution.py:319
  151.7 6.0 %collective-permute-done.7.arrived = f32[448,128]{1,0:T(8,128)S(1)} collective-permute-done((f32[448,128]{1,0:T(8,128)S(1)}, f32[448,128]{1,0:T(8,128)S(1)}, u32[]{:S(2)}, u32[]{:S(2)}) %collective-permute-start.7) | collective-permute-done | bytes 229408 | tf_op jit(solution)/shard_map/ppermute | solution.py:319
  157.7 6.0 %shard_map.56 = (f32[320,128]{1,0:T(8,128)S(1)}, f32[320,128]{1,0:T(8,128)S(1)}, f32[320,128]{1,0:T(8,128)S(1)}) custom-call(f32[448,128]{1,0:T(8,128)S(1)} %get-tuple-element.51.mine, f32[448,128]{1,0:T(8,128)S(1)} %collective-permute-done.7.arrived, f32[512,128]{1,0:T(8,128)S(1)} %shard_map.55.later, f32[512,128]{1,0:T(8,128)S(1)} %collective-permute-done.8.later_arrived), custom_call_target="tpu_custom_call" | custom-call | flops 3000000000 | tf_op jit(solution)/shard_map/pallas_call | solution.py:73
  163.7 6.1 %collective-permute-start.9 = (f32[320,128]{1,0:T(8,128)S(1)}, f32[320,128]{1,0:T(8,128)S(1)}, u32[]{:S(2)}, u32[]{:S(2)}) collective-permute-start(f32[320,128]{1,0:T(8,128)S(1)} %get-tuple-element.56.mine), channel_id=1, source_target_pairs={{0,128},{4,132},{8,136},{12,140},{16,144},{20,148},{24,152},{28,15... | collective-permute-start | bytes 491528 | tf_op jit(solution)/shard_map/ppermute | solution.py:319
  173.5 3.4 %all-to-all-start.5 = ((f32[4,16,1024]{2,1,0:T(8,128)}), f32[4,16,1024]{2,1,0:T(8,128)S(1)}, u32[]{:S(2)}, u32[]{:S(2)}) async-start(f32[4,16,1024]{2,1,0:T(8,128)} %broadcast_in_dim.14), calls=%async_computation.5 | async-start | bytes 524288 | tf_op jit(solution)/shard_map/all_to_all | solution.py:296
  176.9 2.5 %collective-permute-done.10.later_arrived = f32[192,128]{1,0:T(8,128)} collective-permute-done((f32[192,128]{1,0:T(8,128)}, f32[192,128]{1,0:T(8,128)}, u32[]{:S(2)}, u32[]{:S(2)}) %collective-permute-start.10) | collective-permute-done | bytes 98336 | tf_op jit(solution)/shard_map/ppermute | solution.py:319
  179.4 7.4 %shard_map.58 = (f32[192,128]{1,0:T(8,128)}, f32[192,128]{1,0:T(8,128)}, f32[192,128]{1,0:T(8,128)S(1)}) custom-call(f32[320,128]{1,0:T(8,128)S(1)} %get-tuple-element.56.mine, f32[320,128]{1,0:T(8,128)S(1)} %collective-permute-done.9.arrived, f32[192,128]{1,0:T(8,128)} %shard_map.57.later, f32[192,128]{1,0:T(8,128)} %collective-permute-done.10.later_arrived), custom_call_target="tpu_custom_call" | custom-call | flops 3000000000 | tf_op jit(solution)/shard_map/pallas_call | solution.py:73
  187.5 6.8 %collective-permute-start.11 = (f32[192,128]{1,0:T(8,128)}, f32[192,128]{1,0:T(8,128)S(1)}, u32[]{:S(2)}, u32[]{:S(2)}) collective-permute-start(f32[192,128]{1,0:T(8,128)} %get-tuple-element.59.mine), channel_id=1, source_target_pairs={{0,384},{4,388},{8,392},{12,396},{16,400},{20,404},{24,408},{28,41... | collective-permute-start | bytes 294920 | tf_op jit(solution)/shard_map/ppermute | solution.py:319
  202.5 5.2 %shard_map.59 = (f32[64,256]{1,0:T(8,128)S(1)}, f32[128,256]{1,0:T(8,128)S(1)}) custom-call(f32[64,1024]{1,0:T(8,128)S(1)} %bitcast.3, f32[4,432,128]{2,1,0:T(8,128)S(1)} %all_to_all.37.everyone, f32[4,240,256]{2,1,0:T(8,128)S(1)} %get-tuple-element.36.send, f32[1024,256]{1,0:T(8,128)S(1)} %copy-done.3, f32[768,128]{1,0:T(8,128)S(1)} %copy-done.8, ...), custom_call_target="tpu_custom_call" | custom-call | flops 3000000000 | tf_op jit(solution)/shard_map/pallas_call | solution.py:73
  207.8 6.6 %shard_map.60 = f32[64,256]{1,0:T(8,128)S(1)} custom-call(f32[192,128]{1,0:T(8,128)} %get-tuple-element.59.mine, f32[192,128]{1,0:T(8,128)S(1)} %collective-permute-done.11.arrived, f32[64,256]{1,0:T(8,128)S(1)} %get-tuple-element.65.base, f32[128,256]{1,0:T(8,128)S(1)} %get-tuple-element.66.slope), custom_call_target="tpu_custom_call" | custom-call | flops 3000000000 | tf_op jit(solution)/shard_map/pallas_call | solution.py:73
  214.4 10.2 %all_to_all.38.solved = f32[4,16,256]{2,1,0:T(8,128)S(1)} all-to-all(f32[4,16,256]{2,1,0:T(8,128)S(1)} %bitcast.4), channel_id=1, replica_groups=mesh['leaf'=128,'rhs'=4] {'rhs'}, dimensions={0} | all-to-all | bytes 131072 | tf_op jit(solution)/shard_map/all_to_all | solution.py:416
  224.5 2.4 %shard_map.61 = f32[16,1024]{1,0:T(8,128)} custom-call(f32[4,16,256]{2,1,0:T(8,128)S(1)} %all_to_all.38.solved, s32[1,1024]{1,0:T(1,128)S(1)} %copy-done.6), custom_call_target="tpu_custom_call" | custom-call | flops 3000000000 | tf_op jit(solution)/shard_map/pallas_call | solution.py:73
  (84 shorter events, 33.5 us)
Async XLA Ops:
  0.0 1.5 copy-start
  1.5 1.2 copy-start.2
  6.8 18.6 %copy-start.1 = (bf16[7,128,1024]{2,1,0:T(8,128)(2,1)S(1)}, bf16[7,128,1024]{2,1,0:T(8,128)(2,1)}, u32[]{:S(2)}) copy-start(bf16[7,128,1024]{2,1,0:T(8,128)(2,1)} %bases.3) | copy-start | bytes 5505028
  28.0 4.0 %collective-permute-start = (f32[1344,128]{1,0:T(8,128)S(1)}, f32[1344,128]{1,0:T(8,128)S(1)}, u32[]{:S(2)}, u32[]{:S(2)}) collective-permute-start(f32[1344,128]{1,0:T(8,128)S(1)} %shard_map.47.mine), channel_id=1, source_target_pairs={{0,4},{4,0},{8,12},{12,8},{16,20},{20,16},{24,28},{28,24},{32,36},... | collective-permute-start | bytes 2064392 | tf_op jit(solution)/shard_map/ppermute | solution.py:319
  52.8 3.1 %copy-start.7 = (f32[768,128]{1,0:T(8,128)}, f32[768,128]{1,0:T(8,128)S(1)}, u32[]{:S(2)}) copy-start(f32[768,128]{1,0:T(8,128)S(1)} %get-tuple-element.38.far.f1) | copy-start | bytes 1179652
  52.8 3.1 %copy-start.19 = (f32[128,128]{1,0:T(8,128)}, f32[128,128]{1,0:T(8,128)S(1)}, u32[]{:S(2)}) copy-start(f32[128,128]{1,0:T(8,128)S(1)} %get-tuple-element.61.i1) | copy-start | bytes 196612
  52.8 6.6 %collective-permute-start.1 = (f32[208,128]{1,0:T(8,128)S(1)}, f32[208,128]{1,0:T(8,128)S(1)}, u32[]{:S(2)}, u32[]{:S(2)}) collective-permute-start(f32[208,128]{1,0:T(8,128)S(1)} %get-tuple-element.37.mine), channel_id=1, source_target_pairs={{0,8},{4,12},{8,0},{12,4},{16,24},{20,28},{24,16},{28,20},{32,40},... | collective-permute-start | bytes 319496 | tf_op jit(solution)/shard_map/ppermute | solution.py:319
  60.2 12.1 %all-to-all-start.2 = ((f32[4,192,128]{2,1,0:T(8,128)}), f32[4,192,128]{2,1,0:T(8,128)S(1)}, u32[]{:S(2)}, u32[]{:S(2)}) async-start(f32[4,192,128]{2,1,0:T(8,128)} %broadcast_in_dim.11), calls=%async_computation.2 | async-start | bytes 786432 | tf_op jit(solution)/shard_map/all_to_all | solution.py:296
  63.7 8.6 %collective-permute-start.2 = (f32[560,128]{1,0:T(8,128)S(1)}, f32[560,128]{1,0:T(8,128)S(1)}, u32[]{:S(2)}, u32[]{:S(2)}) collective-permute-start(f32[560,128]{1,0:T(8,128)S(1)} %shard_map.49.later), channel_id=1, source_target_pairs={{0,8},{4,12},{8,0},{12,4},{16,24},{20,28},{24,16},{28,20},{32,40},... | collective-permute-start | bytes 860168 | tf_op jit(solution)/shard_map/ppermute | solution.py:319
  79.2 4.7 %copy-start.9 = (f32[640,128]{1,0:T(8,128)}, f32[640,128]{1,0:T(8,128)S(1)}, u32[]{:S(2)}) copy-start(f32[640,128]{1,0:T(8,128)S(1)} %get-tuple-element.43.far.f2) | copy-start | bytes 983044
  79.2 7.3 %collective-permute-start.3 = (f32[176,128]{1,0:T(8,128)S(1)}, f32[176,128]{1,0:T(8,128)S(1)}, u32[]{:S(2)}, u32[]{:S(2)}) collective-permute-start(f32[176,128]{1,0:T(8,128)S(1)} %get-tuple-element.42.mine), channel_id=1, source_target_pairs={{0,16},{4,20},{8,24},{12,28},{16,0},{20,4},{24,8},{28,12},{32,48},... | collective-permute-start | bytes 270344 | tf_op jit(solution)/shard_map/ppermute | solution.py:319
  87.3 13.9 %all-to-all-start.3 = ((f32[4,160,128]{2,1,0:T(8,128)}), f32[4,160,128]{2,1,0:T(8,128)S(1)}, u32[]{:S(2)}, u32[]{:S(2)}) async-start(f32[4,160,128]{2,1,0:T(8,128)} %broadcast_in_dim.12), calls=%async_computation.3 | async-start | bytes 655360 | tf_op jit(solution)/shard_map/all_to_all | solution.py:296
  91.9 9.3 %collective-permute-start.4 = (f32[384,128]{1,0:T(8,128)S(1)}, f32[384,128]{1,0:T(8,128)S(1)}, u32[]{:S(2)}, u32[]{:S(2)}) collective-permute-start(f32[384,128]{1,0:T(8,128)S(1)} %shard_map.51.later), channel_id=1, source_target_pairs={{0,16},{4,20},{8,24},{12,28},{16,0},{20,4},{24,8},{28,12},{32,48},... | collective-permute-start | bytes 589832 | tf_op jit(solution)/shard_map/ppermute | solution.py:319
  107.0 7.6 %copy-start.11 = (f32[512,128]{1,0:T(8,128)}, f32[512,128]{1,0:T(8,128)S(1)}, u32[]{:S(2)}) copy-start(f32[512,128]{1,0:T(8,128)S(1)} %get-tuple-element.48.far.f3) | copy-start | bytes 786436
  107.1 7.6 %copy-start.23 = (f32[128,128]{1,0:T(8,128)}, f32[128,128]{1,0:T(8,128)S(1)}, u32[]{:S(2)}) copy-start(f32[128,128]{1,0:T(8,128)S(1)} %get-tuple-element.63.i3) | copy-start | bytes 196612
  107.1 10.9 %collective-permute-start.5 = (f32[144,128]{1,0:T(8,128)S(1)}, f32[144,128]{1,0:T(8,128)S(1)}, u32[]{:S(2)}, u32[]{:S(2)}) collective-permute-start(f32[144,128]{1,0:T(8,128)S(1)} %get-tuple-element.47), channel_id=1, source_target_pairs={{0,48},{4,52},{8,56},{12,60},{16,32},{20,36},{24,40},{28,44},{32,1... | collective-permute-start | bytes 221192 | tf_op jit(solution)/shard_map/ppermute | solution.py:319
  114.6 9.0 %collective-permute-start.6 = (f32[240,128]{1,0:T(8,128)S(1)}, f32[240,128]{1,0:T(8,128)S(1)}, u32[]{:S(2)}, u32[]{:S(2)}) collective-permute-start(f32[240,128]{1,0:T(8,128)S(1)} %shard_map.53), channel_id=1, source_target_pairs={{0,48},{4,52},{8,56},{12,60},{16,32},{20,36},{24,40},{28,44},{32,1... | collective-permute-start | bytes 368648 | tf_op jit(solution)/shard_map/ppermute | solution.py:319
  145.5 12.2 %collective-permute-start.8 = (f32[512,128]{1,0:T(8,128)S(1)}, f32[512,128]{1,0:T(8,128)S(1)}, u32[]{:S(2)}, u32[]{:S(2)}) collective-permute-start(f32[512,128]{1,0:T(8,128)S(1)} %shard_map.55.later), channel_id=1, source_target_pairs={{0,64},{4,68},{8,72},{12,76},{16,80},{20,84},{24,88},{28,92},{32,9... | collective-permute-start | bytes 786440 | tf_op jit(solution)/shard_map/ppermute | solution.py:319
  149.7 7.9 %collective-permute-start.7 = (f32[448,128]{1,0:T(8,128)S(1)}, f32[448,128]{1,0:T(8,128)S(1)}, u32[]{:S(2)}, u32[]{:S(2)}) collective-permute-start(f32[448,128]{1,0:T(8,128)S(1)} %get-tuple-element.51.mine), channel_id=1, source_target_pairs={{0,64},{4,68},{8,72},{12,76},{16,80},{20,84},{24,88},{28,92},{32,9... | collective-permute-start | bytes 688136 | tf_op jit(solution)/shard_map/ppermute | solution.py:319
  163.7 7.0 %copy-start.15 = (f32[320,128]{1,0:T(8,128)}, f32[320,128]{1,0:T(8,128)S(1)}, u32[]{:S(2)}) copy-start(f32[320,128]{1,0:T(8,128)S(1)} %get-tuple-element.58.weights.w5) | copy-start | bytes 491524
  163.7 15.8 %collective-permute-start.9 = (f32[320,128]{1,0:T(8,128)S(1)}, f32[320,128]{1,0:T(8,128)S(1)}, u32[]{:S(2)}, u32[]{:S(2)}) collective-permute-start(f32[320,128]{1,0:T(8,128)S(1)} %get-tuple-element.56.mine), channel_id=1, source_target_pairs={{0,128},{4,132},{8,136},{12,140},{16,144},{20,148},{24,152},{28,15... | collective-permute-start | bytes 491528 | tf_op jit(solution)/shard_map/ppermute | solution.py:319
  170.7 8.8 %collective-permute-start.10 = (f32[192,128]{1,0:T(8,128)}, f32[192,128]{1,0:T(8,128)}, u32[]{:S(2)}, u32[]{:S(2)}) collective-permute-start(f32[192,128]{1,0:T(8,128)} %shard_map.57.later), channel_id=1, source_target_pairs={{0,128},{4,132},{8,136},{12,140},{16,144},{20,148},{24,152},{28,15... | collective-permute-start | bytes 294920 | tf_op jit(solution)/shard_map/ppermute | solution.py:319
  173.5 20.8 %all-to-all-start.5 = ((f32[4,16,1024]{2,1,0:T(8,128)}), f32[4,16,1024]{2,1,0:T(8,128)S(1)}, u32[]{:S(2)}, u32[]{:S(2)}) async-start(f32[4,16,1024]{2,1,0:T(8,128)} %broadcast_in_dim.14), calls=%async_computation.5 | async-start | bytes 524288 | tf_op jit(solution)/shard_map/all_to_all | solution.py:296
  176.9 17.4 %copy-start.3 = (f32[1024,256]{1,0:T(8,128)S(1)}, f32[1024,256]{1,0:T(8,128)}, u32[]{:S(2)}) copy-start(f32[1024,256]{1,0:T(8,128)} %inverse_cols.3) | copy-start | bytes 3145732
  187.5 20.3 %collective-permute-start.11 = (f32[192,128]{1,0:T(8,128)}, f32[192,128]{1,0:T(8,128)S(1)}, u32[]{:S(2)}, u32[]{:S(2)}) collective-permute-start(f32[192,128]{1,0:T(8,128)} %get-tuple-element.59.mine), channel_id=1, source_target_pairs={{0,384},{4,388},{8,392},{12,396},{16,400},{20,404},{24,408},{28,41... | collective-permute-start | bytes 294920 | tf_op jit(solution)/shard_map/ppermute | solution.py:319
  194.3 1.0 copy-start.8
  195.3 1.0 copy-start.10
  196.3 0.9 copy-start.12
  197.2 0.9 copy-start.14
  198.2 0.9 copy-start.16
  199.1 0.9 copy-start.18
  207.7 16.8 %copy-start.6 = (s32[1,1024]{1,0:T(1,128)S(1)}, s32[1,1024]{1,0:T(1,128)}, u32[]{:S(2)}) copy-start(s32[1,1024]{1,0:T(1,128)} %order.3) | copy-start | bytes 12292
  (8 other events, 6.0 us)

commit v3 on v2

--- a/solution.py
+++ b/solution.py
@@ -8,6 +8,7 @@
 from jax.sharding import PartitionSpec as P
 
 HIGHEST = lax.Precision.HIGHEST
+VMEM_BYTES = 24 * 1024 * 1024
 NN = (((1,), (0,)), ((), ()))
 NT = (((1,), (1,)), ((), ()))
 
@@ -38,12 +39,20 @@
     return short_dot(left16, low, dims) + short_dot(left16, middle, dims) + short_dot(left16, high, dims)
 
 
+def two_parts(values):
+    high = values.astype(jnp.bfloat16)
+    return high, (values - high.astype(jnp.float32)).astype(jnp.bfloat16)
+
+
+def close_dot(left, right):
+    left_high, left_low = two_parts(left)
+    right_high, right_low = two_parts(right)
+    small = short_dot(left_high, right_low, NN) + short_dot(left_low, right_high, NN)
+    return small + short_dot(left_high, right_high, NN)
+
+
 def inverse_of(capacity):
-    size = capacity.shape[0]
-    shape = (size, size)
-    eye = jnp.where(
-        lax.broadcasted_iota(jnp.int32, shape, 0) == lax.broadcasted_iota(jnp.int32, shape, 1), 1.0, 0.0
-    )
+    eye = identity(capacity.shape[0])
     bound = jnp.max(jnp.sum(jnp.abs(capacity), axis=1, keepdims=True), axis=0, keepdims=True)
     scale = 2.0 / (1.0 + bound)
     begin = 2.0 * scale * eye - scale * scale * capacity
@@ -54,29 +63,62 @@
         factor = 2.0 * eye - short_dot(short, guess16, NN)
         guess = short_dot(guess16, factor.astype(jnp.bfloat16), NN)
 
+    def improve(inverse):
+        residual = eye - exact_dot(capacity, inverse, NN)
+        size2 = jnp.sum(jnp.sum(residual * residual, axis=1, keepdims=True), axis=0, keepdims=True)
+        return inverse + close_dot(inverse, residual), size2
+
+    better, size2 = improve(guess)
+    better = jnp.where(size2 < 0.25, better, begin)
+    better, size2 = improve(better)
+
     def unfinished(state):
-        return (state[1] == 0) | ((state[1] < 80) & jnp.logical_not(state[2] < 1e-6))
-
-    def improve(state):
-        inverse, count, _ = state
-        residual = eye - exact_dot(capacity, inverse, NN)
-        size2 = jnp.sum(residual * residual)
-        better = inverse + exact_dot(inverse, residual, NN)
-        restart = (count == 0) & jnp.logical_not(size2 < 0.25)
-        return jnp.where(restart, begin, better), count + 1, size2
-
-    return lax.while_loop(unfinished, improve, (guess, 0, jnp.float32(1.0)))[0]
-
-
-def run(body, outs, *args, cost=3):
+        return (state[1] < 80) & jnp.logical_not(state[2] < 1e-6)
+
+    def again(state):
+        inverse, size2 = improve(state[0])
+        return inverse, state[1] + 1, size2[0, 0]
+
+    return lax.while_loop(unfinished, again, (better, 0, size2[0, 0]))[0]
+
+
+def run(body, outs, *args, place=None):
     vmem = pl.BlockSpec(memory_space=pltpu.VMEM)
+    scalars = [] if place is None else [place]
     return pl.pallas_call(
         body,
         out_shape=[jax.ShapeDtypeStruct(shape, jnp.float32) for shape in outs],
-        in_specs=[vmem] * len(args),
+        in_specs=[pl.BlockSpec(memory_space=pltpu.SMEM)] * len(scalars) + [vmem] * len(args),
         out_specs=[vmem] * len(outs),
-        cost_estimate=pl.CostEstimate(flops=cost * 1_000_000_000, bytes_accessed=0, transcendentals=0),
-        compiler_params=pltpu.CompilerParams(vmem_limit_bytes=48 * 1024 * 1024),
+        cost_estimate=pl.CostEstimate(flops=3_000_000_000, bytes_accessed=0, transcendentals=0),
+        compiler_params=pltpu.CompilerParams(vmem_limit_bytes=VMEM_BYTES),
+    )(*scalars, *args)
+
+
+def run_loading(body, outs, *args):
+    def loading(*refs):
+        count = len(args)
+        sources, rest = refs[:count], refs[count:]
+        results, held, done = rest[: len(outs)], rest[len(outs) : -1], rest[-1]
+        copies = [
+            pltpu.make_async_copy(source, target, done.at[place])
+            for place, (source, target) in enumerate(zip(sources, held))
+        ]
+        for copy in copies:
+            copy.start()
+        for copy in copies:
+            copy.wait()
+        body(*held, *results)
+
+    return pl.pallas_call(
+        loading,
+        out_shape=[jax.ShapeDtypeStruct(shape, jnp.float32) for shape in outs],
+        in_specs=[pl.BlockSpec(memory_space=pltpu.HBM)] * len(args),
+        out_specs=[pl.BlockSpec(memory_space=pltpu.VMEM)] * len(outs),
+        scratch_shapes=[pltpu.VMEM(arg.shape, arg.dtype) for arg in args]
+        + [pltpu.SemaphoreType.DMA((len(args),))],
+        cost_estimate=pl.CostEstimate(flops=3_000_000_000, bytes_accessed=0, transcendentals=0),
+        compiler_params=pltpu.CompilerParams(vmem_limit_bytes=VMEM_BYTES),
     )(*args)
 
 
@@ -194,16 +236,16 @@
         at += count
 
 
-def spread_body(everyone, fifth, far, weights, side_weights, inverse):
+def spread_body(everyone, fifth, far, weights):
     groups, _, rank = everyone.shape
     share = rank // groups
     own = fifth.shape[0] - 3 * rank
     own = own // groups
     blocks = [stacked(everyone, level * share, share) for level in range(4)]
-    inverse[...] = inverse_of(blocks[0] + identity(rank))
+    inverse = inverse_of(blocks[0] + identity(rank))
     far[: 3 * rank, :] = jnp.concatenate(blocks[1:], 0)
     far[3 * rank :, :] = stacked(everyone, 4 * share, own)
-    weights[...] = exact_dot(far[...], inverse[...], NN)
+    weights[...] = exact_dot(far[...], inverse, NN)
     update = exact_dot(weights[...], far[:rank, :], NT)
     at = 4 * share + own
     for level in range(3):
@@ -211,84 +253,104 @@
             stacked(everyone, at + level * share, share) - update[level * rank : (level + 1) * rank]
         )
     fifth[3 * rank :, :] = stacked(everyone, at + 3 * share, own) - update[3 * rank :]
-    side_weights[...] = weights[3 * rank :, :]
-
-
-def spread_rest_body(everyone, far, weights, rest):
+
+
+def spread_rest_body(everyone, far, weights, sixth, seventh):
     groups, _, rank = everyone.shape
     share = rank // groups
     own = (far.shape[0] - 3 * rank) // groups
     source = 7 * share + 2 * own
-    at = 0
-    for column in (1, 2):
+    for column, panel in ((1, sixth), (2, seventh)):
         update = exact_dot(weights[column * rank :, :], far[column * rank : (column + 1) * rank, :], NT)
+        at = 0
         for level in range(column, 3):
-            low = (level - column) * rank
-            rest[at : at + rank, :] = stacked(everyone, source, share) - update[low : low + rank]
+            panel[at : at + rank, :] = stacked(everyone, source, share) - update[at : at + rank]
             at += rank
             source += share
-        rest[at : at + groups * own, :] = stacked(everyone, source, own) - update[(3 - column) * rank :]
-        at += groups * own
+        panel[at:, :] = stacked(everyone, source, own) - update[at:]
         source += own
 
 
-def factor_body(mine, arrived, later, later_arrived, panel, upper, weights):
+def factor_body(mine, arrived, upper, weights):
     rank = mine.shape[1]
     upper[...] = mine[rank:, :] + arrived[rank:, :]
     inverse = inverse_of(mine[:rank, :] + arrived[:rank, :] + identity(rank))
     weights[...] = exact_dot(upper[...], inverse, NN)
-    count = panel.shape[0]
-    panel[...] = later[:count, :] + later_arrived[:count, :] - exact_dot(weights[...], upper[:rank, :], NT)
-
-
-def factor_rest_body(later, later_arrived, upper, weights, rest):
+
+
+def next_body(later, later_arrived, upper, weights, panel):
     rank = upper.shape[1]
-    source = weights.shape[0]
-    rest[...] = (
-        later[source:, :] + later_arrived[source:, :]
-        - exact_dot(weights[rank:, :], upper[rank : 2 * rank, :], NT)
-    )
-
-
-def prepare_body(
-    tree, everyone, send, inverse_cols, f1, i1, f2, i2, f3, i3, w4, w5, w6, base, slope
-):
+    panel[...] = later[...] + later_arrived[...] - exact_dot(weights[...], upper[:rank, :], NT)
+
+
+def rest_body(later, later_arrived, upper, weights, rest):
+    rank = upper.shape[1]
+    rest[...] = later[...] + later_arrived[...] - exact_dot(weights[rank:, :], upper[rank : 2 * rank, :], NT)
+
+
+def last_panel_body(place, later, later_arrived, upper, weights, panel):
+    rank = upper.shape[1]
+    own = panel.shape[0] - rank
+    rows = pl.ds(pl.multiple_of(rank + place[0] * own, own), own)
+    left = jnp.concatenate([weights[:rank, :], weights[rows, :]], 0)
+    update = exact_dot(left, upper[:rank, :], NT)
+    panel[:rank, :] = later[:rank, :] + later_arrived[:rank, :] - update[:rank]
+    panel[rank:, :] = later[rows, :] + later_arrived[rows, :] - update[rank:]
+
+
+def carry_first_body(send, far, inverse, carried, gone):
+    groups = send.shape[0]
+    share = inverse.shape[0] // groups
+    applied = [stacked(send, level * share, share) for level in range(7)]
+    gone[...] = applied[0]
+    weights = exact_dot(far[...], inverse[...], NN)
+    carried[...] = jnp.concatenate(applied[1:], 0) - exact_dot(weights, applied[0], NN)
+
+
+def carry_body(before, far, inverse, carried, gone):
+    rank = inverse.shape[0]
+    gone[...] = before[:rank, :]
+    weights = exact_dot(far[...], inverse[...], NN)
+    carried[...] = before[rank:, :] - exact_dot(weights, before[:rank, :], NN)
+
+
+def carry_sides_body(tree, inverse_cols, everyone, i1, i2, i3, g1, g2, g3, before, weights, carried):
     groups, _, rank = everyone.shape
-    share = rank // groups
-    sides = base.shape[0]
+    sides = tree.shape[0]
     own = sides // groups
-    none = jnp.zeros((rank, rank), jnp.float32)
-    found = jnp.concatenate([jnp.zeros((sides, rank), jnp.float32), identity(rank)], 0)
-
-    def lower(side_weights, blocks):
-        return jnp.concatenate([side_weights, none], 0) - exact_dot(found, blocks, NN)
-
-    for weights in (w6, w5, w4):
-        count = weights.shape[0] - sides
-        found = jnp.concatenate([lower(weights[count:, :], weights[:count, :]), found], 1)
     source = everyone.shape[1] - 3 * own
-    for level, far, inverse in ((2, f3, i3), (1, f2, i2), (0, f1, i1)):
-        low = source + level * own
-        side_weights = exact_dot(stacked(everyone, low, own), inverse[...], NN)
-        blocks = exact_dot(far[...], inverse[...], NN)
-        found = jnp.concatenate([lower(side_weights, blocks), found], 1)
-    applied = jnp.concatenate([stacked(send, level * share, share) for level in range(7)], 0)
-    total = exact_dot(found, applied, NN)
-    base[...] = exact_dot(tree[...], inverse_cols[...], NN) - total[:sides]
-    slope[...] = total[sides:]
-
-
-def finish_body(mine, arrived, base, slope, solved):
+    found = exact_dot(tree[...], inverse_cols[...], NN)
+    for level, inverse, gone in ((0, i1, g1), (1, i2, g2), (2, i3, g3)):
+        side_weights = exact_dot(stacked(everyone, source + level * own, own), inverse[...], NN)
+        found = found - exact_dot(side_weights, gone[...], NN)
+    update = exact_dot(weights[...], before[:rank, :], NN)
+    carried[: 3 * rank, :] = before[rank:, :] - update[: 3 * rank]
+    carried[3 * rank :, :] = found - update[3 * rank :]
+
+
+def carry_on_body(before, weights, carried):
+    rank = weights.shape[1]
+    carried[...] = before[rank:, :] - exact_dot(weights[...], before[:rank, :], NN)
+
+
+def carry_last_body(before, weights, send):
+    groups, rows, _ = send.shape
+    rank = weights.shape[1]
+    own = rows - rank
+    carried = before[rank:, :] - exact_dot(weights[...], before[:rank, :], NN)
+    for group in range(groups):
+        send[group, :rank, :] = carried[:rank]
+        send[group, rank:, :] = carried[rank + group * own : rank + (group + 1) * own]
+
+
+def finish_body(mine, arrived, got, order, out):
     rank = mine.shape[1]
+    groups = got.shape[0]
     inverse = inverse_of(mine[:rank, :] + arrived[:rank, :] + identity(rank))
     top = exact_dot(mine[rank:, :] + arrived[rank:, :], inverse, NN)
-    solved[...] = base[...] - exact_dot(top, slope[...], NN)
-
-
-def untangle_body(solved, order, out):
-    groups = solved.shape[0]
-    whole = jnp.concatenate([solved[group] for group in range(groups)], 1)
-    out[...] = dot_left_parts(whole, one_hot(order[...]), NT)
+    slope = jnp.concatenate([got[group, :rank, :] for group in range(groups)], 1)
+    base = jnp.concatenate([got[group, rank:, :] for group in range(groups)], 1)
+    out[...] = dot_left_parts(base - exact_dot(top, slope, NN), one_hot(order[...]), NT)
 
 
 def to_all(block, axis):
@@ -318,7 +380,7 @@
     square = (rank, rank)
     swap = lambda block, height: lax.ppermute(block, "leaf", route(height))
 
-    send, tree = run(
+    send, tree = run_loading(
         start_body,
         [(groups, levels * share + own, piece), (own, leaf)],
         right_sides,
@@ -346,7 +408,13 @@
     (later,) = run(
         first_rest_body, [(15 * share + 5 * own, rank)], everyone, gram, other, far1, own_weights
     )
-    far, inverses, side_uppers = [far1], [inverse1], [side1]
+    tree, later = lax.optimization_barrier((tree, later))
+    spread_tree = lax.dynamic_update_slice(
+        jnp.zeros((sides, leaf), jnp.float32), tree, (lax.axis_index("rhs") * own, 0)
+    )
+    whole_tree = lax.psum(spread_tree, "rhs")
+    carried, gone = run(carry_first_body, [(6 * rank, piece), (rank, piece)], send, far1, inverse1)
+    inverses, gones, side_uppers = [inverse1], [gone], [side1]
     for height in (2, 3):
         above = 7 - height
         later_arrived = swap(later, height)
@@ -369,52 +437,49 @@
             level_rest_body, [(rest_rows, rank)], later, later_arrived, level_far, own_weights
         )
         panel = next_panel
-        far.append(level_far)
+        carried, gone = run(
+            carry_body, [(above * rank, piece), (rank, piece)], carried, level_far, inverse
+        )
         inverses.append(inverse)
+        gones.append(gone)
 
     later_arrived = swap(later, 4)
     everyone = to_all(
         jnp.concatenate([panel + arrived, later + later_arrived] + side_uppers, 0), "rhs"
     )
-    upper_shape = (3 * rank + sides, rank)
-    panel, upper, weights, _, _ = run(
-        spread_body, [upper_shape, upper_shape, upper_shape, (sides, rank), square], everyone
-    )
-    arrived = swap(panel, 5)
-    (later,) = run(spread_rest_body, [(3 * rank + 2 * sides, rank)], everyone, upper, weights)
-    later_arrived = swap(later, 5)
-    kept = [weights]
-    tree, later = lax.optimization_barrier((tree, later))
-    whole_tree = to_all(tree, "rhs").reshape(sides, leaf)
-    next_panel, upper, weights = run(
-        factor_body,
-        [(2 * rank + sides, rank)] * 3,
-        panel,
-        arrived,
-        later,
-        later_arrived,
-    )
-    kept.append(weights)
-    arrived = swap(next_panel, 6)
-    (later,) = run(factor_rest_body, [(rank + sides, rank)], later, later_arrived, upper, weights)
-    later_arrived = swap(later, 6)
-    panel, upper, weights = run(
-        factor_body,
-        [(rank + sides, rank)] * 3,
-        next_panel,
-        arrived,
-        later,
-        later_arrived,
-    )
-    kept.append(weights)
-    arrived = swap(panel, 7)
-    pairs = [item for pair in zip(far, inverses) for item in pair]
-    base, slope = run(
-        prepare_body, [(sides, piece), (rank, piece)], whole_tree, everyone, send, leaf_inverse, *pairs, *kept
-    )
-    (solved,) = run(finish_body, [(sides, piece)], panel, arrived, base, slope)
-    back = lax.all_to_all(solved.reshape(groups, own, piece), "rhs", 0, 0)
-    (result,) = run(untangle_body, [(own, leaf)], back, ordering)
+    heights = lambda count: (count * rank + sides, rank)
+    fifth, upper, weights = run(spread_body, [heights(3)] * 3, everyone)
+    arrived = swap(fifth, 5)
+    sixth, seventh = run(spread_rest_body, [heights(2), heights(1)], everyone, upper, weights)
+    sixth_arrived = swap(sixth, 5)
+    seventh_arrived = swap(seventh, 5)
+    (carried,) = run(
+        carry_sides_body,
+        [(3 * rank + sides, piece)],
+        whole_tree,
+        leaf_inverse,
+        everyone,
+        *inverses,
+        *gones,
+        carried,
+        weights,
+    )
+    upper, weights = run(factor_body, [heights(2)] * 2, fifth, arrived)
+    (sixth,) = run(next_body, [heights(2)], sixth, sixth_arrived, upper, weights)
+    arrived = swap(sixth, 6)
+    (seventh,) = run(rest_body, [heights(1)], seventh, seventh_arrived, upper, weights)
+    seventh_arrived = swap(seventh, 6)
+    (carried,) = run(carry_on_body, [(2 * rank + sides, piece)], carried, weights)
+    upper, weights = run(factor_body, [heights(1)] * 2, sixth, arrived)
+    place = lax.axis_index("rhs").reshape(1)
+    (seventh,) = run(
+        last_panel_body, [(rank + own, rank)], seventh, seventh_arrived, upper, weights, place=place
+    )
+    arrived = swap(seventh, 7)
+    carried, seventh = lax.optimization_barrier((carried, seventh))
+    (send,) = run(carry_last_body, [(groups, rank + own, piece)], carried, weights)
+    got = lax.all_to_all(send, "rhs", 0, 0)
+    (result,) = run(finish_body, [(own, leaf)], seventh, arrived, got, ordering)
     return result
 
 

time: 228 us -> 226 us (level)
  the two profiles are of different devices: /device:TPU:8 before, /device:TPU:16 now
where the time goes in v3:
time: 226 us; the launch traced here: 224 us
  starting transfers between devices  63.8 us (28%)
  Pallas kernels  56.7 us (25%)
  waiting for transfers between devices  41.8 us (18%)
  blocking collectives  32.8 us (15%)
  local copies, waits for them, and re-layouts  15.3 us (7%)
  between operations  13.9 us (6%)
    pallas_call x21, Pallas kernels, run(): pl.pallas_call(body, out_shape=[jax.ShapeDtypeStruct(shape, jnp.float32)...  53.8 us
    ppermute x13, starting transfers between devices, local(): swap = lambda block, height: lax.ppermute(block, 'leaf', route(height))  47.4 us
    ppermute x13, waiting for transfers between devices, local(): swap = lambda block, height: lax.ppermute(block, 'leaf', route(height))  36.7 us
    all_to_all x1, blocking collectives, local(): got = lax.all_to_all(send, 'rhs', 0, 0)  18.6 us
    all_to_all x1, blocking collectives, local(): everyone = lax.all_to_all(jnp.concatenate([shared, parts], 1), 'rhs', 0, 0)  14.2 us
    all_to_all x3, starting transfers between devices, to_all(): lax.all_to_all(jnp.broadcast_to(block[None], (count,) + block.shape), axi...  12.9 us
    unnamed x49, local copies, waits for them, and re-layouts  12.6 us
  transfers between devices with their start and end apart: 18, of which 11 were waited for; matrix products, arithmetic and copies ran while one was open for 0% of the time, Pallas kernels for 14%

profile of v3, /device:TPU:16, one launch (start us, length us, event | category | flops | bytes accessed | tf_op | source)
XLA Modules:
  0.0 224.4 jit_solution(18343077107352800986)
XLA Ops:
  10.8 2.9 %shard_map.46 = (f32[4,240,256]{2,1,0:T(8,128)S(1)}, f32[16,1024]{1,0:T(8,128)S(1)}) custom-call(f32[16,1024]{1,0:T(8,128)S(1)} %copy-done.5, s32[1,1024]{1,0:T(1,128)S(1)} %copy-done.6, f32[1024,256]{1,0:T(8,128)S(1)} %copy-done.2, bf16[7,128,1024]{2,1,0:T(8,128)(2,1)S(1)} %copy-done), custom_call_target="tpu_custom_call" | custom-call | flops 3000000000 | tf_op jit(solution)/shard_map/pallas_call | solution.py:113
  13.7 18.6 %all_to_all.30.got = f32[4,240,256]{2,1,0:T(8,128)S(1)} all-to-all(f32[4,240,256]{2,1,0:T(8,128)S(1)} %get-tuple-element.44.send), channel_id=1, replica_groups=mesh['leaf'=128,'rhs'=4] {'rhs'}, dimensions={0} | all-to-all | bytes 1966080 | tf_op jit(solution)/shard_map/all_to_all | solution.py:391
  32.3 2.6 %shard_map.47.mine = f32[1344,128]{1,0:T(8,128)S(1)} custom-call(f32[4,240,256]{2,1,0:T(8,128)S(1)} %all_to_all.30.got, f32[4,240,256]{2,1,0:T(8,128)S(1)} %get-tuple-element.44.send, bf16[7,128,1024]{2,1,0:T(8,128)(2,1)S(1)} %copy-done.1), custom_call_target="tpu_custom_call" | custom-call | flops 3000000000 | tf_op jit(solution)/shard_map/pallas_call | solution.py:88
  39.1 14.2 %all_to_all.31.everyone = f32[4,336,128]{2,1,0:T(8,128)S(1)} all-to-all(f32[4,336,128]{2,1,0:T(8,128)S(1)} %pad_maximum_fusion), channel_id=1, replica_groups=mesh['leaf'=128,'rhs'=4] {'rhs'}, dimensions={0} | all-to-all | bytes 1376256 | tf_op jit(solution)/shard_map/all_to_all | solution.py:398
  53.3 5.8 %shard_map.48 = (f32[208,128]{1,0:T(8,128)S(1)}, f32[768,128]{1,0:T(8,128)S(1)}, f32[208,128]{1,0:T(8,128)S(1)}, f32[128,128]{1,0:T(8,128)S(1)}, f32[16,128]{1,0:T(8,128)S(1)}) custom-call(f32[4,336,128]{2,1,0:T(8,128)S(1)} %all_to_all.31.everyone, f32[1344,128]{1,0:T(8,128)S(1)} %shard_map.47.mine, f32[1344,128]{1,0:T(8,128)S(1)} %collective-permute-done.arrived), custom_call_target="tpu_custom_call" | custom-call | flops 3000000000 | tf_op jit(solution)/shard_map/pallas_call | solution.py:88
  59.1 3.5 %collective-permute-start.1 = (f32[208,128]{1,0:T(8,128)S(1)}, f32[208,128]{1,0:T(8,128)S(1)}, u32[]{:S(2)}, u32[]{:S(2)}) collective-permute-start(f32[208,128]{1,0:T(8,128)S(1)} %get-tuple-element.48.mine), channel_id=1, source_target_pairs={{0,8},{4,12},{8,0},{12,4},{16,24},{20,28},{24,16},{28,20},{32,40},... | collective-permute-start | bytes 319496 | tf_op jit(solution)/shard_map/ppermute | solution.py:381
  63.4 2.4 %collective-permute-done.1.arrived = f32[208,128]{1,0:T(8,128)S(1)} collective-permute-done((f32[208,128]{1,0:T(8,128)S(1)}, f32[208,128]{1,0:T(8,128)S(1)}, u32[]{:S(2)}, u32[]{:S(2)}) %collective-permute-start.1) | collective-permute-done | bytes 106528 | tf_op jit(solution)/shard_map/ppermute | solution.py:381
  66.5 3.5 %all-to-all-start.2 = ((f32[4,192,128]{2,1,0:T(8,128)}), f32[4,192,128]{2,1,0:T(8,128)S(1)}, u32[]{:S(2)}, u32[]{:S(2)}) async-start(f32[4,192,128]{2,1,0:T(8,128)} %broadcast_in_dim.12), calls=%async_computation.2 | async-start | bytes 786432 | tf_op jit(solution)/shard_map/all_to_all | solution.py:358
  70.0 3.5 %collective-permute-start.2 = (f32[560,128]{1,0:T(8,128)S(1)}, f32[560,128]{1,0:T(8,128)S(1)}, u32[]{:S(2)}, u32[]{:S(2)}) collective-permute-start(f32[560,128]{1,0:T(8,128)S(1)} %shard_map.49.later), channel_id=1, source_target_pairs={{0,8},{4,12},{8,0},{12,4},{16,24},{20,28},{24,16},{28,20},{32,40},... | collective-permute-start | bytes 860168 | tf_op jit(solution)/shard_map/ppermute | solution.py:381
  73.5 5.2 %collective-permute-done.2.later_arrived = f32[560,128]{1,0:T(8,128)S(1)} collective-permute-done((f32[560,128]{1,0:T(8,128)S(1)}, f32[560,128]{1,0:T(8,128)S(1)}, u32[]{:S(2)}, u32[]{:S(2)}) %collective-permute-start.2) | collective-permute-done | bytes 286752 | tf_op jit(solution)/shard_map/ppermute | solution.py:381
  78.6 5.3 %shard_map.50 = (f32[176,128]{1,0:T(8,128)S(1)}, f32[640,128]{1,0:T(8,128)S(1)}, f32[176,128]{1,0:T(8,128)S(1)}, f32[128,128]{1,0:T(8,128)S(1)}) custom-call(f32[4,192,128]{2,1,0:T(8,128)S(1)} %all-to-all-done.2.everyone, f32[208,128]{1,0:T(8,128)S(1)} %get-tuple-element.48.mine, f32[208,128]{1,0:T(8,128)S(1)} %collective-permute-done.1.arrived, ...), custom_call_target="tpu_custom_call" | custom-call | flops 3000000000 | tf_op jit(solution)/shard_map/pallas_call | solution.py:88
  84.0 2.6 %collective-permute-start.3 = (f32[176,128]{1,0:T(8,128)S(1)}, f32[176,128]{1,0:T(8,128)S(1)}, u32[]{:S(2)}, u32[]{:S(2)}) collective-permute-start(f32[176,128]{1,0:T(8,128)S(1)} %get-tuple-element.52.mine), channel_id=1, source_target_pairs={{0,16},{4,20},{8,24},{12,28},{16,0},{20,4},{24,8},{28,12},{32,48},... | collective-permute-start | bytes 270344 | tf_op jit(solution)/shard_map/ppermute | solution.py:381
  87.3 4.1 %collective-permute-done.3.arrived = f32[176,128]{1,0:T(8,128)S(1)} collective-permute-done((f32[176,128]{1,0:T(8,128)S(1)}, f32[176,128]{1,0:T(8,128)S(1)}, u32[]{:S(2)}, u32[]{:S(2)}) %collective-permute-start.3) | collective-permute-done | bytes 90144 | tf_op jit(solution)/shard_map/ppermute | solution.py:381
  92.2 4.6 %all-to-all-start.3 = ((f32[4,160,128]{2,1,0:T(8,128)}), f32[4,160,128]{2,1,0:T(8,128)S(1)}, u32[]{:S(2)}, u32[]{:S(2)}) async-start(f32[4,160,128]{2,1,0:T(8,128)} %broadcast_in_dim.13), calls=%async_computation.3 | async-start | bytes 655360 | tf_op jit(solution)/shard_map/all_to_all | solution.py:358
  96.8 2.5 %collective-permute-start.4 = (f32[384,128]{1,0:T(8,128)S(1)}, f32[384,128]{1,0:T(8,128)S(1)}, u32[]{:S(2)}, u32[]{:S(2)}) collective-permute-start(f32[384,128]{1,0:T(8,128)S(1)} %shard_map.51.later), channel_id=1, source_target_pairs={{0,16},{4,20},{8,24},{12,28},{16,0},{20,4},{24,8},{28,12},{32,48},... | collective-permute-start | bytes 589832 | tf_op jit(solution)/shard_map/ppermute | solution.py:381
  100.2 5.2 %collective-permute-done.4.later_arrived = f32[384,128]{1,0:T(8,128)S(1)} collective-permute-done((f32[384,128]{1,0:T(8,128)S(1)}, f32[384,128]{1,0:T(8,128)S(1)}, u32[]{:S(2)}, u32[]{:S(2)}) %collective-permute-start.4) | collective-permute-done | bytes 196640 | tf_op jit(solution)/shard_map/ppermute | solution.py:381
  105.4 5.3 %shard_map.52 = (f32[144,128]{1,0:T(8,128)S(1)}, f32[512,128]{1,0:T(8,128)S(1)}, f32[144,128]{1,0:T(8,128)S(1)}, f32[128,128]{1,0:T(8,128)S(1)}) custom-call(f32[4,160,128]{2,1,0:T(8,128)S(1)} %all-to-all-done.3.everyone, f32[176,128]{1,0:T(8,128)S(1)} %get-tuple-element.52.mine, f32[176,128]{1,0:T(8,128)S(1)} %collective-permute-done.3.arrived, ...), custom_call_target="tpu_custom_call" | custom-call | flops 3000000000 | tf_op jit(solution)/shard_map/pallas_call | solution.py:88
  110.7 8.2 %collective-permute-start.5 = (f32[144,128]{1,0:T(8,128)S(1)}, f32[144,128]{1,0:T(8,128)S(1)}, u32[]{:S(2)}, u32[]{:S(2)}) collective-permute-start(f32[144,128]{1,0:T(8,128)S(1)} %get-tuple-element.57), channel_id=1, source_target_pairs={{0,48},{4,52},{8,56},{12,60},{16,32},{20,36},{24,40},{28,44},{32,1... | collective-permute-start | bytes 221192 | tf_op jit(solution)/shard_map/ppermute | solution.py:381
  122.7 5.6 %collective-permute-done.6 = f32[240,128]{1,0:T(8,128)S(1)} collective-permute-done((f32[240,128]{1,0:T(8,128)S(1)}, f32[240,128]{1,0:T(8,128)S(1)}, u32[]{:S(2)}, u32[]{:S(2)}) %collective-permute-start.6) | collective-permute-done | bytes 122912 | tf_op jit(solution)/shard_map/ppermute | solution.py:381
  129.4 4.8 %all-to-all-start.4 = ((f32[4,432,128]{2,1,0:T(8,128)}), f32[4,432,128]{2,1,0:T(8,128)S(1)}, u32[]{:S(2)}, u32[]{:S(2)}) async-start(f32[4,432,128]{2,1,0:T(8,128)} %broadcast_in_dim.14), calls=%async_computation.4 | async-start | bytes 1769472 | tf_op jit(solution)/shard_map/all_to_all | solution.py:358
  140.0 4.2 %all-to-all-done.4.everyone = f32[4,432,128]{2,1,0:T(8,128)S(1)} async-done(((f32[4,432,128]{2,1,0:T(8,128)}), f32[4,432,128]{2,1,0:T(8,128)S(1)}, u32[]{:S(2)}, u32[]{:S(2)}) %all-to-all-start.4) | async-done | bytes 884768 | tf_op jit(solution)/shard_map/all_to_all | solution.py:358
  144.2 5.7 %shard_map.57 = (f32[448,128]{1,0:T(8,128)S(1)}, f32[448,128]{1,0:T(8,128)S(1)}, f32[448,128]{1,0:T(8,128)S(1)}) custom-call(f32[4,432,128]{2,1,0:T(8,128)S(1)} %all-to-all-done.4.everyone), custom_call_target="tpu_custom_call" | custom-call | flops 3000000000 | tf_op jit(solution)/shard_map/pallas_call | solution.py:88
  150.0 4.3 %collective-permute-start.7 = (f32[448,128]{1,0:T(8,128)S(1)}, f32[448,128]{1,0:T(8,128)S(1)}, u32[]{:S(2)}, u32[]{:S(2)}) collective-permute-start(f32[448,128]{1,0:T(8,128)S(1)} %get-tuple-element.71.mine), channel_id=1, source_target_pairs={{0,64},{4,68},{8,72},{12,76},{16,80},{20,84},{24,88},{28,92},{32,9... | collective-permute-start | bytes 688136 | tf_op jit(solution)/shard_map/ppermute | solution.py:381
  156.6 3.9 %collective-permute-start.10 = (f32[320,128]{1,0:T(8,128)S(1)}, f32[320,128]{1,0:T(8,128)S(1)}, u32[]{:S(2)}, u32[]{:S(2)}) collective-permute-start(f32[320,128]{1,0:T(8,128)S(1)} %get-tuple-element.76.later), channel_id=1, source_target_pairs={{0,64},{4,68},{8,72},{12,76},{16,80},{20,84},{24,88},{28,92},{32,9... | collective-permute-start | bytes 491528 | tf_op jit(solution)/shard_map/ppermute | solution.py:381
  169.2 5.1 %shard_map.59 = (f32[320,128]{1,0:T(8,128)S(1)}, f32[320,128]{1,0:T(8,128)S(1)}) custom-call(f32[448,128]{1,0:T(8,128)S(1)} %get-tuple-element.71.mine, f32[448,128]{1,0:T(8,128)S(1)} %collective-permute-done.7.arrived), custom_call_target="tpu_custom_call" | custom-call | flops 3000000000 | tf_op jit(solution)/shard_map/pallas_call | solution.py:88
  174.5 6.1 %collective-permute-start.9 = (f32[192,128]{1,0:T(8,128)S(1)}, f32[192,128]{1,0:T(8,128)S(1)}, u32[]{:S(2)}, u32[]{:S(2)}) collective-permute-start(f32[192,128]{1,0:T(8,128)S(1)} %shard_map.62.later), channel_id=1, source_target_pairs={{0,128},{4,132},{8,136},{12,140},{16,144},{20,148},{24,152},{28,15... | collective-permute-start | bytes 294920 | tf_op jit(solution)/shard_map/ppermute | solution.py:381
  183.3 7.4 %collective-permute-done.11.arrived = f32[320,128]{1,0:T(8,128)S(1)} collective-permute-done((f32[320,128]{1,0:T(8,128)S(1)}, f32[320,128]{1,0:T(8,128)S(1)}, u32[]{:S(2)}, u32[]{:S(2)}) %collective-permute-start.11) | collective-permute-done | bytes 163872 | tf_op jit(solution)/shard_map/ppermute | solution.py:381
  190.7 5.0 %shard_map.64 = (f32[192,128]{1,0:T(8,128)S(1)}, f32[192,128]{1,0:T(8,128)S(1)}) custom-call(f32[320,128]{1,0:T(8,128)S(1)} %shard_map.63.mine, f32[320,128]{1,0:T(8,128)S(1)} %collective-permute-done.11.arrived), custom_call_target="tpu_custom_call" | custom-call | flops 3000000000 | tf_op jit(solution)/shard_map/pallas_call | solution.py:88
  197.2 3.5 %all-to-all-start.5 = ((f32[4,144,256]{2,1,0:T(8,128)}), f32[4,144,256]{2,1,0:T(8,128)S(1)}, u32[]{:S(2)}, u32[]{:S(2)}) async-start(f32[4,144,256]{2,1,0:T(8,128)} %shard_map.66), calls=%async_computation.5 | async-start | bytes 1179648 | tf_op jit(solution)/shard_map/all_to_all | solution.py:481
  200.7 5.1 %collective-permute-start.12 = (f32[144,128]{1,0:T(8,128)S(1)}, f32[144,128]{1,0:T(8,128)S(1)}, u32[]{:S(2)}, u32[]{:S(2)}) collective-permute-start(f32[144,128]{1,0:T(8,128)S(1)} %shard_map.65.mine), channel_id=1, source_target_pairs={{0,384},{4,388},{8,392},{12,396},{16,400},{20,404},{24,408},{28,41... | collective-permute-start | bytes 221192 | tf_op jit(solution)/shard_map/ppermute | solution.py:381
  205.8 3.4 %collective-permute-done.12.arrived = f32[144,128]{1,0:T(8,128)S(1)} collective-permute-done((f32[144,128]{1,0:T(8,128)S(1)}, f32[144,128]{1,0:T(8,128)S(1)}, u32[]{:S(2)}, u32[]{:S(2)}) %collective-permute-start.12) | collective-permute-done | bytes 73760 | tf_op jit(solution)/shard_map/ppermute | solution.py:381
  209.9 7.6 %shard_map.67 = f32[16,1024]{1,0:T(8,128)} custom-call(f32[144,128]{1,0:T(8,128)S(1)} %shard_map.65.mine, f32[144,128]{1,0:T(8,128)S(1)} %collective-permute-done.12.arrived, f32[4,144,256]{2,1,0:T(8,128)S(1)} %all-to-all-done.5.got, s32[1,1024]{1,0:T(1,128)S(1)} %copy-done.7), custom_call_target="tpu_custom_call" | custom-call | flops 3000000000 | tf_op jit(solution)/shard_map/pallas_call | solution.py:88
  (94 shorter events, 38.7 us)
Async XLA Ops:
  6.5 1.5 copy-start
  8.0 1.2 copy-start.2
  13.7 18.6 %copy-start.1 = (bf16[7,128,1024]{2,1,0:T(8,128)(2,1)S(1)}, bf16[7,128,1024]{2,1,0:T(8,128)(2,1)}, u32[]{:S(2)}) copy-start(bf16[7,128,1024]{2,1,0:T(8,128)(2,1)} %bases.1) | copy-start | bytes 5505028
  34.9 4.0 %collective-permute-start = (f32[1344,128]{1,0:T(8,128)S(1)}, f32[1344,128]{1,0:T(8,128)S(1)}, u32[]{:S(2)}, u32[]{:S(2)}) collective-permute-start(f32[1344,128]{1,0:T(8,128)S(1)} %shard_map.47.mine), channel_id=1, source_target_pairs={{0,4},{4,0},{8,12},{12,8},{16,20},{20,16},{24,28},{28,24},{32,36},... | collective-permute-start | bytes 2064392 | tf_op jit(solution)/shard_map/ppermute | solution.py:381
  59.1 6.6 %collective-permute-start.1 = (f32[208,128]{1,0:T(8,128)S(1)}, f32[208,128]{1,0:T(8,128)S(1)}, u32[]{:S(2)}, u32[]{:S(2)}) collective-permute-start(f32[208,128]{1,0:T(8,128)S(1)} %get-tuple-element.48.mine), channel_id=1, source_target_pairs={{0,8},{4,12},{8,0},{12,4},{16,24},{20,28},{24,16},{28,20},{32,40},... | collective-permute-start | bytes 319496 | tf_op jit(solution)/shard_map/ppermute | solution.py:381
  66.5 12.1 %all-to-all-start.2 = ((f32[4,192,128]{2,1,0:T(8,128)}), f32[4,192,128]{2,1,0:T(8,128)S(1)}, u32[]{:S(2)}, u32[]{:S(2)}) async-start(f32[4,192,128]{2,1,0:T(8,128)} %broadcast_in_dim.12), calls=%async_computation.2 | async-start | bytes 786432 | tf_op jit(solution)/shard_map/all_to_all | solution.py:358
  70.0 8.6 %collective-permute-start.2 = (f32[560,128]{1,0:T(8,128)S(1)}, f32[560,128]{1,0:T(8,128)S(1)}, u32[]{:S(2)}, u32[]{:S(2)}) collective-permute-start(f32[560,128]{1,0:T(8,128)S(1)} %shard_map.49.later), channel_id=1, source_target_pairs={{0,8},{4,12},{8,0},{12,4},{16,24},{20,28},{24,16},{28,20},{32,40},... | collective-permute-start | bytes 860168 | tf_op jit(solution)/shard_map/ppermute | solution.py:381
  84.0 52.6 %copy-start.18 = (f32[128,128]{1,0:T(8,128)}, f32[128,128]{1,0:T(8,128)S(1)}, u32[]{:S(2)}) copy-start(f32[128,128]{1,0:T(8,128)S(1)} %get-tuple-element.62.inverse.i2) | copy-start | bytes 196612
  84.0 7.4 %collective-permute-start.3 = (f32[176,128]{1,0:T(8,128)S(1)}, f32[176,128]{1,0:T(8,128)S(1)}, u32[]{:S(2)}, u32[]{:S(2)}) collective-permute-start(f32[176,128]{1,0:T(8,128)S(1)} %get-tuple-element.52.mine), channel_id=1, source_target_pairs={{0,16},{4,20},{8,24},{12,28},{16,0},{20,4},{24,8},{28,12},{32,48},... | collective-permute-start | bytes 270344 | tf_op jit(solution)/shard_map/ppermute | solution.py:381
  92.2 13.2 %all-to-all-start.3 = ((f32[4,160,128]{2,1,0:T(8,128)}), f32[4,160,128]{2,1,0:T(8,128)S(1)}, u32[]{:S(2)}, u32[]{:S(2)}) async-start(f32[4,160,128]{2,1,0:T(8,128)} %broadcast_in_dim.13), calls=%async_computation.3 | async-start | bytes 655360 | tf_op jit(solution)/shard_map/all_to_all | solution.py:358
  96.8 63.7 %all-reduce.2.cloned.1.call-start = ((), (), s32[]{:S(2)}) async-start(), calls=%async_computation.6 | async-start | bytes 524288 | tf_op jit(solution)/shard_map/psum | solution.py:415
  96.8 8.5 %collective-permute-start.4 = (f32[384,128]{1,0:T(8,128)S(1)}, f32[384,128]{1,0:T(8,128)S(1)}, u32[]{:S(2)}, u32[]{:S(2)}) collective-permute-start(f32[384,128]{1,0:T(8,128)S(1)} %shard_map.51.later), channel_id=1, source_target_pairs={{0,16},{4,20},{8,24},{12,28},{16,0},{20,4},{24,8},{28,12},{32,48},... | collective-permute-start | bytes 589832 | tf_op jit(solution)/shard_map/ppermute | solution.py:381
  110.7 8.8 %copy-start.16 = (f32[512,128]{1,0:T(8,128)}, f32[512,128]{1,0:T(8,128)S(1)}, u32[]{:S(2)}) copy-start(f32[512,128]{1,0:T(8,128)S(1)} %get-tuple-element.58.far) | copy-start | bytes 786436
  110.7 8.8 %copy-start.20 = (f32[128,128]{1,0:T(8,128)}, f32[128,128]{1,0:T(8,128)S(1)}, u32[]{:S(2)}) copy-start(f32[128,128]{1,0:T(8,128)S(1)} %get-tuple-element.63.inverse.i3) | copy-start | bytes 196612
  110.7 12.0 %collective-permute-start.5 = (f32[144,128]{1,0:T(8,128)S(1)}, f32[144,128]{1,0:T(8,128)S(1)}, u32[]{:S(2)}, u32[]{:S(2)}) collective-permute-start(f32[144,128]{1,0:T(8,128)S(1)} %get-tuple-element.57), channel_id=1, source_target_pairs={{0,48},{4,52},{8,56},{12,60},{16,32},{20,36},{24,40},{28,44},{32,1... | collective-permute-start | bytes 221192 | tf_op jit(solution)/shard_map/ppermute | solution.py:381
  119.5 8.9 %collective-permute-start.6 = (f32[240,128]{1,0:T(8,128)S(1)}, f32[240,128]{1,0:T(8,128)S(1)}, u32[]{:S(2)}, u32[]{:S(2)}) collective-permute-start(f32[240,128]{1,0:T(8,128)S(1)} %shard_map.53), channel_id=1, source_target_pairs={{0,48},{4,52},{8,56},{12,60},{16,32},{20,36},{24,40},{28,44},{32,1... | collective-permute-start | bytes 368648 | tf_op jit(solution)/shard_map/ppermute | solution.py:381
  129.4 14.8 %all-to-all-start.4 = ((f32[4,432,128]{2,1,0:T(8,128)}), f32[4,432,128]{2,1,0:T(8,128)S(1)}, u32[]{:S(2)}, u32[]{:S(2)}) async-start(f32[4,432,128]{2,1,0:T(8,128)} %broadcast_in_dim.14), calls=%async_computation.4 | async-start | bytes 1769472 | tf_op jit(solution)/shard_map/all_to_all | solution.py:358
  136.6 2.2 copy-start.17
  136.6 2.2 copy-start.21
  140.0 10.0 %copy-start.14 = (f32[128,256]{1,0:T(8,128)}, f32[128,256]{1,0:T(8,128)S(1)}, u32[]{:S(2)}) copy-start(f32[128,256]{1,0:T(8,128)S(1)} %get-tuple-element.68.g3) | copy-start | bytes 393220
  150.0 4.7 %copy-start.8 = (f32[448,128]{1,0:T(8,128)}, f32[448,128]{1,0:T(8,128)S(1)}, u32[]{:S(2)}) copy-start(f32[448,128]{1,0:T(8,128)S(1)} %get-tuple-element.70.weights) | copy-start | bytes 688132
  150.0 19.2 %collective-permute-start.7 = (f32[448,128]{1,0:T(8,128)S(1)}, f32[448,128]{1,0:T(8,128)S(1)}, u32[]{:S(2)}, u32[]{:S(2)}) collective-permute-start(f32[448,128]{1,0:T(8,128)S(1)} %get-tuple-element.71.mine), channel_id=1, source_target_pairs={{0,64},{4,68},{8,72},{12,76},{16,80},{20,84},{24,88},{28,92},{32,9... | collective-permute-start | bytes 688136 | tf_op jit(solution)/shard_map/ppermute | solution.py:381
  154.3 6.3 %copy-start.3 = (f32[1024,256]{1,0:T(8,128)S(1)}, f32[1024,256]{1,0:T(8,128)}, u32[]{:S(2)}) copy-start(f32[1024,256]{1,0:T(8,128)} %inverse_cols.1) | copy-start | bytes 3145732
  154.7 19.6 %collective-permute-start.8 = (f32[192,128]{1,0:T(8,128)S(1)}, f32[192,128]{1,0:T(8,128)S(1)}, u32[]{:S(2)}, u32[]{:S(2)}) collective-permute-start(f32[192,128]{1,0:T(8,128)S(1)} %get-tuple-element.74.later), channel_id=1, source_target_pairs={{0,64},{4,68},{8,72},{12,76},{16,80},{20,84},{24,88},{28,92},{32,9... | collective-permute-start | bytes 294920 | tf_op jit(solution)/shard_map/ppermute | solution.py:381
  156.6 24.0 %collective-permute-start.10 = (f32[320,128]{1,0:T(8,128)S(1)}, f32[320,128]{1,0:T(8,128)S(1)}, u32[]{:S(2)}, u32[]{:S(2)}) collective-permute-start(f32[320,128]{1,0:T(8,128)S(1)} %get-tuple-element.76.later), channel_id=1, source_target_pairs={{0,64},{4,68},{8,72},{12,76},{16,80},{20,84},{24,88},{28,92},{32,9... | collective-permute-start | bytes 491528 | tf_op jit(solution)/shard_map/ppermute | solution.py:381
  160.6 1.0 copy-start.4
  161.5 0.9 copy-start.9
  174.5 21.2 %collective-permute-start.9 = (f32[192,128]{1,0:T(8,128)S(1)}, f32[192,128]{1,0:T(8,128)S(1)}, u32[]{:S(2)}, u32[]{:S(2)}) collective-permute-start(f32[192,128]{1,0:T(8,128)S(1)} %shard_map.62.later), channel_id=1, source_target_pairs={{0,128},{4,132},{8,136},{12,140},{16,144},{20,148},{24,152},{28,15... | collective-permute-start | bytes 294920 | tf_op jit(solution)/shard_map/ppermute | solution.py:381
  180.9 9.8 %collective-permute-start.11 = (f32[320,128]{1,0:T(8,128)S(1)}, f32[320,128]{1,0:T(8,128)S(1)}, u32[]{:S(2)}, u32[]{:S(2)}) collective-permute-start(f32[320,128]{1,0:T(8,128)S(1)} %shard_map.63.mine), channel_id=1, source_target_pairs={{0,128},{4,132},{8,136},{12,140},{16,144},{20,148},{24,152},{28,15... | collective-permute-start | bytes 491528 | tf_op jit(solution)/shard_map/ppermute | solution.py:381
  196.0 13.9 %copy-start.7 = (s32[1,1024]{1,0:T(1,128)S(1)}, s32[1,1024]{1,0:T(1,128)}, u32[]{:S(2)}) copy-start(s32[1,1024]{1,0:T(1,128)} %order.1) | copy-start | bytes 12292
  197.2 12.7 %all-to-all-start.5 = ((f32[4,144,256]{2,1,0:T(8,128)}), f32[4,144,256]{2,1,0:T(8,128)S(1)}, u32[]{:S(2)}, u32[]{:S(2)}) async-start(f32[4,144,256]{2,1,0:T(8,128)} %shard_map.66), calls=%async_computation.5 | async-start | bytes 1179648 | tf_op jit(solution)/shard_map/all_to_all | solution.py:481
  200.7 8.5 %collective-permute-start.12 = (f32[144,128]{1,0:T(8,128)S(1)}, f32[144,128]{1,0:T(8,128)S(1)}, u32[]{:S(2)}, u32[]{:S(2)}) collective-permute-start(f32[144,128]{1,0:T(8,128)S(1)} %shard_map.65.mine), channel_id=1, source_target_pairs={{0,384},{4,388},{8,392},{12,396},{16,400},{20,404},{24,408},{28,41... | collective-permute-start | bytes 221192 | tf_op jit(solution)/shard_map/ppermute | solution.py:381
  (10 other events, 7.9 us)
Sparse Core Ops, SparseCore 0:
  100.3 59.5 all-reduce.1

commit v4 on v3

--- a/solution.py
+++ b/solution.py
@@ -9,6 +9,7 @@
 
 HIGHEST = lax.Precision.HIGHEST
 VMEM_BYTES = 24 * 1024 * 1024
+START_BYTES = 60 * 1024 * 1024
 NN = (((1,), (0,)), ((), ()))
 NT = (((1,), (1,)), ((), ()))
 
@@ -82,15 +83,19 @@
     return lax.while_loop(unfinished, again, (better, 0, size2[0, 0]))[0]
 
 
+def shape_of(out):
+    return out if isinstance(out, jax.ShapeDtypeStruct) else jax.ShapeDtypeStruct(out, jnp.float32)
+
+
 def run(body, outs, *args, place=None):
     vmem = pl.BlockSpec(memory_space=pltpu.VMEM)
     scalars = [] if place is None else [place]
     return pl.pallas_call(
         body,
-        out_shape=[jax.ShapeDtypeStruct(shape, jnp.float32) for shape in outs],
+        out_shape=[shape_of(out) for out in outs],
         in_specs=[pl.BlockSpec(memory_space=pltpu.SMEM)] * len(scalars) + [vmem] * len(args),
         out_specs=[vmem] * len(outs),
-        cost_estimate=pl.CostEstimate(flops=3_000_000_000, bytes_accessed=0, transcendentals=0),
+        cost_estimate=pl.CostEstimate(flops=1_000_000_000, bytes_accessed=0, transcendentals=0),
         compiler_params=pltpu.CompilerParams(vmem_limit_bytes=VMEM_BYTES),
     )(*scalars, *args)
 
@@ -112,13 +117,13 @@
 
     return pl.pallas_call(
         loading,
-        out_shape=[jax.ShapeDtypeStruct(shape, jnp.float32) for shape in outs],
+        out_shape=[shape_of(out) for out in outs],
         in_specs=[pl.BlockSpec(memory_space=pltpu.HBM)] * len(args),
         out_specs=[pl.BlockSpec(memory_space=pltpu.VMEM)] * len(outs),
         scratch_shapes=[pltpu.VMEM(arg.shape, arg.dtype) for arg in args]
         + [pltpu.SemaphoreType.DMA((len(args),))],
-        cost_estimate=pl.CostEstimate(flops=3_000_000_000, bytes_accessed=0, transcendentals=0),
-        compiler_params=pltpu.CompilerParams(vmem_limit_bytes=VMEM_BYTES),
+        cost_estimate=pl.CostEstimate(flops=1_000_000_000, bytes_accessed=0, transcendentals=0),
+        compiler_params=pltpu.CompilerParams(vmem_limit_bytes=START_BYTES),
     )(*args)
 
 
@@ -139,37 +144,47 @@
     return jnp.concatenate([everyone[group, low : low + count, :] for group in range(everyone.shape[0])], 0)
 
 
-def start_body(sides, order, inverse_cols, bases, send, tree):
+def start_body(sides, order, inverse_cols, bases, send, hot):
     levels, rank, leaf = bases.shape
     groups, _, piece = send.shape
     share = rank // groups
-    tree[...] = dot_left_parts(sides[...], one_hot(order[...]), NN)
+    own = sides.shape[0]
+    hot[...] = one_hot(order[...])
+    tree = dot_left_parts(sides[...], hot[...], NN)
     applied = dot_right_parts(bases[...].reshape(levels * rank, leaf), inverse_cols[...], NN)
     for group in range(groups):
         for level in range(levels):
             low = level * rank + group * share
             send[group, level * share : (level + 1) * share, :] = applied[low : low + share]
-        send[group, levels * share :, :] = tree[:, group * piece : (group + 1) * piece]
-
-
-def gram_body(got, send, bases, gram):
+        for part in range(groups):
+            low = levels * share + part * own
+            send[group, low : low + own, :] = tree[:, part * piece : (part + 1) * piece]
+
+
+def gram_body(place, got, send, bases, gram, tree):
     levels, rank, leaf = bases.shape
     groups, rows, piece = got.shape
     share = rank // groups
-    own = rows - levels * share
-    applied = jnp.concatenate([got[group, : levels * share, :] for group in range(groups)], 1)
+    v_rows = levels * share
+    own = (rows - v_rows) // groups
+    applied = jnp.concatenate([got[group, :v_rows, :] for group in range(groups)], 1)
     product = dot_left_parts(applied, bases[...].reshape(levels * rank, leaf), NT)
     at = 0
     for column in range(levels):
         count = (levels - column) * share
         gram[at : at + count, :] = product[column * share :, column * rank : (column + 1) * rank]
         at += count
-    sides = stacked(got, levels * share, own)
+    mine = pl.ds(pl.multiple_of(v_rows + place[0] * own, own), own)
+    sides = jnp.concatenate([got[group, mine, :] for group in range(groups)], 0)
     for level in range(levels):
         block = exact_dot(sides, stacked(send, level * share, share), NT)
         for group in range(groups):
             low = at + (group * levels + level) * own
             gram[low : low + own, :] = block[group * own : (group + 1) * own]
+    for group in range(groups):
+        tree[group * own : (group + 1) * own, :] = jnp.concatenate(
+            [got[group, v_rows + part * own : v_rows + (part + 1) * own, :] for part in range(groups)], 1
+        )
 
 
 def first_body(everyone, mine, arrived, panel, weights, own_weights, inverse, side_upper):
@@ -210,10 +225,9 @@
         at += count + own
 
 
-def level_body(everyone, mine, arrived, later, later_arrived, panel, far, own_weights, inverse):
-    groups, rows, rank = everyone.shape
-    share = rank // groups
-    above = rows // share - 1
+def level_body(above, everyone, mine, arrived, later, later_arrived, panel, far, own_weights, inverse):
+    groups, _, rank = everyone.shape
+    share = rank // groups
     far[...] = jnp.concatenate([stacked(everyone, level * share, share) for level in range(1, above + 1)], 0)
     inverse[...] = inverse_of(stacked(everyone, 0, share) + identity(rank))
     own_weights[...] = exact_dot(mine[share:, :] + arrived[share:, :], inverse[...], NN)
@@ -255,20 +269,18 @@
     fifth[3 * rank :, :] = stacked(everyone, at + 3 * share, own) - update[3 * rank :]
 
 
-def spread_rest_body(everyone, far, weights, sixth, seventh):
+def spread_rest_body(column, everyone, far, weights, panel):
     groups, _, rank = everyone.shape
     share = rank // groups
     own = (far.shape[0] - 3 * rank) // groups
-    source = 7 * share + 2 * own
-    for column, panel in ((1, sixth), (2, seventh)):
-        update = exact_dot(weights[column * rank :, :], far[column * rank : (column + 1) * rank, :], NT)
-        at = 0
-        for level in range(column, 3):
-            panel[at : at + rank, :] = stacked(everyone, source, share) - update[at : at + rank]
-            at += rank
-            source += share
-        panel[at:, :] = stacked(everyone, source, own) - update[at:]
-        source += own
+    source = (7 if column == 1 else 9) * share + (2 if column == 1 else 3) * own
+    update = exact_dot(weights[column * rank :, :], far[column * rank : (column + 1) * rank, :], NT)
+    at = 0
+    for level in range(column, 3):
+        panel[at : at + rank, :] = stacked(everyone, source, share) - update[at : at + rank]
+        at += rank
+        source += share
+    panel[at:, :] = stacked(everyone, source, own) - update[at:]
 
 
 def factor_body(mine, arrived, upper, weights):
@@ -298,34 +310,33 @@
     panel[rank:, :] = later[rows, :] + later_arrived[rows, :] - update[rank:]
 
 
-def carry_first_body(send, far, inverse, carried, gone):
-    groups = send.shape[0]
-    share = inverse.shape[0] // groups
-    applied = [stacked(send, level * share, share) for level in range(7)]
-    gone[...] = applied[0]
-    weights = exact_dot(far[...], inverse[...], NN)
-    carried[...] = jnp.concatenate(applied[1:], 0) - exact_dot(weights, applied[0], NN)
-
-
-def carry_body(before, far, inverse, carried, gone):
+def carry_step(applied, sides, far, side_far, inverse):
     rank = inverse.shape[0]
-    gone[...] = before[:rank, :]
-    weights = exact_dot(far[...], inverse[...], NN)
-    carried[...] = before[rank:, :] - exact_dot(weights, before[:rank, :], NN)
-
-
-def carry_sides_body(tree, inverse_cols, everyone, i1, i2, i3, g1, g2, g3, before, weights, carried):
+    gone = applied[:rank]
+    sides = sides - exact_dot(exact_dot(side_far, inverse, NN), gone, NN)
+    return applied[rank:] - exact_dot(exact_dot(far, inverse, NN), gone, NN), sides
+
+
+def carry_first_body(send, tree, inverse_cols, far1, inverse1, everyone, far2, inverse2, carried):
+    groups = everyone.shape[0]
+    share = inverse1.shape[0] // groups
+    own = tree.shape[0] // groups
+    applied = jnp.concatenate([stacked(send, level * share, share) for level in range(7)], 0)
+    sides = exact_dot(tree[...], inverse_cols[...], NN)
+    applied, sides = carry_step(applied, sides, far1[...], stacked(everyone, 6 * share + own, own), inverse1[...])
+    applied, sides = carry_step(applied, sides, far2[...], stacked(everyone, 6 * share, own), inverse2[...])
+    carried[...] = jnp.concatenate([applied, sides], 0)
+
+
+def carry_body(above, before, everyone, far, inverse, carried):
     groups, _, rank = everyone.shape
-    sides = tree.shape[0]
-    own = sides // groups
-    source = everyone.shape[1] - 3 * own
-    found = exact_dot(tree[...], inverse_cols[...], NN)
-    for level, inverse, gone in ((0, i1, g1), (1, i2, g2), (2, i3, g3)):
-        side_weights = exact_dot(stacked(everyone, source + level * own, own), inverse[...], NN)
-        found = found - exact_dot(side_weights, gone[...], NN)
-    update = exact_dot(weights[...], before[:rank, :], NN)
-    carried[: 3 * rank, :] = before[rank:, :] - update[: 3 * rank]
-    carried[3 * rank :, :] = found - update[3 * rank :]
+    share = rank // groups
+    count = (above + 1) * rank
+    own = (before.shape[0] - count) // groups
+    applied, sides = carry_step(
+        before[:count, :], before[count:, :], far[...], stacked(everyone, (above + 1) * share, own), inverse[...]
+    )
+    carried[...] = jnp.concatenate([applied, sides], 0)
 
 
 def carry_on_body(before, weights, carried):
@@ -343,14 +354,14 @@
         send[group, rank:, :] = carried[rank + group * own : rank + (group + 1) * own]
 
 
-def finish_body(mine, arrived, got, order, out):
+def finish_body(mine, arrived, got, hot, out):
     rank = mine.shape[1]
     groups = got.shape[0]
     inverse = inverse_of(mine[:rank, :] + arrived[:rank, :] + identity(rank))
     top = exact_dot(mine[rank:, :] + arrived[rank:, :], inverse, NN)
     slope = jnp.concatenate([got[group, :rank, :] for group in range(groups)], 1)
     base = jnp.concatenate([got[group, rank:, :] for group in range(groups)], 1)
-    out[...] = dot_left_parts(base - exact_dot(top, slope, NN), one_hot(order[...]), NT)
+    out[...] = dot_left_parts(base - exact_dot(top, slope, NN), hot[...], NT)
 
 
 def to_all(block, axis):
@@ -380,9 +391,13 @@
     square = (rank, rank)
     swap = lambda block, height: lax.ppermute(block, "leaf", route(height))
 
-    send, tree = run_loading(
+    place = lax.axis_index("rhs").reshape(1)
+    send, hot = run_loading(
         start_body,
-        [(groups, levels * share + own, piece), (own, leaf)],
+        [
+            (groups, levels * share + sides, piece),
+            jax.ShapeDtypeStruct((leaf, leaf), jnp.bfloat16),
+        ],
         right_sides,
         ordering,
         leaf_inverse,
@@ -390,7 +405,9 @@
     )
     got = lax.all_to_all(send, "rhs", 0, 0)
     rows = 28 * share
-    (gram,) = run(gram_body, [(rows + groups * levels * own, rank)], got, send, bases)
+    gram, tree = run(
+        gram_body, [(rows + groups * levels * own, rank), (sides, leaf)], got, send, bases, place=place
+    )
     other = swap(gram, 1)
     total = gram + other
     shared = jnp.broadcast_to(total[: 7 * share][None], (groups, 7 * share, rank))
@@ -408,22 +425,16 @@
     (later,) = run(
         first_rest_body, [(15 * share + 5 * own, rank)], everyone, gram, other, far1, own_weights
     )
-    tree, later = lax.optimization_barrier((tree, later))
-    spread_tree = lax.dynamic_update_slice(
-        jnp.zeros((sides, leaf), jnp.float32), tree, (lax.axis_index("rhs") * own, 0)
-    )
-    whole_tree = lax.psum(spread_tree, "rhs")
-    carried, gone = run(carry_first_body, [(6 * rank, piece), (rank, piece)], send, far1, inverse1)
-    inverses, gones, side_uppers = [inverse1], [gone], [side1]
     for height in (2, 3):
         above = 7 - height
         later_arrived = swap(later, height)
-        near = panel[: (above + 1) * share] + arrived[: (above + 1) * share]
+        near = panel + arrived
+        if height == 2:
+            near = jnp.concatenate([near, side1], 0)
         near, later = lax.optimization_barrier((near, later))
         everyone = to_all(near, "rhs")
-        side_uppers.append(panel[(above + 1) * share :] + arrived[(above + 1) * share :])
-        next_panel, level_far, own_weights, inverse = run(
-            level_body,
+        next_panel, far, own_weights, inverse = run(
+            functools.partial(level_body, above),
             [(above * share + own, rank), (above * rank, rank), (above * share + own, rank), square],
             everyone,
             panel,
@@ -433,45 +444,50 @@
         )
         arrived = swap(next_panel, height + 1)
         rest_rows = above * (above - 1) // 2 * share + (above - 1) * own
-        (later,) = run(
-            level_rest_body, [(rest_rows, rank)], later, later_arrived, level_far, own_weights
-        )
+        (later,) = run(level_rest_body, [(rest_rows, rank)], later, later_arrived, far, own_weights)
         panel = next_panel
-        carried, gone = run(
-            carry_body, [(above * rank, piece), (rank, piece)], carried, level_far, inverse
-        )
-        inverses.append(inverse)
-        gones.append(gone)
+        if height == 2:
+            (carried,) = run(
+                carry_first_body,
+                [(5 * rank + sides, piece)],
+                send,
+                tree,
+                leaf_inverse,
+                far1,
+                inverse1,
+                everyone,
+                far,
+                inverse,
+            )
+        else:
+            (carried,) = run(
+                functools.partial(carry_body, above),
+                [(4 * rank + sides, piece)],
+                carried,
+                everyone,
+                far,
+                inverse,
+            )
 
     later_arrived = swap(later, 4)
-    everyone = to_all(
-        jnp.concatenate([panel + arrived, later + later_arrived] + side_uppers, 0), "rhs"
-    )
+    everyone = to_all(jnp.concatenate([panel + arrived, later + later_arrived], 0), "rhs")
     heights = lambda count: (count * rank + sides, rank)
     fifth, upper, weights = run(spread_body, [heights(3)] * 3, everyone)
     arrived = swap(fifth, 5)
-    sixth, seventh = run(spread_rest_body, [heights(2), heights(1)], everyone, upper, weights)
+    (sixth,) = run(functools.partial(spread_rest_body, 1), [heights(2)], everyone, upper, weights)
     sixth_arrived = swap(sixth, 5)
+    everyone, sixth = lax.optimization_barrier((everyone, sixth))
+    (seventh,) = run(functools.partial(spread_rest_body, 2), [heights(1)], everyone, upper, weights)
     seventh_arrived = swap(seventh, 5)
-    (carried,) = run(
-        carry_sides_body,
-        [(3 * rank + sides, piece)],
-        whole_tree,
-        leaf_inverse,
-        everyone,
-        *inverses,
-        *gones,
-        carried,
-        weights,
-    )
+    (carried,) = run(carry_on_body, [(3 * rank + sides, piece)], carried, weights)
     upper, weights = run(factor_body, [heights(2)] * 2, fifth, arrived)
     (sixth,) = run(next_body, [heights(2)], sixth, sixth_arrived, upper, weights)
     arrived = swap(sixth, 6)
+    sixth, seventh = lax.optimization_barrier((sixth, seventh))
     (seventh,) = run(rest_body, [heights(1)], seventh, seventh_arrived, upper, weights)
     seventh_arrived = swap(seventh, 6)
     (carried,) = run(carry_on_body, [(2 * rank + sides, piece)], carried, weights)
     upper, weights = run(factor_body, [heights(1)] * 2, sixth, arrived)
-    place = lax.axis_index("rhs").reshape(1)
     (seventh,) = run(
         last_panel_body, [(rank + own, rank)], seventh, seventh_arrived, upper, weights, place=place
     )
@@ -479,7 +495,7 @@
     carried, seventh = lax.optimization_barrier((carried, seventh))
     (send,) = run(carry_last_body, [(groups, rank + own, piece)], carried, weights)
     got = lax.all_to_all(send, "rhs", 0, 0)
-    (result,) = run(finish_body, [(own, leaf)], seventh, arrived, got, ordering)
+    (result,) = run(finish_body, [(own, leaf)], seventh, arrived, got, hot)
     return result
 
 

time: 226 us -> 200 us (0.88)
  the two profiles are of different devices: /device:TPU:16 before, /device:TPU:10 now
where the time goes in v4:
time: 200 us; the launch traced here: 199 us
  starting transfers between devices  75.5 us (38%)
  Pallas kernels  56.6 us (28%)
  waiting for transfers between devices  44 us (22%)
  blocking collectives  14.2 us (7%)
  local copies, waits for them, and re-layouts  8.11 us (4%)
    ppermute x13, starting transfers between devices, local(): swap = lambda block, height: lax.ppermute(block, 'leaf', route(height))  51.3 us
    pallas_call x21, Pallas kernels, run(): pl.pallas_call(body, out_shape=[shape_of(out) for out in outs], in_specs=...  50.9 us
    ppermute x13, waiting for transfers between devices, local(): swap = lambda block, height: lax.ppermute(block, 'leaf', route(height))  29 us
    all_to_all x2, waiting for transfers between devices, local(): got = lax.all_to_all(send, 'rhs', 0, 0)  15 us
    all_to_all x3, starting transfers between devices, to_all(): lax.all_to_all(jnp.broadcast_to(block[None], (count,) + block.shape), axi...  14.5 us
    all_to_all x1, blocking collectives, local(): everyone = lax.all_to_all(jnp.concatenate([shared, parts], 1), 'rhs', 0, 0)  14.2 us
    all_to_all x2, starting transfers between devices, local(): got = lax.all_to_all(send, 'rhs', 0, 0)  9.78 us
    pallas_call x1, Pallas kernels, run_loading(): pl.pallas_call(loading, out_shape=[shape_of(out) for out in outs], in_spe...  5.72 us
  transfers between devices with their start and end apart: 18, of which 9 were waited for; matrix products, arithmetic and copies ran while one was open for 0% of the time, Pallas kernels for 9%

profile of v4, /device:TPU:10, one launch (start us, length us, event | category | flops | bytes accessed | tf_op | source)
XLA Modules:
  0.0 199.2 jit_solution(3595521863589209082)
XLA Ops:
  0.0 5.7 %shard_map.46 = (f32[4,288,256]{2,1,0:T(8,128)}, bf16[1024,1024]{1,0:T(8,128)(2,1)}) custom-call(f32[16,1024]{1,0:T(8,128)} %refs_0_.1, s32[1,1024]{1,0:T(1,128)} %refs_1_.1, f32[1024,256]{1,0:T(8,128)} %inverse_cols.1, bf16[7,128,1024]{2,1,0:T(8,128)(2,1)} %bases.1), custom_call_target="tpu_custom_call" | custom-call | flops 1000000000 | tf_op jit(solution)/shard_map/pallas_call | solution.py:118
  5.7 5.0 %all-to-all-start = ((f32[4,288,256]{2,1,0:T(8,128)}), f32[4,288,256]{2,1,0:T(8,128)S(1)}, u32[]{:S(2)}, u32[]{:S(2)}) async-start(f32[4,288,256]{2,1,0:T(8,128)} %get-tuple-element.39.send), calls=%async_computation | async-start | bytes 2359296 | tf_op jit(solution)/shard_map/all_to_all | solution.py:406
  10.7 15.0 %all-to-all-done.got = f32[4,288,256]{2,1,0:T(8,128)S(1)} async-done(((f32[4,288,256]{2,1,0:T(8,128)}), f32[4,288,256]{2,1,0:T(8,128)S(1)}, u32[]{:S(2)}, u32[]{:S(2)}) %all-to-all-start) | async-done | bytes 1179680 | tf_op jit(solution)/shard_map/all_to_all | solution.py:406
  27.3 2.6 %shard_map.47 = (f32[1344,128]{1,0:T(8,128)S(1)}, f32[64,1024]{1,0:T(8,128)S(1)}) custom-call(s32[1]{0:T(128)} %bitcast.place, f32[4,288,256]{2,1,0:T(8,128)S(1)} %all-to-all-done.got, f32[4,288,256]{2,1,0:T(8,128)S(1)} %copy-done, bf16[7,128,1024]{2,1,0:T(8,128)(2,1)S(1)} %copy-done.1), custom_call_target="tpu_custom_call" | custom-call | flops 1000000000 | tf_op jit(solution)/shard_map/pallas_call | solution.py:93
  34.1 14.2 %all_to_all.30.everyone = f32[4,336,128]{2,1,0:T(8,128)S(1)} all-to-all(f32[4,336,128]{2,1,0:T(8,128)S(1)} %pad_maximum_fusion), channel_id=1, replica_groups=mesh['leaf'=128,'rhs'=4] {'rhs'}, dimensions={0} | all-to-all | bytes 1376256 | tf_op jit(solution)/shard_map/all_to_all | solution.py:415
  48.3 5.8 %shard_map.48 = (f32[208,128]{1,0:T(8,128)S(1)}, f32[768,128]{1,0:T(8,128)S(1)}, f32[208,128]{1,0:T(8,128)S(1)}, f32[128,128]{1,0:T(8,128)S(1)}, f32[16,128]{1,0:T(8,128)S(1)}) custom-call(f32[4,336,128]{2,1,0:T(8,128)S(1)} %all_to_all.30.everyone, f32[1344,128]{1,0:T(8,128)S(1)} %get-tuple-element.41.mine, f32[1344,128]{1,0:T(8,128)S(1)} %collective-permute-done.arrived), custom_call_target="tpu_custom_call" | custom-call | flops 1000000000 | tf_op jit(solution)/shard_map/pallas_call | solution.py:93
  54.1 2.4 %collective-permute-start.1 = (f32[208,128]{1,0:T(8,128)S(1)}, f32[208,128]{1,0:T(8,128)S(1)}, u32[]{:S(2)}, u32[]{:S(2)}) collective-permute-start(f32[208,128]{1,0:T(8,128)S(1)} %get-tuple-element.44.mine), channel_id=1, source_target_pairs={{0,8},{4,12},{8,0},{12,4},{16,24},{20,28},{24,16},{28,20},{32,40},... | collective-permute-start | bytes 319496 | tf_op jit(solution)/shard_map/ppermute | solution.py:392
  57.2 3.5 %collective-permute-done.1.arrived = f32[208,128]{1,0:T(8,128)S(1)} collective-permute-done((f32[208,128]{1,0:T(8,128)S(1)}, f32[208,128]{1,0:T(8,128)S(1)}, u32[]{:S(2)}, u32[]{:S(2)}) %collective-permute-start.1) | collective-permute-done | bytes 106528 | tf_op jit(solution)/shard_map/ppermute | solution.py:392
  61.5 4.9 %all-to-all-start.2 = ((f32[4,224,128]{2,1,0:T(8,128)}), f32[4,224,128]{2,1,0:T(8,128)S(1)}, u32[]{:S(2)}, u32[]{:S(2)}) async-start(f32[4,224,128]{2,1,0:T(8,128)} %broadcast_in_dim.9), calls=%async_computation.2 | async-start | bytes 917504 | tf_op jit(solution)/shard_map/all_to_all | solution.py:369
  66.4 2.3 %collective-permute-start.2 = (f32[560,128]{1,0:T(8,128)S(1)}, f32[560,128]{1,0:T(8,128)S(1)}, u32[]{:S(2)}, u32[]{:S(2)}) collective-permute-start(f32[560,128]{1,0:T(8,128)S(1)} %shard_map.49.later), channel_id=1, source_target_pairs={{0,8},{4,12},{8,0},{12,4},{16,24},{20,28},{24,16},{28,20},{32,40},... | collective-permute-start | bytes 860168 | tf_op jit(solution)/shard_map/ppermute | solution.py:392
  68.8 6.2 %collective-permute-done.2.later_arrived = f32[560,128]{1,0:T(8,128)S(1)} collective-permute-done((f32[560,128]{1,0:T(8,128)S(1)}, f32[560,128]{1,0:T(8,128)S(1)}, u32[]{:S(2)}, u32[]{:S(2)}) %collective-permute-start.2) | collective-permute-done | bytes 286752 | tf_op jit(solution)/shard_map/ppermute | solution.py:392
  75.0 5.3 %shard_map.50 = (f32[176,128]{1,0:T(8,128)S(1)}, f32[640,128]{1,0:T(8,128)S(1)}, f32[176,128]{1,0:T(8,128)S(1)}, f32[128,128]{1,0:T(8,128)S(1)}) custom-call(f32[4,224,128]{2,1,0:T(8,128)S(1)} %all-to-all-done.2.everyone, f32[208,128]{1,0:T(8,128)S(1)} %get-tuple-element.44.mine, f32[208,128]{1,0:T(8,128)S(1)} %collective-permute-done.1.arrived, ...), custom_call_target="tpu_custom_call" | custom-call | flops 1000000000 | tf_op jit(solution)/shard_map/pallas_call | solution.py:93
  80.3 4.5 %collective-permute-start.3 = (f32[176,128]{1,0:T(8,128)S(1)}, f32[176,128]{1,0:T(8,128)S(1)}, u32[]{:S(2)}, u32[]{:S(2)}) collective-permute-start(f32[176,128]{1,0:T(8,128)S(1)} %get-tuple-element.51.mine), channel_id=1, source_target_pairs={{0,16},{4,20},{8,24},{12,28},{16,0},{20,4},{24,8},{28,12},{32,48},... | collective-permute-start | bytes 270344 | tf_op jit(solution)/shard_map/ppermute | solution.py:392
  85.5 2.2 %collective-permute-done.3.arrived = f32[176,128]{1,0:T(8,128)S(1)} collective-permute-done((f32[176,128]{1,0:T(8,128)S(1)}, f32[176,128]{1,0:T(8,128)S(1)}, u32[]{:S(2)}, u32[]{:S(2)}) %collective-permute-start.3) | collective-permute-done | bytes 90144 | tf_op jit(solution)/shard_map/ppermute | solution.py:392
  88.5 4.8 %all-to-all-start.3 = ((f32[4,176,128]{2,1,0:T(8,128)}), f32[4,176,128]{2,1,0:T(8,128)S(1)}, u32[]{:S(2)}, u32[]{:S(2)}) async-start(f32[4,176,128]{2,1,0:T(8,128)} %broadcast_in_dim.10), calls=%async_computation.3 | async-start | bytes 720896 | tf_op jit(solution)/shard_map/all_to_all | solution.py:369
  93.3 5.3 %collective-permute-start.4 = (f32[384,128]{1,0:T(8,128)S(1)}, f32[384,128]{1,0:T(8,128)S(1)}, u32[]{:S(2)}, u32[]{:S(2)}) collective-permute-start(f32[384,128]{1,0:T(8,128)S(1)} %shard_map.52.later), channel_id=1, source_target_pairs={{0,16},{4,20},{8,24},{12,28},{16,0},{20,4},{24,8},{28,12},{32,48},... | collective-permute-start | bytes 589832 | tf_op jit(solution)/shard_map/ppermute | solution.py:392
  98.6 4.4 %collective-permute-done.4.later_arrived = f32[384,128]{1,0:T(8,128)S(1)} collective-permute-done((f32[384,128]{1,0:T(8,128)S(1)}, f32[384,128]{1,0:T(8,128)S(1)}, u32[]{:S(2)}, u32[]{:S(2)}) %collective-permute-start.4) | collective-permute-done | bytes 196640 | tf_op jit(solution)/shard_map/ppermute | solution.py:392
  103.0 5.3 %shard_map.53 = (f32[144,128]{1,0:T(8,128)S(1)}, f32[512,128]{1,0:T(8,128)S(1)}, f32[144,128]{1,0:T(8,128)S(1)}, f32[128,128]{1,0:T(8,128)S(1)}) custom-call(f32[4,176,128]{2,1,0:T(8,128)S(1)} %all-to-all-done.3.everyone, f32[176,128]{1,0:T(8,128)S(1)} %get-tuple-element.51.mine, f32[176,128]{1,0:T(8,128)S(1)} %collective-permute-done.3.arrived, ...), custom_call_target="tpu_custom_call" | custom-call | flops 1000000000 | tf_op jit(solution)/shard_map/pallas_call | solution.py:93
  109.0 7.2 %collective-permute-start.6 = (f32[240,128]{1,0:T(8,128)S(1)}, f32[240,128]{1,0:T(8,128)S(1)}, u32[]{:S(2)}, u32[]{:S(2)}) collective-permute-start(f32[240,128]{1,0:T(8,128)S(1)} %shard_map.55), channel_id=1, source_target_pairs={{0,48},{4,52},{8,56},{12,60},{16,32},{20,36},{24,40},{28,44},{32,1... | collective-permute-start | bytes 368648 | tf_op jit(solution)/shard_map/ppermute | solution.py:392
  118.1 6.4 %collective-permute-done.5 = f32[144,128]{1,0:T(8,128)S(1)} collective-permute-done((f32[144,128]{1,0:T(8,128)S(1)}, f32[144,128]{1,0:T(8,128)S(1)}, u32[]{:S(2)}, u32[]{:S(2)}) %collective-permute-start.5) | collective-permute-done | bytes 73760 | tf_op jit(solution)/shard_map/ppermute | solution.py:392
  125.6 4.8 %all-to-all-start.4 = ((f32[4,384,128]{2,1,0:T(8,128)}), f32[4,384,128]{2,1,0:T(8,128)S(1)}, u32[]{:S(2)}, u32[]{:S(2)}) async-start(f32[4,384,128]{2,1,0:T(8,128)} %broadcast_in_dim.11), calls=%async_computation.4 | async-start | bytes 1572864 | tf_op jit(solution)/shard_map/all_to_all | solution.py:369
  134.1 3.9 %shard_map.51.before = f32[704,256]{1,0:T(8,128)S(1)} custom-call(f32[4,288,256]{2,1,0:T(8,128)S(1)} %copy-done, f32[64,1024]{1,0:T(8,128)S(1)} %copy-done.10, f32[1024,256]{1,0:T(8,128)S(1)} %copy-done.2, f32[768,128]{1,0:T(8,128)S(1)} %copy-done.4, f32[128,128]{1,0:T(8,128)S(1)} %get-tuple-element.43.inverse1, f32[4,224,128]{2,1,0:T(8,128)S(1)} %all-to-all-done.2.everyone, ...), custom_call_target="tpu_custom_call" | custom-call | flops 1000000000 | tf_op jit(solution)/shard_map/pallas_call | solution.py:93
  139.4 5.7 %shard_map.56 = (f32[448,128]{1,0:T(8,128)S(1)}, f32[448,128]{1,0:T(8,128)S(1)}, f32[448,128]{1,0:T(8,128)S(1)}) custom-call(f32[4,384,128]{2,1,0:T(8,128)S(1)} %all-to-all-done.4.everyone), custom_call_target="tpu_custom_call" | custom-call | flops 1000000000 | tf_op jit(solution)/shard_map/pallas_call | solution.py:93
  145.1 4.3 %collective-permute-start.7 = (f32[448,128]{1,0:T(8,128)S(1)}, f32[448,128]{1,0:T(8,128)S(1)}, u32[]{:S(2)}, u32[]{:S(2)}) collective-permute-start(f32[448,128]{1,0:T(8,128)S(1)} %get-tuple-element.60.mine), channel_id=1, source_target_pairs={{0,64},{4,68},{8,72},{12,76},{16,80},{20,84},{24,88},{28,92},{32,9... | collective-permute-start | bytes 688136 | tf_op jit(solution)/shard_map/ppermute | solution.py:392
  151.9 3.9 %collective-permute-start.9 = (f32[192,128]{1,0:T(8,128)S(1)}, f32[192,128]{1,0:T(8,128)S(1)}, u32[]{:S(2)}, u32[]{:S(2)}) collective-permute-start(f32[192,128]{1,0:T(8,128)S(1)} %shard_map.62.later), channel_id=1, source_target_pairs={{0,64},{4,68},{8,72},{12,76},{16,80},{20,84},{24,88},{28,92},{32,9... | collective-permute-start | bytes 294920 | tf_op jit(solution)/shard_map/ppermute | solution.py:392
  156.3 5.1 %shard_map.58 = (f32[320,128]{1,0:T(8,128)S(1)}, f32[320,128]{1,0:T(8,128)S(1)}) custom-call(f32[448,128]{1,0:T(8,128)S(1)} %get-tuple-element.60.mine, f32[448,128]{1,0:T(8,128)S(1)} %collective-permute-done.7.arrived), custom_call_target="tpu_custom_call" | custom-call | flops 1000000000 | tf_op jit(solution)/shard_map/pallas_call | solution.py:93
  161.7 6.1 %collective-permute-start.11 = (f32[320,128]{1,0:T(8,128)S(1)}, f32[320,128]{1,0:T(8,128)S(1)}, u32[]{:S(2)}, u32[]{:S(2)}) collective-permute-start(f32[320,128]{1,0:T(8,128)S(1)} %shard_map.61.mine), channel_id=1, source_target_pairs={{0,128},{4,132},{8,136},{12,140},{16,144},{20,148},{24,152},{28,15... | collective-permute-start | bytes 491528 | tf_op jit(solution)/shard_map/ppermute | solution.py:392
  172.3 5.0 %shard_map.64 = (f32[192,128]{1,0:T(8,128)S(1)}, f32[192,128]{1,0:T(8,128)S(1)}) custom-call(f32[320,128]{1,0:T(8,128)S(1)} %shard_map.61.mine, f32[320,128]{1,0:T(8,128)S(1)} %collective-permute-done.11.arrived), custom_call_target="tpu_custom_call" | custom-call | flops 1000000000 | tf_op jit(solution)/shard_map/pallas_call | solution.py:93
  178.8 4.8 %all-to-all-start.5 = ((f32[4,144,256]{2,1,0:T(8,128)}), f32[4,144,256]{2,1,0:T(8,128)S(1)}, u32[]{:S(2)}, u32[]{:S(2)}) async-start(f32[4,144,256]{2,1,0:T(8,128)} %shard_map.66), calls=%async_computation.5 | async-start | bytes 1179648 | tf_op jit(solution)/shard_map/all_to_all | solution.py:497
  183.6 7.7 %collective-permute-start.12 = (f32[144,128]{1,0:T(8,128)S(1)}, f32[144,128]{1,0:T(8,128)S(1)}, u32[]{:S(2)}, u32[]{:S(2)}) collective-permute-start(f32[144,128]{1,0:T(8,128)S(1)} %shard_map.65.mine), channel_id=1, source_target_pairs={{0,384},{4,388},{8,392},{12,396},{16,400},{20,404},{24,408},{28,41... | collective-permute-start | bytes 221192 | tf_op jit(solution)/shard_map/ppermute | solution.py:392
  191.2 2.3 %collective-permute-done.12.arrived = f32[144,128]{1,0:T(8,128)S(1)} collective-permute-done((f32[144,128]{1,0:T(8,128)S(1)}, f32[144,128]{1,0:T(8,128)S(1)}, u32[]{:S(2)}, u32[]{:S(2)}) %collective-permute-start.12) | collective-permute-done | bytes 73760 | tf_op jit(solution)/shard_map/ppermute | solution.py:392
  193.5 5.6 %shard_map.67 = f32[16,1024]{1,0:T(8,128)} custom-call(f32[144,128]{1,0:T(8,128)S(1)} %shard_map.65.mine, f32[144,128]{1,0:T(8,128)S(1)} %collective-permute-done.12.arrived, f32[4,144,256]{2,1,0:T(8,128)S(1)} %all-to-all-done.5.got, bf16[1024,1024]{1,0:T(8,128)(2,1)S(1)} %copy-done.13), custom_call_target="tpu_custom_call" | custom-call | flops 1000000000 | tf_op jit(solution)/shard_map/pallas_call | solution.py:93
  (77 shorter events, 26.6 us)
Async XLA Ops:
  5.7 20.0 %copy-start = (f32[4,288,256]{2,1,0:T(8,128)S(1)}, f32[4,288,256]{2,1,0:T(8,128)}, u32[]{:S(2)}) copy-start(f32[4,288,256]{2,1,0:T(8,128)} %get-tuple-element.39.send) | copy-start | bytes 3538948
  5.7 20.0 %all-to-all-start = ((f32[4,288,256]{2,1,0:T(8,128)}), f32[4,288,256]{2,1,0:T(8,128)S(1)}, u32[]{:S(2)}, u32[]{:S(2)}) async-start(f32[4,288,256]{2,1,0:T(8,128)} %get-tuple-element.39.send), calls=%async_computation | async-start | bytes 2359296 | tf_op jit(solution)/shard_map/all_to_all | solution.py:406
  25.8 1.5 copy-start.1
  29.8 4.2 %copy-start.9 = (f32[64,1024]{1,0:T(8,128)}, f32[64,1024]{1,0:T(8,128)S(1)}, u32[]{:S(2)}) copy-start(f32[64,1024]{1,0:T(8,128)S(1)} %get-tuple-element.40.tree) | copy-start | bytes 786436
  29.8 4.0 %collective-permute-start = (f32[1344,128]{1,0:T(8,128)S(1)}, f32[1344,128]{1,0:T(8,128)S(1)}, u32[]{:S(2)}, u32[]{:S(2)}) collective-permute-start(f32[1344,128]{1,0:T(8,128)S(1)} %get-tuple-element.41.mine), channel_id=1, source_target_pairs={{0,4},{4,0},{8,12},{12,8},{16,20},{20,16},{24,28},{28,24},{32,36},... | collective-permute-start | bytes 2064392 | tf_op jit(solution)/shard_map/ppermute | solution.py:392
  54.1 3.1 %copy-start.3 = (f32[768,128]{1,0:T(8,128)}, f32[768,128]{1,0:T(8,128)S(1)}, u32[]{:S(2)}) copy-start(f32[768,128]{1,0:T(8,128)S(1)} %get-tuple-element.42.far.far1) | copy-start | bytes 1179652
  54.1 6.6 %collective-permute-start.1 = (f32[208,128]{1,0:T(8,128)S(1)}, f32[208,128]{1,0:T(8,128)S(1)}, u32[]{:S(2)}, u32[]{:S(2)}) collective-permute-start(f32[208,128]{1,0:T(8,128)S(1)} %get-tuple-element.44.mine), channel_id=1, source_target_pairs={{0,8},{4,12},{8,0},{12,4},{16,24},{20,28},{24,16},{28,20},{32,40},... | collective-permute-start | bytes 319496 | tf_op jit(solution)/shard_map/ppermute | solution.py:392
  61.5 13.4 %all-to-all-start.2 = ((f32[4,224,128]{2,1,0:T(8,128)}), f32[4,224,128]{2,1,0:T(8,128)S(1)}, u32[]{:S(2)}, u32[]{:S(2)}) async-start(f32[4,224,128]{2,1,0:T(8,128)} %broadcast_in_dim.9), calls=%async_computation.2 | async-start | bytes 917504 | tf_op jit(solution)/shard_map/all_to_all | solution.py:369
  66.4 8.5 %collective-permute-start.2 = (f32[560,128]{1,0:T(8,128)S(1)}, f32[560,128]{1,0:T(8,128)S(1)}, u32[]{:S(2)}, u32[]{:S(2)}) collective-permute-start(f32[560,128]{1,0:T(8,128)S(1)} %shard_map.49.later), channel_id=1, source_target_pairs={{0,8},{4,12},{8,0},{12,4},{16,24},{20,28},{24,16},{28,20},{32,40},... | collective-permute-start | bytes 860168 | tf_op jit(solution)/shard_map/ppermute | solution.py:392
  80.3 5.2 %copy-start.7 = (f32[640,128]{1,0:T(8,128)}, f32[640,128]{1,0:T(8,128)S(1)}, u32[]{:S(2)}) copy-start(f32[640,128]{1,0:T(8,128)S(1)} %get-tuple-element.49.far2.far) | copy-start | bytes 983044
  80.3 5.2 %copy-start.11 = (f32[128,128]{1,0:T(8,128)}, f32[128,128]{1,0:T(8,128)S(1)}, u32[]{:S(2)}) copy-start(f32[128,128]{1,0:T(8,128)S(1)} %get-tuple-element.50.inverse2) | copy-start | bytes 196612
  80.3 7.4 %collective-permute-start.3 = (f32[176,128]{1,0:T(8,128)S(1)}, f32[176,128]{1,0:T(8,128)S(1)}, u32[]{:S(2)}, u32[]{:S(2)}) collective-permute-start(f32[176,128]{1,0:T(8,128)S(1)} %get-tuple-element.51.mine), channel_id=1, source_target_pairs={{0,16},{4,20},{8,24},{12,28},{16,0},{20,4},{24,8},{28,12},{32,48},... | collective-permute-start | bytes 270344 | tf_op jit(solution)/shard_map/ppermute | solution.py:392
  88.5 14.5 %all-to-all-start.3 = ((f32[4,176,128]{2,1,0:T(8,128)}), f32[4,176,128]{2,1,0:T(8,128)S(1)}, u32[]{:S(2)}, u32[]{:S(2)}) async-start(f32[4,176,128]{2,1,0:T(8,128)} %broadcast_in_dim.10), calls=%async_computation.3 | async-start | bytes 720896 | tf_op jit(solution)/shard_map/all_to_all | solution.py:369
  93.3 9.7 %collective-permute-start.4 = (f32[384,128]{1,0:T(8,128)S(1)}, f32[384,128]{1,0:T(8,128)S(1)}, u32[]{:S(2)}, u32[]{:S(2)}) collective-permute-start(f32[384,128]{1,0:T(8,128)S(1)} %shard_map.52.later), channel_id=1, source_target_pairs={{0,16},{4,20},{8,24},{12,28},{16,0},{20,4},{24,8},{28,12},{32,48},... | collective-permute-start | bytes 589832 | tf_op jit(solution)/shard_map/ppermute | solution.py:392
  103.0 5.3 %copy-start.5 = (f32[4,176,128]{2,1,0:T(8,128)}, f32[4,176,128]{2,1,0:T(8,128)S(1)}, u32[]{:S(2)}) copy-start(f32[4,176,128]{2,1,0:T(8,128)S(1)} %all-to-all-done.3.everyone) | copy-start | bytes 1081348
  109.0 21.3 %copy-start.2 = (f32[1024,256]{1,0:T(8,128)S(1)}, f32[1024,256]{1,0:T(8,128)}, u32[]{:S(2)}) copy-start(f32[1024,256]{1,0:T(8,128)} %inverse_cols.1) | copy-start | bytes 3145732
  109.0 15.5 %collective-permute-start.6 = (f32[240,128]{1,0:T(8,128)S(1)}, f32[240,128]{1,0:T(8,128)S(1)}, u32[]{:S(2)}, u32[]{:S(2)}) collective-permute-start(f32[240,128]{1,0:T(8,128)S(1)} %shard_map.55), channel_id=1, source_target_pairs={{0,48},{4,52},{8,56},{12,60},{16,32},{20,36},{24,40},{28,44},{32,1... | collective-permute-start | bytes 368648 | tf_op jit(solution)/shard_map/ppermute | solution.py:392
  116.2 8.4 %collective-permute-start.5 = (f32[144,128]{1,0:T(8,128)S(1)}, f32[144,128]{1,0:T(8,128)S(1)}, u32[]{:S(2)}, u32[]{:S(2)}) collective-permute-start(f32[144,128]{1,0:T(8,128)S(1)} %get-tuple-element.57), channel_id=1, source_target_pairs={{0,48},{4,52},{8,56},{12,60},{16,32},{20,36},{24,40},{28,44},{32,1... | collective-permute-start | bytes 221192 | tf_op jit(solution)/shard_map/ppermute | solution.py:392
  125.6 13.8 %all-to-all-start.4 = ((f32[4,384,128]{2,1,0:T(8,128)}), f32[4,384,128]{2,1,0:T(8,128)S(1)}, u32[]{:S(2)}, u32[]{:S(2)}) async-start(f32[4,384,128]{2,1,0:T(8,128)} %broadcast_in_dim.11), calls=%async_computation.4 | async-start | bytes 1572864 | tf_op jit(solution)/shard_map/all_to_all | solution.py:369
  130.4 1.0 copy-start.4
  131.4 1.0 copy-start.8
  134.1 3.9 %copy-start.6 = (f32[4,176,128]{2,1,0:T(8,128)S(1)}, f32[4,176,128]{2,1,0:T(8,128)}, u32[]{:S(2)}) copy-start(f32[4,176,128]{2,1,0:T(8,128)} %copy-done.5) | copy-start | bytes 1081348
  134.1 3.9 %copy-start.15 = (f32[512,128]{1,0:T(8,128)S(1)}, f32[512,128]{1,0:T(8,128)}, u32[]{:S(2)}) copy-start(f32[512,128]{1,0:T(8,128)} %copy-done.14) | copy-start | bytes 786436
  134.1 3.9 %copy-start.17 = (f32[128,128]{1,0:T(8,128)S(1)}, f32[128,128]{1,0:T(8,128)}, u32[]{:S(2)}) copy-start(f32[128,128]{1,0:T(8,128)} %copy-done.16) | copy-start | bytes 196612
  145.1 11.2 %collective-permute-start.7 = (f32[448,128]{1,0:T(8,128)S(1)}, f32[448,128]{1,0:T(8,128)S(1)}, u32[]{:S(2)}, u32[]{:S(2)}) collective-permute-start(f32[448,128]{1,0:T(8,128)S(1)} %get-tuple-element.60.mine), channel_id=1, source_target_pairs={{0,64},{4,68},{8,72},{12,76},{16,80},{20,84},{24,88},{28,92},{32,9... | collective-permute-start | bytes 688136 | tf_op jit(solution)/shard_map/ppermute | solution.py:392
  149.7 11.7 %collective-permute-start.8 = (f32[320,128]{1,0:T(8,128)S(1)}, f32[320,128]{1,0:T(8,128)S(1)}, u32[]{:S(2)}, u32[]{:S(2)}) collective-permute-start(f32[320,128]{1,0:T(8,128)S(1)} %shard_map.60.later), channel_id=1, source_target_pairs={{0,64},{4,68},{8,72},{12,76},{16,80},{20,84},{24,88},{28,92},{32,9... | collective-permute-start | bytes 491528 | tf_op jit(solution)/shard_map/ppermute | solution.py:392
  151.9 16.0 %collective-permute-start.9 = (f32[192,128]{1,0:T(8,128)S(1)}, f32[192,128]{1,0:T(8,128)S(1)}, u32[]{:S(2)}, u32[]{:S(2)}) collective-permute-start(f32[192,128]{1,0:T(8,128)S(1)} %shard_map.62.later), channel_id=1, source_target_pairs={{0,64},{4,68},{8,72},{12,76},{16,80},{20,84},{24,88},{28,92},{32,9... | collective-permute-start | bytes 294920 | tf_op jit(solution)/shard_map/ppermute | solution.py:392
  161.7 10.6 %collective-permute-start.11 = (f32[320,128]{1,0:T(8,128)S(1)}, f32[320,128]{1,0:T(8,128)S(1)}, u32[]{:S(2)}, u32[]{:S(2)}) collective-permute-start(f32[320,128]{1,0:T(8,128)S(1)} %shard_map.61.mine), channel_id=1, source_target_pairs={{0,128},{4,132},{8,136},{12,140},{16,144},{20,148},{24,152},{28,15... | collective-permute-start | bytes 491528 | tf_op jit(solution)/shard_map/ppermute | solution.py:392
  168.1 9.2 %collective-permute-start.10 = (f32[192,128]{1,0:T(8,128)S(1)}, f32[192,128]{1,0:T(8,128)S(1)}, u32[]{:S(2)}, u32[]{:S(2)}) collective-permute-start(f32[192,128]{1,0:T(8,128)S(1)} %shard_map.63.later), channel_id=1, source_target_pairs={{0,128},{4,132},{8,136},{12,140},{16,144},{20,148},{24,152},{28,15... | collective-permute-start | bytes 294920 | tf_op jit(solution)/shard_map/ppermute | solution.py:392
  177.6 15.9 %copy-start.13 = (bf16[1024,1024]{1,0:T(8,128)(2,1)S(1)}, bf16[1024,1024]{1,0:T(8,128)(2,1)}, u32[]{:S(2)}) copy-start(bf16[1024,1024]{1,0:T(8,128)(2,1)} %get-tuple-element.72.hot) | copy-start | bytes 6291460
  178.8 14.8 %all-to-all-start.5 = ((f32[4,144,256]{2,1,0:T(8,128)}), f32[4,144,256]{2,1,0:T(8,128)S(1)}, u32[]{:S(2)}, u32[]{:S(2)}) async-start(f32[4,144,256]{2,1,0:T(8,128)} %shard_map.66), calls=%async_computation.5 | async-start | bytes 1179648 | tf_op jit(solution)/shard_map/all_to_all | solution.py:497
  183.6 10.0 %collective-permute-start.12 = (f32[144,128]{1,0:T(8,128)S(1)}, f32[144,128]{1,0:T(8,128)S(1)}, u32[]{:S(2)}, u32[]{:S(2)}) collective-permute-start(f32[144,128]{1,0:T(8,128)S(1)} %shard_map.65.mine), channel_id=1, source_target_pairs={{0,384},{4,388},{8,392},{12,396},{16,400},{20,404},{24,408},{28,41... | collective-permute-start | bytes 221192 | tf_op jit(solution)/shard_map/ppermute | solution.py:392
  (4 other events, 3.2 us)

commit v5 on v4

--- a/solution.py
+++ b/solution.py
@@ -56,22 +56,20 @@
     eye = identity(capacity.shape[0])
     bound = jnp.max(jnp.sum(jnp.abs(capacity), axis=1, keepdims=True), axis=0, keepdims=True)
     scale = 2.0 / (1.0 + bound)
-    begin = 2.0 * scale * eye - scale * scale * capacity
-    guess = begin
-    short = capacity.astype(jnp.bfloat16)
+    power = eye - scale * capacity
+    series = eye + power
+    begin = scale * series
     for _ in range(4):
-        guess16 = guess.astype(jnp.bfloat16)
-        factor = 2.0 * eye - short_dot(short, guess16, NN)
-        guess = short_dot(guess16, factor.astype(jnp.bfloat16), NN)
+        power = close_dot(power, power)
+        series = series + close_dot(series, power)
 
     def improve(inverse):
         residual = eye - exact_dot(capacity, inverse, NN)
         size2 = jnp.sum(jnp.sum(residual * residual, axis=1, keepdims=True), axis=0, keepdims=True)
         return inverse + close_dot(inverse, residual), size2
 
-    better, size2 = improve(guess)
+    better, size2 = improve(scale * series)
     better = jnp.where(size2 < 0.25, better, begin)
-    better, size2 = improve(better)
 
     def unfinished(state):
         return (state[1] < 80) & jnp.logical_not(state[2] < 1e-6)
@@ -101,19 +99,24 @@
 
 
 def run_loading(body, outs, *args):
+    parts = [arg.shape[0] if arg.ndim == 3 else 1 for arg in args]
+    first = [sum(parts[:index]) for index in range(len(parts))]
+
     def loading(*refs):
         count = len(args)
         sources, rest = refs[:count], refs[count:]
         results, held, done = rest[: len(outs)], rest[len(outs) : -1], rest[-1]
-        copies = [
-            pltpu.make_async_copy(source, target, done.at[place])
-            for place, (source, target) in enumerate(zip(sources, held))
-        ]
-        for copy in copies:
-            copy.start()
-        for copy in copies:
-            copy.wait()
-        body(*held, *results)
+
+        def copy(index, part):
+            source, target = sources[index], held[index]
+            if parts[index] > 1:
+                source, target = source.at[part], target.at[part]
+            return pltpu.make_async_copy(source, target, done.at[first[index] + part])
+
+        for index in range(count):
+            for part in range(parts[index]):
+                copy(index, part).start()
+        body(lambda index, part=0: copy(index, part).wait(), *held, *results)
 
     return pl.pallas_call(
         loading,
@@ -121,7 +124,7 @@
         in_specs=[pl.BlockSpec(memory_space=pltpu.HBM)] * len(args),
         out_specs=[pl.BlockSpec(memory_space=pltpu.VMEM)] * len(outs),
         scratch_shapes=[pltpu.VMEM(arg.shape, arg.dtype) for arg in args]
-        + [pltpu.SemaphoreType.DMA((len(args),))],
+        + [pltpu.SemaphoreType.DMA((sum(parts),))],
         cost_estimate=pl.CostEstimate(flops=1_000_000_000, bytes_accessed=0, transcendentals=0),
         compiler_params=pltpu.CompilerParams(vmem_limit_bytes=START_BYTES),
     )(*args)
@@ -144,21 +147,27 @@
     return jnp.concatenate([everyone[group, low : low + count, :] for group in range(everyone.shape[0])], 0)
 
 
-def start_body(sides, order, inverse_cols, bases, send, hot):
+def start_body(wait, order, sides, inverse_cols, bases, send, hot):
     levels, rank, leaf = bases.shape
     groups, _, piece = send.shape
     share = rank // groups
     own = sides.shape[0]
+    wait(0)
     hot[...] = one_hot(order[...])
+    wait(1)
     tree = dot_left_parts(sides[...], hot[...], NN)
-    applied = dot_right_parts(bases[...].reshape(levels * rank, leaf), inverse_cols[...], NN)
     for group in range(groups):
-        for level in range(levels):
-            low = level * rank + group * share
-            send[group, level * share : (level + 1) * share, :] = applied[low : low + share]
         for part in range(groups):
             low = levels * share + part * own
             send[group, low : low + own, :] = tree[:, part * piece : (part + 1) * piece]
+    wait(2)
+    high, middle, low_part = three_parts(inverse_cols[...])
+    for level in range(levels):
+        wait(3, level)
+        rows = bases[level]
+        applied = short_dot(rows, low_part, NN) + short_dot(rows, middle, NN) + short_dot(rows, high, NN)
+        for group in range(groups):
+            send[group, level * share : (level + 1) * share, :] = applied[group * share : (group + 1) * share]
 
 
 def gram_body(place, got, send, bases, gram, tree):
@@ -225,14 +234,30 @@
         at += count + own
 
 
-def level_body(above, everyone, mine, arrived, later, later_arrived, panel, far, own_weights, inverse):
+def level_body(above, place, everyone, later, later_arrived, panel, far, own_weights, inverse):
     groups, _, rank = everyone.shape
     share = rank // groups
     far[...] = jnp.concatenate([stacked(everyone, level * share, share) for level in range(1, above + 1)], 0)
     inverse[...] = inverse_of(stacked(everyone, 0, share) + identity(rank))
-    own_weights[...] = exact_dot(mine[share:, :] + arrived[share:, :], inverse[...], NN)
+    own_upper = everyone[place[0], share : share + own_weights.shape[0], :]
+    own_weights[...] = exact_dot(own_upper, inverse[...], NN)
     count = panel.shape[0]
     panel[...] = later[:count, :] + later_arrived[:count, :] - exact_dot(own_weights[...], far[:rank, :], NT)
+
+
+def level_all_body(above, place, everyone, later, later_arrived, panels, far, own_weights, inverse):
+    groups, _, rank = everyone.shape
+    share = rank // groups
+    far[...] = jnp.concatenate([stacked(everyone, level * share, share) for level in range(1, above + 1)], 0)
+    inverse[...] = inverse_of(stacked(everyone, 0, share) + identity(rank))
+    own_upper = everyone[place[0], share : share + own_weights.shape[0], :]
+    own_weights[...] = exact_dot(own_upper, inverse[...], NN)
+    at = 0
+    for column in range(above):
+        count = own_weights.shape[0] - column * share
+        update = exact_dot(own_weights[column * share :, :], far[column * rank : (column + 1) * rank, :], NT)
+        panels[at : at + count, :] = later[at : at + count, :] + later_arrived[at : at + count, :] - update
+        at += count
 
 
 def level_rest_body(later, later_arrived, far, own_weights, rest):
@@ -317,12 +342,16 @@
     return applied[rank:] - exact_dot(exact_dot(far, inverse, NN), gone, NN), sides
 
 
-def carry_first_body(send, tree, inverse_cols, far1, inverse1, everyone, far2, inverse2, carried):
+def base_body(tree, inverse_cols, base):
+    base[...] = exact_dot(tree[...], inverse_cols[...], NN)
+
+
+def carry_first_body(send, base, far1, inverse1, everyone, far2, inverse2, carried):
     groups = everyone.shape[0]
     share = inverse1.shape[0] // groups
-    own = tree.shape[0] // groups
+    own = base.shape[0] // groups
     applied = jnp.concatenate([stacked(send, level * share, share) for level in range(7)], 0)
-    sides = exact_dot(tree[...], inverse_cols[...], NN)
+    sides = base[...]
     applied, sides = carry_step(applied, sides, far1[...], stacked(everyone, 6 * share + own, own), inverse1[...])
     applied, sides = carry_step(applied, sides, far2[...], stacked(everyone, 6 * share, own), inverse2[...])
     carried[...] = jnp.concatenate([applied, sides], 0)
@@ -364,9 +393,22 @@
     out[...] = dot_left_parts(base - exact_dot(top, slope, NN), hot[...], NT)
 
 
-def to_all(block, axis):
-    count = lax.axis_size(axis)
-    return lax.all_to_all(jnp.broadcast_to(block[None], (count,) + block.shape), axis, 0, 0)
+def add_body(*refs):
+    send = refs[-1]
+    mine, arrived, others = refs[0], refs[1], refs[2:-1]
+    count = mine.shape[0]
+    total = mine[...] + arrived[...]
+    for group in range(send.shape[0]):
+        send[group, :count, :] = total
+        for other in others:
+            send[group, count:, :] = other[...]
+
+
+def sum_to_all(mine, arrived, *others):
+    groups = lax.axis_size("rhs")
+    rows = sum(block.shape[0] for block in (mine,) + others)
+    (send,) = run(add_body, [(groups, rows, mine.shape[1])], mine, arrived, *others)
+    return lax.all_to_all(send, "rhs", 0, 0)
 
 
 def route(height):
@@ -398,8 +440,8 @@
             (groups, levels * share + sides, piece),
             jax.ShapeDtypeStruct((leaf, leaf), jnp.bfloat16),
         ],
+        ordering,
         right_sides,
-        ordering,
         leaf_inverse,
         bases,
     )
@@ -428,31 +470,31 @@
     for height in (2, 3):
         above = 7 - height
         later_arrived = swap(later, height)
-        near = panel + arrived
+        arrived, later = lax.optimization_barrier((arrived, later))
+        everyone = sum_to_all(panel, arrived, side1) if height == 2 else sum_to_all(panel, arrived)
         if height == 2:
-            near = jnp.concatenate([near, side1], 0)
-        near, later = lax.optimization_barrier((near, later))
-        everyone = to_all(near, "rhs")
-        next_panel, far, own_weights, inverse = run(
-            functools.partial(level_body, above),
-            [(above * share + own, rank), (above * rank, rank), (above * share + own, rank), square],
-            everyone,
-            panel,
-            arrived,
-            later,
-            later_arrived,
-        )
-        arrived = swap(next_panel, height + 1)
-        rest_rows = above * (above - 1) // 2 * share + (above - 1) * own
-        (later,) = run(level_rest_body, [(rest_rows, rank)], later, later_arrived, far, own_weights)
-        panel = next_panel
+            (base,) = run(base_body, [(sides, piece)], tree, leaf_inverse)
+            everyone, base = lax.optimization_barrier((everyone, base))
+        else:
+            everyone, carried = lax.optimization_barrier((everyone, carried))
         if height == 2:
+            next_panel, far, own_weights, inverse = run(
+                functools.partial(level_body, above),
+                [(above * share + own, rank), (above * rank, rank), (above * share + own, rank), square],
+                everyone,
+                later,
+                later_arrived,
+                place=place,
+            )
+            arrived = swap(next_panel, 3)
+            rest_rows = above * (above - 1) // 2 * share + (above - 1) * own
+            (later,) = run(level_rest_body, [(rest_rows, rank)], later, later_arrived, far, own_weights)
+            panel = next_panel
             (carried,) = run(
                 carry_first_body,
                 [(5 * rank + sides, piece)],
                 send,
-                tree,
-                leaf_inverse,
+                base,
                 far1,
                 inverse1,
                 everyone,
@@ -460,6 +502,20 @@
                 inverse,
             )
         else:
+            panels, far, _, inverse = run(
+                functools.partial(level_all_body, above),
+                [
+                    (above * (above + 1) // 2 * share + above * own, rank),
+                    (above * rank, rank),
+                    (above * share + own, rank),
+                    square,
+                ],
+                everyone,
+                later,
+                later_arrived,
+                place=place,
+            )
+            panels_arrived = swap(panels, 4)
             (carried,) = run(
                 functools.partial(carry_body, above),
                 [(4 * rank + sides, piece)],
@@ -468,9 +524,8 @@
                 far,
                 inverse,
             )
-
-    later_arrived = swap(later, 4)
-    everyone = to_all(jnp.concatenate([panel + arrived, later + later_arrived], 0), "rhs")
+    panels_arrived, carried = lax.optimization_barrier((panels_arrived, carried))
+    everyone = sum_to_all(panels, panels_arrived)
     heights = lambda count: (count * rank + sides, rank)
     fifth, upper, weights = run(spread_body, [heights(3)] * 3, everyone)
     arrived = swap(fifth, 5)

time: 200 us -> 199 us (level)
  blocking collectives: 14.2 us -> 26.8 us
  starting transfers between devices: 75.5 us -> 66.4 us
  waiting for transfers between devices: 44 us -> 37.4 us
  Pallas kernels: 56.6 us -> 61 us
  local copies, waits for them, and re-layouts: 8.11 us -> 5.7 us
    all_to_all x0 -> x1, blocking collectives: none -> 12.6 us  [sum_to_all(): return lax.all_to_all(send, 'rhs', 0, 0)]
    ppermute x13 -> x12, waiting for transfers between devices: 29 us -> 19.8 us  [local(): swap = lambda block, height: lax.ppermute(block, 'leaf', route(height))]
    all_to_all x3 -> x2, starting transfers between devices: 14.5 us -> 9.69 us  [sum_to_all(): return lax.all_to_all(send, 'rhs', 0, 0)]
    ppermute x13 -> x12, starting transfers between devices: 51.3 us -> 46.8 us  [local(): swap = lambda block, height: lax.ppermute(block, 'leaf', route(height))]
    all_to_all x3 -> x2, waiting for transfers between devices: 0.01 us -> 2.55 us  [sum_to_all(): return lax.all_to_all(send, 'rhs', 0, 0)]
    pallas_call x21 -> x24, Pallas kernels: 50.9 us -> 53.4 us  [run(): pl.pallas_call(body, out_shape=[shape_of(out) for out in outs], in_specs=...]
    broadcast_in_dim x3 -> x0, local copies, waits for them, and re-layouts: 2.53 us -> none  [to_all(): jnp.broadcast_to(block[None], (count,) + block.shape)]
    unnamed x36 -> x28, local copies, waits for them, and re-layouts: 5.52 us -> 5.64 us
  transfers between devices with their start and end apart: 18 -> 16, of which waited for: 9 -> 9; matrix products, arithmetic and copies ran while one was open for 0% -> 0% of each run, Pallas kernels for 9% -> 9%
where the time goes in v5:
time: 199 us; the launch traced here: 198 us
  starting transfers between devices  66.4 us (33%)
  Pallas kernels  61 us (31%)
  waiting for transfers between devices  37.4 us (19%)
  blocking collectives  26.8 us (13%)
  local copies, waits for them, and re-layouts  5.7 us (3%)
    pallas_call x24, Pallas kernels, run(): pl.pallas_call(body, out_shape=[shape_of(out) for out in outs], in_specs=...  53.4 us
    ppermute x12, starting transfers between devices, local(): swap = lambda block, height: lax.ppermute(block, 'leaf', route(height))  46.8 us
    ppermute x12, waiting for transfers between devices, local(): swap = lambda block, height: lax.ppermute(block, 'leaf', route(height))  19.8 us
    all_to_all x2, waiting for transfers between devices, local(): got = lax.all_to_all(send, 'rhs', 0, 0)  15 us
    all_to_all x1, blocking collectives, local(): everyone = lax.all_to_all(jnp.concatenate([shared, parts], 1), 'rhs', 0, 0)  14.2 us
    all_to_all x1, blocking collectives, sum_to_all(): return lax.all_to_all(send, 'rhs', 0, 0)  12.6 us
    all_to_all x2, starting transfers between devices, local(): got = lax.all_to_all(send, 'rhs', 0, 0)  9.87 us
    all_to_all x2, starting transfers between devices, sum_to_all(): return lax.all_to_all(send, 'rhs', 0, 0)  9.69 us
  transfers between devices with their start and end apart: 16, of which 9 were waited for; matrix products, arithmetic and copies ran while one was open for 0% of the time, Pallas kernels for 9%

profile of v5, /device:TPU:10, one launch (start us, length us, event | category | flops | bytes accessed | tf_op | source)
XLA Modules:
  0.0 197.9 jit_solution(4830663674176518583)
XLA Ops:
  0.0 7.6 %shard_map.46 = (f32[4,288,256]{2,1,0:T(8,128)}, bf16[1024,1024]{1,0:T(8,128)(2,1)}) custom-call(s32[1,1024]{1,0:T(1,128)} %refs_0_.1, f32[16,1024]{1,0:T(8,128)} %refs_1_.1, f32[1024,256]{1,0:T(8,128)} %inverse_cols.1, bf16[7,128,1024]{2,1,0:T(8,128)(2,1)} %bases.1), custom_call_target="tpu_custom_call" | custom-call | flops 1000000000 | tf_op jit(solution)/shard_map/pallas_call | solution.py:121
  7.6 5.0 %all-to-all-start = ((f32[4,288,256]{2,1,0:T(8,128)}), f32[4,288,256]{2,1,0:T(8,128)S(1)}, u32[]{:S(2)}, u32[]{:S(2)}) async-start(f32[4,288,256]{2,1,0:T(8,128)} %get-tuple-element.44.send), calls=%async_computation | async-start | bytes 2359296 | tf_op jit(solution)/shard_map/all_to_all | solution.py:448
  12.6 15.0 %all-to-all-done.got = f32[4,288,256]{2,1,0:T(8,128)S(1)} async-done(((f32[4,288,256]{2,1,0:T(8,128)}), f32[4,288,256]{2,1,0:T(8,128)S(1)}, u32[]{:S(2)}, u32[]{:S(2)}) %all-to-all-start) | async-done | bytes 1179680 | tf_op jit(solution)/shard_map/all_to_all | solution.py:448
  29.1 2.6 %shard_map.47 = (f32[1344,128]{1,0:T(8,128)S(1)}, f32[64,1024]{1,0:T(8,128)S(1)}) custom-call(s32[1]{0:T(128)} %bitcast.place, f32[4,288,256]{2,1,0:T(8,128)S(1)} %all-to-all-done.got, f32[4,288,256]{2,1,0:T(8,128)S(1)} %copy-done, bf16[7,128,1024]{2,1,0:T(8,128)(2,1)S(1)} %copy-done.1), custom_call_target="tpu_custom_call" | custom-call | flops 1000000000 | tf_op jit(solution)/shard_map/pallas_call | solution.py:91
  35.9 14.2 %all_to_all.30.everyone = f32[4,336,128]{2,1,0:T(8,128)S(1)} all-to-all(f32[4,336,128]{2,1,0:T(8,128)S(1)} %pad_maximum_fusion), channel_id=1, replica_groups=mesh['leaf'=128,'rhs'=4] {'rhs'}, dimensions={0} | all-to-all | bytes 1376256 | tf_op jit(solution)/shard_map/all_to_all | solution.py:457
  50.1 5.6 %shard_map.48 = (f32[208,128]{1,0:T(8,128)S(1)}, f32[768,128]{1,0:T(8,128)S(1)}, f32[208,128]{1,0:T(8,128)S(1)}, f32[128,128]{1,0:T(8,128)S(1)}, f32[16,128]{1,0:T(8,128)S(1)}) custom-call(f32[4,336,128]{2,1,0:T(8,128)S(1)} %all_to_all.30.everyone, f32[1344,128]{1,0:T(8,128)S(1)} %get-tuple-element.45.mine, f32[1344,128]{1,0:T(8,128)S(1)} %collective-permute-done.arrived), custom_call_target="tpu_custom_call" | custom-call | flops 1000000000 | tf_op jit(solution)/shard_map/pallas_call | solution.py:91
  55.8 2.4 %collective-permute-start.1 = (f32[208,128]{1,0:T(8,128)S(1)}, f32[208,128]{1,0:T(8,128)S(1)}, u32[]{:S(2)}, u32[]{:S(2)}) collective-permute-start(f32[208,128]{1,0:T(8,128)S(1)} %get-tuple-element.46.refs_0_), channel_id=1, source_target_pairs={{0,8},{4,12},{8,0},{12,4},{16,24},{20,28},{24,16},{28,20},{32,40},... | collective-permute-start | bytes 319496 | tf_op jit(solution)/shard_map/ppermute | solution.py:434
  58.9 3.5 %collective-permute-done.1.refs_1_ = f32[208,128]{1,0:T(8,128)S(1)} collective-permute-done((f32[208,128]{1,0:T(8,128)S(1)}, f32[208,128]{1,0:T(8,128)S(1)}, u32[]{:S(2)}, u32[]{:S(2)}) %collective-permute-start.1) | collective-permute-done | bytes 106528 | tf_op jit(solution)/shard_map/ppermute | solution.py:434
  63.2 4.9 %all-to-all-start.2 = ((f32[4,224,128]{2,1,0:T(8,128)}), f32[4,224,128]{2,1,0:T(8,128)S(1)}, u32[]{:S(2)}, u32[]{:S(2)}) async-start(f32[4,224,128]{2,1,0:T(8,128)} %shard_map.50), calls=%async_computation.2 | async-start | bytes 917504 | tf_op jit(solution)/shard_map/all_to_all | solution.py:411
  68.1 2.4 %collective-permute-start.2 = (f32[560,128]{1,0:T(8,128)S(1)}, f32[560,128]{1,0:T(8,128)S(1)}, u32[]{:S(2)}, u32[]{:S(2)}) collective-permute-start(f32[560,128]{1,0:T(8,128)S(1)} %shard_map.49.later), channel_id=1, source_target_pairs={{0,8},{4,12},{8,0},{12,4},{16,24},{20,28},{24,16},{28,20},{32,40},... | collective-permute-start | bytes 860168 | tf_op jit(solution)/shard_map/ppermute | solution.py:434
  71.8 2.5 %all-to-all-done.2.everyone = f32[4,224,128]{2,1,0:T(8,128)S(1)} async-done(((f32[4,224,128]{2,1,0:T(8,128)}), f32[4,224,128]{2,1,0:T(8,128)S(1)}, u32[]{:S(2)}, u32[]{:S(2)}) %all-to-all-start.2) | async-done | bytes 458784 | tf_op jit(solution)/shard_map/all_to_all | solution.py:411
  74.4 2.2 %collective-permute-done.2.later_arrived = f32[560,128]{1,0:T(8,128)S(1)} collective-permute-done((f32[560,128]{1,0:T(8,128)S(1)}, f32[560,128]{1,0:T(8,128)S(1)}, u32[]{:S(2)}, u32[]{:S(2)}) %collective-permute-start.2) | collective-permute-done | bytes 286752 | tf_op jit(solution)/shard_map/ppermute | solution.py:434
  76.6 5.2 %shard_map.52 = (f32[176,128]{1,0:T(8,128)S(1)}, f32[640,128]{1,0:T(8,128)S(1)}, f32[176,128]{1,0:T(8,128)S(1)}, f32[128,128]{1,0:T(8,128)S(1)}) custom-call(s32[1]{0:T(128)} %bitcast.place, f32[4,224,128]{2,1,0:T(8,128)S(1)} %all-to-all-done.2.everyone, f32[560,128]{1,0:T(8,128)S(1)} %shard_map.49.later, f32[560,128]{1,0:T(8,128)S(1)} %collective-permute-done.2.later_arrived), custom_call_target="tpu_custom_call" | custom-call | flops 1000000000 | tf_op jit(solution)/shard_map/pallas_call | solution.py:91
  81.8 4.9 %collective-permute-start.3 = (f32[176,128]{1,0:T(8,128)S(1)}, f32[176,128]{1,0:T(8,128)S(1)}, u32[]{:S(2)}, u32[]{:S(2)}) collective-permute-start(f32[176,128]{1,0:T(8,128)S(1)} %get-tuple-element.54.refs_0_), channel_id=1, source_target_pairs={{0,16},{4,20},{8,24},{12,28},{16,0},{20,4},{24,8},{28,12},{32,48},... | collective-permute-start | bytes 270344 | tf_op jit(solution)/shard_map/ppermute | solution.py:434
  87.4 2.2 %collective-permute-done.3.refs_1_ = f32[176,128]{1,0:T(8,128)S(1)} collective-permute-done((f32[176,128]{1,0:T(8,128)S(1)}, f32[176,128]{1,0:T(8,128)S(1)}, u32[]{:S(2)}, u32[]{:S(2)}) %collective-permute-start.3) | collective-permute-done | bytes 90144 | tf_op jit(solution)/shard_map/ppermute | solution.py:434
  90.4 4.8 %all-to-all-start.3 = ((f32[4,176,128]{2,1,0:T(8,128)}), f32[4,176,128]{2,1,0:T(8,128)S(1)}, u32[]{:S(2)}, u32[]{:S(2)}) async-start(f32[4,176,128]{2,1,0:T(8,128)} %shard_map.54), calls=%async_computation.3 | async-start | bytes 720896 | tf_op jit(solution)/shard_map/all_to_all | solution.py:411
  95.2 5.5 %collective-permute-start.4 = (f32[384,128]{1,0:T(8,128)S(1)}, f32[384,128]{1,0:T(8,128)S(1)}, u32[]{:S(2)}, u32[]{:S(2)}) collective-permute-start(f32[384,128]{1,0:T(8,128)S(1)} %shard_map.53.later), channel_id=1, source_target_pairs={{0,16},{4,20},{8,24},{12,28},{16,0},{20,4},{24,8},{28,12},{32,48},... | collective-permute-start | bytes 589832 | tf_op jit(solution)/shard_map/ppermute | solution.py:434
  104.1 3.3 %shard_map.55.before = f32[704,256]{1,0:T(8,128)S(1)} custom-call(f32[4,288,256]{2,1,0:T(8,128)S(1)} %copy-done, f32[64,256]{1,0:T(8,128)S(1)} %copy-done.11, f32[768,128]{1,0:T(8,128)S(1)} %copy-done.5, f32[128,128]{1,0:T(8,128)S(1)} %copy-done.9, f32[4,224,128]{2,1,0:T(8,128)S(1)} %all-to-all-done.2.everyone, f32[640,128]{1,0:T(8,128)S(1)} %copy-done.7, ...), custom_call_target="tpu_custom_call" | custom-call | flops 1000000000 | tf_op jit(solution)/shard_map/pallas_call | solution.py:91
  107.4 5.5 %shard_map.56 = (f32[384,128]{1,0:T(8,128)S(1)}, f32[512,128]{1,0:T(8,128)S(1)}, f32[144,128]{1,0:T(8,128)}, f32[128,128]{1,0:T(8,128)S(1)}) custom-call(s32[1]{0:T(128)} %bitcast.place, f32[4,176,128]{2,1,0:T(8,128)S(1)} %all-to-all-done.3.everyone, f32[384,128]{1,0:T(8,128)S(1)} %shard_map.53.later, f32[384,128]{1,0:T(8,128)S(1)} %collective-permute-done.4.later_arrived), custom_call_target="tpu_custom_call" | custom-call | flops 1000000000 | tf_op jit(solution)/shard_map/pallas_call | solution.py:91
  112.9 4.1 %collective-permute-start.5 = (f32[384,128]{1,0:T(8,128)S(1)}, f32[384,128]{1,0:T(8,128)S(1)}, u32[]{:S(2)}, u32[]{:S(2)}) collective-permute-start(f32[384,128]{1,0:T(8,128)S(1)} %get-tuple-element.63.refs_0_), channel_id=1, source_target_pairs={{0,48},{4,52},{8,56},{12,60},{16,32},{20,36},{24,40},{28,44},{32,1... | collective-permute-start | bytes 589832 | tf_op jit(solution)/shard_map/ppermute | solution.py:434
  118.3 5.6 %collective-permute-done.5.refs_1_ = f32[384,128]{1,0:T(8,128)S(1)} collective-permute-done((f32[384,128]{1,0:T(8,128)S(1)}, f32[384,128]{1,0:T(8,128)S(1)}, u32[]{:S(2)}, u32[]{:S(2)}) %collective-permute-start.5) | collective-permute-done | bytes 196640 | tf_op jit(solution)/shard_map/ppermute | solution.py:434
  124.0 12.6 %all_to_all.31.everyone = f32[4,384,128]{2,1,0:T(8,128)S(1)} all-to-all(f32[4,384,128]{2,1,0:T(8,128)S(1)} %shard_map.58), channel_id=1, replica_groups=mesh['leaf'=128,'rhs'=4] {'rhs'}, dimensions={0} | all-to-all | bytes 1572864 | tf_op jit(solution)/shard_map/all_to_all | solution.py:411
  136.7 5.5 %shard_map.59 = (f32[448,128]{1,0:T(8,128)S(1)}, f32[448,128]{1,0:T(8,128)S(1)}, f32[448,128]{1,0:T(8,128)S(1)}) custom-call(f32[4,384,128]{2,1,0:T(8,128)S(1)} %all_to_all.31.everyone), custom_call_target="tpu_custom_call" | custom-call | flops 1000000000 | tf_op jit(solution)/shard_map/pallas_call | solution.py:91
  142.2 4.3 %collective-permute-start.6 = (f32[448,128]{1,0:T(8,128)S(1)}, f32[448,128]{1,0:T(8,128)S(1)}, u32[]{:S(2)}, u32[]{:S(2)}) collective-permute-start(f32[448,128]{1,0:T(8,128)S(1)} %get-tuple-element.70.mine), channel_id=1, source_target_pairs={{0,64},{4,68},{8,72},{12,76},{16,80},{20,84},{24,88},{28,92},{32,9... | collective-permute-start | bytes 688136 | tf_op jit(solution)/shard_map/ppermute | solution.py:434
  149.0 3.9 %collective-permute-start.8 = (f32[192,128]{1,0:T(8,128)S(1)}, f32[192,128]{1,0:T(8,128)S(1)}, u32[]{:S(2)}, u32[]{:S(2)}) collective-permute-start(f32[192,128]{1,0:T(8,128)S(1)} %shard_map.65.later), channel_id=1, source_target_pairs={{0,64},{4,68},{8,72},{12,76},{16,80},{20,84},{24,88},{28,92},{32,9... | collective-permute-start | bytes 294920 | tf_op jit(solution)/shard_map/ppermute | solution.py:434
  153.5 4.9 %shard_map.61 = (f32[320,128]{1,0:T(8,128)S(1)}, f32[320,128]{1,0:T(8,128)S(1)}) custom-call(f32[448,128]{1,0:T(8,128)S(1)} %get-tuple-element.70.mine, f32[448,128]{1,0:T(8,128)S(1)} %collective-permute-done.6.arrived), custom_call_target="tpu_custom_call" | custom-call | flops 1000000000 | tf_op jit(solution)/shard_map/pallas_call | solution.py:91
  158.7 6.1 %collective-permute-start.10 = (f32[320,128]{1,0:T(8,128)S(1)}, f32[320,128]{1,0:T(8,128)S(1)}, u32[]{:S(2)}, u32[]{:S(2)}) collective-permute-start(f32[320,128]{1,0:T(8,128)S(1)} %shard_map.64.mine), channel_id=1, source_target_pairs={{0,128},{4,132},{8,136},{12,140},{16,144},{20,148},{24,152},{28,15... | collective-permute-start | bytes 491528 | tf_op jit(solution)/shard_map/ppermute | solution.py:434
  169.3 4.9 %shard_map.67 = (f32[192,128]{1,0:T(8,128)S(1)}, f32[192,128]{1,0:T(8,128)S(1)}) custom-call(f32[320,128]{1,0:T(8,128)S(1)} %shard_map.64.mine, f32[320,128]{1,0:T(8,128)S(1)} %collective-permute-done.10.arrived), custom_call_target="tpu_custom_call" | custom-call | flops 1000000000 | tf_op jit(solution)/shard_map/pallas_call | solution.py:91
  175.6 4.9 %all-to-all-start.5 = ((f32[4,144,256]{2,1,0:T(8,128)}), f32[4,144,256]{2,1,0:T(8,128)S(1)}, u32[]{:S(2)}, u32[]{:S(2)}) async-start(f32[4,144,256]{2,1,0:T(8,128)} %shard_map.69), calls=%async_computation.5 | async-start | bytes 1179648 | tf_op jit(solution)/shard_map/all_to_all | solution.py:552
  180.5 7.7 %collective-permute-start.11 = (f32[144,128]{1,0:T(8,128)S(1)}, f32[144,128]{1,0:T(8,128)S(1)}, u32[]{:S(2)}, u32[]{:S(2)}) collective-permute-start(f32[144,128]{1,0:T(8,128)S(1)} %shard_map.68.mine), channel_id=1, source_target_pairs={{0,384},{4,388},{8,392},{12,396},{16,400},{20,404},{24,408},{28,41... | collective-permute-start | bytes 221192 | tf_op jit(solution)/shard_map/ppermute | solution.py:434
  188.1 2.3 %collective-permute-done.11.arrived = f32[144,128]{1,0:T(8,128)S(1)} collective-permute-done((f32[144,128]{1,0:T(8,128)S(1)}, f32[144,128]{1,0:T(8,128)S(1)}, u32[]{:S(2)}, u32[]{:S(2)}) %collective-permute-start.11) | collective-permute-done | bytes 73760 | tf_op jit(solution)/shard_map/ppermute | solution.py:434
  190.5 7.4 %shard_map.70 = f32[16,1024]{1,0:T(8,128)} custom-call(f32[144,128]{1,0:T(8,128)S(1)} %shard_map.68.mine, f32[144,128]{1,0:T(8,128)S(1)} %collective-permute-done.11.arrived, f32[4,144,256]{2,1,0:T(8,128)S(1)} %all-to-all-done.5.got, bf16[1024,1024]{1,0:T(8,128)(2,1)S(1)} %copy-done.3), custom_call_target="tpu_custom_call" | custom-call | flops 1000000000 | tf_op jit(solution)/shard_map/pallas_call | solution.py:91
  (60 shorter events, 24.1 us)
Async XLA Ops:
  7.6 20.0 %copy-start = (f32[4,288,256]{2,1,0:T(8,128)S(1)}, f32[4,288,256]{2,1,0:T(8,128)}, u32[]{:S(2)}) copy-start(f32[4,288,256]{2,1,0:T(8,128)} %get-tuple-element.44.send) | copy-start | bytes 3538948
  7.6 20.0 %all-to-all-start = ((f32[4,288,256]{2,1,0:T(8,128)}), f32[4,288,256]{2,1,0:T(8,128)S(1)}, u32[]{:S(2)}, u32[]{:S(2)}) async-start(f32[4,288,256]{2,1,0:T(8,128)} %get-tuple-element.44.send), calls=%async_computation | async-start | bytes 2359296 | tf_op jit(solution)/shard_map/all_to_all | solution.py:448
  27.6 1.5 copy-start.1
  31.7 4.0 %collective-permute-start = (f32[1344,128]{1,0:T(8,128)S(1)}, f32[1344,128]{1,0:T(8,128)S(1)}, u32[]{:S(2)}, u32[]{:S(2)}) collective-permute-start(f32[1344,128]{1,0:T(8,128)S(1)} %get-tuple-element.45.mine), channel_id=1, source_target_pairs={{0,4},{4,0},{8,12},{12,8},{16,20},{20,16},{24,28},{28,24},{32,36},... | collective-permute-start | bytes 2064392 | tf_op jit(solution)/shard_map/ppermute | solution.py:434
  55.8 3.1 %copy-start.4 = (f32[768,128]{1,0:T(8,128)}, f32[768,128]{1,0:T(8,128)S(1)}, u32[]{:S(2)}) copy-start(f32[768,128]{1,0:T(8,128)S(1)} %get-tuple-element.47.far.far1) | copy-start | bytes 1179652
  55.8 3.1 %copy-start.8 = (f32[128,128]{1,0:T(8,128)}, f32[128,128]{1,0:T(8,128)S(1)}, u32[]{:S(2)}) copy-start(f32[128,128]{1,0:T(8,128)S(1)} %get-tuple-element.59.inverse1) | copy-start | bytes 196612
  55.8 6.6 %collective-permute-start.1 = (f32[208,128]{1,0:T(8,128)S(1)}, f32[208,128]{1,0:T(8,128)S(1)}, u32[]{:S(2)}, u32[]{:S(2)}) collective-permute-start(f32[208,128]{1,0:T(8,128)S(1)} %get-tuple-element.46.refs_0_), channel_id=1, source_target_pairs={{0,8},{4,12},{8,0},{12,4},{16,24},{20,28},{24,16},{28,20},{32,40},... | collective-permute-start | bytes 319496 | tf_op jit(solution)/shard_map/ppermute | solution.py:434
  62.4 8.1 %copy-start.2 = (f32[1024,256]{1,0:T(8,128)S(1)}, f32[1024,256]{1,0:T(8,128)}, u32[]{:S(2)}) copy-start(f32[1024,256]{1,0:T(8,128)} %inverse_cols.1) | copy-start | bytes 3145732
  63.2 11.2 %all-to-all-start.2 = ((f32[4,224,128]{2,1,0:T(8,128)}), f32[4,224,128]{2,1,0:T(8,128)S(1)}, u32[]{:S(2)}, u32[]{:S(2)}) async-start(f32[4,224,128]{2,1,0:T(8,128)} %shard_map.50), calls=%async_computation.2 | async-start | bytes 917504 | tf_op jit(solution)/shard_map/all_to_all | solution.py:411
  68.1 8.5 %collective-permute-start.2 = (f32[560,128]{1,0:T(8,128)S(1)}, f32[560,128]{1,0:T(8,128)S(1)}, u32[]{:S(2)}, u32[]{:S(2)}) collective-permute-start(f32[560,128]{1,0:T(8,128)S(1)} %shard_map.49.later), channel_id=1, source_target_pairs={{0,8},{4,12},{8,0},{12,4},{16,24},{20,28},{24,16},{28,20},{32,40},... | collective-permute-start | bytes 860168 | tf_op jit(solution)/shard_map/ppermute | solution.py:434
  71.2 0.6 copy-start.10
  81.8 5.6 %copy-start.6 = (f32[640,128]{1,0:T(8,128)}, f32[640,128]{1,0:T(8,128)S(1)}, u32[]{:S(2)}) copy-start(f32[640,128]{1,0:T(8,128)S(1)} %get-tuple-element.55.far.far2) | copy-start | bytes 983044
  81.8 5.6 %copy-start.12 = (f32[128,128]{1,0:T(8,128)}, f32[128,128]{1,0:T(8,128)S(1)}, u32[]{:S(2)}) copy-start(f32[128,128]{1,0:T(8,128)S(1)} %get-tuple-element.60.inverse2) | copy-start | bytes 196612
  81.8 7.8 %collective-permute-start.3 = (f32[176,128]{1,0:T(8,128)S(1)}, f32[176,128]{1,0:T(8,128)S(1)}, u32[]{:S(2)}, u32[]{:S(2)}) collective-permute-start(f32[176,128]{1,0:T(8,128)S(1)} %get-tuple-element.54.refs_0_), channel_id=1, source_target_pairs={{0,16},{4,20},{8,24},{12,28},{16,0},{20,4},{24,8},{28,12},{32,48},... | collective-permute-start | bytes 270344 | tf_op jit(solution)/shard_map/ppermute | solution.py:434
  87.4 13.3 %copy-start.5 = (f32[768,128]{1,0:T(8,128)S(1)}, f32[768,128]{1,0:T(8,128)}, u32[]{:S(2)}) copy-start(f32[768,128]{1,0:T(8,128)} %copy-done.4) | copy-start | bytes 1179652
  90.4 17.0 %all-to-all-start.3 = ((f32[4,176,128]{2,1,0:T(8,128)}), f32[4,176,128]{2,1,0:T(8,128)S(1)}, u32[]{:S(2)}, u32[]{:S(2)}) async-start(f32[4,176,128]{2,1,0:T(8,128)} %shard_map.54), calls=%async_computation.3 | async-start | bytes 720896 | tf_op jit(solution)/shard_map/all_to_all | solution.py:411
  95.2 12.3 %collective-permute-start.4 = (f32[384,128]{1,0:T(8,128)S(1)}, f32[384,128]{1,0:T(8,128)S(1)}, u32[]{:S(2)}, u32[]{:S(2)}) collective-permute-start(f32[384,128]{1,0:T(8,128)S(1)} %shard_map.53.later), channel_id=1, source_target_pairs={{0,16},{4,20},{8,24},{12,28},{16,0},{20,4},{24,8},{28,12},{32,48},... | collective-permute-start | bytes 589832 | tf_op jit(solution)/shard_map/ppermute | solution.py:434
  100.6 1.0 copy-start.7
  101.6 0.8 copy-start.9
  102.4 0.8 copy-start.11
  103.3 0.8 copy-start.13
  112.9 11.0 %collective-permute-start.5 = (f32[384,128]{1,0:T(8,128)S(1)}, f32[384,128]{1,0:T(8,128)S(1)}, u32[]{:S(2)}, u32[]{:S(2)}) collective-permute-start(f32[384,128]{1,0:T(8,128)S(1)} %get-tuple-element.63.refs_0_), channel_id=1, source_target_pairs={{0,48},{4,52},{8,56},{12,60},{16,32},{20,36},{24,40},{28,44},{32,1... | collective-permute-start | bytes 589832 | tf_op jit(solution)/shard_map/ppermute | solution.py:434
  142.2 11.3 %collective-permute-start.6 = (f32[448,128]{1,0:T(8,128)S(1)}, f32[448,128]{1,0:T(8,128)S(1)}, u32[]{:S(2)}, u32[]{:S(2)}) collective-permute-start(f32[448,128]{1,0:T(8,128)S(1)} %get-tuple-element.70.mine), channel_id=1, source_target_pairs={{0,64},{4,68},{8,72},{12,76},{16,80},{20,84},{24,88},{28,92},{32,9... | collective-permute-start | bytes 688136 | tf_op jit(solution)/shard_map/ppermute | solution.py:434
  146.8 11.6 %collective-permute-start.7 = (f32[320,128]{1,0:T(8,128)S(1)}, f32[320,128]{1,0:T(8,128)S(1)}, u32[]{:S(2)}, u32[]{:S(2)}) collective-permute-start(f32[320,128]{1,0:T(8,128)S(1)} %shard_map.63.later), channel_id=1, source_target_pairs={{0,64},{4,68},{8,72},{12,76},{16,80},{20,84},{24,88},{28,92},{32,9... | collective-permute-start | bytes 491528 | tf_op jit(solution)/shard_map/ppermute | solution.py:434
  149.0 15.8 %collective-permute-start.8 = (f32[192,128]{1,0:T(8,128)S(1)}, f32[192,128]{1,0:T(8,128)S(1)}, u32[]{:S(2)}, u32[]{:S(2)}) collective-permute-start(f32[192,128]{1,0:T(8,128)S(1)} %shard_map.65.later), channel_id=1, source_target_pairs={{0,64},{4,68},{8,72},{12,76},{16,80},{20,84},{24,88},{28,92},{32,9... | collective-permute-start | bytes 294920 | tf_op jit(solution)/shard_map/ppermute | solution.py:434
  158.7 10.6 %collective-permute-start.10 = (f32[320,128]{1,0:T(8,128)S(1)}, f32[320,128]{1,0:T(8,128)S(1)}, u32[]{:S(2)}, u32[]{:S(2)}) collective-permute-start(f32[320,128]{1,0:T(8,128)S(1)} %shard_map.64.mine), channel_id=1, source_target_pairs={{0,128},{4,132},{8,136},{12,140},{16,144},{20,148},{24,152},{28,15... | collective-permute-start | bytes 491528 | tf_op jit(solution)/shard_map/ppermute | solution.py:434
  165.1 9.1 %collective-permute-start.9 = (f32[192,128]{1,0:T(8,128)S(1)}, f32[192,128]{1,0:T(8,128)S(1)}, u32[]{:S(2)}, u32[]{:S(2)}) collective-permute-start(f32[192,128]{1,0:T(8,128)S(1)} %shard_map.66.later), channel_id=1, source_target_pairs={{0,128},{4,132},{8,136},{12,140},{16,144},{20,148},{24,152},{28,15... | collective-permute-start | bytes 294920 | tf_op jit(solution)/shard_map/ppermute | solution.py:434
  174.4 16.0 %copy-start.3 = (bf16[1024,1024]{1,0:T(8,128)(2,1)S(1)}, bf16[1024,1024]{1,0:T(8,128)(2,1)}, u32[]{:S(2)}) copy-start(bf16[1024,1024]{1,0:T(8,128)(2,1)} %get-tuple-element.82.hot) | copy-start | bytes 6291460
  175.6 14.9 %all-to-all-start.5 = ((f32[4,144,256]{2,1,0:T(8,128)}), f32[4,144,256]{2,1,0:T(8,128)S(1)}, u32[]{:S(2)}, u32[]{:S(2)}) async-start(f32[4,144,256]{2,1,0:T(8,128)} %shard_map.69), calls=%async_computation.5 | async-start | bytes 1179648 | tf_op jit(solution)/shard_map/all_to_all | solution.py:552
  180.5 10.0 %collective-permute-start.11 = (f32[144,128]{1,0:T(8,128)S(1)}, f32[144,128]{1,0:T(8,128)S(1)}, u32[]{:S(2)}, u32[]{:S(2)}) collective-permute-start(f32[144,128]{1,0:T(8,128)S(1)} %shard_map.68.mine), channel_id=1, source_target_pairs={{0,384},{4,388},{8,392},{12,396},{16,400},{20,404},{24,408},{28,41... | collective-permute-start | bytes 221192 | tf_op jit(solution)/shard_map/ppermute | solution.py:434

commit v6 on v5

--- a/solution.py
+++ b/solution.py
@@ -98,12 +98,15 @@
     )(*scalars, *args)
 
 
-def run_loading(body, outs, *args):
+def run_loading(body, outs, *args, place=None):
     parts = [arg.shape[0] if arg.ndim == 3 else 1 for arg in args]
     first = [sum(parts[:index]) for index in range(len(parts))]
 
+    scalars = [] if place is None else [place]
+
     def loading(*refs):
         count = len(args)
+        given, refs = refs[: len(scalars)], refs[len(scalars) :]
         sources, rest = refs[:count], refs[count:]
         results, held, done = rest[: len(outs)], rest[len(outs) : -1], rest[-1]
 
@@ -116,18 +119,19 @@
         for index in range(count):
             for part in range(parts[index]):
                 copy(index, part).start()
-        body(lambda index, part=0: copy(index, part).wait(), *held, *results)
+        body(lambda index, part=0: copy(index, part).wait(), *given, *held, *results)
 
     return pl.pallas_call(
         loading,
         out_shape=[shape_of(out) for out in outs],
-        in_specs=[pl.BlockSpec(memory_space=pltpu.HBM)] * len(args),
+        in_specs=[pl.BlockSpec(memory_space=pltpu.SMEM)] * len(scalars)
+        + [pl.BlockSpec(memory_space=pltpu.HBM)] * len(args),
         out_specs=[pl.BlockSpec(memory_space=pltpu.VMEM)] * len(outs),
         scratch_shapes=[pltpu.VMEM(arg.shape, arg.dtype) for arg in args]
         + [pltpu.SemaphoreType.DMA((sum(parts),))],
         cost_estimate=pl.CostEstimate(flops=1_000_000_000, bytes_accessed=0, transcendentals=0),
         compiler_params=pltpu.CompilerParams(vmem_limit_bytes=START_BYTES),
-    )(*args)
+    )(*scalars, *args)
 
 
 def one_hot(order):
@@ -164,25 +168,35 @@
     high, middle, low_part = three_parts(inverse_cols[...])
     for level in range(levels):
         wait(3, level)
-        rows = bases[level]
-        applied = short_dot(rows, low_part, NN) + short_dot(rows, middle, NN) + short_dot(rows, high, NN)
-        for group in range(groups):
-            send[group, level * share : (level + 1) * share, :] = applied[group * share : (group + 1) * share]
-
-
-def gram_body(place, got, send, bases, gram, tree):
+    rows = bases[...].reshape(levels * rank, leaf)
+    applied = short_dot(rows, low_part, NN) + short_dot(rows, middle, NN) + short_dot(rows, high, NN)
+    for group in range(groups):
+        for level in range(levels):
+            low = level * rank + group * share
+            send[group, level * share : (level + 1) * share, :] = applied[low : low + share]
+
+
+def gram_body(wait, place, got, bases, send, gram, tree):
     levels, rank, leaf = bases.shape
     groups, rows, piece = got.shape
     share = rank // groups
     v_rows = levels * share
     own = (rows - v_rows) // groups
-    applied = jnp.concatenate([got[group, :v_rows, :] for group in range(groups)], 1)
-    product = dot_left_parts(applied, bases[...].reshape(levels * rank, leaf), NT)
+    for group in range(groups):
+        wait(0, group)
+    applied = three_parts(jnp.concatenate([got[group, :v_rows, :] for group in range(groups)], 1))
     at = 0
     for column in range(levels):
         count = (levels - column) * share
-        gram[at : at + count, :] = product[column * share :, column * rank : (column + 1) * rank]
+        wait(1, column)
+        high, middle, low = [part[column * share :] for part in applied]
+        right = bases[column]
+        gram[at : at + count, :] = (
+            short_dot(low, right, NT) + short_dot(middle, right, NT) + short_dot(high, right, NT)
+        )
         at += count
+    for group in range(groups):
+        wait(2, group)
     mine = pl.ds(pl.multiple_of(v_rows + place[0] * own, own), own)
     sides = jnp.concatenate([got[group, mine, :] for group in range(groups)], 0)
     for level in range(levels):
@@ -196,31 +210,32 @@
         )
 
 
-def first_body(everyone, mine, arrived, panel, weights, own_weights, inverse, side_upper):
-    groups, _, rank = everyone.shape
-    share = rank // groups
-    own = side_upper.shape[0]
+def first_body(everyone, mine, arrived, panel, weights, own_weights, inverse, side_weights):
+    groups, _, rank = everyone.shape
+    share = rank // groups
+    own = side_weights.shape[0]
     far = jnp.concatenate([stacked(everyone, level * share, share) for level in range(1, 7)], 0)
     inverse[...] = inverse_of(stacked(everyone, 0, share) + identity(rank))
     side_row = lambda level: sum(
         everyone[group, 7 * share + level * own : 7 * share + (level + 1) * own, :] for group in range(groups)
     )
-    side_upper[...] = side_row(0)
-    upper = jnp.concatenate([mine[share : 7 * share, :] + arrived[share : 7 * share, :], side_upper[...]], 0)
+    upper = jnp.concatenate([mine[share : 7 * share, :] + arrived[share : 7 * share, :], side_row(0)], 0)
     own_weights[...] = exact_dot(upper, inverse[...], NN)
+    side_weights[...] = own_weights[6 * share :, :]
     update = exact_dot(own_weights[...], far[:rank], NT)
     panel[: 6 * share, :] = mine[7 * share : 13 * share, :] + arrived[7 * share : 13 * share, :] - update[: 6 * share]
     panel[6 * share :, :] = side_row(1) - update[6 * share :]
     weights[...] = far
 
 
-def first_rest_body(everyone, mine, arrived, far, own_weights, rest):
+def first_rest_body(everyone, mine, arrived, far, own_weights, inverse, rest, far_weights):
     groups, _, rank = everyone.shape
     share = rank // groups
     own = own_weights.shape[0] - 6 * share
     side_row = lambda level: sum(
         everyone[group, 7 * share + level * own : 7 * share + (level + 1) * own, :] for group in range(groups)
     )
+    far_weights[...] = exact_dot(far[...], inverse[...], NN)
     at = 0
     source = 13 * share
     for column in range(2, 7):
@@ -260,9 +275,16 @@
         at += count
 
 
-def level_rest_body(later, later_arrived, far, own_weights, rest):
-    rank = far.shape[1]
-    share = rank // 4
+def level_rest_body(everyone, later, later_arrived, far, own_weights, inverse, rest, far_weights, side_weights):
+    groups, _, rank = everyone.shape
+    share = rank // groups
+    above = far.shape[0] // rank
+    own = own_weights.shape[0] - above * share
+    sides = groups * own
+    low = (above + 1) * share
+    far_weights[: above * rank, :] = exact_dot(far[...], inverse[...], NN)
+    far_weights[above * rank :, :] = exact_dot(stacked(everyone, low, own), inverse[...], NN)
+    side_weights[...] = stacked(everyone, low + own, own)
     at = 0
     source = own_weights.shape[0]
     for column in range(1, far.shape[0] // rank):
@@ -346,15 +368,16 @@
     base[...] = exact_dot(tree[...], inverse_cols[...], NN)
 
 
-def carry_first_body(send, base, far1, inverse1, everyone, far2, inverse2, carried):
-    groups = everyone.shape[0]
-    share = inverse1.shape[0] // groups
-    own = base.shape[0] // groups
-    applied = jnp.concatenate([stacked(send, level * share, share) for level in range(7)], 0)
-    sides = base[...]
-    applied, sides = carry_step(applied, sides, far1[...], stacked(everyone, 6 * share + own, own), inverse1[...])
-    applied, sides = carry_step(applied, sides, far2[...], stacked(everyone, 6 * share, own), inverse2[...])
-    carried[...] = jnp.concatenate([applied, sides], 0)
+def carry_first_body(send, base, far_weights1, side_weights1, weights2, carried):
+    groups = send.shape[0]
+    rank = weights2.shape[1]
+    share = rank // groups
+    applied = [stacked(send, level * share, share) for level in range(7)]
+    rest = jnp.concatenate(applied[1:], 0) - exact_dot(far_weights1[...], applied[0], NN)
+    sides = base[...] - exact_dot(side_weights1[...], applied[0], NN)
+    update = exact_dot(weights2[...], rest[:rank], NN)
+    carried[: 5 * rank, :] = rest[rank:] - update[: 5 * rank]
+    carried[5 * rank :, :] = sides - update[5 * rank :]
 
 
 def carry_body(above, before, everyone, far, inverse, carried):
@@ -447,8 +470,8 @@
     )
     got = lax.all_to_all(send, "rhs", 0, 0)
     rows = 28 * share
-    gram, tree = run(
-        gram_body, [(rows + groups * levels * own, rank), (sides, leaf)], got, send, bases, place=place
+    gram, tree = run_loading(
+        gram_body, [(rows + groups * levels * own, rank), (sides, leaf)], got, bases, send, place=place
     )
     other = swap(gram, 1)
     total = gram + other
@@ -464,8 +487,15 @@
         other,
     )
     arrived = swap(panel, 2)
-    (later,) = run(
-        first_rest_body, [(15 * share + 5 * own, rank)], everyone, gram, other, far1, own_weights
+    later, far_weights1 = run(
+        first_rest_body,
+        [(15 * share + 5 * own, rank), (6 * rank, rank)],
+        everyone,
+        gram,
+        other,
+        far1,
+        own_weights,
+        inverse1,
     )
     for height in (2, 3):
         above = 7 - height
@@ -488,18 +518,25 @@
             )
             arrived = swap(next_panel, 3)
             rest_rows = above * (above - 1) // 2 * share + (above - 1) * own
-            (later,) = run(level_rest_body, [(rest_rows, rank)], later, later_arrived, far, own_weights)
+            later, far_weights2, side_weights1 = run(
+                level_rest_body,
+                [(rest_rows, rank), (above * rank + sides, rank), (sides, rank)],
+                everyone,
+                later,
+                later_arrived,
+                far,
+                own_weights,
+                inverse,
+            )
             panel = next_panel
             (carried,) = run(
                 carry_first_body,
                 [(5 * rank + sides, piece)],
                 send,
                 base,
-                far1,
-                inverse1,
-                everyone,
-                far,
-                inverse,
+                far_weights1,
+                side_weights1,
+                far_weights2,
             )
         else:
             panels, far, _, inverse = run(

time: 199 us -> 201 us (1.010)
  the two profiles are of different devices: /device:TPU:10 before, /device:TPU:18 now
where the time goes in v6:
time: 201 us; the launch traced here: 200 us
  starting transfers between devices  66.4 us (33%)
  Pallas kernels  63.7 us (32%)
  waiting for transfers between devices  38.8 us (19%)
  blocking collectives  27 us (13%)
  local copies, waits for them, and re-layouts  2.81 us (1%)
    pallas_call x23, Pallas kernels, run(): pl.pallas_call(body, out_shape=[shape_of(out) for out in outs], in_specs=...  50.9 us
    ppermute x12, starting transfers between devices, local(): swap = lambda block, height: lax.ppermute(block, 'leaf', route(height))  47 us
    ppermute x12, waiting for transfers between devices, local(): swap = lambda block, height: lax.ppermute(block, 'leaf', route(height))  21.7 us
    all_to_all x2, waiting for transfers between devices, local(): got = lax.all_to_all(send, 'rhs', 0, 0)  15 us
    all_to_all x1, blocking collectives, local(): everyone = lax.all_to_all(jnp.concatenate([shared, parts], 1), 'rhs', 0, 0)  14.3 us
    pallas_call x2, Pallas kernels, run_loading(): pl.pallas_call(loading, out_shape=[shape_of(out) for out in outs], in_spe...  12.8 us
    all_to_all x1, blocking collectives, sum_to_all(): return lax.all_to_all(send, 'rhs', 0, 0)  12.6 us
    all_to_all x2, starting transfers between devices, local(): got = lax.all_to_all(send, 'rhs', 0, 0)  9.74 us
  transfers between devices with their start and end apart: 16, of which 10 were waited for; matrix products, arithmetic and copies ran while one was open for 0% of the time, Pallas kernels for 9%

profile of v6, /device:TPU:18, one launch (start us, length us, event | category | flops | bytes accessed | tf_op | source)
XLA Modules:
  0.0 200.2 jit_solution(6935565379137940088)
XLA Ops:
  0.0 5.0 %shard_map.46 = (f32[4,288,256]{2,1,0:T(8,128)}, bf16[1024,1024]{1,0:T(8,128)(2,1)}) custom-call(s32[1,1024]{1,0:T(1,128)} %refs_0_.1, f32[16,1024]{1,0:T(8,128)} %refs_1_.1, f32[1024,256]{1,0:T(8,128)} %inverse_cols.1, bf16[7,128,1024]{2,1,0:T(8,128)(2,1)} %refs_2_.3), custom_call_target="tpu_custom_call" | custom-call | flops 1000000000 | tf_op jit(solution)/shard_map/pallas_call | solution.py:124
  5.0 4.8 %all-to-all-start = ((f32[4,288,256]{2,1,0:T(8,128)}), f32[4,288,256]{2,1,0:T(8,128)S(1)}, u32[]{:S(2)}, u32[]{:S(2)}) async-start(f32[4,288,256]{2,1,0:T(8,128)} %get-tuple-element.49.refs_3_.send), calls=%async_computation | async-start | bytes 2359296 | tf_op jit(solution)/shard_map/all_to_all | solution.py:471
  9.8 15.0 %all-to-all-done.refs_1_ = f32[4,288,256]{2,1,0:T(8,128)S(1)} async-done(((f32[4,288,256]{2,1,0:T(8,128)}), f32[4,288,256]{2,1,0:T(8,128)S(1)}, u32[]{:S(2)}, u32[]{:S(2)}) %all-to-all-start) | async-done | bytes 1179680 | tf_op jit(solution)/shard_map/all_to_all | solution.py:471
  25.9 7.8 %shard_map.47 = (f32[1344,128]{1,0:T(8,128)}, f32[64,1024]{1,0:T(8,128)}) custom-call(s32[1]{0:T(128)} %bitcast.refs_0_.place, f32[4,288,256]{2,1,0:T(8,128)} %copy-done.7, bf16[7,128,1024]{2,1,0:T(8,128)(2,1)} %refs_2_.3, f32[4,288,256]{2,1,0:T(8,128)} %get-tuple-element.49.refs_3_.send), custom_call_target="tpu_custom_call" | custom-call | flops 1000000000 | tf_op jit(solution)/shard_map/pallas_call | solution.py:124
  35.7 2.3 %collective-permute-done.arrived = f32[1344,128]{1,0:T(8,128)S(1)} collective-permute-done((f32[1344,128]{1,0:T(8,128)}, f32[1344,128]{1,0:T(8,128)S(1)}, u32[]{:S(2)}, u32[]{:S(2)}) %collective-permute-start) | collective-permute-done | bytes 688160 | tf_op jit(solution)/shard_map/ppermute | solution.py:457
  39.3 14.3 %all_to_all.30.everyone = f32[4,336,128]{2,1,0:T(8,128)S(1)} all-to-all(f32[4,336,128]{2,1,0:T(8,128)S(1)} %pad_maximum_fusion), channel_id=1, replica_groups=mesh['leaf'=128,'rhs'=4] {'rhs'}, dimensions={0} | all-to-all | bytes 1376256 | tf_op jit(solution)/shard_map/all_to_all | solution.py:480
  53.6 5.6 %shard_map.48 = (f32[208,128]{1,0:T(8,128)S(1)}, f32[768,128]{1,0:T(8,128)S(1)}, f32[208,128]{1,0:T(8,128)S(1)}, f32[128,128]{1,0:T(8,128)S(1)}, f32[16,128]{1,0:T(8,128)S(1)}) custom-call(f32[4,336,128]{2,1,0:T(8,128)S(1)} %all_to_all.30.everyone, f32[1344,128]{1,0:T(8,128)S(1)} %copy-done.1, f32[1344,128]{1,0:T(8,128)S(1)} %collective-permute-done.arrived), custom_call_target="tpu_custom_call" | custom-call | flops 1000000000 | tf_op jit(solution)/shard_map/pallas_call | solution.py:91
  59.3 3.5 %collective-permute-start.1 = (f32[208,128]{1,0:T(8,128)S(1)}, f32[208,128]{1,0:T(8,128)S(1)}, u32[]{:S(2)}, u32[]{:S(2)}) collective-permute-start(f32[208,128]{1,0:T(8,128)S(1)} %get-tuple-element.51.refs_0_), channel_id=1, source_target_pairs={{0,8},{4,12},{8,0},{12,4},{16,24},{20,28},{24,16},{28,20},{32,40},... | collective-permute-start | bytes 319496 | tf_op jit(solution)/shard_map/ppermute | solution.py:457
  66.7 4.9 %all-to-all-start.2 = ((f32[4,224,128]{2,1,0:T(8,128)}), f32[4,224,128]{2,1,0:T(8,128)S(1)}, u32[]{:S(2)}, u32[]{:S(2)}) async-start(f32[4,224,128]{2,1,0:T(8,128)} %shard_map.50), calls=%async_computation.2 | async-start | bytes 917504 | tf_op jit(solution)/shard_map/all_to_all | solution.py:434
  71.6 3.5 %collective-permute-start.2 = (f32[560,128]{1,0:T(8,128)S(1)}, f32[560,128]{1,0:T(8,128)S(1)}, u32[]{:S(2)}, u32[]{:S(2)}) collective-permute-start(f32[560,128]{1,0:T(8,128)S(1)} %get-tuple-element.60.later), channel_id=1, source_target_pairs={{0,8},{4,12},{8,0},{12,4},{16,24},{20,28},{24,16},{28,20},{32,40},... | collective-permute-start | bytes 860168 | tf_op jit(solution)/shard_map/ppermute | solution.py:457
  77.8 2.2 %collective-permute-done.2.later_arrived = f32[560,128]{1,0:T(8,128)S(1)} collective-permute-done((f32[560,128]{1,0:T(8,128)S(1)}, f32[560,128]{1,0:T(8,128)S(1)}, u32[]{:S(2)}, u32[]{:S(2)}) %collective-permute-start.2) | collective-permute-done | bytes 286752 | tf_op jit(solution)/shard_map/ppermute | solution.py:457
  80.1 5.6 %shard_map.52 = (f32[176,128]{1,0:T(8,128)S(1)}, f32[640,128]{1,0:T(8,128)S(1)}, f32[176,128]{1,0:T(8,128)S(1)}, f32[128,128]{1,0:T(8,128)S(1)}) custom-call(s32[1]{0:T(128)} %bitcast.refs_0_.place, f32[4,224,128]{2,1,0:T(8,128)S(1)} %all-to-all-done.2.everyone, f32[560,128]{1,0:T(8,128)S(1)} %get-tuple-element.60.later, ...), custom_call_target="tpu_custom_call" | custom-call | flops 1000000000 | tf_op jit(solution)/shard_map/pallas_call | solution.py:91
  85.7 2.2 %collective-permute-start.3 = (f32[176,128]{1,0:T(8,128)S(1)}, f32[176,128]{1,0:T(8,128)S(1)}, u32[]{:S(2)}, u32[]{:S(2)}) collective-permute-start(f32[176,128]{1,0:T(8,128)S(1)} %get-tuple-element.61.refs_0_), channel_id=1, source_target_pairs={{0,16},{4,20},{8,24},{12,28},{16,0},{20,4},{24,8},{28,12},{32,48},... | collective-permute-start | bytes 270344 | tf_op jit(solution)/shard_map/ppermute | solution.py:457
  89.6 3.5 %collective-permute-done.3.refs_1_ = f32[176,128]{1,0:T(8,128)S(1)} collective-permute-done((f32[176,128]{1,0:T(8,128)S(1)}, f32[176,128]{1,0:T(8,128)S(1)}, u32[]{:S(2)}, u32[]{:S(2)}) %collective-permute-start.3) | collective-permute-done | bytes 90144 | tf_op jit(solution)/shard_map/ppermute | solution.py:457
  93.8 4.8 %all-to-all-start.3 = ((f32[4,176,128]{2,1,0:T(8,128)}), f32[4,176,128]{2,1,0:T(8,128)S(1)}, u32[]{:S(2)}, u32[]{:S(2)}) async-start(f32[4,176,128]{2,1,0:T(8,128)} %shard_map.54), calls=%async_computation.3 | async-start | bytes 720896 | tf_op jit(solution)/shard_map/all_to_all | solution.py:434
  98.6 2.3 %collective-permute-start.4 = (f32[384,128]{1,0:T(8,128)S(1)}, f32[384,128]{1,0:T(8,128)S(1)}, u32[]{:S(2)}, u32[]{:S(2)}) collective-permute-start(f32[384,128]{1,0:T(8,128)S(1)} %get-tuple-element.72.later), channel_id=1, source_target_pairs={{0,16},{4,20},{8,24},{12,28},{16,0},{20,4},{24,8},{28,12},{32,48},... | collective-permute-start | bytes 589832 | tf_op jit(solution)/shard_map/ppermute | solution.py:457
  102.0 2.4 %shard_map.55.before = f32[704,256]{1,0:T(8,128)S(1)} custom-call(f32[4,288,256]{2,1,0:T(8,128)S(1)} %copy-done, f32[64,256]{1,0:T(8,128)S(1)} %shard_map.51.base, f32[768,128]{1,0:T(8,128)S(1)} %get-tuple-element.68.far_weights1, f32[64,128]{1,0:T(8,128)S(1)} %get-tuple-element.69.side_weights1, f32[704,128]{1,0:T(8,128)S(1)} %copy-done.6), custom_call_target="tpu_custom_call" | custom-call | flops 1000000000 | tf_op jit(solution)/shard_map/pallas_call | solution.py:91
  104.4 2.8 %collective-permute-done.4.later_arrived = f32[384,128]{1,0:T(8,128)S(1)} collective-permute-done((f32[384,128]{1,0:T(8,128)S(1)}, f32[384,128]{1,0:T(8,128)S(1)}, u32[]{:S(2)}, u32[]{:S(2)}) %collective-permute-start.4) | collective-permute-done | bytes 196640 | tf_op jit(solution)/shard_map/ppermute | solution.py:457
  107.2 5.5 %shard_map.56 = (f32[384,128]{1,0:T(8,128)S(1)}, f32[512,128]{1,0:T(8,128)S(1)}, f32[144,128]{1,0:T(8,128)}, f32[128,128]{1,0:T(8,128)S(1)}) custom-call(s32[1]{0:T(128)} %bitcast.refs_0_.place, f32[4,176,128]{2,1,0:T(8,128)S(1)} %all-to-all-done.3.everyone, f32[384,128]{1,0:T(8,128)S(1)} %get-tuple-element.72.later, ...), custom_call_target="tpu_custom_call" | custom-call | flops 1000000000 | tf_op jit(solution)/shard_map/pallas_call | solution.py:91
  112.7 7.8 %collective-permute-start.5 = (f32[384,128]{1,0:T(8,128)S(1)}, f32[384,128]{1,0:T(8,128)S(1)}, u32[]{:S(2)}, u32[]{:S(2)}) collective-permute-start(f32[384,128]{1,0:T(8,128)S(1)} %get-tuple-element.73.refs_0_), channel_id=1, source_target_pairs={{0,48},{4,52},{8,56},{12,60},{16,32},{20,36},{24,40},{28,44},{32,1... | collective-permute-start | bytes 589832 | tf_op jit(solution)/shard_map/ppermute | solution.py:457
  121.9 4.4 %collective-permute-done.5.refs_1_ = f32[384,128]{1,0:T(8,128)S(1)} collective-permute-done((f32[384,128]{1,0:T(8,128)S(1)}, f32[384,128]{1,0:T(8,128)S(1)}, u32[]{:S(2)}, u32[]{:S(2)}) %collective-permute-start.5) | collective-permute-done | bytes 196640 | tf_op jit(solution)/shard_map/ppermute | solution.py:457
  126.3 12.6 %all_to_all.31.everyone = f32[4,384,128]{2,1,0:T(8,128)S(1)} all-to-all(f32[4,384,128]{2,1,0:T(8,128)S(1)} %shard_map.58), channel_id=1, replica_groups=mesh['leaf'=128,'rhs'=4] {'rhs'}, dimensions={0} | all-to-all | bytes 1572864 | tf_op jit(solution)/shard_map/all_to_all | solution.py:434
  139.0 5.5 %shard_map.59 = (f32[448,128]{1,0:T(8,128)S(1)}, f32[448,128]{1,0:T(8,128)S(1)}, f32[448,128]{1,0:T(8,128)S(1)}) custom-call(f32[4,384,128]{2,1,0:T(8,128)S(1)} %all_to_all.31.everyone), custom_call_target="tpu_custom_call" | custom-call | flops 1000000000 | tf_op jit(solution)/shard_map/pallas_call | solution.py:91
  144.5 4.3 %collective-permute-start.6 = (f32[448,128]{1,0:T(8,128)S(1)}, f32[448,128]{1,0:T(8,128)S(1)}, u32[]{:S(2)}, u32[]{:S(2)}) collective-permute-start(f32[448,128]{1,0:T(8,128)S(1)} %get-tuple-element.80.mine), channel_id=1, source_target_pairs={{0,64},{4,68},{8,72},{12,76},{16,80},{20,84},{24,88},{28,92},{32,9... | collective-permute-start | bytes 688136 | tf_op jit(solution)/shard_map/ppermute | solution.py:457
  151.3 3.9 %collective-permute-start.8 = (f32[192,128]{1,0:T(8,128)S(1)}, f32[192,128]{1,0:T(8,128)S(1)}, u32[]{:S(2)}, u32[]{:S(2)}) collective-permute-start(f32[192,128]{1,0:T(8,128)S(1)} %shard_map.65.later), channel_id=1, source_target_pairs={{0,64},{4,68},{8,72},{12,76},{16,80},{20,84},{24,88},{28,92},{32,9... | collective-permute-start | bytes 294920 | tf_op jit(solution)/shard_map/ppermute | solution.py:457
  155.7 4.9 %shard_map.61 = (f32[320,128]{1,0:T(8,128)S(1)}, f32[320,128]{1,0:T(8,128)S(1)}) custom-call(f32[448,128]{1,0:T(8,128)S(1)} %get-tuple-element.80.mine, f32[448,128]{1,0:T(8,128)S(1)} %collective-permute-done.6.arrived), custom_call_target="tpu_custom_call" | custom-call | flops 1000000000 | tf_op jit(solution)/shard_map/pallas_call | solution.py:91
  161.0 5.7 %collective-permute-start.10 = (f32[320,128]{1,0:T(8,128)S(1)}, f32[320,128]{1,0:T(8,128)S(1)}, u32[]{:S(2)}, u32[]{:S(2)}) collective-permute-start(f32[320,128]{1,0:T(8,128)S(1)} %shard_map.64.mine), channel_id=1, source_target_pairs={{0,128},{4,132},{8,136},{12,140},{16,144},{20,148},{24,152},{28,15... | collective-permute-start | bytes 491528 | tf_op jit(solution)/shard_map/ppermute | solution.py:457
  171.2 4.9 %shard_map.67 = (f32[192,128]{1,0:T(8,128)S(1)}, f32[192,128]{1,0:T(8,128)S(1)}) custom-call(f32[320,128]{1,0:T(8,128)S(1)} %shard_map.64.mine, f32[320,128]{1,0:T(8,128)S(1)} %collective-permute-done.10.arrived), custom_call_target="tpu_custom_call" | custom-call | flops 1000000000 | tf_op jit(solution)/shard_map/pallas_call | solution.py:91
  177.5 4.9 %all-to-all-start.5 = ((f32[4,144,256]{2,1,0:T(8,128)}), f32[4,144,256]{2,1,0:T(8,128)S(1)}, u32[]{:S(2)}, u32[]{:S(2)}) async-start(f32[4,144,256]{2,1,0:T(8,128)} %shard_map.69), calls=%async_computation.5 | async-start | bytes 1179648 | tf_op jit(solution)/shard_map/all_to_all | solution.py:589
  182.4 8.0 %collective-permute-start.11 = (f32[144,128]{1,0:T(8,128)S(1)}, f32[144,128]{1,0:T(8,128)S(1)}, u32[]{:S(2)}, u32[]{:S(2)}) collective-permute-start(f32[144,128]{1,0:T(8,128)S(1)} %shard_map.68.mine), channel_id=1, source_target_pairs={{0,384},{4,388},{8,392},{12,396},{16,400},{20,404},{24,408},{28,41... | collective-permute-start | bytes 221192 | tf_op jit(solution)/shard_map/ppermute | solution.py:457
  190.4 2.4 %collective-permute-done.11.arrived = f32[144,128]{1,0:T(8,128)S(1)} collective-permute-done((f32[144,128]{1,0:T(8,128)S(1)}, f32[144,128]{1,0:T(8,128)S(1)}, u32[]{:S(2)}, u32[]{:S(2)}) %collective-permute-start.11) | collective-permute-done | bytes 73760 | tf_op jit(solution)/shard_map/ppermute | solution.py:457
  192.8 7.5 %shard_map.70 = f32[16,1024]{1,0:T(8,128)} custom-call(f32[144,128]{1,0:T(8,128)S(1)} %shard_map.68.mine, f32[144,128]{1,0:T(8,128)S(1)} %collective-permute-done.11.arrived, f32[4,144,256]{2,1,0:T(8,128)S(1)} %all-to-all-done.5.got, bf16[1024,1024]{1,0:T(8,128)(2,1)S(1)} %copy-done.4), custom_call_target="tpu_custom_call" | custom-call | flops 1000000000 | tf_op jit(solution)/shard_map/pallas_call | solution.py:91
  (48 shorter events, 24.9 us)
Async XLA Ops:
  5.0 19.9 %all-to-all-start = ((f32[4,288,256]{2,1,0:T(8,128)}), f32[4,288,256]{2,1,0:T(8,128)S(1)}, u32[]{:S(2)}, u32[]{:S(2)}) async-start(f32[4,288,256]{2,1,0:T(8,128)} %get-tuple-element.49.refs_3_.send), calls=%async_computation | async-start | bytes 2359296 | tf_op jit(solution)/shard_map/all_to_all | solution.py:471
  24.9 1.0 copy-start.7
  33.7 4.2 %collective-permute-start = (f32[1344,128]{1,0:T(8,128)}, f32[1344,128]{1,0:T(8,128)S(1)}, u32[]{:S(2)}, u32[]{:S(2)}) collective-permute-start(f32[1344,128]{1,0:T(8,128)} %get-tuple-element.50.mine), channel_id=1, source_target_pairs={{0,4},{4,0},{8,12},{12,8},{16,20},{20,16},{24,28},{28,24},{32,36},... | collective-permute-start | bytes 2064392 | tf_op jit(solution)/shard_map/ppermute | solution.py:457
  39.2 14.5 %copy-start.1 = (f32[1344,128]{1,0:T(8,128)S(1)}, f32[1344,128]{1,0:T(8,128)}, u32[]{:S(2)}) copy-start(f32[1344,128]{1,0:T(8,128)} %get-tuple-element.50.mine) | copy-start | bytes 2064388
  59.3 6.6 %collective-permute-start.1 = (f32[208,128]{1,0:T(8,128)S(1)}, f32[208,128]{1,0:T(8,128)S(1)}, u32[]{:S(2)}, u32[]{:S(2)}) collective-permute-start(f32[208,128]{1,0:T(8,128)S(1)} %get-tuple-element.51.refs_0_), channel_id=1, source_target_pairs={{0,8},{4,12},{8,0},{12,4},{16,24},{20,28},{24,16},{28,20},{32,40},... | collective-permute-start | bytes 319496 | tf_op jit(solution)/shard_map/ppermute | solution.py:457
  65.9 9.2 %copy-start.2 = (f32[1024,256]{1,0:T(8,128)S(1)}, f32[1024,256]{1,0:T(8,128)}, u32[]{:S(2)}) copy-start(f32[1024,256]{1,0:T(8,128)} %inverse_cols.1) | copy-start | bytes 3145732
  65.9 9.2 %copy-start.3 = (f32[64,1024]{1,0:T(8,128)S(1)}, f32[64,1024]{1,0:T(8,128)}, u32[]{:S(2)}) copy-start(f32[64,1024]{1,0:T(8,128)} %get-tuple-element.58.tree) | copy-start | bytes 786436
  66.7 11.2 %all-to-all-start.2 = ((f32[4,224,128]{2,1,0:T(8,128)}), f32[4,224,128]{2,1,0:T(8,128)S(1)}, u32[]{:S(2)}, u32[]{:S(2)}) async-start(f32[4,224,128]{2,1,0:T(8,128)} %shard_map.50), calls=%async_computation.2 | async-start | bytes 917504 | tf_op jit(solution)/shard_map/all_to_all | solution.py:434
  71.6 8.5 %collective-permute-start.2 = (f32[560,128]{1,0:T(8,128)S(1)}, f32[560,128]{1,0:T(8,128)S(1)}, u32[]{:S(2)}, u32[]{:S(2)}) collective-permute-start(f32[560,128]{1,0:T(8,128)S(1)} %get-tuple-element.60.later), channel_id=1, source_target_pairs={{0,8},{4,12},{8,0},{12,4},{16,24},{20,28},{24,16},{28,20},{32,40},... | collective-permute-start | bytes 860168 | tf_op jit(solution)/shard_map/ppermute | solution.py:457
  85.7 7.4 %collective-permute-start.3 = (f32[176,128]{1,0:T(8,128)S(1)}, f32[176,128]{1,0:T(8,128)S(1)}, u32[]{:S(2)}, u32[]{:S(2)}) collective-permute-start(f32[176,128]{1,0:T(8,128)S(1)} %get-tuple-element.61.refs_0_), channel_id=1, source_target_pairs={{0,16},{4,20},{8,24},{12,28},{16,0},{20,4},{24,8},{28,12},{32,48},... | collective-permute-start | bytes 270344 | tf_op jit(solution)/shard_map/ppermute | solution.py:457
  88.8 0.7 copy-start.5
  93.1 7.9 %copy-start = (f32[4,288,256]{2,1,0:T(8,128)S(1)}, f32[4,288,256]{2,1,0:T(8,128)}, u32[]{:S(2)}) copy-start(f32[4,288,256]{2,1,0:T(8,128)} %get-tuple-element.49.refs_3_.send) | copy-start | bytes 3538948
  93.8 10.5 %all-to-all-start.3 = ((f32[4,176,128]{2,1,0:T(8,128)}), f32[4,176,128]{2,1,0:T(8,128)S(1)}, u32[]{:S(2)}, u32[]{:S(2)}) async-start(f32[4,176,128]{2,1,0:T(8,128)} %shard_map.54), calls=%async_computation.3 | async-start | bytes 720896 | tf_op jit(solution)/shard_map/all_to_all | solution.py:434
  98.6 8.5 %collective-permute-start.4 = (f32[384,128]{1,0:T(8,128)S(1)}, f32[384,128]{1,0:T(8,128)S(1)}, u32[]{:S(2)}, u32[]{:S(2)}) collective-permute-start(f32[384,128]{1,0:T(8,128)S(1)} %get-tuple-element.72.later), channel_id=1, source_target_pairs={{0,16},{4,20},{8,24},{12,28},{16,0},{20,4},{24,8},{28,12},{32,48},... | collective-permute-start | bytes 589832 | tf_op jit(solution)/shard_map/ppermute | solution.py:457
  101.0 1.0 copy-start.6
  112.7 13.6 %collective-permute-start.5 = (f32[384,128]{1,0:T(8,128)S(1)}, f32[384,128]{1,0:T(8,128)S(1)}, u32[]{:S(2)}, u32[]{:S(2)}) collective-permute-start(f32[384,128]{1,0:T(8,128)S(1)} %get-tuple-element.73.refs_0_), channel_id=1, source_target_pairs={{0,48},{4,52},{8,56},{12,60},{16,32},{20,36},{24,40},{28,44},{32,1... | collective-permute-start | bytes 589832 | tf_op jit(solution)/shard_map/ppermute | solution.py:457
  144.5 11.2 %collective-permute-start.6 = (f32[448,128]{1,0:T(8,128)S(1)}, f32[448,128]{1,0:T(8,128)S(1)}, u32[]{:S(2)}, u32[]{:S(2)}) collective-permute-start(f32[448,128]{1,0:T(8,128)S(1)} %get-tuple-element.80.mine), channel_id=1, source_target_pairs={{0,64},{4,68},{8,72},{12,76},{16,80},{20,84},{24,88},{28,92},{32,9... | collective-permute-start | bytes 688136 | tf_op jit(solution)/shard_map/ppermute | solution.py:457
  149.1 11.6 %collective-permute-start.7 = (f32[320,128]{1,0:T(8,128)S(1)}, f32[320,128]{1,0:T(8,128)S(1)}, u32[]{:S(2)}, u32[]{:S(2)}) collective-permute-start(f32[320,128]{1,0:T(8,128)S(1)} %shard_map.63.later), channel_id=1, source_target_pairs={{0,64},{4,68},{8,72},{12,76},{16,80},{20,84},{24,88},{28,92},{32,9... | collective-permute-start | bytes 491528 | tf_op jit(solution)/shard_map/ppermute | solution.py:457
  151.3 15.4 %collective-permute-start.8 = (f32[192,128]{1,0:T(8,128)S(1)}, f32[192,128]{1,0:T(8,128)S(1)}, u32[]{:S(2)}, u32[]{:S(2)}) collective-permute-start(f32[192,128]{1,0:T(8,128)S(1)} %shard_map.65.later), channel_id=1, source_target_pairs={{0,64},{4,68},{8,72},{12,76},{16,80},{20,84},{24,88},{28,92},{32,9... | collective-permute-start | bytes 294920 | tf_op jit(solution)/shard_map/ppermute | solution.py:457
  161.0 10.2 %collective-permute-start.10 = (f32[320,128]{1,0:T(8,128)S(1)}, f32[320,128]{1,0:T(8,128)S(1)}, u32[]{:S(2)}, u32[]{:S(2)}) collective-permute-start(f32[320,128]{1,0:T(8,128)S(1)} %shard_map.64.mine), channel_id=1, source_target_pairs={{0,128},{4,132},{8,136},{12,140},{16,144},{20,148},{24,152},{28,15... | collective-permute-start | bytes 491528 | tf_op jit(solution)/shard_map/ppermute | solution.py:457
  167.0 9.1 %collective-permute-start.9 = (f32[192,128]{1,0:T(8,128)S(1)}, f32[192,128]{1,0:T(8,128)S(1)}, u32[]{:S(2)}, u32[]{:S(2)}) collective-permute-start(f32[192,128]{1,0:T(8,128)S(1)} %shard_map.66.later), channel_id=1, source_target_pairs={{0,128},{4,132},{8,136},{12,140},{16,144},{20,148},{24,152},{28,15... | collective-permute-start | bytes 294920 | tf_op jit(solution)/shard_map/ppermute | solution.py:457
  176.3 16.5 %copy-start.4 = (bf16[1024,1024]{1,0:T(8,128)(2,1)S(1)}, bf16[1024,1024]{1,0:T(8,128)(2,1)}, u32[]{:S(2)}) copy-start(bf16[1024,1024]{1,0:T(8,128)(2,1)} %get-tuple-element.92.hot) | copy-start | bytes 6291460
  177.5 15.3 %all-to-all-start.5 = ((f32[4,144,256]{2,1,0:T(8,128)}), f32[4,144,256]{2,1,0:T(8,128)S(1)}, u32[]{:S(2)}, u32[]{:S(2)}) async-start(f32[4,144,256]{2,1,0:T(8,128)} %shard_map.69), calls=%async_computation.5 | async-start | bytes 1179648 | tf_op jit(solution)/shard_map/all_to_all | solution.py:589
  182.4 10.4 %collective-permute-start.11 = (f32[144,128]{1,0:T(8,128)S(1)}, f32[144,128]{1,0:T(8,128)S(1)}, u32[]{:S(2)}, u32[]{:S(2)}) collective-permute-start(f32[144,128]{1,0:T(8,128)S(1)} %shard_map.68.mine), channel_id=1, source_target_pairs={{0,384},{4,388},{8,392},{12,396},{16,400},{20,404},{24,408},{28,41... | collective-permute-start | bytes 221192 | tf_op jit(solution)/shard_map/ppermute | solution.py:457

commit v7 on v6

--- a/solution.py
+++ b/solution.py
@@ -151,7 +151,7 @@
     return jnp.concatenate([everyone[group, low : low + count, :] for group in range(everyone.shape[0])], 0)
 
 
-def start_body(wait, order, sides, inverse_cols, bases, send, hot):
+def start_body(wait, order, sides, inverse_cols, bases, send, hot, tree):
     levels, rank, leaf = bases.shape
     groups, _, piece = send.shape
     share = rank // groups
@@ -159,11 +159,11 @@
     wait(0)
     hot[...] = one_hot(order[...])
     wait(1)
-    tree = dot_left_parts(sides[...], hot[...], NN)
+    ordered = dot_left_parts(sides[...], hot[...], NN)
     for group in range(groups):
-        for part in range(groups):
-            low = levels * share + part * own
-            send[group, low : low + own, :] = tree[:, part * piece : (part + 1) * piece]
+        send[group, levels * share :, :] = ordered[:, group * piece : (group + 1) * piece]
+    for part in range(leaf // rank):
+        tree[part * own : (part + 1) * own, :] = ordered[:, part * rank : (part + 1) * rank]
     wait(2)
     high, middle, low_part = three_parts(inverse_cols[...])
     for level in range(levels):
@@ -176,38 +176,27 @@
             send[group, level * share : (level + 1) * share, :] = applied[low : low + share]
 
 
-def gram_body(wait, place, got, bases, send, gram, tree):
+def gram_body(got, send, bases, gram):
     levels, rank, leaf = bases.shape
     groups, rows, piece = got.shape
     share = rank // groups
-    v_rows = levels * share
-    own = (rows - v_rows) // groups
-    for group in range(groups):
-        wait(0, group)
-    applied = three_parts(jnp.concatenate([got[group, :v_rows, :] for group in range(groups)], 1))
+    own = rows - levels * share
+    applied = three_parts(jnp.concatenate([got[group, : levels * share, :] for group in range(groups)], 1))
     at = 0
     for column in range(levels):
         count = (levels - column) * share
-        wait(1, column)
         high, middle, low = [part[column * share :] for part in applied]
         right = bases[column]
         gram[at : at + count, :] = (
             short_dot(low, right, NT) + short_dot(middle, right, NT) + short_dot(high, right, NT)
         )
         at += count
-    for group in range(groups):
-        wait(2, group)
-    mine = pl.ds(pl.multiple_of(v_rows + place[0] * own, own), own)
-    sides = jnp.concatenate([got[group, mine, :] for group in range(groups)], 0)
+    sides = stacked(got, levels * share, own)
     for level in range(levels):
         block = exact_dot(sides, stacked(send, level * share, share), NT)
         for group in range(groups):
             low = at + (group * levels + level) * own
             gram[low : low + own, :] = block[group * own : (group + 1) * own]
-    for group in range(groups):
-        tree[group * own : (group + 1) * own, :] = jnp.concatenate(
-            [got[group, v_rows + part * own : v_rows + (part + 1) * own, :] for part in range(groups)], 1
-        )
 
 
 def first_body(everyone, mine, arrived, panel, weights, own_weights, inverse, side_weights):
@@ -260,13 +249,18 @@
     panel[...] = later[:count, :] + later_arrived[:count, :] - exact_dot(own_weights[...], far[:rank, :], NT)
 
 
-def level_all_body(above, place, everyone, later, later_arrived, panels, far, own_weights, inverse):
+def level_factor_body(above, place, everyone, far, own_weights, inverse):
     groups, _, rank = everyone.shape
     share = rank // groups
     far[...] = jnp.concatenate([stacked(everyone, level * share, share) for level in range(1, above + 1)], 0)
     inverse[...] = inverse_of(stacked(everyone, 0, share) + identity(rank))
     own_upper = everyone[place[0], share : share + own_weights.shape[0], :]
     own_weights[...] = exact_dot(own_upper, inverse[...], NN)
+
+
+def level_all_body(above, later, later_arrived, far, own_weights, panels):
+    rank = far.shape[1]
+    share = rank // 4
     at = 0
     for column in range(above):
         count = own_weights.shape[0] - column * share
@@ -282,9 +276,9 @@
     own = own_weights.shape[0] - above * share
     sides = groups * own
     low = (above + 1) * share
-    far_weights[: above * rank, :] = exact_dot(far[...], inverse[...], NN)
-    far_weights[above * rank :, :] = exact_dot(stacked(everyone, low, own), inverse[...], NN)
-    side_weights[...] = stacked(everyone, low + own, own)
+    far_weights[...] = exact_dot(far[...], inverse[...], NN)
+    side_weights[:sides, :] = stacked(everyone, low + own, own)
+    side_weights[sides:, :] = exact_dot(stacked(everyone, low, own), inverse[...], NN)
     at = 0
     source = own_weights.shape[0]
     for column in range(1, far.shape[0] // rank):
@@ -364,31 +358,34 @@
     return applied[rank:] - exact_dot(exact_dot(far, inverse, NN), gone, NN), sides
 
 
-def base_body(tree, inverse_cols, base):
-    base[...] = exact_dot(tree[...], inverse_cols[...], NN)
-
-
-def carry_first_body(send, base, far_weights1, side_weights1, weights2, carried):
+def carry_first_body(send, weights1, weights2, carried, gone):
     groups = send.shape[0]
     rank = weights2.shape[1]
     share = rank // groups
     applied = [stacked(send, level * share, share) for level in range(7)]
-    rest = jnp.concatenate(applied[1:], 0) - exact_dot(far_weights1[...], applied[0], NN)
-    sides = base[...] - exact_dot(side_weights1[...], applied[0], NN)
-    update = exact_dot(weights2[...], rest[:rank], NN)
-    carried[: 5 * rank, :] = rest[rank:] - update[: 5 * rank]
-    carried[5 * rank :, :] = sides - update[5 * rank :]
-
-
-def carry_body(above, before, everyone, far, inverse, carried):
-    groups, _, rank = everyone.shape
-    share = rank // groups
-    count = (above + 1) * rank
-    own = (before.shape[0] - count) // groups
-    applied, sides = carry_step(
-        before[:count, :], before[count:, :], far[...], stacked(everyone, (above + 1) * share, own), inverse[...]
-    )
-    carried[...] = jnp.concatenate([applied, sides], 0)
+    rest = jnp.concatenate(applied[1:], 0) - exact_dot(weights1[...], applied[0], NN)
+    carried[...] = rest[rank:] - exact_dot(weights2[...], rest[:rank], NN)
+    gone[:rank, :] = applied[0]
+    gone[rank:, :] = rest[:rank]
+
+
+def carry_body(above, before, gone, side_weights, everyone, far, inverse, inverse_cols, carried):
+    groups, rows, rank = everyone.shape
+    share = rank // groups
+    low = (above + 1) * share
+    sides = side_weights.shape[0] // 2
+    own = sides // groups
+    parts = (rows - low - own) // own
+    tree = jnp.concatenate(
+        [stacked(everyone, low + own + part * own, own) for part in range(parts)], 1
+    )
+    found = exact_dot(tree, inverse_cols[...], NN)
+    for place in range(2):
+        weights = side_weights[place * sides : (place + 1) * sides, :]
+        found = found - exact_dot(weights, gone[place * rank : (place + 1) * rank, :], NN)
+    applied, found = carry_step(before[...], found, far[...], stacked(everyone, low, own), inverse[...])
+    carried[: above * rank, :] = applied
+    carried[above * rank :, :] = found
 
 
 def carry_on_body(before, weights, carried):
@@ -424,7 +421,7 @@
     for group in range(send.shape[0]):
         send[group, :count, :] = total
         for other in others:
-            send[group, count:, :] = other[...]
+            send[group, count : count + other.shape[0], :] = other[...]
 
 
 def sum_to_all(mine, arrived, *others):
@@ -457,11 +454,12 @@
     swap = lambda block, height: lax.ppermute(block, "leaf", route(height))
 
     place = lax.axis_index("rhs").reshape(1)
-    send, hot = run_loading(
+    send, hot, tree = run_loading(
         start_body,
         [
-            (groups, levels * share + sides, piece),
+            (groups, levels * share + own, piece),
             jax.ShapeDtypeStruct((leaf, leaf), jnp.bfloat16),
+            (leaf // rank * own, rank),
         ],
         ordering,
         right_sides,
@@ -470,9 +468,7 @@
     )
     got = lax.all_to_all(send, "rhs", 0, 0)
     rows = 28 * share
-    gram, tree = run_loading(
-        gram_body, [(rows + groups * levels * own, rank), (sides, leaf)], got, bases, send, place=place
-    )
+    (gram,) = run(gram_body, [(rows + groups * levels * own, rank)], got, send, bases)
     other = swap(gram, 1)
     total = gram + other
     shared = jnp.broadcast_to(total[: 7 * share][None], (groups, 7 * share, rank))
@@ -501,11 +497,8 @@
         above = 7 - height
         later_arrived = swap(later, height)
         arrived, later = lax.optimization_barrier((arrived, later))
-        everyone = sum_to_all(panel, arrived, side1) if height == 2 else sum_to_all(panel, arrived)
-        if height == 2:
-            (base,) = run(base_body, [(sides, piece)], tree, leaf_inverse)
-            everyone, base = lax.optimization_barrier((everyone, base))
-        else:
+        everyone = sum_to_all(panel, arrived, side1) if height == 2 else sum_to_all(panel, arrived, tree)
+        if height == 3:
             everyone, carried = lax.optimization_barrier((everyone, carried))
         if height == 2:
             next_panel, far, own_weights, inverse = run(
@@ -518,9 +511,9 @@
             )
             arrived = swap(next_panel, 3)
             rest_rows = above * (above - 1) // 2 * share + (above - 1) * own
-            later, far_weights2, side_weights1 = run(
+            later, far_weights2, side_weights = run(
                 level_rest_body,
-                [(rest_rows, rank), (above * rank + sides, rank), (sides, rank)],
+                [(rest_rows, rank), (above * rank, rank), (2 * sides, rank)],
                 everyone,
                 later,
                 later_arrived,
@@ -529,37 +522,39 @@
                 inverse,
             )
             panel = next_panel
-            (carried,) = run(
+            carried, gone = run(
                 carry_first_body,
-                [(5 * rank + sides, piece)],
+                [(5 * rank, piece), (2 * rank, piece)],
                 send,
-                base,
                 far_weights1,
-                side_weights1,
                 far_weights2,
             )
         else:
-            panels, far, _, inverse = run(
+            far, own_weights, inverse = run(
+                functools.partial(level_factor_body, above),
+                [(above * rank, rank), (above * share + own, rank), square],
+                everyone,
+                place=place,
+            )
+            (panels,) = run(
                 functools.partial(level_all_body, above),
-                [
-                    (above * (above + 1) // 2 * share + above * own, rank),
-                    (above * rank, rank),
-                    (above * share + own, rank),
-                    square,
-                ],
-                everyone,
+                [(above * (above + 1) // 2 * share + above * own, rank)],
                 later,
                 later_arrived,
-                place=place,
+                far,
+                own_weights,
             )
             panels_arrived = swap(panels, 4)
             (carried,) = run(
                 functools.partial(carry_body, above),
                 [(4 * rank + sides, piece)],
                 carried,
+                gone,
+                side_weights,
                 everyone,
                 far,
                 inverse,
+                leaf_inverse,
             )
     panels_arrived, carried = lax.optimization_barrier((panels_arrived, carried))
     everyone = sum_to_all(panels, panels_arrived)

time: 201 us -> 189 us (0.940)
  the two profiles are of different devices: /device:TPU:18 before, /device:TPU:10 now
where the time goes in v7:
time: 189 us; the launch traced here: 188 us
  starting transfers between devices  63.1 us (33%)
  Pallas kernels  57.8 us (31%)
  blocking collectives  44.4 us (23%)
  waiting for transfers between devices  20.9 us (11%)
    pallas_call x24, Pallas kernels, run(): pl.pallas_call(body, out_shape=[shape_of(out) for out in outs], in_specs=...  52.8 us
    ppermute x12, starting transfers between devices, local(): swap = lambda block, height: lax.ppermute(block, 'leaf', route(height))  48.5 us
    ppermute x12, waiting for transfers between devices, local(): swap = lambda block, height: lax.ppermute(block, 'leaf', route(height))  20.9 us
    all_to_all x1, blocking collectives, local(): got = lax.all_to_all(send, 'rhs', 0, 0)  17.9 us
    all_to_all x1, blocking collectives, local(): everyone = lax.all_to_all(jnp.concatenate([shared, parts], 1), 'rhs', 0, 0)  14.2 us
    all_to_all x1, blocking collectives, sum_to_all(): return lax.all_to_all(send, 'rhs', 0, 0)  12.3 us
    all_to_all x2, starting transfers between devices, sum_to_all(): return lax.all_to_all(send, 'rhs', 0, 0)  9.69 us
    pallas_call x1, Pallas kernels, run_loading(): pl.pallas_call(loading, out_shape=[shape_of(out) for out in outs], in_spe...  5.04 us
  transfers between devices with their start and end apart: 15, of which 7 were waited for; matrix products, arithmetic and copies ran while one was open for 0% of the time, Pallas kernels for 12%

profile of v7, /device:TPU:10, one launch (start us, length us, event | category | flops | bytes accessed | tf_op | source)
XLA Modules:
  0.0 188.5 jit_solution(14002474393629251043)
XLA Ops:
  0.0 5.0 %shard_map.46 = (f32[4,240,256]{2,1,0:T(8,128)}, bf16[1024,1024]{1,0:T(8,128)(2,1)}, f32[128,128]{1,0:T(8,128)}) custom-call(s32[1,1024]{1,0:T(1,128)} %refs_0_.1, f32[16,1024]{1,0:T(8,128)} %refs_1_.1, f32[1024,256]{1,0:T(8,128)} %inverse_cols.1, bf16[7,128,1024]{2,1,0:T(8,128)(2,1)} %bases.1), custom_call_target="tpu_custom_call" | custom-call | flops 1000000000 | tf_op jit(solution)/shard_map/pallas_call | solution.py:124
  5.1 17.9 %all_to_all.30.got = f32[4,240,256]{2,1,0:T(8,128)S(1)} all-to-all(f32[4,240,256]{2,1,0:T(8,128)} %get-tuple-element.48.send), channel_id=1, replica_groups=mesh['leaf'=128,'rhs'=4] {'rhs'}, dimensions={0} | all-to-all | bytes 1966080 | tf_op jit(solution)/shard_map/all_to_all | solution.py:469
  23.0 2.6 %shard_map.47.mine = f32[1344,128]{1,0:T(8,128)S(1)} custom-call(f32[4,240,256]{2,1,0:T(8,128)S(1)} %all_to_all.30.got, f32[4,240,256]{2,1,0:T(8,128)S(1)} %copy-done, bf16[7,128,1024]{2,1,0:T(8,128)(2,1)S(1)} %copy-done.1), custom_call_target="tpu_custom_call" | custom-call | flops 1000000000 | tf_op jit(solution)/shard_map/pallas_call | solution.py:91
  25.6 1.9 %collective-permute-start = (f32[1344,128]{1,0:T(8,128)S(1)}, f32[1344,128]{1,0:T(8,128)S(1)}, u32[]{:S(2)}, u32[]{:S(2)}) collective-permute-start(f32[1344,128]{1,0:T(8,128)S(1)} %shard_map.47.mine), channel_id=1, source_target_pairs={{0,4},{4,0},{8,12},{12,8},{16,20},{20,16},{24,28},{28,24},{32,36},... | collective-permute-start | bytes 2064392 | tf_op jit(solution)/shard_map/ppermute | solution.py:454
  27.5 2.1 %collective-permute-done.arrived = f32[1344,128]{1,0:T(8,128)S(1)} collective-permute-done((f32[1344,128]{1,0:T(8,128)S(1)}, f32[1344,128]{1,0:T(8,128)S(1)}, u32[]{:S(2)}, u32[]{:S(2)}) %collective-permute-start) | collective-permute-done | bytes 688160 | tf_op jit(solution)/shard_map/ppermute | solution.py:454
  29.8 14.2 %all_to_all.31.everyone = f32[4,336,128]{2,1,0:T(8,128)S(1)} all-to-all(f32[4,336,128]{2,1,0:T(8,128)S(1)} %pad_maximum_fusion), channel_id=1, replica_groups=mesh['leaf'=128,'rhs'=4] {'rhs'}, dimensions={0} | all-to-all | bytes 1376256 | tf_op jit(solution)/shard_map/all_to_all | solution.py:476
  44.0 5.6 %shard_map.48 = (f32[208,128]{1,0:T(8,128)S(1)}, f32[768,128]{1,0:T(8,128)S(1)}, f32[208,128]{1,0:T(8,128)S(1)}, f32[128,128]{1,0:T(8,128)S(1)}, f32[16,128]{1,0:T(8,128)S(1)}) custom-call(f32[4,336,128]{2,1,0:T(8,128)S(1)} %all_to_all.31.everyone, f32[1344,128]{1,0:T(8,128)S(1)} %shard_map.47.mine, f32[1344,128]{1,0:T(8,128)S(1)} %collective-permute-done.arrived), custom_call_target="tpu_custom_call" | custom-call | flops 1000000000 | tf_op jit(solution)/shard_map/pallas_call | solution.py:91
  49.7 3.1 %collective-permute-start.1 = (f32[208,128]{1,0:T(8,128)S(1)}, f32[208,128]{1,0:T(8,128)S(1)}, u32[]{:S(2)}, u32[]{:S(2)}) collective-permute-start(f32[208,128]{1,0:T(8,128)S(1)} %get-tuple-element.49.refs_0_), channel_id=1, source_target_pairs={{0,8},{4,12},{8,0},{12,4},{16,24},{20,28},{24,16},{28,20},{32,40},... | collective-permute-start | bytes 319496 | tf_op jit(solution)/shard_map/ppermute | solution.py:454
  57.1 4.9 %all-to-all-start.2 = ((f32[4,224,128]{2,1,0:T(8,128)}), f32[4,224,128]{2,1,0:T(8,128)S(1)}, u32[]{:S(2)}, u32[]{:S(2)}) async-start(f32[4,224,128]{2,1,0:T(8,128)} %shard_map.50), calls=%async_computation.2 | async-start | bytes 917504 | tf_op jit(solution)/shard_map/all_to_all | solution.py:431
  62.0 3.0 %collective-permute-start.2 = (f32[560,128]{1,0:T(8,128)S(1)}, f32[560,128]{1,0:T(8,128)S(1)}, u32[]{:S(2)}, u32[]{:S(2)}) collective-permute-start(f32[560,128]{1,0:T(8,128)S(1)} %get-tuple-element.56.later), channel_id=1, source_target_pairs={{0,8},{4,12},{8,0},{12,4},{16,24},{20,28},{24,16},{28,20},{32,40},... | collective-permute-start | bytes 860168 | tf_op jit(solution)/shard_map/ppermute | solution.py:454
  65.0 5.5 %collective-permute-done.2.later_arrived = f32[560,128]{1,0:T(8,128)S(1)} collective-permute-done((f32[560,128]{1,0:T(8,128)S(1)}, f32[560,128]{1,0:T(8,128)S(1)}, u32[]{:S(2)}, u32[]{:S(2)}) %collective-permute-start.2) | collective-permute-done | bytes 286752 | tf_op jit(solution)/shard_map/ppermute | solution.py:454
  70.5 5.2 %shard_map.51 = (f32[176,128]{1,0:T(8,128)S(1)}, f32[640,128]{1,0:T(8,128)S(1)}, f32[176,128]{1,0:T(8,128)S(1)}, f32[128,128]{1,0:T(8,128)S(1)}) custom-call(s32[1]{0:T(128)} %bitcast.place, f32[4,224,128]{2,1,0:T(8,128)S(1)} %all-to-all-done.2.everyone, f32[560,128]{1,0:T(8,128)S(1)} %get-tuple-element.56.later, ...), custom_call_target="tpu_custom_call" | custom-call | flops 1000000000 | tf_op jit(solution)/shard_map/pallas_call | solution.py:91
  75.7 4.6 %collective-permute-start.3 = (f32[176,128]{1,0:T(8,128)S(1)}, f32[176,128]{1,0:T(8,128)S(1)}, u32[]{:S(2)}, u32[]{:S(2)}) collective-permute-start(f32[176,128]{1,0:T(8,128)S(1)} %get-tuple-element.57.refs_0_), channel_id=1, source_target_pairs={{0,16},{4,20},{8,24},{12,28},{16,0},{20,4},{24,8},{28,12},{32,48},... | collective-permute-start | bytes 270344 | tf_op jit(solution)/shard_map/ppermute | solution.py:454
  81.2 2.0 %collective-permute-done.3.refs_1_ = f32[176,128]{1,0:T(8,128)S(1)} collective-permute-done((f32[176,128]{1,0:T(8,128)S(1)}, f32[176,128]{1,0:T(8,128)S(1)}, u32[]{:S(2)}, u32[]{:S(2)}) %collective-permute-start.3) | collective-permute-done | bytes 90144 | tf_op jit(solution)/shard_map/ppermute | solution.py:454
  84.1 4.8 %all-to-all-start.3 = ((f32[4,304,128]{2,1,0:T(8,128)}), f32[4,304,128]{2,1,0:T(8,128)S(1)}, u32[]{:S(2)}, u32[]{:S(2)}) async-start(f32[4,304,128]{2,1,0:T(8,128)} %shard_map.53), calls=%async_computation.3 | async-start | bytes 1245184 | tf_op jit(solution)/shard_map/all_to_all | solution.py:431
  88.9 5.2 %collective-permute-start.4 = (f32[384,128]{1,0:T(8,128)S(1)}, f32[384,128]{1,0:T(8,128)S(1)}, u32[]{:S(2)}, u32[]{:S(2)}) collective-permute-start(f32[384,128]{1,0:T(8,128)S(1)} %get-tuple-element.62.later), channel_id=1, source_target_pairs={{0,16},{4,20},{8,24},{12,28},{16,0},{20,4},{24,8},{28,12},{32,48},... | collective-permute-start | bytes 589832 | tf_op jit(solution)/shard_map/ppermute | solution.py:454
  95.2 2.2 %shard_map.54 = (f32[640,256]{1,0:T(8,128)S(1)}, f32[256,256]{1,0:T(8,128)S(1)}) custom-call(f32[4,240,256]{2,1,0:T(8,128)S(1)} %copy-done, f32[768,128]{1,0:T(8,128)S(1)} %copy-done.5, f32[640,128]{1,0:T(8,128)S(1)} %get-tuple-element.66.weights2), custom_call_target="tpu_custom_call" | custom-call | flops 1000000000 | tf_op jit(solution)/shard_map/pallas_call | solution.py:91
  97.4 5.0 %shard_map.55 = (f32[512,128]{1,0:T(8,128)S(1)}, f32[144,128]{1,0:T(8,128)S(1)}, f32[128,128]{1,0:T(8,128)S(1)}) custom-call(s32[1]{0:T(128)} %bitcast.place, f32[4,304,128]{2,1,0:T(8,128)S(1)} %all-to-all-done.3.everyone), custom_call_target="tpu_custom_call" | custom-call | flops 1000000000 | tf_op jit(solution)/shard_map/pallas_call | solution.py:91
  103.1 4.8 %collective-permute-start.5 = (f32[384,128]{1,0:T(8,128)S(1)}, f32[384,128]{1,0:T(8,128)S(1)}, u32[]{:S(2)}, u32[]{:S(2)}) collective-permute-start(f32[384,128]{1,0:T(8,128)S(1)} %shard_map.56.refs_0_), channel_id=1, source_target_pairs={{0,48},{4,52},{8,56},{12,60},{16,32},{20,36},{24,40},{28,44},{32,1... | collective-permute-start | bytes 589832 | tf_op jit(solution)/shard_map/ppermute | solution.py:454
  109.5 5.3 %collective-permute-done.5.refs_1_ = f32[384,128]{1,0:T(8,128)S(1)} collective-permute-done((f32[384,128]{1,0:T(8,128)S(1)}, f32[384,128]{1,0:T(8,128)S(1)}, u32[]{:S(2)}, u32[]{:S(2)}) %collective-permute-start.5) | collective-permute-done | bytes 196640 | tf_op jit(solution)/shard_map/ppermute | solution.py:454
  114.9 12.3 %all_to_all.32.everyone = f32[4,384,128]{2,1,0:T(8,128)S(1)} all-to-all(f32[4,384,128]{2,1,0:T(8,128)S(1)} %shard_map.58), channel_id=1, replica_groups=mesh['leaf'=128,'rhs'=4] {'rhs'}, dimensions={0} | all-to-all | bytes 1572864 | tf_op jit(solution)/shard_map/all_to_all | solution.py:431
  127.2 5.5 %shard_map.59 = (f32[448,128]{1,0:T(8,128)S(1)}, f32[448,128]{1,0:T(8,128)S(1)}, f32[448,128]{1,0:T(8,128)S(1)}) custom-call(f32[4,384,128]{2,1,0:T(8,128)S(1)} %all_to_all.32.everyone), custom_call_target="tpu_custom_call" | custom-call | flops 1000000000 | tf_op jit(solution)/shard_map/pallas_call | solution.py:91
  132.8 4.3 %collective-permute-start.6 = (f32[448,128]{1,0:T(8,128)S(1)}, f32[448,128]{1,0:T(8,128)S(1)}, u32[]{:S(2)}, u32[]{:S(2)}) collective-permute-start(f32[448,128]{1,0:T(8,128)S(1)} %get-tuple-element.78.mine), channel_id=1, source_target_pairs={{0,64},{4,68},{8,72},{12,76},{16,80},{20,84},{24,88},{28,92},{32,9... | collective-permute-start | bytes 688136 | tf_op jit(solution)/shard_map/ppermute | solution.py:454
  139.5 3.9 %collective-permute-start.8 = (f32[192,128]{1,0:T(8,128)S(1)}, f32[192,128]{1,0:T(8,128)S(1)}, u32[]{:S(2)}, u32[]{:S(2)}) collective-permute-start(f32[192,128]{1,0:T(8,128)S(1)} %shard_map.65.later), channel_id=1, source_target_pairs={{0,64},{4,68},{8,72},{12,76},{16,80},{20,84},{24,88},{28,92},{32,9... | collective-permute-start | bytes 294920 | tf_op jit(solution)/shard_map/ppermute | solution.py:454
  144.0 4.9 %shard_map.61 = (f32[320,128]{1,0:T(8,128)S(1)}, f32[320,128]{1,0:T(8,128)S(1)}) custom-call(f32[448,128]{1,0:T(8,128)S(1)} %get-tuple-element.78.mine, f32[448,128]{1,0:T(8,128)S(1)} %collective-permute-done.6.arrived), custom_call_target="tpu_custom_call" | custom-call | flops 1000000000 | tf_op jit(solution)/shard_map/pallas_call | solution.py:91
  149.3 6.1 %collective-permute-start.10 = (f32[320,128]{1,0:T(8,128)S(1)}, f32[320,128]{1,0:T(8,128)S(1)}, u32[]{:S(2)}, u32[]{:S(2)}) collective-permute-start(f32[320,128]{1,0:T(8,128)S(1)} %shard_map.64.mine), channel_id=1, source_target_pairs={{0,128},{4,132},{8,136},{12,140},{16,144},{20,148},{24,152},{28,15... | collective-permute-start | bytes 491528 | tf_op jit(solution)/shard_map/ppermute | solution.py:454
  155.6 1.9 %collective-permute-start.9 = (f32[192,128]{1,0:T(8,128)S(1)}, f32[192,128]{1,0:T(8,128)S(1)}, u32[]{:S(2)}, u32[]{:S(2)}) collective-permute-start(f32[192,128]{1,0:T(8,128)S(1)} %shard_map.66.later), channel_id=1, source_target_pairs={{0,128},{4,132},{8,136},{12,140},{16,144},{20,148},{24,152},{28,15... | collective-permute-start | bytes 294920 | tf_op jit(solution)/shard_map/ppermute | solution.py:454
  159.8 4.9 %shard_map.67 = (f32[192,128]{1,0:T(8,128)S(1)}, f32[192,128]{1,0:T(8,128)S(1)}) custom-call(f32[320,128]{1,0:T(8,128)S(1)} %shard_map.64.mine, f32[320,128]{1,0:T(8,128)S(1)} %collective-permute-done.10.arrived), custom_call_target="tpu_custom_call" | custom-call | flops 1000000000 | tf_op jit(solution)/shard_map/pallas_call | solution.py:91
  166.1 4.9 %all-to-all-start.5 = ((f32[4,144,256]{2,1,0:T(8,128)}), f32[4,144,256]{2,1,0:T(8,128)S(1)}, u32[]{:S(2)}, u32[]{:S(2)}) async-start(f32[4,144,256]{2,1,0:T(8,128)} %shard_map.69), calls=%async_computation.5 | async-start | bytes 1179648 | tf_op jit(solution)/shard_map/all_to_all | solution.py:584
  171.0 7.7 %collective-permute-start.11 = (f32[144,128]{1,0:T(8,128)S(1)}, f32[144,128]{1,0:T(8,128)S(1)}, u32[]{:S(2)}, u32[]{:S(2)}) collective-permute-start(f32[144,128]{1,0:T(8,128)S(1)} %shard_map.68.mine), channel_id=1, source_target_pairs={{0,384},{4,388},{8,392},{12,396},{16,400},{20,404},{24,408},{28,41... | collective-permute-start | bytes 221192 | tf_op jit(solution)/shard_map/ppermute | solution.py:454
  178.7 2.3 %collective-permute-done.11.arrived = f32[144,128]{1,0:T(8,128)S(1)} collective-permute-done((f32[144,128]{1,0:T(8,128)S(1)}, f32[144,128]{1,0:T(8,128)S(1)}, u32[]{:S(2)}, u32[]{:S(2)}) %collective-permute-start.11) | collective-permute-done | bytes 73760 | tf_op jit(solution)/shard_map/ppermute | solution.py:454
  181.0 7.5 %shard_map.70 = f32[16,1024]{1,0:T(8,128)} custom-call(f32[144,128]{1,0:T(8,128)S(1)} %shard_map.68.mine, f32[144,128]{1,0:T(8,128)S(1)} %collective-permute-done.11.arrived, f32[4,144,256]{2,1,0:T(8,128)S(1)} %all-to-all-done.5.got, bf16[1024,1024]{1,0:T(8,128)(2,1)S(1)} %copy-done.3), custom_call_target="tpu_custom_call" | custom-call | flops 1000000000 | tf_op jit(solution)/shard_map/pallas_call | solution.py:91
  (45 shorter events, 16.9 us)
Async XLA Ops:
  0.0 23.0 %copy-start.1 = (bf16[7,128,1024]{2,1,0:T(8,128)(2,1)S(1)}, bf16[7,128,1024]{2,1,0:T(8,128)(2,1)}, u32[]{:S(2)}) copy-start(bf16[7,128,1024]{2,1,0:T(8,128)(2,1)} %bases.1) | copy-start | bytes 5505028
  5.1 17.9 %copy-start = (f32[4,240,256]{2,1,0:T(8,128)S(1)}, f32[4,240,256]{2,1,0:T(8,128)}, u32[]{:S(2)}) copy-start(f32[4,240,256]{2,1,0:T(8,128)} %get-tuple-element.48.send) | copy-start | bytes 2949124
  25.6 4.0 %collective-permute-start = (f32[1344,128]{1,0:T(8,128)S(1)}, f32[1344,128]{1,0:T(8,128)S(1)}, u32[]{:S(2)}, u32[]{:S(2)}) collective-permute-start(f32[1344,128]{1,0:T(8,128)S(1)} %shard_map.47.mine), channel_id=1, source_target_pairs={{0,4},{4,0},{8,12},{12,8},{16,20},{20,16},{24,28},{28,24},{32,36},... | collective-permute-start | bytes 2064392 | tf_op jit(solution)/shard_map/ppermute | solution.py:454
  49.7 6.6 %collective-permute-start.1 = (f32[208,128]{1,0:T(8,128)S(1)}, f32[208,128]{1,0:T(8,128)S(1)}, u32[]{:S(2)}, u32[]{:S(2)}) collective-permute-start(f32[208,128]{1,0:T(8,128)S(1)} %get-tuple-element.49.refs_0_), channel_id=1, source_target_pairs={{0,8},{4,12},{8,0},{12,4},{16,24},{20,28},{24,16},{28,20},{32,40},... | collective-permute-start | bytes 319496 | tf_op jit(solution)/shard_map/ppermute | solution.py:454
  53.7 0.7 copy-start.4
  57.1 13.4 %all-to-all-start.2 = ((f32[4,224,128]{2,1,0:T(8,128)}), f32[4,224,128]{2,1,0:T(8,128)S(1)}, u32[]{:S(2)}, u32[]{:S(2)}) async-start(f32[4,224,128]{2,1,0:T(8,128)} %shard_map.50), calls=%async_computation.2 | async-start | bytes 917504 | tf_op jit(solution)/shard_map/all_to_all | solution.py:431
  62.0 8.5 %collective-permute-start.2 = (f32[560,128]{1,0:T(8,128)S(1)}, f32[560,128]{1,0:T(8,128)S(1)}, u32[]{:S(2)}, u32[]{:S(2)}) collective-permute-start(f32[560,128]{1,0:T(8,128)S(1)} %get-tuple-element.56.later), channel_id=1, source_target_pairs={{0,8},{4,12},{8,0},{12,4},{16,24},{20,28},{24,16},{28,20},{32,40},... | collective-permute-start | bytes 860168 | tf_op jit(solution)/shard_map/ppermute | solution.py:454
  75.7 7.6 %copy-start.6 = (f32[128,128]{1,0:T(8,128)S(1)}, f32[128,128]{1,0:T(8,128)}, u32[]{:S(2)}) copy-start(f32[128,128]{1,0:T(8,128)} %get-tuple-element.64.refs_2_) | copy-start | bytes 196612
  75.7 7.6 %collective-permute-start.3 = (f32[176,128]{1,0:T(8,128)S(1)}, f32[176,128]{1,0:T(8,128)S(1)}, u32[]{:S(2)}, u32[]{:S(2)}) collective-permute-start(f32[176,128]{1,0:T(8,128)S(1)} %get-tuple-element.57.refs_0_), channel_id=1, source_target_pairs={{0,16},{4,20},{8,24},{12,28},{16,0},{20,4},{24,8},{28,12},{32,48},... | collective-permute-start | bytes 270344 | tf_op jit(solution)/shard_map/ppermute | solution.py:454
  84.1 13.3 %all-to-all-start.3 = ((f32[4,304,128]{2,1,0:T(8,128)}), f32[4,304,128]{2,1,0:T(8,128)S(1)}, u32[]{:S(2)}, u32[]{:S(2)}) async-start(f32[4,304,128]{2,1,0:T(8,128)} %shard_map.53), calls=%async_computation.3 | async-start | bytes 1245184 | tf_op jit(solution)/shard_map/all_to_all | solution.py:431
  88.9 13.5 %collective-permute-start.4 = (f32[384,128]{1,0:T(8,128)S(1)}, f32[384,128]{1,0:T(8,128)S(1)}, u32[]{:S(2)}, u32[]{:S(2)}) collective-permute-start(f32[384,128]{1,0:T(8,128)S(1)} %get-tuple-element.62.later), channel_id=1, source_target_pairs={{0,16},{4,20},{8,24},{12,28},{16,0},{20,4},{24,8},{28,12},{32,48},... | collective-permute-start | bytes 589832 | tf_op jit(solution)/shard_map/ppermute | solution.py:454
  94.2 1.0 copy-start.5
  102.4 5.5 %copy-start.2 = (f32[1024,256]{1,0:T(8,128)S(1)}, f32[1024,256]{1,0:T(8,128)}, u32[]{:S(2)}) copy-start(f32[1024,256]{1,0:T(8,128)} %inverse_cols.1) | copy-start | bytes 3145732
  103.1 11.8 %collective-permute-start.5 = (f32[384,128]{1,0:T(8,128)S(1)}, f32[384,128]{1,0:T(8,128)S(1)}, u32[]{:S(2)}, u32[]{:S(2)}) collective-permute-start(f32[384,128]{1,0:T(8,128)S(1)} %shard_map.56.refs_0_), channel_id=1, source_target_pairs={{0,48},{4,52},{8,56},{12,60},{16,32},{20,36},{24,40},{28,44},{32,1... | collective-permute-start | bytes 589832 | tf_op jit(solution)/shard_map/ppermute | solution.py:454
  132.8 11.2 %collective-permute-start.6 = (f32[448,128]{1,0:T(8,128)S(1)}, f32[448,128]{1,0:T(8,128)S(1)}, u32[]{:S(2)}, u32[]{:S(2)}) collective-permute-start(f32[448,128]{1,0:T(8,128)S(1)} %get-tuple-element.78.mine), channel_id=1, source_target_pairs={{0,64},{4,68},{8,72},{12,76},{16,80},{20,84},{24,88},{28,92},{32,9... | collective-permute-start | bytes 688136 | tf_op jit(solution)/shard_map/ppermute | solution.py:454
  137.4 11.6 %collective-permute-start.7 = (f32[320,128]{1,0:T(8,128)S(1)}, f32[320,128]{1,0:T(8,128)S(1)}, u32[]{:S(2)}, u32[]{:S(2)}) collective-permute-start(f32[320,128]{1,0:T(8,128)S(1)} %shard_map.63.later), channel_id=1, source_target_pairs={{0,64},{4,68},{8,72},{12,76},{16,80},{20,84},{24,88},{28,92},{32,9... | collective-permute-start | bytes 491528 | tf_op jit(solution)/shard_map/ppermute | solution.py:454
  139.5 15.8 %collective-permute-start.8 = (f32[192,128]{1,0:T(8,128)S(1)}, f32[192,128]{1,0:T(8,128)S(1)}, u32[]{:S(2)}, u32[]{:S(2)}) collective-permute-start(f32[192,128]{1,0:T(8,128)S(1)} %shard_map.65.later), channel_id=1, source_target_pairs={{0,64},{4,68},{8,72},{12,76},{16,80},{20,84},{24,88},{28,92},{32,9... | collective-permute-start | bytes 294920 | tf_op jit(solution)/shard_map/ppermute | solution.py:454
  149.3 10.6 %collective-permute-start.10 = (f32[320,128]{1,0:T(8,128)S(1)}, f32[320,128]{1,0:T(8,128)S(1)}, u32[]{:S(2)}, u32[]{:S(2)}) collective-permute-start(f32[320,128]{1,0:T(8,128)S(1)} %shard_map.64.mine), channel_id=1, source_target_pairs={{0,128},{4,132},{8,136},{12,140},{16,144},{20,148},{24,152},{28,15... | collective-permute-start | bytes 491528 | tf_op jit(solution)/shard_map/ppermute | solution.py:454
  155.6 9.1 %collective-permute-start.9 = (f32[192,128]{1,0:T(8,128)S(1)}, f32[192,128]{1,0:T(8,128)S(1)}, u32[]{:S(2)}, u32[]{:S(2)}) collective-permute-start(f32[192,128]{1,0:T(8,128)S(1)} %shard_map.66.later), channel_id=1, source_target_pairs={{0,128},{4,132},{8,136},{12,140},{16,144},{20,148},{24,152},{28,15... | collective-permute-start | bytes 294920 | tf_op jit(solution)/shard_map/ppermute | solution.py:454
  165.0 16.1 %copy-start.3 = (bf16[1024,1024]{1,0:T(8,128)(2,1)S(1)}, bf16[1024,1024]{1,0:T(8,128)(2,1)}, u32[]{:S(2)}) copy-start(bf16[1024,1024]{1,0:T(8,128)(2,1)} %get-tuple-element.90.hot) | copy-start | bytes 6291460
  166.1 14.9 %all-to-all-start.5 = ((f32[4,144,256]{2,1,0:T(8,128)}), f32[4,144,256]{2,1,0:T(8,128)S(1)}, u32[]{:S(2)}, u32[]{:S(2)}) async-start(f32[4,144,256]{2,1,0:T(8,128)} %shard_map.69), calls=%async_computation.5 | async-start | bytes 1179648 | tf_op jit(solution)/shard_map/all_to_all | solution.py:584
  171.0 10.0 %collective-permute-start.11 = (f32[144,128]{1,0:T(8,128)S(1)}, f32[144,128]{1,0:T(8,128)S(1)}, u32[]{:S(2)}, u32[]{:S(2)}) collective-permute-start(f32[144,128]{1,0:T(8,128)S(1)} %shard_map.68.mine), channel_id=1, source_target_pairs={{0,384},{4,388},{8,392},{12,396},{16,400},{20,404},{24,408},{28,41... | collective-permute-start | bytes 221192 | tf_op jit(solution)/shard_map/ppermute | solution.py:454

commit v8 on v7

--- a/solution.py
+++ b/solution.py
@@ -238,15 +238,11 @@
         at += count + own
 
 
-def level_body(above, place, everyone, later, later_arrived, panel, far, own_weights, inverse):
-    groups, _, rank = everyone.shape
-    share = rank // groups
-    far[...] = jnp.concatenate([stacked(everyone, level * share, share) for level in range(1, above + 1)], 0)
-    inverse[...] = inverse_of(stacked(everyone, 0, share) + identity(rank))
-    own_upper = everyone[place[0], share : share + own_weights.shape[0], :]
-    own_weights[...] = exact_dot(own_upper, inverse[...], NN)
+def level_panel_body(later, later_arrived, far, own_weights, panel):
+    rank = far.shape[1]
     count = panel.shape[0]
-    panel[...] = later[:count, :] + later_arrived[:count, :] - exact_dot(own_weights[...], far[:rank, :], NT)
+    update = exact_dot(own_weights[...], far[:rank, :], NT)
+    panel[...] = later[:count, :] + later_arrived[:count, :] - update
 
 
 def level_factor_body(above, place, everyone, far, own_weights, inverse):
@@ -500,14 +496,15 @@
         everyone = sum_to_all(panel, arrived, side1) if height == 2 else sum_to_all(panel, arrived, tree)
         if height == 3:
             everyone, carried = lax.optimization_barrier((everyone, carried))
+        far, own_weights, inverse = run(
+            functools.partial(level_factor_body, above),
+            [(above * rank, rank), (above * share + own, rank), square],
+            everyone,
+            place=place,
+        )
         if height == 2:
-            next_panel, far, own_weights, inverse = run(
-                functools.partial(level_body, above),
-                [(above * share + own, rank), (above * rank, rank), (above * share + own, rank), square],
-                everyone,
-                later,
-                later_arrived,
-                place=place,
+            (next_panel,) = run(
+                level_panel_body, [(above * share + own, rank)], later, later_arrived, far, own_weights
             )
             arrived = swap(next_panel, 3)
             rest_rows = above * (above - 1) // 2 * share + (above - 1) * own
@@ -530,12 +527,6 @@
                 far_weights2,
             )
         else:
-            far, own_weights, inverse = run(
-                functools.partial(level_factor_body, above),
-                [(above * rank, rank), (above * share + own, rank), square],
-                everyone,
-                place=place,
-            )
             (panels,) = run(
                 functools.partial(level_all_body, above),
                 [(above * (above + 1) // 2 * share + above * own, rank)],
@@ -579,8 +570,8 @@
         last_panel_body, [(rank + own, rank)], seventh, seventh_arrived, upper, weights, place=place
     )
     arrived = swap(seventh, 7)
-    carried, seventh = lax.optimization_barrier((carried, seventh))
     (send,) = run(carry_last_body, [(groups, rank + own, piece)], carried, weights)
+    send, seventh = lax.optimization_barrier((send, seventh))
     got = lax.all_to_all(send, "rhs", 0, 0)
     (result,) = run(finish_body, [(own, leaf)], seventh, arrived, got, hot)
     return result

time: 189 us -> 188 us (level)
  waiting for transfers between devices: 20.9 us -> 18.7 us
    ppermute x12, waiting for transfers between devices: 20.9 us -> 15.5 us  [local(): swap = lambda block, height: lax.ppermute(block, 'leaf', route(height))]
    all_to_all x2, waiting for transfers between devices: 0.01 us -> 3.22 us  [sum_to_all(): return lax.all_to_all(send, 'rhs', 0, 0)]
    pallas_call x24 -> x25, Pallas kernels: 52.8 us -> 53.1 us  [run(): pl.pallas_call(body, out_shape=[shape_of(out) for out in outs], in_specs=...]
  transfers between devices with their start and end apart: 15 -> 15, of which waited for: 7 -> 7; matrix products, arithmetic and copies ran while one was open for 0% -> 0% of each run, Pallas kernels for 12% -> 16%
where the time goes in v8:
time: 188 us; the launch traced here: 187 us
  starting transfers between devices  63.3 us (34%)
  Pallas kernels  58.1 us (31%)
  blocking collectives  44.4 us (24%)
  waiting for transfers between devices  18.7 us (10%)
    pallas_call x25, Pallas kernels, run(): pl.pallas_call(body, out_shape=[shape_of(out) for out in outs], in_specs=...  53.1 us
    ppermute x12, starting transfers between devices, local(): swap = lambda block, height: lax.ppermute(block, 'leaf', route(height))  48.5 us
    all_to_all x1, blocking collectives, local(): got = lax.all_to_all(send, 'rhs', 0, 0)  17.9 us
    ppermute x12, waiting for transfers between devices, local(): swap = lambda block, height: lax.ppermute(block, 'leaf', route(height))  15.5 us
    all_to_all x1, blocking collectives, local(): everyone = lax.all_to_all(jnp.concatenate([shared, parts], 1), 'rhs', 0, 0)  14.2 us
    all_to_all x1, blocking collectives, sum_to_all(): return lax.all_to_all(send, 'rhs', 0, 0)  12.3 us
    all_to_all x2, starting transfers between devices, sum_to_all(): return lax.all_to_all(send, 'rhs', 0, 0)  9.79 us
    all_to_all x1, starting transfers between devices, local(): got = lax.all_to_all(send, 'rhs', 0, 0)  5.05 us
  transfers between devices with their start and end apart: 15, of which 7 were waited for; matrix products, arithmetic and copies ran while one was open for 0% of the time, Pallas kernels for 16%

profile of v8, /device:TPU:10, one launch (start us, length us, event | category | flops | bytes accessed | tf_op | source)
XLA Modules:
  0.0 186.8 jit_solution(12341418284104801110)
XLA Ops:
  0.0 5.0 %shard_map.46 = (f32[4,240,256]{2,1,0:T(8,128)}, bf16[1024,1024]{1,0:T(8,128)(2,1)}, f32[128,128]{1,0:T(8,128)}) custom-call(s32[1,1024]{1,0:T(1,128)} %refs_0_.1, f32[16,1024]{1,0:T(8,128)} %refs_1_.1, f32[1024,256]{1,0:T(8,128)} %inverse_cols.1, bf16[7,128,1024]{2,1,0:T(8,128)(2,1)} %bases.1), custom_call_target="tpu_custom_call" | custom-call | flops 1000000000 | tf_op jit(solution)/shard_map/pallas_call | solution.py:124
  5.1 17.9 %all_to_all.30.got = f32[4,240,256]{2,1,0:T(8,128)S(1)} all-to-all(f32[4,240,256]{2,1,0:T(8,128)} %get-tuple-element.47.send), channel_id=1, replica_groups=mesh['leaf'=128,'rhs'=4] {'rhs'}, dimensions={0} | all-to-all | bytes 1966080 | tf_op jit(solution)/shard_map/all_to_all | solution.py:465
  23.0 2.6 %shard_map.47.mine = f32[1344,128]{1,0:T(8,128)S(1)} custom-call(f32[4,240,256]{2,1,0:T(8,128)S(1)} %all_to_all.30.got, f32[4,240,256]{2,1,0:T(8,128)S(1)} %copy-done, bf16[7,128,1024]{2,1,0:T(8,128)(2,1)S(1)} %copy-done.1), custom_call_target="tpu_custom_call" | custom-call | flops 1000000000 | tf_op jit(solution)/shard_map/pallas_call | solution.py:91
  25.6 1.9 %collective-permute-start = (f32[1344,128]{1,0:T(8,128)S(1)}, f32[1344,128]{1,0:T(8,128)S(1)}, u32[]{:S(2)}, u32[]{:S(2)}) collective-permute-start(f32[1344,128]{1,0:T(8,128)S(1)} %shard_map.47.mine), channel_id=1, source_target_pairs={{0,4},{4,0},{8,12},{12,8},{16,20},{20,16},{24,28},{28,24},{32,36},... | collective-permute-start | bytes 2064392 | tf_op jit(solution)/shard_map/ppermute | solution.py:450
  27.5 2.1 %collective-permute-done.arrived = f32[1344,128]{1,0:T(8,128)S(1)} collective-permute-done((f32[1344,128]{1,0:T(8,128)S(1)}, f32[1344,128]{1,0:T(8,128)S(1)}, u32[]{:S(2)}, u32[]{:S(2)}) %collective-permute-start) | collective-permute-done | bytes 688160 | tf_op jit(solution)/shard_map/ppermute | solution.py:450
  29.8 14.2 %all_to_all.31.everyone = f32[4,336,128]{2,1,0:T(8,128)S(1)} all-to-all(f32[4,336,128]{2,1,0:T(8,128)S(1)} %pad_maximum_fusion), channel_id=1, replica_groups=mesh['leaf'=128,'rhs'=4] {'rhs'}, dimensions={0} | all-to-all | bytes 1376256 | tf_op jit(solution)/shard_map/all_to_all | solution.py:472
  44.0 5.6 %shard_map.48 = (f32[208,128]{1,0:T(8,128)S(1)}, f32[768,128]{1,0:T(8,128)S(1)}, f32[208,128]{1,0:T(8,128)S(1)}, f32[128,128]{1,0:T(8,128)S(1)}, f32[16,128]{1,0:T(8,128)S(1)}) custom-call(f32[4,336,128]{2,1,0:T(8,128)S(1)} %all_to_all.31.everyone, f32[1344,128]{1,0:T(8,128)S(1)} %shard_map.47.mine, f32[1344,128]{1,0:T(8,128)S(1)} %collective-permute-done.arrived), custom_call_target="tpu_custom_call" | custom-call | flops 1000000000 | tf_op jit(solution)/shard_map/pallas_call | solution.py:91
  49.7 3.1 %collective-permute-start.1 = (f32[208,128]{1,0:T(8,128)S(1)}, f32[208,128]{1,0:T(8,128)S(1)}, u32[]{:S(2)}, u32[]{:S(2)}) collective-permute-start(f32[208,128]{1,0:T(8,128)S(1)} %get-tuple-element.48.refs_0_), channel_id=1, source_target_pairs={{0,8},{4,12},{8,0},{12,4},{16,24},{20,28},{24,16},{28,20},{32,40},... | collective-permute-start | bytes 319496 | tf_op jit(solution)/shard_map/ppermute | solution.py:450
  57.1 4.9 %all-to-all-start.2 = ((f32[4,224,128]{2,1,0:T(8,128)}), f32[4,224,128]{2,1,0:T(8,128)S(1)}, u32[]{:S(2)}, u32[]{:S(2)}) async-start(f32[4,224,128]{2,1,0:T(8,128)} %shard_map.50), calls=%async_computation.2 | async-start | bytes 917504 | tf_op jit(solution)/shard_map/all_to_all | solution.py:427
  62.0 3.0 %collective-permute-start.2 = (f32[560,128]{1,0:T(8,128)S(1)}, f32[560,128]{1,0:T(8,128)S(1)}, u32[]{:S(2)}, u32[]{:S(2)}) collective-permute-start(f32[560,128]{1,0:T(8,128)S(1)} %get-tuple-element.53.later), channel_id=1, source_target_pairs={{0,8},{4,12},{8,0},{12,4},{16,24},{20,28},{24,16},{28,20},{32,40},... | collective-permute-start | bytes 860168 | tf_op jit(solution)/shard_map/ppermute | solution.py:450
  65.0 3.2 %all-to-all-done.2.everyone = f32[4,224,128]{2,1,0:T(8,128)S(1)} async-done(((f32[4,224,128]{2,1,0:T(8,128)}), f32[4,224,128]{2,1,0:T(8,128)S(1)}, u32[]{:S(2)}, u32[]{:S(2)}) %all-to-all-start.2) | async-done | bytes 458784 | tf_op jit(solution)/shard_map/all_to_all | solution.py:427
  68.3 5.3 %shard_map.51 = (f32[640,128]{1,0:T(8,128)S(1)}, f32[176,128]{1,0:T(8,128)S(1)}, f32[128,128]{1,0:T(8,128)S(1)}) custom-call(s32[1]{0:T(128)} %bitcast.1.place, f32[4,224,128]{2,1,0:T(8,128)S(1)} %all-to-all-done.2.everyone), custom_call_target="tpu_custom_call" | custom-call | flops 1000000000 | tf_op jit(solution)/shard_map/pallas_call | solution.py:91
  73.8 4.6 %collective-permute-start.3 = (f32[176,128]{1,0:T(8,128)S(1)}, f32[176,128]{1,0:T(8,128)S(1)}, u32[]{:S(2)}, u32[]{:S(2)}) collective-permute-start(f32[176,128]{1,0:T(8,128)S(1)} %shard_map.52.refs_0_), channel_id=1, source_target_pairs={{0,16},{4,20},{8,24},{12,28},{16,0},{20,4},{24,8},{28,12},{32,48},... | collective-permute-start | bytes 270344 | tf_op jit(solution)/shard_map/ppermute | solution.py:450
  79.3 2.0 %collective-permute-done.3.refs_1_ = f32[176,128]{1,0:T(8,128)S(1)} collective-permute-done((f32[176,128]{1,0:T(8,128)S(1)}, f32[176,128]{1,0:T(8,128)S(1)}, u32[]{:S(2)}, u32[]{:S(2)}) %collective-permute-start.3) | collective-permute-done | bytes 90144 | tf_op jit(solution)/shard_map/ppermute | solution.py:450
  82.3 4.9 %all-to-all-start.3 = ((f32[4,304,128]{2,1,0:T(8,128)}), f32[4,304,128]{2,1,0:T(8,128)S(1)}, u32[]{:S(2)}, u32[]{:S(2)}) async-start(f32[4,304,128]{2,1,0:T(8,128)} %shard_map.54), calls=%async_computation.3 | async-start | bytes 1245184 | tf_op jit(solution)/shard_map/all_to_all | solution.py:427
  87.2 5.2 %collective-permute-start.4 = (f32[384,128]{1,0:T(8,128)S(1)}, f32[384,128]{1,0:T(8,128)S(1)}, u32[]{:S(2)}, u32[]{:S(2)}) collective-permute-start(f32[384,128]{1,0:T(8,128)S(1)} %get-tuple-element.60.later), channel_id=1, source_target_pairs={{0,16},{4,20},{8,24},{12,28},{16,0},{20,4},{24,8},{28,12},{32,48},... | collective-permute-start | bytes 589832 | tf_op jit(solution)/shard_map/ppermute | solution.py:450
  93.4 2.2 %shard_map.55 = (f32[640,256]{1,0:T(8,128)S(1)}, f32[256,256]{1,0:T(8,128)S(1)}) custom-call(f32[4,240,256]{2,1,0:T(8,128)S(1)} %copy-done, f32[768,128]{1,0:T(8,128)S(1)} %copy-done.5, f32[640,128]{1,0:T(8,128)S(1)} %get-tuple-element.64.weights2), custom_call_target="tpu_custom_call" | custom-call | flops 1000000000 | tf_op jit(solution)/shard_map/pallas_call | solution.py:91
  95.6 5.0 %shard_map.56 = (f32[512,128]{1,0:T(8,128)S(1)}, f32[144,128]{1,0:T(8,128)S(1)}, f32[128,128]{1,0:T(8,128)S(1)}) custom-call(s32[1]{0:T(128)} %bitcast.1.place, f32[4,304,128]{2,1,0:T(8,128)S(1)} %all-to-all-done.3.everyone), custom_call_target="tpu_custom_call" | custom-call | flops 1000000000 | tf_op jit(solution)/shard_map/pallas_call | solution.py:91
  101.3 4.8 %collective-permute-start.5 = (f32[384,128]{1,0:T(8,128)S(1)}, f32[384,128]{1,0:T(8,128)S(1)}, u32[]{:S(2)}, u32[]{:S(2)}) collective-permute-start(f32[384,128]{1,0:T(8,128)S(1)} %shard_map.57.refs_0_), channel_id=1, source_target_pairs={{0,48},{4,52},{8,56},{12,60},{16,32},{20,36},{24,40},{28,44},{32,1... | collective-permute-start | bytes 589832 | tf_op jit(solution)/shard_map/ppermute | solution.py:450
  107.8 5.3 %collective-permute-done.5.refs_1_ = f32[384,128]{1,0:T(8,128)S(1)} collective-permute-done((f32[384,128]{1,0:T(8,128)S(1)}, f32[384,128]{1,0:T(8,128)S(1)}, u32[]{:S(2)}, u32[]{:S(2)}) %collective-permute-start.5) | collective-permute-done | bytes 196640 | tf_op jit(solution)/shard_map/ppermute | solution.py:450
  113.1 12.3 %all_to_all.32.everyone = f32[4,384,128]{2,1,0:T(8,128)S(1)} all-to-all(f32[4,384,128]{2,1,0:T(8,128)S(1)} %shard_map.59), channel_id=1, replica_groups=mesh['leaf'=128,'rhs'=4] {'rhs'}, dimensions={0} | all-to-all | bytes 1572864 | tf_op jit(solution)/shard_map/all_to_all | solution.py:427
  125.4 5.5 %shard_map.60 = (f32[448,128]{1,0:T(8,128)S(1)}, f32[448,128]{1,0:T(8,128)S(1)}, f32[448,128]{1,0:T(8,128)S(1)}) custom-call(f32[4,384,128]{2,1,0:T(8,128)S(1)} %all_to_all.32.everyone), custom_call_target="tpu_custom_call" | custom-call | flops 1000000000 | tf_op jit(solution)/shard_map/pallas_call | solution.py:91
  131.0 4.3 %collective-permute-start.6 = (f32[448,128]{1,0:T(8,128)S(1)}, f32[448,128]{1,0:T(8,128)S(1)}, u32[]{:S(2)}, u32[]{:S(2)}) collective-permute-start(f32[448,128]{1,0:T(8,128)S(1)} %get-tuple-element.76.mine), channel_id=1, source_target_pairs={{0,64},{4,68},{8,72},{12,76},{16,80},{20,84},{24,88},{28,92},{32,9... | collective-permute-start | bytes 688136 | tf_op jit(solution)/shard_map/ppermute | solution.py:450
  137.8 3.9 %collective-permute-start.9 = (f32[192,128]{1,0:T(8,128)S(1)}, f32[192,128]{1,0:T(8,128)S(1)}, u32[]{:S(2)}, u32[]{:S(2)}) collective-permute-start(f32[192,128]{1,0:T(8,128)S(1)} %shard_map.66.later), channel_id=1, source_target_pairs={{0,64},{4,68},{8,72},{12,76},{16,80},{20,84},{24,88},{28,92},{32,9... | collective-permute-start | bytes 294920 | tf_op jit(solution)/shard_map/ppermute | solution.py:450
  142.2 4.9 %shard_map.62 = (f32[320,128]{1,0:T(8,128)S(1)}, f32[320,128]{1,0:T(8,128)S(1)}) custom-call(f32[448,128]{1,0:T(8,128)S(1)} %get-tuple-element.76.mine, f32[448,128]{1,0:T(8,128)S(1)} %collective-permute-done.6.arrived), custom_call_target="tpu_custom_call" | custom-call | flops 1000000000 | tf_op jit(solution)/shard_map/pallas_call | solution.py:91
  147.5 6.1 %collective-permute-start.8 = (f32[320,128]{1,0:T(8,128)S(1)}, f32[320,128]{1,0:T(8,128)S(1)}, u32[]{:S(2)}, u32[]{:S(2)}) collective-permute-start(f32[320,128]{1,0:T(8,128)S(1)} %shard_map.65.mine), channel_id=1, source_target_pairs={{0,128},{4,132},{8,136},{12,140},{16,144},{20,148},{24,152},{28,15... | collective-permute-start | bytes 491528 | tf_op jit(solution)/shard_map/ppermute | solution.py:450
  153.9 1.9 %collective-permute-start.10 = (f32[192,128]{1,0:T(8,128)S(1)}, f32[192,128]{1,0:T(8,128)S(1)}, u32[]{:S(2)}, u32[]{:S(2)}) collective-permute-start(f32[192,128]{1,0:T(8,128)S(1)} %shard_map.69.later), channel_id=1, source_target_pairs={{0,128},{4,132},{8,136},{12,140},{16,144},{20,148},{24,152},{28,15... | collective-permute-start | bytes 294920 | tf_op jit(solution)/shard_map/ppermute | solution.py:450
  158.1 4.9 %shard_map.67 = (f32[192,128]{1,0:T(8,128)S(1)}, f32[192,128]{1,0:T(8,128)S(1)}) custom-call(f32[320,128]{1,0:T(8,128)S(1)} %shard_map.65.mine, f32[320,128]{1,0:T(8,128)S(1)} %collective-permute-done.8.arrived), custom_call_target="tpu_custom_call" | custom-call | flops 1000000000 | tf_op jit(solution)/shard_map/pallas_call | solution.py:91
  164.3 5.0 %all-to-all-start.5 = ((f32[4,144,256]{2,1,0:T(8,128)}), f32[4,144,256]{2,1,0:T(8,128)S(1)}, u32[]{:S(2)}, u32[]{:S(2)}) async-start(f32[4,144,256]{2,1,0:T(8,128)} %shard_map.68), calls=%async_computation.5 | async-start | bytes 1179648 | tf_op jit(solution)/shard_map/all_to_all | solution.py:575
  169.4 7.7 %collective-permute-start.11 = (f32[144,128]{1,0:T(8,128)S(1)}, f32[144,128]{1,0:T(8,128)S(1)}, u32[]{:S(2)}, u32[]{:S(2)}) collective-permute-start(f32[144,128]{1,0:T(8,128)S(1)} %shard_map.70.mine), channel_id=1, source_target_pairs={{0,384},{4,388},{8,392},{12,396},{16,400},{20,404},{24,408},{28,41... | collective-permute-start | bytes 221192 | tf_op jit(solution)/shard_map/ppermute | solution.py:450
  177.1 2.3 %collective-permute-done.11.arrived = f32[144,128]{1,0:T(8,128)S(1)} collective-permute-done((f32[144,128]{1,0:T(8,128)S(1)}, f32[144,128]{1,0:T(8,128)S(1)}, u32[]{:S(2)}, u32[]{:S(2)}) %collective-permute-start.11) | collective-permute-done | bytes 73760 | tf_op jit(solution)/shard_map/ppermute | solution.py:450
  179.4 7.5 %shard_map.71 = f32[16,1024]{1,0:T(8,128)} custom-call(f32[144,128]{1,0:T(8,128)S(1)} %shard_map.70.mine, f32[144,128]{1,0:T(8,128)S(1)} %collective-permute-done.11.arrived, f32[4,144,256]{2,1,0:T(8,128)S(1)} %all-to-all-done.5.got, bf16[1024,1024]{1,0:T(8,128)(2,1)S(1)} %copy-done.3), custom_call_target="tpu_custom_call" | custom-call | flops 1000000000 | tf_op jit(solution)/shard_map/pallas_call | solution.py:91
  (46 shorter events, 17.1 us)
Async XLA Ops:
  0.0 23.0 %copy-start.1 = (bf16[7,128,1024]{2,1,0:T(8,128)(2,1)S(1)}, bf16[7,128,1024]{2,1,0:T(8,128)(2,1)}, u32[]{:S(2)}) copy-start(bf16[7,128,1024]{2,1,0:T(8,128)(2,1)} %bases.1) | copy-start | bytes 5505028
  5.1 17.9 %copy-start = (f32[4,240,256]{2,1,0:T(8,128)S(1)}, f32[4,240,256]{2,1,0:T(8,128)}, u32[]{:S(2)}) copy-start(f32[4,240,256]{2,1,0:T(8,128)} %get-tuple-element.47.send) | copy-start | bytes 2949124
  25.6 4.0 %collective-permute-start = (f32[1344,128]{1,0:T(8,128)S(1)}, f32[1344,128]{1,0:T(8,128)S(1)}, u32[]{:S(2)}, u32[]{:S(2)}) collective-permute-start(f32[1344,128]{1,0:T(8,128)S(1)} %shard_map.47.mine), channel_id=1, source_target_pairs={{0,4},{4,0},{8,12},{12,8},{16,20},{20,16},{24,28},{28,24},{32,36},... | collective-permute-start | bytes 2064392 | tf_op jit(solution)/shard_map/ppermute | solution.py:450
  49.7 6.6 %collective-permute-start.1 = (f32[208,128]{1,0:T(8,128)S(1)}, f32[208,128]{1,0:T(8,128)S(1)}, u32[]{:S(2)}, u32[]{:S(2)}) collective-permute-start(f32[208,128]{1,0:T(8,128)S(1)} %get-tuple-element.48.refs_0_), channel_id=1, source_target_pairs={{0,8},{4,12},{8,0},{12,4},{16,24},{20,28},{24,16},{28,20},{32,40},... | collective-permute-start | bytes 319496 | tf_op jit(solution)/shard_map/ppermute | solution.py:450
  53.7 0.7 copy-start.4
  57.1 11.2 %all-to-all-start.2 = ((f32[4,224,128]{2,1,0:T(8,128)}), f32[4,224,128]{2,1,0:T(8,128)S(1)}, u32[]{:S(2)}, u32[]{:S(2)}) async-start(f32[4,224,128]{2,1,0:T(8,128)} %shard_map.50), calls=%async_computation.2 | async-start | bytes 917504 | tf_op jit(solution)/shard_map/all_to_all | solution.py:427
  62.0 11.6 %collective-permute-start.2 = (f32[560,128]{1,0:T(8,128)S(1)}, f32[560,128]{1,0:T(8,128)S(1)}, u32[]{:S(2)}, u32[]{:S(2)}) collective-permute-start(f32[560,128]{1,0:T(8,128)S(1)} %get-tuple-element.53.later), channel_id=1, source_target_pairs={{0,8},{4,12},{8,0},{12,4},{16,24},{20,28},{24,16},{28,20},{32,40},... | collective-permute-start | bytes 860168 | tf_op jit(solution)/shard_map/ppermute | solution.py:450
  73.8 7.6 %copy-start.6 = (f32[128,128]{1,0:T(8,128)S(1)}, f32[128,128]{1,0:T(8,128)}, u32[]{:S(2)}) copy-start(f32[128,128]{1,0:T(8,128)} %get-tuple-element.62.refs_2_) | copy-start | bytes 196612
  73.8 7.6 %collective-permute-start.3 = (f32[176,128]{1,0:T(8,128)S(1)}, f32[176,128]{1,0:T(8,128)S(1)}, u32[]{:S(2)}, u32[]{:S(2)}) collective-permute-start(f32[176,128]{1,0:T(8,128)S(1)} %shard_map.52.refs_0_), channel_id=1, source_target_pairs={{0,16},{4,20},{8,24},{12,28},{16,0},{20,4},{24,8},{28,12},{32,48},... | collective-permute-start | bytes 270344 | tf_op jit(solution)/shard_map/ppermute | solution.py:450
  82.3 13.4 %all-to-all-start.3 = ((f32[4,304,128]{2,1,0:T(8,128)}), f32[4,304,128]{2,1,0:T(8,128)S(1)}, u32[]{:S(2)}, u32[]{:S(2)}) async-start(f32[4,304,128]{2,1,0:T(8,128)} %shard_map.54), calls=%async_computation.3 | async-start | bytes 1245184 | tf_op jit(solution)/shard_map/all_to_all | solution.py:427
  87.2 13.5 %collective-permute-start.4 = (f32[384,128]{1,0:T(8,128)S(1)}, f32[384,128]{1,0:T(8,128)S(1)}, u32[]{:S(2)}, u32[]{:S(2)}) collective-permute-start(f32[384,128]{1,0:T(8,128)S(1)} %get-tuple-element.60.later), channel_id=1, source_target_pairs={{0,16},{4,20},{8,24},{12,28},{16,0},{20,4},{24,8},{28,12},{32,48},... | collective-permute-start | bytes 589832 | tf_op jit(solution)/shard_map/ppermute | solution.py:450
  92.4 1.0 copy-start.5
  100.7 5.5 %copy-start.2 = (f32[1024,256]{1,0:T(8,128)S(1)}, f32[1024,256]{1,0:T(8,128)}, u32[]{:S(2)}) copy-start(f32[1024,256]{1,0:T(8,128)} %inverse_cols.1) | copy-start | bytes 3145732
  101.3 11.8 %collective-permute-start.5 = (f32[384,128]{1,0:T(8,128)S(1)}, f32[384,128]{1,0:T(8,128)S(1)}, u32[]{:S(2)}, u32[]{:S(2)}) collective-permute-start(f32[384,128]{1,0:T(8,128)S(1)} %shard_map.57.refs_0_), channel_id=1, source_target_pairs={{0,48},{4,52},{8,56},{12,60},{16,32},{20,36},{24,40},{28,44},{32,1... | collective-permute-start | bytes 589832 | tf_op jit(solution)/shard_map/ppermute | solution.py:450
  131.0 11.2 %collective-permute-start.6 = (f32[448,128]{1,0:T(8,128)S(1)}, f32[448,128]{1,0:T(8,128)S(1)}, u32[]{:S(2)}, u32[]{:S(2)}) collective-permute-start(f32[448,128]{1,0:T(8,128)S(1)} %get-tuple-element.76.mine), channel_id=1, source_target_pairs={{0,64},{4,68},{8,72},{12,76},{16,80},{20,84},{24,88},{28,92},{32,9... | collective-permute-start | bytes 688136 | tf_op jit(solution)/shard_map/ppermute | solution.py:450
  135.6 11.6 %collective-permute-start.7 = (f32[320,128]{1,0:T(8,128)S(1)}, f32[320,128]{1,0:T(8,128)S(1)}, u32[]{:S(2)}, u32[]{:S(2)}) collective-permute-start(f32[320,128]{1,0:T(8,128)S(1)} %shard_map.64.later), channel_id=1, source_target_pairs={{0,64},{4,68},{8,72},{12,76},{16,80},{20,84},{24,88},{28,92},{32,9... | collective-permute-start | bytes 491528 | tf_op jit(solution)/shard_map/ppermute | solution.py:450
  137.8 15.8 %collective-permute-start.9 = (f32[192,128]{1,0:T(8,128)S(1)}, f32[192,128]{1,0:T(8,128)S(1)}, u32[]{:S(2)}, u32[]{:S(2)}) collective-permute-start(f32[192,128]{1,0:T(8,128)S(1)} %shard_map.66.later), channel_id=1, source_target_pairs={{0,64},{4,68},{8,72},{12,76},{16,80},{20,84},{24,88},{28,92},{32,9... | collective-permute-start | bytes 294920 | tf_op jit(solution)/shard_map/ppermute | solution.py:450
  147.5 10.6 %collective-permute-start.8 = (f32[320,128]{1,0:T(8,128)S(1)}, f32[320,128]{1,0:T(8,128)S(1)}, u32[]{:S(2)}, u32[]{:S(2)}) collective-permute-start(f32[320,128]{1,0:T(8,128)S(1)} %shard_map.65.mine), channel_id=1, source_target_pairs={{0,128},{4,132},{8,136},{12,140},{16,144},{20,148},{24,152},{28,15... | collective-permute-start | bytes 491528 | tf_op jit(solution)/shard_map/ppermute | solution.py:450
  153.9 10.2 %collective-permute-start.10 = (f32[192,128]{1,0:T(8,128)S(1)}, f32[192,128]{1,0:T(8,128)S(1)}, u32[]{:S(2)}, u32[]{:S(2)}) collective-permute-start(f32[192,128]{1,0:T(8,128)S(1)} %shard_map.69.later), channel_id=1, source_target_pairs={{0,128},{4,132},{8,136},{12,140},{16,144},{20,148},{24,152},{28,15... | collective-permute-start | bytes 294920 | tf_op jit(solution)/shard_map/ppermute | solution.py:450
  164.1 15.3 %copy-start.3 = (bf16[1024,1024]{1,0:T(8,128)(2,1)S(1)}, bf16[1024,1024]{1,0:T(8,128)(2,1)}, u32[]{:S(2)}) copy-start(bf16[1024,1024]{1,0:T(8,128)(2,1)} %get-tuple-element.88.hot) | copy-start | bytes 6291460
  164.3 15.0 %all-to-all-start.5 = ((f32[4,144,256]{2,1,0:T(8,128)}), f32[4,144,256]{2,1,0:T(8,128)S(1)}, u32[]{:S(2)}, u32[]{:S(2)}) async-start(f32[4,144,256]{2,1,0:T(8,128)} %shard_map.68), calls=%async_computation.5 | async-start | bytes 1179648 | tf_op jit(solution)/shard_map/all_to_all | solution.py:575
  169.4 10.0 %collective-permute-start.11 = (f32[144,128]{1,0:T(8,128)S(1)}, f32[144,128]{1,0:T(8,128)S(1)}, u32[]{:S(2)}, u32[]{:S(2)}) collective-permute-start(f32[144,128]{1,0:T(8,128)S(1)} %shard_map.70.mine), channel_id=1, source_target_pairs={{0,384},{4,388},{8,392},{12,396},{16,400},{20,404},{24,408},{28,41... | collective-permute-start | bytes 221192 | tf_op jit(solution)/shard_map/ppermute | solution.py:450

commit v9 on v8

--- a/solution.py
+++ b/solution.py
@@ -151,15 +151,15 @@
     return jnp.concatenate([everyone[group, low : low + count, :] for group in range(everyone.shape[0])], 0)
 
 
-def start_body(wait, order, sides, inverse_cols, bases, send, hot, tree):
+def start_body(wait, order, sides, inverse_cols, bases, send, tree):
     levels, rank, leaf = bases.shape
     groups, _, piece = send.shape
     share = rank // groups
     own = sides.shape[0]
     wait(0)
-    hot[...] = one_hot(order[...])
+    hot = one_hot(order[...])
     wait(1)
-    ordered = dot_left_parts(sides[...], hot[...], NN)
+    ordered = dot_left_parts(sides[...], hot, NN)
     for group in range(groups):
         send[group, levels * share :, :] = ordered[:, group * piece : (group + 1) * piece]
     for part in range(leaf // rank):
@@ -174,6 +174,11 @@
         for level in range(levels):
             low = level * rank + group * share
             send[group, level * share : (level + 1) * share, :] = applied[low : low + share]
+
+
+def places_body(order, hot):
+    columns = lax.broadcasted_iota(jnp.int32, hot.shape, 1)
+    hot[...] = jnp.where(columns == order[...], 1.0, 0.0).astype(jnp.bfloat16)
 
 
 def gram_body(got, send, bases, gram):
@@ -406,7 +411,7 @@
     top = exact_dot(mine[rank:, :] + arrived[rank:, :], inverse, NN)
     slope = jnp.concatenate([got[group, :rank, :] for group in range(groups)], 1)
     base = jnp.concatenate([got[group, rank:, :] for group in range(groups)], 1)
-    out[...] = dot_left_parts(base - exact_dot(top, slope, NN), hot[...], NT)
+    out[...] = dot_left_parts(base - exact_dot(top, slope, NN), hot[...], NN)
 
 
 def add_body(*refs):
@@ -450,11 +455,10 @@
     swap = lambda block, height: lax.ppermute(block, "leaf", route(height))
 
     place = lax.axis_index("rhs").reshape(1)
-    send, hot, tree = run_loading(
+    send, tree = run_loading(
         start_body,
         [
             (groups, levels * share + own, piece),
-            jax.ShapeDtypeStruct((leaf, leaf), jnp.bfloat16),
             (leaf // rank * own, rank),
         ],
         ordering,
@@ -573,6 +577,10 @@
     (send,) = run(carry_last_body, [(groups, rank + own, piece)], carried, weights)
     send, seventh = lax.optimization_barrier((send, seventh))
     got = lax.all_to_all(send, "rhs", 0, 0)
+    late_order, carried = lax.optimization_barrier((ordering, carried))
+    (hot,) = run(
+        places_body, [jax.ShapeDtypeStruct((leaf, leaf), jnp.bfloat16)], late_order.reshape(leaf, 1)
+    )
     (result,) = run(finish_body, [(own, leaf)], seventh, arrived, got, hot)
     return result
 

time: 188 us -> 188 us (level)
  the two profiles are of different devices: /device:TPU:10 before, /device:TPU:74 now
where the time goes in v9:
time: 188 us; the launch traced here: 187 us
  starting transfers between devices  63 us (34%)
  Pallas kernels  57.9 us (31%)
  blocking collectives  44.7 us (24%)
  waiting for transfers between devices  19 us (10%)
  local copies, waits for them, and re-layouts  2.05 us (1%)
    pallas_call x26, Pallas kernels, run(): pl.pallas_call(body, out_shape=[shape_of(out) for out in outs], in_specs=...  52.7 us
    ppermute x12, starting transfers between devices, local(): swap = lambda block, height: lax.ppermute(block, 'leaf', route(height))  48.3 us
    all_to_all x1, blocking collectives, local(): got = lax.all_to_all(send, 'rhs', 0, 0)  17.9 us
    ppermute x12, waiting for transfers between devices, local(): swap = lambda block, height: lax.ppermute(block, 'leaf', route(height))  15.1 us
    all_to_all x1, blocking collectives, local(): everyone = lax.all_to_all(jnp.concatenate([shared, parts], 1), 'rhs', 0, 0)  14.2 us
    all_to_all x1, blocking collectives, sum_to_all(): return lax.all_to_all(send, 'rhs', 0, 0)  12.6 us
    all_to_all x2, starting transfers between devices, sum_to_all(): return lax.all_to_all(send, 'rhs', 0, 0)  9.8 us
    pallas_call x1, Pallas kernels, run_loading(): pl.pallas_call(loading, out_shape=[shape_of(out) for out in outs], in_spe...  5.24 us
  transfers between devices with their start and end apart: 15, of which 7 were waited for; matrix products, arithmetic and copies ran while one was open for 0% of the time, Pallas kernels for 16%

profile of v9, /device:TPU:74, one launch (start us, length us, event | category | flops | bytes accessed | tf_op | source)
XLA Modules:
  0.0 187.2 jit_solution(8727052103774631619)
XLA Ops:
  0.0 5.2 %shard_map.46 = (f32[4,240,256]{2,1,0:T(8,128)}, f32[128,128]{1,0:T(8,128)}) custom-call(s32[1,1024]{1,0:T(1,128)} %refs_0_.1, f32[16,1024]{1,0:T(8,128)} %refs_1_.1, f32[1024,256]{1,0:T(8,128)} %inverse_cols.1, bf16[7,128,1024]{2,1,0:T(8,128)(2,1)} %bases.1), custom_call_target="tpu_custom_call" | custom-call | flops 1000000000 | tf_op jit(solution)/shard_map/pallas_call | solution.py:124
  5.3 17.9 %all_to_all.30.got = f32[4,240,256]{2,1,0:T(8,128)S(1)} all-to-all(f32[4,240,256]{2,1,0:T(8,128)} %get-tuple-element.47.send), channel_id=1, replica_groups=mesh['leaf'=128,'rhs'=4] {'rhs'}, dimensions={0} | all-to-all | bytes 1966080 | tf_op jit(solution)/shard_map/all_to_all | solution.py:469
  23.2 2.6 %shard_map.47.mine = f32[1344,128]{1,0:T(8,128)S(1)} custom-call(f32[4,240,256]{2,1,0:T(8,128)S(1)} %all_to_all.30.got, f32[4,240,256]{2,1,0:T(8,128)S(1)} %copy-done, bf16[7,128,1024]{2,1,0:T(8,128)(2,1)S(1)} %copy-done.1), custom_call_target="tpu_custom_call" | custom-call | flops 1000000000 | tf_op jit(solution)/shard_map/pallas_call | solution.py:91
  27.7 2.1 %collective-permute-done.arrived = f32[1344,128]{1,0:T(8,128)S(1)} collective-permute-done((f32[1344,128]{1,0:T(8,128)S(1)}, f32[1344,128]{1,0:T(8,128)S(1)}, u32[]{:S(2)}, u32[]{:S(2)}) %collective-permute-start) | collective-permute-done | bytes 688160 | tf_op jit(solution)/shard_map/ppermute | solution.py:455
  30.0 14.2 %all_to_all.31.everyone = f32[4,336,128]{2,1,0:T(8,128)S(1)} all-to-all(f32[4,336,128]{2,1,0:T(8,128)S(1)} %pad_maximum_fusion), channel_id=1, replica_groups=mesh['leaf'=128,'rhs'=4] {'rhs'}, dimensions={0} | all-to-all | bytes 1376256 | tf_op jit(solution)/shard_map/all_to_all | solution.py:476
  44.2 5.6 %shard_map.48 = (f32[208,128]{1,0:T(8,128)S(1)}, f32[768,128]{1,0:T(8,128)S(1)}, f32[208,128]{1,0:T(8,128)S(1)}, f32[128,128]{1,0:T(8,128)S(1)}, f32[16,128]{1,0:T(8,128)S(1)}) custom-call(f32[4,336,128]{2,1,0:T(8,128)S(1)} %all_to_all.31.everyone, f32[1344,128]{1,0:T(8,128)S(1)} %shard_map.47.mine, f32[1344,128]{1,0:T(8,128)S(1)} %collective-permute-done.arrived), custom_call_target="tpu_custom_call" | custom-call | flops 1000000000 | tf_op jit(solution)/shard_map/pallas_call | solution.py:91
  49.9 2.4 %collective-permute-start.1 = (f32[208,128]{1,0:T(8,128)S(1)}, f32[208,128]{1,0:T(8,128)S(1)}, u32[]{:S(2)}, u32[]{:S(2)}) collective-permute-start(f32[208,128]{1,0:T(8,128)S(1)} %get-tuple-element.48.refs_0_), channel_id=1, source_target_pairs={{0,8},{4,12},{8,0},{12,4},{16,24},{20,28},{24,16},{28,20},{32,40},... | collective-permute-start | bytes 319496 | tf_op jit(solution)/shard_map/ppermute | solution.py:455
  54.0 2.5 %collective-permute-done.1.refs_1_ = f32[208,128]{1,0:T(8,128)S(1)} collective-permute-done((f32[208,128]{1,0:T(8,128)S(1)}, f32[208,128]{1,0:T(8,128)S(1)}, u32[]{:S(2)}, u32[]{:S(2)}) %collective-permute-start.1) | collective-permute-done | bytes 106528 | tf_op jit(solution)/shard_map/ppermute | solution.py:455
  57.3 4.9 %all-to-all-start.2 = ((f32[4,224,128]{2,1,0:T(8,128)}), f32[4,224,128]{2,1,0:T(8,128)S(1)}, u32[]{:S(2)}, u32[]{:S(2)}) async-start(f32[4,224,128]{2,1,0:T(8,128)} %shard_map.50), calls=%async_computation.2 | async-start | bytes 917504 | tf_op jit(solution)/shard_map/all_to_all | solution.py:432
  62.2 2.3 %collective-permute-start.2 = (f32[560,128]{1,0:T(8,128)S(1)}, f32[560,128]{1,0:T(8,128)S(1)}, u32[]{:S(2)}, u32[]{:S(2)}) collective-permute-start(f32[560,128]{1,0:T(8,128)S(1)} %get-tuple-element.53.later), channel_id=1, source_target_pairs={{0,8},{4,12},{8,0},{12,4},{16,24},{20,28},{24,16},{28,20},{32,40},... | collective-permute-start | bytes 860168 | tf_op jit(solution)/shard_map/ppermute | solution.py:455
  64.5 3.9 %all-to-all-done.2.everyone = f32[4,224,128]{2,1,0:T(8,128)S(1)} async-done(((f32[4,224,128]{2,1,0:T(8,128)}), f32[4,224,128]{2,1,0:T(8,128)S(1)}, u32[]{:S(2)}, u32[]{:S(2)}) %all-to-all-start.2) | async-done | bytes 458784 | tf_op jit(solution)/shard_map/all_to_all | solution.py:432
  68.4 5.3 %shard_map.51 = (f32[640,128]{1,0:T(8,128)S(1)}, f32[176,128]{1,0:T(8,128)S(1)}, f32[128,128]{1,0:T(8,128)S(1)}) custom-call(s32[1]{0:T(128)} %bitcast.1.place, f32[4,224,128]{2,1,0:T(8,128)S(1)} %all-to-all-done.2.everyone), custom_call_target="tpu_custom_call" | custom-call | flops 1000000000 | tf_op jit(solution)/shard_map/pallas_call | solution.py:91
  74.0 4.6 %collective-permute-start.3 = (f32[176,128]{1,0:T(8,128)S(1)}, f32[176,128]{1,0:T(8,128)S(1)}, u32[]{:S(2)}, u32[]{:S(2)}) collective-permute-start(f32[176,128]{1,0:T(8,128)S(1)} %shard_map.52.refs_0_), channel_id=1, source_target_pairs={{0,16},{4,20},{8,24},{12,28},{16,0},{20,4},{24,8},{28,12},{32,48},... | collective-permute-start | bytes 270344 | tf_op jit(solution)/shard_map/ppermute | solution.py:455
  79.5 2.0 %collective-permute-done.3.refs_1_ = f32[176,128]{1,0:T(8,128)S(1)} collective-permute-done((f32[176,128]{1,0:T(8,128)S(1)}, f32[176,128]{1,0:T(8,128)S(1)}, u32[]{:S(2)}, u32[]{:S(2)}) %collective-permute-start.3) | collective-permute-done | bytes 90144 | tf_op jit(solution)/shard_map/ppermute | solution.py:455
  82.4 4.9 %all-to-all-start.3 = ((f32[4,304,128]{2,1,0:T(8,128)}), f32[4,304,128]{2,1,0:T(8,128)S(1)}, u32[]{:S(2)}, u32[]{:S(2)}) async-start(f32[4,304,128]{2,1,0:T(8,128)} %shard_map.54), calls=%async_computation.3 | async-start | bytes 1245184 | tf_op jit(solution)/shard_map/all_to_all | solution.py:432
  87.3 5.3 %collective-permute-start.4 = (f32[384,128]{1,0:T(8,128)S(1)}, f32[384,128]{1,0:T(8,128)S(1)}, u32[]{:S(2)}, u32[]{:S(2)}) collective-permute-start(f32[384,128]{1,0:T(8,128)S(1)} %get-tuple-element.60.later), channel_id=1, source_target_pairs={{0,16},{4,20},{8,24},{12,28},{16,0},{20,4},{24,8},{28,12},{32,48},... | collective-permute-start | bytes 589832 | tf_op jit(solution)/shard_map/ppermute | solution.py:455
  93.6 2.2 %shard_map.55 = (f32[640,256]{1,0:T(8,128)S(1)}, f32[256,256]{1,0:T(8,128)S(1)}) custom-call(f32[4,240,256]{2,1,0:T(8,128)S(1)} %copy-done, f32[768,128]{1,0:T(8,128)S(1)} %copy-done.4, f32[640,128]{1,0:T(8,128)S(1)} %get-tuple-element.64.weights2), custom_call_target="tpu_custom_call" | custom-call | flops 1000000000 | tf_op jit(solution)/shard_map/pallas_call | solution.py:91
  95.8 5.0 %shard_map.56 = (f32[512,128]{1,0:T(8,128)S(1)}, f32[144,128]{1,0:T(8,128)S(1)}, f32[128,128]{1,0:T(8,128)S(1)}) custom-call(s32[1]{0:T(128)} %bitcast.1.place, f32[4,304,128]{2,1,0:T(8,128)S(1)} %all-to-all-done.3.everyone), custom_call_target="tpu_custom_call" | custom-call | flops 1000000000 | tf_op jit(solution)/shard_map/pallas_call | solution.py:91
  101.5 4.8 %collective-permute-start.5 = (f32[384,128]{1,0:T(8,128)S(1)}, f32[384,128]{1,0:T(8,128)S(1)}, u32[]{:S(2)}, u32[]{:S(2)}) collective-permute-start(f32[384,128]{1,0:T(8,128)S(1)} %shard_map.57.refs_0_), channel_id=1, source_target_pairs={{0,48},{4,52},{8,56},{12,60},{16,32},{20,36},{24,40},{28,44},{32,1... | collective-permute-start | bytes 589832 | tf_op jit(solution)/shard_map/ppermute | solution.py:455
  108.0 4.6 %collective-permute-done.5.refs_1_ = f32[384,128]{1,0:T(8,128)S(1)} collective-permute-done((f32[384,128]{1,0:T(8,128)S(1)}, f32[384,128]{1,0:T(8,128)S(1)}, u32[]{:S(2)}, u32[]{:S(2)}) %collective-permute-start.5) | collective-permute-done | bytes 196640 | tf_op jit(solution)/shard_map/ppermute | solution.py:455
  112.6 12.6 %all_to_all.32.everyone = f32[4,384,128]{2,1,0:T(8,128)S(1)} all-to-all(f32[4,384,128]{2,1,0:T(8,128)S(1)} %shard_map.59), channel_id=1, replica_groups=mesh['leaf'=128,'rhs'=4] {'rhs'}, dimensions={0} | all-to-all | bytes 1572864 | tf_op jit(solution)/shard_map/all_to_all | solution.py:432
  125.2 5.5 %shard_map.60 = (f32[448,128]{1,0:T(8,128)S(1)}, f32[448,128]{1,0:T(8,128)S(1)}, f32[448,128]{1,0:T(8,128)S(1)}) custom-call(f32[4,384,128]{2,1,0:T(8,128)S(1)} %all_to_all.32.everyone), custom_call_target="tpu_custom_call" | custom-call | flops 1000000000 | tf_op jit(solution)/shard_map/pallas_call | solution.py:91
  133.0 3.9 %collective-permute-start.7 = (f32[320,128]{1,0:T(8,128)S(1)}, f32[320,128]{1,0:T(8,128)S(1)}, u32[]{:S(2)}, u32[]{:S(2)}) collective-permute-start(f32[320,128]{1,0:T(8,128)S(1)} %shard_map.64.later), channel_id=1, source_target_pairs={{0,64},{4,68},{8,72},{12,76},{16,80},{20,84},{24,88},{28,92},{32,9... | collective-permute-start | bytes 491528 | tf_op jit(solution)/shard_map/ppermute | solution.py:455
  137.2 1.9 %collective-permute-start.9 = (f32[192,128]{1,0:T(8,128)S(1)}, f32[192,128]{1,0:T(8,128)S(1)}, u32[]{:S(2)}, u32[]{:S(2)}) collective-permute-start(f32[192,128]{1,0:T(8,128)S(1)} %shard_map.66.later), channel_id=1, source_target_pairs={{0,64},{4,68},{8,72},{12,76},{16,80},{20,84},{24,88},{28,92},{32,9... | collective-permute-start | bytes 294920 | tf_op jit(solution)/shard_map/ppermute | solution.py:455
  139.7 4.9 %shard_map.62 = (f32[320,128]{1,0:T(8,128)S(1)}, f32[320,128]{1,0:T(8,128)S(1)}) custom-call(f32[448,128]{1,0:T(8,128)S(1)} %get-tuple-element.76.mine, f32[448,128]{1,0:T(8,128)S(1)} %collective-permute-done.6.arrived), custom_call_target="tpu_custom_call" | custom-call | flops 1000000000 | tf_op jit(solution)/shard_map/pallas_call | solution.py:91
  144.9 6.1 %collective-permute-start.8 = (f32[320,128]{1,0:T(8,128)S(1)}, f32[320,128]{1,0:T(8,128)S(1)}, u32[]{:S(2)}, u32[]{:S(2)}) collective-permute-start(f32[320,128]{1,0:T(8,128)S(1)} %shard_map.65.mine), channel_id=1, source_target_pairs={{0,128},{4,132},{8,136},{12,140},{16,144},{20,148},{24,152},{28,15... | collective-permute-start | bytes 491528 | tf_op jit(solution)/shard_map/ppermute | solution.py:455
  151.3 1.9 %collective-permute-start.10 = (f32[192,128]{1,0:T(8,128)S(1)}, f32[192,128]{1,0:T(8,128)S(1)}, u32[]{:S(2)}, u32[]{:S(2)}) collective-permute-start(f32[192,128]{1,0:T(8,128)S(1)} %shard_map.69.later), channel_id=1, source_target_pairs={{0,128},{4,132},{8,136},{12,140},{16,144},{20,148},{24,152},{28,15... | collective-permute-start | bytes 294920 | tf_op jit(solution)/shard_map/ppermute | solution.py:455
  153.6 2.0 %collective-permute-done.8.arrived = f32[320,128]{1,0:T(8,128)S(1)} collective-permute-done((f32[320,128]{1,0:T(8,128)S(1)}, f32[320,128]{1,0:T(8,128)S(1)}, u32[]{:S(2)}, u32[]{:S(2)}) %collective-permute-start.8) | collective-permute-done | bytes 163872 | tf_op jit(solution)/shard_map/ppermute | solution.py:455
  155.6 4.9 %shard_map.67 = (f32[192,128]{1,0:T(8,128)S(1)}, f32[192,128]{1,0:T(8,128)S(1)}) custom-call(f32[320,128]{1,0:T(8,128)S(1)} %shard_map.65.mine, f32[320,128]{1,0:T(8,128)S(1)} %collective-permute-done.8.arrived), custom_call_target="tpu_custom_call" | custom-call | flops 1000000000 | tf_op jit(solution)/shard_map/pallas_call | solution.py:91
  161.9 4.9 %all-to-all-start.5 = ((f32[4,144,256]{2,1,0:T(8,128)}), f32[4,144,256]{2,1,0:T(8,128)S(1)}, u32[]{:S(2)}, u32[]{:S(2)}) async-start(f32[4,144,256]{2,1,0:T(8,128)} %shard_map.68), calls=%async_computation.5 | async-start | bytes 1179648 | tf_op jit(solution)/shard_map/all_to_all | solution.py:579
  167.0 11.2 %collective-permute-start.11 = (f32[144,128]{1,0:T(8,128)S(1)}, f32[144,128]{1,0:T(8,128)S(1)}, u32[]{:S(2)}, u32[]{:S(2)}) collective-permute-start(f32[144,128]{1,0:T(8,128)S(1)} %shard_map.70.mine), channel_id=1, source_target_pairs={{0,384},{4,388},{8,392},{12,396},{16,400},{20,404},{24,408},{28,41... | collective-permute-start | bytes 221192 | tf_op jit(solution)/shard_map/ppermute | solution.py:455
  180.5 6.6 %shard_map.72 = f32[16,1024]{1,0:T(8,128)} custom-call(f32[144,128]{1,0:T(8,128)S(1)} %shard_map.70.mine, f32[144,128]{1,0:T(8,128)S(1)} %collective-permute-done.11.arrived, f32[4,144,256]{2,1,0:T(8,128)S(1)} %all-to-all-done.5.got, bf16[1024,1024]{1,0:T(8,128)(2,1)S(1)} %shard_map.71.hot), custom_call_target="tpu_custom_call" | custom-call | flops 1000000000 | tf_op jit(solution)/shard_map/pallas_call | solution.py:91
  (48 shorter events, 17.9 us)
Async XLA Ops:
  0.0 23.2 %copy-start.1 = (bf16[7,128,1024]{2,1,0:T(8,128)(2,1)S(1)}, bf16[7,128,1024]{2,1,0:T(8,128)(2,1)}, u32[]{:S(2)}) copy-start(bf16[7,128,1024]{2,1,0:T(8,128)(2,1)} %bases.1) | copy-start | bytes 5505028
  5.3 17.9 %copy-start = (f32[4,240,256]{2,1,0:T(8,128)S(1)}, f32[4,240,256]{2,1,0:T(8,128)}, u32[]{:S(2)}) copy-start(f32[4,240,256]{2,1,0:T(8,128)} %get-tuple-element.47.send) | copy-start | bytes 2949124
  25.8 4.0 %collective-permute-start = (f32[1344,128]{1,0:T(8,128)S(1)}, f32[1344,128]{1,0:T(8,128)S(1)}, u32[]{:S(2)}, u32[]{:S(2)}) collective-permute-start(f32[1344,128]{1,0:T(8,128)S(1)} %shard_map.47.mine), channel_id=1, source_target_pairs={{0,4},{4,0},{8,12},{12,8},{16,20},{20,16},{24,28},{28,24},{32,36},... | collective-permute-start | bytes 2064392 | tf_op jit(solution)/shard_map/ppermute | solution.py:455
  49.9 6.6 %collective-permute-start.1 = (f32[208,128]{1,0:T(8,128)S(1)}, f32[208,128]{1,0:T(8,128)S(1)}, u32[]{:S(2)}, u32[]{:S(2)}) collective-permute-start(f32[208,128]{1,0:T(8,128)S(1)} %get-tuple-element.48.refs_0_), channel_id=1, source_target_pairs={{0,8},{4,12},{8,0},{12,4},{16,24},{20,28},{24,16},{28,20},{32,40},... | collective-permute-start | bytes 319496 | tf_op jit(solution)/shard_map/ppermute | solution.py:455
  53.2 0.8 copy-start.3
  57.3 11.2 %all-to-all-start.2 = ((f32[4,224,128]{2,1,0:T(8,128)}), f32[4,224,128]{2,1,0:T(8,128)S(1)}, u32[]{:S(2)}, u32[]{:S(2)}) async-start(f32[4,224,128]{2,1,0:T(8,128)} %shard_map.50), calls=%async_computation.2 | async-start | bytes 917504 | tf_op jit(solution)/shard_map/all_to_all | solution.py:432
  62.2 11.6 %collective-permute-start.2 = (f32[560,128]{1,0:T(8,128)S(1)}, f32[560,128]{1,0:T(8,128)S(1)}, u32[]{:S(2)}, u32[]{:S(2)}) collective-permute-start(f32[560,128]{1,0:T(8,128)S(1)} %get-tuple-element.53.later), channel_id=1, source_target_pairs={{0,8},{4,12},{8,0},{12,4},{16,24},{20,28},{24,16},{28,20},{32,40},... | collective-permute-start | bytes 860168 | tf_op jit(solution)/shard_map/ppermute | solution.py:455
  74.0 7.5 %copy-start.5 = (f32[128,128]{1,0:T(8,128)S(1)}, f32[128,128]{1,0:T(8,128)}, u32[]{:S(2)}) copy-start(f32[128,128]{1,0:T(8,128)} %get-tuple-element.62.refs_2_) | copy-start | bytes 196612
  74.0 7.5 %collective-permute-start.3 = (f32[176,128]{1,0:T(8,128)S(1)}, f32[176,128]{1,0:T(8,128)S(1)}, u32[]{:S(2)}, u32[]{:S(2)}) collective-permute-start(f32[176,128]{1,0:T(8,128)S(1)} %shard_map.52.refs_0_), channel_id=1, source_target_pairs={{0,16},{4,20},{8,24},{12,28},{16,0},{20,4},{24,8},{28,12},{32,48},... | collective-permute-start | bytes 270344 | tf_op jit(solution)/shard_map/ppermute | solution.py:455
  82.4 13.4 %all-to-all-start.3 = ((f32[4,304,128]{2,1,0:T(8,128)}), f32[4,304,128]{2,1,0:T(8,128)S(1)}, u32[]{:S(2)}, u32[]{:S(2)}) async-start(f32[4,304,128]{2,1,0:T(8,128)} %shard_map.54), calls=%async_computation.3 | async-start | bytes 1245184 | tf_op jit(solution)/shard_map/all_to_all | solution.py:432
  87.3 13.6 %collective-permute-start.4 = (f32[384,128]{1,0:T(8,128)S(1)}, f32[384,128]{1,0:T(8,128)S(1)}, u32[]{:S(2)}, u32[]{:S(2)}) collective-permute-start(f32[384,128]{1,0:T(8,128)S(1)} %get-tuple-element.60.later), channel_id=1, source_target_pairs={{0,16},{4,20},{8,24},{12,28},{16,0},{20,4},{24,8},{28,12},{32,48},... | collective-permute-start | bytes 589832 | tf_op jit(solution)/shard_map/ppermute | solution.py:455
  92.6 1.0 copy-start.4
  100.8 5.5 %copy-start.2 = (f32[1024,256]{1,0:T(8,128)S(1)}, f32[1024,256]{1,0:T(8,128)}, u32[]{:S(2)}) copy-start(f32[1024,256]{1,0:T(8,128)} %inverse_cols.1) | copy-start | bytes 3145732
  101.5 11.1 %collective-permute-start.5 = (f32[384,128]{1,0:T(8,128)S(1)}, f32[384,128]{1,0:T(8,128)S(1)}, u32[]{:S(2)}, u32[]{:S(2)}) collective-permute-start(f32[384,128]{1,0:T(8,128)S(1)} %shard_map.57.refs_0_), channel_id=1, source_target_pairs={{0,48},{4,52},{8,56},{12,60},{16,32},{20,36},{24,40},{28,44},{32,1... | collective-permute-start | bytes 589832 | tf_op jit(solution)/shard_map/ppermute | solution.py:455
  130.8 8.9 %collective-permute-start.6 = (f32[448,128]{1,0:T(8,128)S(1)}, f32[448,128]{1,0:T(8,128)S(1)}, u32[]{:S(2)}, u32[]{:S(2)}) collective-permute-start(f32[448,128]{1,0:T(8,128)S(1)} %get-tuple-element.76.mine), channel_id=1, source_target_pairs={{0,64},{4,68},{8,72},{12,76},{16,80},{20,84},{24,88},{28,92},{32,9... | collective-permute-start | bytes 688136 | tf_op jit(solution)/shard_map/ppermute | solution.py:455
  133.0 11.6 %collective-permute-start.7 = (f32[320,128]{1,0:T(8,128)S(1)}, f32[320,128]{1,0:T(8,128)S(1)}, u32[]{:S(2)}, u32[]{:S(2)}) collective-permute-start(f32[320,128]{1,0:T(8,128)S(1)} %shard_map.64.later), channel_id=1, source_target_pairs={{0,64},{4,68},{8,72},{12,76},{16,80},{20,84},{24,88},{28,92},{32,9... | collective-permute-start | bytes 491528 | tf_op jit(solution)/shard_map/ppermute | solution.py:455
  137.2 13.8 %collective-permute-start.9 = (f32[192,128]{1,0:T(8,128)S(1)}, f32[192,128]{1,0:T(8,128)S(1)}, u32[]{:S(2)}, u32[]{:S(2)}) collective-permute-start(f32[192,128]{1,0:T(8,128)S(1)} %shard_map.66.later), channel_id=1, source_target_pairs={{0,64},{4,68},{8,72},{12,76},{16,80},{20,84},{24,88},{28,92},{32,9... | collective-permute-start | bytes 294920 | tf_op jit(solution)/shard_map/ppermute | solution.py:455
  144.9 10.7 %collective-permute-start.8 = (f32[320,128]{1,0:T(8,128)S(1)}, f32[320,128]{1,0:T(8,128)S(1)}, u32[]{:S(2)}, u32[]{:S(2)}) collective-permute-start(f32[320,128]{1,0:T(8,128)S(1)} %shard_map.65.mine), channel_id=1, source_target_pairs={{0,128},{4,132},{8,136},{12,140},{16,144},{20,148},{24,152},{28,15... | collective-permute-start | bytes 491528 | tf_op jit(solution)/shard_map/ppermute | solution.py:455
  151.3 10.3 %collective-permute-start.10 = (f32[192,128]{1,0:T(8,128)S(1)}, f32[192,128]{1,0:T(8,128)S(1)}, u32[]{:S(2)}, u32[]{:S(2)}) collective-permute-start(f32[192,128]{1,0:T(8,128)S(1)} %shard_map.69.later), channel_id=1, source_target_pairs={{0,128},{4,132},{8,136},{12,140},{16,144},{20,148},{24,152},{28,15... | collective-permute-start | bytes 294920 | tf_op jit(solution)/shard_map/ppermute | solution.py:455
  161.6 5.2 %copy-start.6 = (s32[1,1024]{1,0:T(1,128)S(1)}, s32[1,1024]{1,0:T(1,128)}, u32[]{:S(2)}) copy-start(s32[1,1024]{1,0:T(1,128)} %refs_0_.1) | copy-start | bytes 12292
  161.9 18.7 %all-to-all-start.5 = ((f32[4,144,256]{2,1,0:T(8,128)}), f32[4,144,256]{2,1,0:T(8,128)S(1)}, u32[]{:S(2)}, u32[]{:S(2)}) async-start(f32[4,144,256]{2,1,0:T(8,128)} %shard_map.68), calls=%async_computation.5 | async-start | bytes 1179648 | tf_op jit(solution)/shard_map/all_to_all | solution.py:579
  167.0 13.5 %collective-permute-start.11 = (f32[144,128]{1,0:T(8,128)S(1)}, f32[144,128]{1,0:T(8,128)S(1)}, u32[]{:S(2)}, u32[]{:S(2)}) collective-permute-start(f32[144,128]{1,0:T(8,128)S(1)} %shard_map.70.mine), channel_id=1, source_target_pairs={{0,384},{4,388},{8,392},{12,396},{16,400},{20,404},{24,408},{28,41... | collective-permute-start | bytes 221192 | tf_op jit(solution)/shard_map/ppermute | solution.py:455

commit v10 on v9

--- a/solution.py
+++ b/solution.py
@@ -398,7 +398,7 @@
     groups, rows, _ = send.shape
     rank = weights.shape[1]
     own = rows - rank
-    carried = before[rank:, :] - exact_dot(weights[...], before[:rank, :], NN)
+    carried = before[rank:, :] - close_dot(weights[...], before[:rank, :])
     for group in range(groups):
         send[group, :rank, :] = carried[:rank]
         send[group, rank:, :] = carried[rank + group * own : rank + (group + 1) * own]
@@ -411,7 +411,7 @@
     top = exact_dot(mine[rank:, :] + arrived[rank:, :], inverse, NN)
     slope = jnp.concatenate([got[group, :rank, :] for group in range(groups)], 1)
     base = jnp.concatenate([got[group, rank:, :] for group in range(groups)], 1)
-    out[...] = dot_left_parts(base - exact_dot(top, slope, NN), hot[...], NN)
+    out[...] = dot_left_parts(base - close_dot(top, slope), hot[...], NN)
 
 
 def add_body(*refs):

time: 188 us -> 187 us (level)
  the two profiles are of different devices: /device:TPU:74 before, /device:TPU:10 now
where the time goes in v10:
time: 187 us; the launch traced here: 186 us
  starting transfers between devices  63.1 us (34%)
  Pallas kernels  57.8 us (31%)
  blocking collectives  44.4 us (24%)
  waiting for transfers between devices  18.3 us (10%)
  local copies, waits for them, and re-layouts  2.05 us (1%)
    pallas_call x26, Pallas kernels, run(): pl.pallas_call(body, out_shape=[shape_of(out) for out in outs], in_specs=...  52.6 us
    ppermute x12, starting transfers between devices, local(): swap = lambda block, height: lax.ppermute(block, 'leaf', route(height))  48.4 us
    all_to_all x1, blocking collectives, local(): got = lax.all_to_all(send, 'rhs', 0, 0)  17.9 us
    ppermute x12, waiting for transfers between devices, local(): swap = lambda block, height: lax.ppermute(block, 'leaf', route(height))  15 us
    all_to_all x1, blocking collectives, local(): everyone = lax.all_to_all(jnp.concatenate([shared, parts], 1), 'rhs', 0, 0)  14.2 us
    all_to_all x1, blocking collectives, sum_to_all(): return lax.all_to_all(send, 'rhs', 0, 0)  12.3 us
    all_to_all x2, starting transfers between devices, sum_to_all(): return lax.all_to_all(send, 'rhs', 0, 0)  9.8 us
    pallas_call x1, Pallas kernels, run_loading(): pl.pallas_call(loading, out_shape=[shape_of(out) for out in outs], in_spe...  5.24 us
  transfers between devices with their start and end apart: 15, of which 7 were waited for; matrix products, arithmetic and copies ran while one was open for 0% of the time, Pallas kernels for 16%

profile of v10, /device:TPU:10, one launch (start us, length us, event | category | flops | bytes accessed | tf_op | source)
XLA Modules:
  0.0 186.1 jit_solution(13423231819225793001)
XLA Ops:
  0.0 5.2 %shard_map.46 = (f32[4,240,256]{2,1,0:T(8,128)}, f32[128,128]{1,0:T(8,128)}) custom-call(s32[1,1024]{1,0:T(1,128)} %refs_0_.1, f32[16,1024]{1,0:T(8,128)} %refs_1_.1, f32[1024,256]{1,0:T(8,128)} %inverse_cols.1, bf16[7,128,1024]{2,1,0:T(8,128)(2,1)} %bases.1), custom_call_target="tpu_custom_call" | custom-call | flops 1000000000 | tf_op jit(solution)/shard_map/pallas_call | solution.py:124
  5.3 17.9 %all_to_all.30.got = f32[4,240,256]{2,1,0:T(8,128)S(1)} all-to-all(f32[4,240,256]{2,1,0:T(8,128)} %get-tuple-element.47.send), channel_id=1, replica_groups=mesh['leaf'=128,'rhs'=4] {'rhs'}, dimensions={0} | all-to-all | bytes 1966080 | tf_op jit(solution)/shard_map/all_to_all | solution.py:469
  23.2 2.6 %shard_map.47.mine = f32[1344,128]{1,0:T(8,128)S(1)} custom-call(f32[4,240,256]{2,1,0:T(8,128)S(1)} %all_to_all.30.got, f32[4,240,256]{2,1,0:T(8,128)S(1)} %copy-done, bf16[7,128,1024]{2,1,0:T(8,128)(2,1)S(1)} %copy-done.1), custom_call_target="tpu_custom_call" | custom-call | flops 1000000000 | tf_op jit(solution)/shard_map/pallas_call | solution.py:91
  25.8 1.9 %collective-permute-start = (f32[1344,128]{1,0:T(8,128)S(1)}, f32[1344,128]{1,0:T(8,128)S(1)}, u32[]{:S(2)}, u32[]{:S(2)}) collective-permute-start(f32[1344,128]{1,0:T(8,128)S(1)} %shard_map.47.mine), channel_id=1, source_target_pairs={{0,4},{4,0},{8,12},{12,8},{16,20},{20,16},{24,28},{28,24},{32,36},... | collective-permute-start | bytes 2064392 | tf_op jit(solution)/shard_map/ppermute | solution.py:455
  27.7 2.1 %collective-permute-done.arrived = f32[1344,128]{1,0:T(8,128)S(1)} collective-permute-done((f32[1344,128]{1,0:T(8,128)S(1)}, f32[1344,128]{1,0:T(8,128)S(1)}, u32[]{:S(2)}, u32[]{:S(2)}) %collective-permute-start) | collective-permute-done | bytes 688160 | tf_op jit(solution)/shard_map/ppermute | solution.py:455
  30.0 14.2 %all_to_all.31.everyone = f32[4,336,128]{2,1,0:T(8,128)S(1)} all-to-all(f32[4,336,128]{2,1,0:T(8,128)S(1)} %pad_maximum_fusion), channel_id=1, replica_groups=mesh['leaf'=128,'rhs'=4] {'rhs'}, dimensions={0} | all-to-all | bytes 1376256 | tf_op jit(solution)/shard_map/all_to_all | solution.py:476
  44.2 5.6 %shard_map.48 = (f32[208,128]{1,0:T(8,128)S(1)}, f32[768,128]{1,0:T(8,128)S(1)}, f32[208,128]{1,0:T(8,128)S(1)}, f32[128,128]{1,0:T(8,128)S(1)}, f32[16,128]{1,0:T(8,128)S(1)}) custom-call(f32[4,336,128]{2,1,0:T(8,128)S(1)} %all_to_all.31.everyone, f32[1344,128]{1,0:T(8,128)S(1)} %shard_map.47.mine, f32[1344,128]{1,0:T(8,128)S(1)} %collective-permute-done.arrived), custom_call_target="tpu_custom_call" | custom-call | flops 1000000000 | tf_op jit(solution)/shard_map/pallas_call | solution.py:91
  49.9 3.1 %collective-permute-start.1 = (f32[208,128]{1,0:T(8,128)S(1)}, f32[208,128]{1,0:T(8,128)S(1)}, u32[]{:S(2)}, u32[]{:S(2)}) collective-permute-start(f32[208,128]{1,0:T(8,128)S(1)} %get-tuple-element.48.refs_0_), channel_id=1, source_target_pairs={{0,8},{4,12},{8,0},{12,4},{16,24},{20,28},{24,16},{28,20},{32,40},... | collective-permute-start | bytes 319496 | tf_op jit(solution)/shard_map/ppermute | solution.py:455
  57.3 4.9 %all-to-all-start.2 = ((f32[4,224,128]{2,1,0:T(8,128)}), f32[4,224,128]{2,1,0:T(8,128)S(1)}, u32[]{:S(2)}, u32[]{:S(2)}) async-start(f32[4,224,128]{2,1,0:T(8,128)} %shard_map.50), calls=%async_computation.2 | async-start | bytes 917504 | tf_op jit(solution)/shard_map/all_to_all | solution.py:432
  62.2 3.0 %collective-permute-start.2 = (f32[560,128]{1,0:T(8,128)S(1)}, f32[560,128]{1,0:T(8,128)S(1)}, u32[]{:S(2)}, u32[]{:S(2)}) collective-permute-start(f32[560,128]{1,0:T(8,128)S(1)} %get-tuple-element.53.later), channel_id=1, source_target_pairs={{0,8},{4,12},{8,0},{12,4},{16,24},{20,28},{24,16},{28,20},{32,40},... | collective-permute-start | bytes 860168 | tf_op jit(solution)/shard_map/ppermute | solution.py:455
  65.2 3.2 %all-to-all-done.2.everyone = f32[4,224,128]{2,1,0:T(8,128)S(1)} async-done(((f32[4,224,128]{2,1,0:T(8,128)}), f32[4,224,128]{2,1,0:T(8,128)S(1)}, u32[]{:S(2)}, u32[]{:S(2)}) %all-to-all-start.2) | async-done | bytes 458784 | tf_op jit(solution)/shard_map/all_to_all | solution.py:432
  68.5 5.3 %shard_map.51 = (f32[640,128]{1,0:T(8,128)S(1)}, f32[176,128]{1,0:T(8,128)S(1)}, f32[128,128]{1,0:T(8,128)S(1)}) custom-call(s32[1]{0:T(128)} %bitcast.1.place, f32[4,224,128]{2,1,0:T(8,128)S(1)} %all-to-all-done.2.everyone), custom_call_target="tpu_custom_call" | custom-call | flops 1000000000 | tf_op jit(solution)/shard_map/pallas_call | solution.py:91
  74.0 4.6 %collective-permute-start.3 = (f32[176,128]{1,0:T(8,128)S(1)}, f32[176,128]{1,0:T(8,128)S(1)}, u32[]{:S(2)}, u32[]{:S(2)}) collective-permute-start(f32[176,128]{1,0:T(8,128)S(1)} %shard_map.52.refs_0_), channel_id=1, source_target_pairs={{0,16},{4,20},{8,24},{12,28},{16,0},{20,4},{24,8},{28,12},{32,48},... | collective-permute-start | bytes 270344 | tf_op jit(solution)/shard_map/ppermute | solution.py:455
  79.5 2.1 %collective-permute-done.3.refs_1_ = f32[176,128]{1,0:T(8,128)S(1)} collective-permute-done((f32[176,128]{1,0:T(8,128)S(1)}, f32[176,128]{1,0:T(8,128)S(1)}, u32[]{:S(2)}, u32[]{:S(2)}) %collective-permute-start.3) | collective-permute-done | bytes 90144 | tf_op jit(solution)/shard_map/ppermute | solution.py:455
  82.4 4.9 %all-to-all-start.3 = ((f32[4,304,128]{2,1,0:T(8,128)}), f32[4,304,128]{2,1,0:T(8,128)S(1)}, u32[]{:S(2)}, u32[]{:S(2)}) async-start(f32[4,304,128]{2,1,0:T(8,128)} %shard_map.54), calls=%async_computation.3 | async-start | bytes 1245184 | tf_op jit(solution)/shard_map/all_to_all | solution.py:432
  87.4 5.2 %collective-permute-start.4 = (f32[384,128]{1,0:T(8,128)S(1)}, f32[384,128]{1,0:T(8,128)S(1)}, u32[]{:S(2)}, u32[]{:S(2)}) collective-permute-start(f32[384,128]{1,0:T(8,128)S(1)} %get-tuple-element.60.later), channel_id=1, source_target_pairs={{0,16},{4,20},{8,24},{12,28},{16,0},{20,4},{24,8},{28,12},{32,48},... | collective-permute-start | bytes 589832 | tf_op jit(solution)/shard_map/ppermute | solution.py:455
  93.6 2.2 %shard_map.55 = (f32[640,256]{1,0:T(8,128)S(1)}, f32[256,256]{1,0:T(8,128)S(1)}) custom-call(f32[4,240,256]{2,1,0:T(8,128)S(1)} %copy-done, f32[768,128]{1,0:T(8,128)S(1)} %copy-done.4, f32[640,128]{1,0:T(8,128)S(1)} %get-tuple-element.64.weights2), custom_call_target="tpu_custom_call" | custom-call | flops 1000000000 | tf_op jit(solution)/shard_map/pallas_call | solution.py:91
  95.8 5.0 %shard_map.56 = (f32[512,128]{1,0:T(8,128)S(1)}, f32[144,128]{1,0:T(8,128)S(1)}, f32[128,128]{1,0:T(8,128)S(1)}) custom-call(s32[1]{0:T(128)} %bitcast.1.place, f32[4,304,128]{2,1,0:T(8,128)S(1)} %all-to-all-done.3.everyone), custom_call_target="tpu_custom_call" | custom-call | flops 1000000000 | tf_op jit(solution)/shard_map/pallas_call | solution.py:91
  101.5 4.8 %collective-permute-start.5 = (f32[384,128]{1,0:T(8,128)S(1)}, f32[384,128]{1,0:T(8,128)S(1)}, u32[]{:S(2)}, u32[]{:S(2)}) collective-permute-start(f32[384,128]{1,0:T(8,128)S(1)} %shard_map.57.refs_0_), channel_id=1, source_target_pairs={{0,48},{4,52},{8,56},{12,60},{16,32},{20,36},{24,40},{28,44},{32,1... | collective-permute-start | bytes 589832 | tf_op jit(solution)/shard_map/ppermute | solution.py:455
  108.0 5.3 %collective-permute-done.5.refs_1_ = f32[384,128]{1,0:T(8,128)S(1)} collective-permute-done((f32[384,128]{1,0:T(8,128)S(1)}, f32[384,128]{1,0:T(8,128)S(1)}, u32[]{:S(2)}, u32[]{:S(2)}) %collective-permute-start.5) | collective-permute-done | bytes 196640 | tf_op jit(solution)/shard_map/ppermute | solution.py:455
  113.3 12.3 %all_to_all.32.everyone = f32[4,384,128]{2,1,0:T(8,128)S(1)} all-to-all(f32[4,384,128]{2,1,0:T(8,128)S(1)} %shard_map.59), channel_id=1, replica_groups=mesh['leaf'=128,'rhs'=4] {'rhs'}, dimensions={0} | all-to-all | bytes 1572864 | tf_op jit(solution)/shard_map/all_to_all | solution.py:432
  125.6 5.5 %shard_map.60 = (f32[448,128]{1,0:T(8,128)S(1)}, f32[448,128]{1,0:T(8,128)S(1)}, f32[448,128]{1,0:T(8,128)S(1)}) custom-call(f32[4,384,128]{2,1,0:T(8,128)S(1)} %all_to_all.32.everyone), custom_call_target="tpu_custom_call" | custom-call | flops 1000000000 | tf_op jit(solution)/shard_map/pallas_call | solution.py:91
  131.2 4.3 %collective-permute-start.6 = (f32[448,128]{1,0:T(8,128)S(1)}, f32[448,128]{1,0:T(8,128)S(1)}, u32[]{:S(2)}, u32[]{:S(2)}) collective-permute-start(f32[448,128]{1,0:T(8,128)S(1)} %get-tuple-element.76.mine), channel_id=1, source_target_pairs={{0,64},{4,68},{8,72},{12,76},{16,80},{20,84},{24,88},{28,92},{32,9... | collective-permute-start | bytes 688136 | tf_op jit(solution)/shard_map/ppermute | solution.py:455
  135.8 1.9 %collective-permute-start.7 = (f32[320,128]{1,0:T(8,128)S(1)}, f32[320,128]{1,0:T(8,128)S(1)}, u32[]{:S(2)}, u32[]{:S(2)}) collective-permute-start(f32[320,128]{1,0:T(8,128)S(1)} %shard_map.64.later), channel_id=1, source_target_pairs={{0,64},{4,68},{8,72},{12,76},{16,80},{20,84},{24,88},{28,92},{32,9... | collective-permute-start | bytes 491528 | tf_op jit(solution)/shard_map/ppermute | solution.py:455
  138.0 3.9 %collective-permute-start.9 = (f32[192,128]{1,0:T(8,128)S(1)}, f32[192,128]{1,0:T(8,128)S(1)}, u32[]{:S(2)}, u32[]{:S(2)}) collective-permute-start(f32[192,128]{1,0:T(8,128)S(1)} %shard_map.66.later), channel_id=1, source_target_pairs={{0,64},{4,68},{8,72},{12,76},{16,80},{20,84},{24,88},{28,92},{32,9... | collective-permute-start | bytes 294920 | tf_op jit(solution)/shard_map/ppermute | solution.py:455
  142.4 4.9 %shard_map.62 = (f32[320,128]{1,0:T(8,128)S(1)}, f32[320,128]{1,0:T(8,128)S(1)}) custom-call(f32[448,128]{1,0:T(8,128)S(1)} %get-tuple-element.76.mine, f32[448,128]{1,0:T(8,128)S(1)} %collective-permute-done.6.arrived), custom_call_target="tpu_custom_call" | custom-call | flops 1000000000 | tf_op jit(solution)/shard_map/pallas_call | solution.py:91
  147.7 6.1 %collective-permute-start.8 = (f32[320,128]{1,0:T(8,128)S(1)}, f32[320,128]{1,0:T(8,128)S(1)}, u32[]{:S(2)}, u32[]{:S(2)}) collective-permute-start(f32[320,128]{1,0:T(8,128)S(1)} %shard_map.65.mine), channel_id=1, source_target_pairs={{0,128},{4,132},{8,136},{12,140},{16,144},{20,148},{24,152},{28,15... | collective-permute-start | bytes 491528 | tf_op jit(solution)/shard_map/ppermute | solution.py:455
  154.0 1.9 %collective-permute-start.10 = (f32[192,128]{1,0:T(8,128)S(1)}, f32[192,128]{1,0:T(8,128)S(1)}, u32[]{:S(2)}, u32[]{:S(2)}) collective-permute-start(f32[192,128]{1,0:T(8,128)S(1)} %shard_map.69.later), channel_id=1, source_target_pairs={{0,128},{4,132},{8,136},{12,140},{16,144},{20,148},{24,152},{28,15... | collective-permute-start | bytes 294920 | tf_op jit(solution)/shard_map/ppermute | solution.py:455
  158.3 4.9 %shard_map.67 = (f32[192,128]{1,0:T(8,128)S(1)}, f32[192,128]{1,0:T(8,128)S(1)}) custom-call(f32[320,128]{1,0:T(8,128)S(1)} %shard_map.65.mine, f32[320,128]{1,0:T(8,128)S(1)} %collective-permute-done.8.arrived), custom_call_target="tpu_custom_call" | custom-call | flops 1000000000 | tf_op jit(solution)/shard_map/pallas_call | solution.py:91
  164.4 4.9 %all-to-all-start.5 = ((f32[4,144,256]{2,1,0:T(8,128)}), f32[4,144,256]{2,1,0:T(8,128)S(1)}, u32[]{:S(2)}, u32[]{:S(2)}) async-start(f32[4,144,256]{2,1,0:T(8,128)} %shard_map.68), calls=%async_computation.5 | async-start | bytes 1179648 | tf_op jit(solution)/shard_map/all_to_all | solution.py:579
  169.6 7.6 %collective-permute-start.11 = (f32[144,128]{1,0:T(8,128)S(1)}, f32[144,128]{1,0:T(8,128)S(1)}, u32[]{:S(2)}, u32[]{:S(2)}) collective-permute-start(f32[144,128]{1,0:T(8,128)S(1)} %shard_map.70.mine), channel_id=1, source_target_pairs={{0,384},{4,388},{8,392},{12,396},{16,400},{20,404},{24,408},{28,41... | collective-permute-start | bytes 221192 | tf_op jit(solution)/shard_map/ppermute | solution.py:455
  179.5 6.6 %shard_map.72 = f32[16,1024]{1,0:T(8,128)} custom-call(f32[144,128]{1,0:T(8,128)S(1)} %shard_map.70.mine, f32[144,128]{1,0:T(8,128)S(1)} %collective-permute-done.11.arrived, f32[4,144,256]{2,1,0:T(8,128)S(1)} %all-to-all-done.5.got, bf16[1024,1024]{1,0:T(8,128)(2,1)S(1)} %shard_map.71.hot), custom_call_target="tpu_custom_call" | custom-call | flops 1000000000 | tf_op jit(solution)/shard_map/pallas_call | solution.py:91
  (48 shorter events, 17.6 us)
Async XLA Ops:
  0.0 23.2 %copy-start.1 = (bf16[7,128,1024]{2,1,0:T(8,128)(2,1)S(1)}, bf16[7,128,1024]{2,1,0:T(8,128)(2,1)}, u32[]{:S(2)}) copy-start(bf16[7,128,1024]{2,1,0:T(8,128)(2,1)} %bases.1) | copy-start | bytes 5505028
  5.3 17.9 %copy-start = (f32[4,240,256]{2,1,0:T(8,128)S(1)}, f32[4,240,256]{2,1,0:T(8,128)}, u32[]{:S(2)}) copy-start(f32[4,240,256]{2,1,0:T(8,128)} %get-tuple-element.47.send) | copy-start | bytes 2949124
  25.8 4.0 %collective-permute-start = (f32[1344,128]{1,0:T(8,128)S(1)}, f32[1344,128]{1,0:T(8,128)S(1)}, u32[]{:S(2)}, u32[]{:S(2)}) collective-permute-start(f32[1344,128]{1,0:T(8,128)S(1)} %shard_map.47.mine), channel_id=1, source_target_pairs={{0,4},{4,0},{8,12},{12,8},{16,20},{20,16},{24,28},{28,24},{32,36},... | collective-permute-start | bytes 2064392 | tf_op jit(solution)/shard_map/ppermute | solution.py:455
  49.9 6.6 %collective-permute-start.1 = (f32[208,128]{1,0:T(8,128)S(1)}, f32[208,128]{1,0:T(8,128)S(1)}, u32[]{:S(2)}, u32[]{:S(2)}) collective-permute-start(f32[208,128]{1,0:T(8,128)S(1)} %get-tuple-element.48.refs_0_), channel_id=1, source_target_pairs={{0,8},{4,12},{8,0},{12,4},{16,24},{20,28},{24,16},{28,20},{32,40},... | collective-permute-start | bytes 319496 | tf_op jit(solution)/shard_map/ppermute | solution.py:455
  53.9 0.8 copy-start.3
  57.3 11.2 %all-to-all-start.2 = ((f32[4,224,128]{2,1,0:T(8,128)}), f32[4,224,128]{2,1,0:T(8,128)S(1)}, u32[]{:S(2)}, u32[]{:S(2)}) async-start(f32[4,224,128]{2,1,0:T(8,128)} %shard_map.50), calls=%async_computation.2 | async-start | bytes 917504 | tf_op jit(solution)/shard_map/all_to_all | solution.py:432
  62.2 11.6 %collective-permute-start.2 = (f32[560,128]{1,0:T(8,128)S(1)}, f32[560,128]{1,0:T(8,128)S(1)}, u32[]{:S(2)}, u32[]{:S(2)}) collective-permute-start(f32[560,128]{1,0:T(8,128)S(1)} %get-tuple-element.53.later), channel_id=1, source_target_pairs={{0,8},{4,12},{8,0},{12,4},{16,24},{20,28},{24,16},{28,20},{32,40},... | collective-permute-start | bytes 860168 | tf_op jit(solution)/shard_map/ppermute | solution.py:455
  74.0 7.6 %copy-start.5 = (f32[128,128]{1,0:T(8,128)S(1)}, f32[128,128]{1,0:T(8,128)}, u32[]{:S(2)}) copy-start(f32[128,128]{1,0:T(8,128)} %get-tuple-element.62.refs_2_) | copy-start | bytes 196612
  74.0 7.6 %collective-permute-start.3 = (f32[176,128]{1,0:T(8,128)S(1)}, f32[176,128]{1,0:T(8,128)S(1)}, u32[]{:S(2)}, u32[]{:S(2)}) collective-permute-start(f32[176,128]{1,0:T(8,128)S(1)} %shard_map.52.refs_0_), channel_id=1, source_target_pairs={{0,16},{4,20},{8,24},{12,28},{16,0},{20,4},{24,8},{28,12},{32,48},... | collective-permute-start | bytes 270344 | tf_op jit(solution)/shard_map/ppermute | solution.py:455
  82.4 13.4 %all-to-all-start.3 = ((f32[4,304,128]{2,1,0:T(8,128)}), f32[4,304,128]{2,1,0:T(8,128)S(1)}, u32[]{:S(2)}, u32[]{:S(2)}) async-start(f32[4,304,128]{2,1,0:T(8,128)} %shard_map.54), calls=%async_computation.3 | async-start | bytes 1245184 | tf_op jit(solution)/shard_map/all_to_all | solution.py:432
  87.4 13.5 %collective-permute-start.4 = (f32[384,128]{1,0:T(8,128)S(1)}, f32[384,128]{1,0:T(8,128)S(1)}, u32[]{:S(2)}, u32[]{:S(2)}) collective-permute-start(f32[384,128]{1,0:T(8,128)S(1)} %get-tuple-element.60.later), channel_id=1, source_target_pairs={{0,16},{4,20},{8,24},{12,28},{16,0},{20,4},{24,8},{28,12},{32,48},... | collective-permute-start | bytes 589832 | tf_op jit(solution)/shard_map/ppermute | solution.py:455
  92.6 1.0 copy-start.4
  100.8 5.5 %copy-start.2 = (f32[1024,256]{1,0:T(8,128)S(1)}, f32[1024,256]{1,0:T(8,128)}, u32[]{:S(2)}) copy-start(f32[1024,256]{1,0:T(8,128)} %inverse_cols.1) | copy-start | bytes 3145732
  101.5 11.8 %collective-permute-start.5 = (f32[384,128]{1,0:T(8,128)S(1)}, f32[384,128]{1,0:T(8,128)S(1)}, u32[]{:S(2)}, u32[]{:S(2)}) collective-permute-start(f32[384,128]{1,0:T(8,128)S(1)} %shard_map.57.refs_0_), channel_id=1, source_target_pairs={{0,48},{4,52},{8,56},{12,60},{16,32},{20,36},{24,40},{28,44},{32,1... | collective-permute-start | bytes 589832 | tf_op jit(solution)/shard_map/ppermute | solution.py:455
  131.2 11.3 %collective-permute-start.6 = (f32[448,128]{1,0:T(8,128)S(1)}, f32[448,128]{1,0:T(8,128)S(1)}, u32[]{:S(2)}, u32[]{:S(2)}) collective-permute-start(f32[448,128]{1,0:T(8,128)S(1)} %get-tuple-element.76.mine), channel_id=1, source_target_pairs={{0,64},{4,68},{8,72},{12,76},{16,80},{20,84},{24,88},{28,92},{32,9... | collective-permute-start | bytes 688136 | tf_op jit(solution)/shard_map/ppermute | solution.py:455
  135.8 11.6 %collective-permute-start.7 = (f32[320,128]{1,0:T(8,128)S(1)}, f32[320,128]{1,0:T(8,128)S(1)}, u32[]{:S(2)}, u32[]{:S(2)}) collective-permute-start(f32[320,128]{1,0:T(8,128)S(1)} %shard_map.64.later), channel_id=1, source_target_pairs={{0,64},{4,68},{8,72},{12,76},{16,80},{20,84},{24,88},{28,92},{32,9... | collective-permute-start | bytes 491528 | tf_op jit(solution)/shard_map/ppermute | solution.py:455
  138.0 15.8 %collective-permute-start.9 = (f32[192,128]{1,0:T(8,128)S(1)}, f32[192,128]{1,0:T(8,128)S(1)}, u32[]{:S(2)}, u32[]{:S(2)}) collective-permute-start(f32[192,128]{1,0:T(8,128)S(1)} %shard_map.66.later), channel_id=1, source_target_pairs={{0,64},{4,68},{8,72},{12,76},{16,80},{20,84},{24,88},{28,92},{32,9... | collective-permute-start | bytes 294920 | tf_op jit(solution)/shard_map/ppermute | solution.py:455
  147.7 10.6 %collective-permute-start.8 = (f32[320,128]{1,0:T(8,128)S(1)}, f32[320,128]{1,0:T(8,128)S(1)}, u32[]{:S(2)}, u32[]{:S(2)}) collective-permute-start(f32[320,128]{1,0:T(8,128)S(1)} %shard_map.65.mine), channel_id=1, source_target_pairs={{0,128},{4,132},{8,136},{12,140},{16,144},{20,148},{24,152},{28,15... | collective-permute-start | bytes 491528 | tf_op jit(solution)/shard_map/ppermute | solution.py:455
  154.0 10.1 %collective-permute-start.10 = (f32[192,128]{1,0:T(8,128)S(1)}, f32[192,128]{1,0:T(8,128)S(1)}, u32[]{:S(2)}, u32[]{:S(2)}) collective-permute-start(f32[192,128]{1,0:T(8,128)S(1)} %shard_map.69.later), channel_id=1, source_target_pairs={{0,128},{4,132},{8,136},{12,140},{16,144},{20,148},{24,152},{28,15... | collective-permute-start | bytes 294920 | tf_op jit(solution)/shard_map/ppermute | solution.py:455
  164.2 5.2 %copy-start.6 = (s32[1,1024]{1,0:T(1,128)S(1)}, s32[1,1024]{1,0:T(1,128)}, u32[]{:S(2)}) copy-start(s32[1,1024]{1,0:T(1,128)} %refs_0_.1) | copy-start | bytes 12292
  164.4 15.1 %all-to-all-start.5 = ((f32[4,144,256]{2,1,0:T(8,128)}), f32[4,144,256]{2,1,0:T(8,128)S(1)}, u32[]{:S(2)}, u32[]{:S(2)}) async-start(f32[4,144,256]{2,1,0:T(8,128)} %shard_map.68), calls=%async_computation.5 | async-start | bytes 1179648 | tf_op jit(solution)/shard_map/all_to_all | solution.py:579
  169.6 9.9 %collective-permute-start.11 = (f32[144,128]{1,0:T(8,128)S(1)}, f32[144,128]{1,0:T(8,128)S(1)}, u32[]{:S(2)}, u32[]{:S(2)}) collective-permute-start(f32[144,128]{1,0:T(8,128)S(1)} %shard_map.70.mine), channel_id=1, source_target_pairs={{0,384},{4,388},{8,392},{12,396},{16,400},{20,404},{24,408},{28,41... | collective-permute-start | bytes 221192 | tf_op jit(solution)/shard_map/ppermute | solution.py:455
